TPU v7x, 32 devices: a whole 2x2x4 slice. The times are simulated.
32 devices in a mesh: seq: 2 (over y), ctx: 4 (over x, core), wt: 4 (over z).
Axes of the slice: x: 2, y: 2, z: 4, core: 2. Of those that a mesh axis runs over, the one named last changes fastest.
Arguments:
- tokens: bfloat16 [16, 1024, 768], P(('seq', 'wt'), 'ctx'), may hold values from -6 to 6
- cotangent: bfloat16 [16, 1024, 768], P(('seq', 'wt'), 'ctx'), may hold values from -6 to 6
- segment_ids: int32 [16, 1024], P(('seq', 'wt'), 'ctx'), may hold values from 0 to 4, as said below
- lengths: int32 [16, 4], P(('seq', 'wt')), may hold values from 32 to 928, as said below
- w_query: bfloat16 [768, 768], P('wt'), may hold values from -0.21875 to 0.21875
- b_query: bfloat16 [768], P('wt'), may hold values from -3 to 3
- w_key: bfloat16 [768, 768], P('wt'), may hold values from -0.21875 to 0.21875
- w_value: bfloat16 [768, 768], P('wt'), may hold values from -0.21875 to 0.21875
- b_value: bfloat16 [768], P('wt'), may hold values from -3 to 3
- w_attn: bfloat16 [768, 768], P('wt'), may hold values from -1.75 to 1.75
- b_attn: bfloat16 [768], P('wt'), may hold values from -2 to 2
- ln1_gain: bfloat16 [768], P('wt'), may hold values from 0.5 to 1.5
- ln1_shift: bfloat16 [768], P('wt'), may hold values from -2 to 2
- w_inner: bfloat16 [768, 3072], P('wt'), may hold values from -0.21875 to 0.21875
- b_inner: bfloat16 [3072], P('wt'), may hold values from -3 to 3
- w_outer: bfloat16 [3072, 768], P('wt'), may hold values from -0.109375 to 0.109375
- b_outer: bfloat16 [768], P('wt'), may hold values from -2 to 2
- ln2_gain: bfloat16 [768], P('wt'), may hold values from 0.5 to 1.5
- ln2_shift: bfloat16 [768], P('wt'), may hold values from -2 to 2
Outputs:
- layer_out: bfloat16 [16, 1024, 768], P(('seq', 'wt'), 'ctx')
- grad_input: bfloat16 [16, 1024, 768], P(('seq', 'wt'), 'ctx')
- grad_w_query: float32 [768, 768], P('wt')
- grad_b_query: float32 [768], P('wt')
- grad_w_key: float32 [768, 768], P('wt')
- grad_w_value: float32 [768, 768], P('wt')
- grad_b_value: float32 [768], P('wt')
- grad_w_attn: float32 [768, 768], P('wt')
- grad_b_attn: float32 [768], P('wt')
- grad_ln1_gain: float32 [768], P('wt')
- grad_ln1_shift: float32 [768], P('wt')
- grad_w_inner: float32 [768, 3072], P('wt')
- grad_b_inner: float32 [3072], P('wt')
- grad_w_outer: float32 [3072, 768], P('wt')
- grad_b_outer: float32 [768], P('wt')
- grad_ln2_gain: float32 [768], P('wt')
- grad_ln2_shift: float32 [768], P('wt')
Inputs may be any that keep to these rules, and one draw needn't show every extreme that they name: `lengths`: the 4 documents of a sequence lie end to end from its first position, and the positions after them are padding; among the 2 sequences that one device holds, one has a single document of 1024 - 3 * max(1, 32) positions, at a place among its documents that varies, and its other documents have max(1, 32) positions each; every other sequence has documents of 64 to 256 positions. `segment_ids`: position t holds d + 1 where it lies in the sequence's document d (counted from 0 in the order of lengths), and 0 in the padding.
All inputs are finite; a program needn't handle non-finite values.
Results may differ from a plain program's by a relative error of at most 0.02.
Values may be sent and summed in bfloat16 or wider, within the bound.
No kernel may reach another device: no remote copies, remote signals or barrier semaphores. Data moves between devices by JAX's collectives and lax.ppermute only.
A program may use at most 320 MiB of HBM per device.

v0:
```python
import math

import jax
import jax.numpy as jnp
from jax import lax
from jax.sharding import PartitionSpec as P

H = 12
HD = 64


NEG = -1000000000.0
EPS = 1e-05


def product(former, latter):
    return jnp.dot(former, latter, preferred_element_type=jnp.float32)


def over_rows(former, latter):
    return lax.dot_general(
        former, latter, (((0,), (0,)), ((), ())), preferred_element_type=jnp.float32
    )


def against(former, latter):
    return lax.dot_general(
        former, latter, (((1,), (1,)), ((), ())), preferred_element_type=jnp.float32
    )


def norm_rows(values, gain, shift):
    center = jnp.mean(values, axis=-1, keepdims=True)
    offset = values - center
    spread = jnp.mean(offset * offset, axis=-1, keepdims=True)
    return offset * lax.rsqrt(spread + EPS) * gain + shift


def exact_gelu(values):
    return jax.nn.gelu(values, approximate=False)


def key_segments(doc_lens, length):
    doc_ends = jnp.cumsum(doc_lens, axis=-1)
    places = jnp.arange(length, dtype=jnp.int32)
    passed = jnp.sum((places[None, :, None] >= doc_ends[:, None, :]).astype(jnp.int32), axis=-1)
    return jnp.where(places[None, :] < doc_ends[:, -1:], passed + 1, 0)


def to_items(matrix, groups):
    seq_count, length, model_width = matrix.shape
    per_group = model_width // (groups * HD)
    shaped = matrix.reshape(seq_count, length, groups, per_group, HD)
    return shaped.transpose(0, 2, 3, 1, 4).reshape(seq_count * groups, per_group, length, HD)


def from_items(blocks, seq_count):
    count_items, per_group, length, head_size = blocks.shape
    groups = count_items // seq_count
    shaped = blocks.reshape(seq_count, groups, per_group, length, head_size)
    return shaped.transpose(0, 3, 1, 2, 4).reshape(
        seq_count, length, groups * per_group * head_size
    )


def masked_scores(head_q, head_k, q_seg, k_seg, factor):
    scores = jnp.einsum("hqd,hkd->hqk", head_q, head_k, preferred_element_type=jnp.float32) * factor
    matching = q_seg[:, None] == k_seg[None, :]
    return jnp.where(matching[None], scores, NEG)


def body(
    tokens,
    cotangent,
    segment_ids,
    lengths,
    w_query,
    b_query,
    w_key,
    w_value,
    b_value,
    w_attn,
    b_attn,
    ln1_gain,
    ln1_shift,
    w_inner,
    b_inner,
    w_outer,
    b_outer,
    ln2_gain,
    ln2_shift,
):
    shards = (
        w_query,
        b_query,
        w_key,
        w_value,
        b_value,
        w_attn,
        b_attn,
        ln1_gain,
        ln1_shift,
        w_inner,
        b_inner,
        w_outer,
        b_outer,
        ln2_gain,
        ln2_shift,
    )
    seq_count, shard_len, model_width = tokens.shape
    row_count = seq_count * shard_len
    groups = H // math.gcd(H, 4)
    factor = 1.0 / math.sqrt(HD)
    full = (
        lax.all_gather(shards[0], "wt", axis=0, tiled=True),
        lax.all_gather(shards[1], "wt", axis=0, tiled=True),
        lax.all_gather(shards[2], "wt", axis=0, tiled=True),
        lax.all_gather(shards[3], "wt", axis=0, tiled=True),
        lax.all_gather(shards[4], "wt", axis=0, tiled=True),
        lax.all_gather(shards[5], "wt", axis=0, tiled=True),
        lax.all_gather(shards[6], "wt", axis=0, tiled=True),
        lax.all_gather(shards[7], "wt", axis=0, tiled=True),
        lax.all_gather(shards[8], "wt", axis=0, tiled=True),
        lax.all_gather(shards[9], "wt", axis=0, tiled=True),
        lax.all_gather(shards[10], "wt", axis=0, tiled=True),
        lax.all_gather(shards[11], "wt", axis=0, tiled=True),
        lax.all_gather(shards[12], "wt", axis=0, tiled=True),
        lax.all_gather(shards[13], "wt", axis=0, tiled=True),
        lax.all_gather(shards[14], "wt", axis=0, tiled=True),
    )
    rows = tokens.reshape(row_count, model_width)
    query = (product(rows, full[0]) + full[1].astype(jnp.float32)).astype(jnp.bfloat16)
    key_rows = product(rows, full[2]).astype(jnp.bfloat16)
    value_rows = (product(rows, full[3]) + full[4].astype(jnp.float32)).astype(jnp.bfloat16)
    local_kv = (
        key_rows.reshape(seq_count, shard_len, model_width),
        value_rows.reshape(seq_count, shard_len, model_width),
    )
    whole_kv = (
        lax.all_gather(local_kv[0], "ctx", axis=1, tiled=True),
        lax.all_gather(local_kv[1], "ctx", axis=1, tiled=True),
    )
    seq_len = whole_kv[0].shape[1]
    key_segs = jnp.repeat(key_segments(lengths, seq_len), groups, axis=0)
    query_segs = jnp.repeat(segment_ids, groups, axis=0)
    query_items = to_items(query.reshape(seq_count, shard_len, model_width), groups)
    key_items = to_items(whole_kv[0], groups)
    value_items = to_items(whole_kv[1], groups)

    def attend(item):
        head_q, head_k, head_v, q_seg, k_seg = item
        scores = masked_scores(head_q, head_k, q_seg, k_seg, factor)
        highest = jnp.max(scores, axis=-1, keepdims=True)
        totals = jnp.sum(jnp.exp(scores - highest), axis=-1, keepdims=True)
        log_sum = highest + jnp.log(totals)
        probs = jnp.exp(scores - log_sum).astype(jnp.bfloat16)
        mixed = jnp.einsum("hqk,hkd->hqd", probs, head_v, preferred_element_type=jnp.float32)
        return (mixed, log_sum[..., 0])

    attn_items, log_sums = lax.map(
        attend, (query_items, key_items, value_items, query_segs, key_segs)
    )
    attn = from_items(attn_items, seq_count).reshape(row_count, model_width).astype(jnp.bfloat16)
    first_sum = rows.astype(jnp.float32) + product(attn, full[5]) + full[6].astype(jnp.float32)
    hidden, first_pull = jax.vjp(
        norm_rows, first_sum, full[7].astype(jnp.float32), full[8].astype(jnp.float32)
    )
    hidden_low = hidden.astype(jnp.bfloat16)
    inner = product(hidden_low, full[9]) + full[10].astype(jnp.float32)
    active, gelu_pull = jax.vjp(exact_gelu, inner)
    active_low = active.astype(jnp.bfloat16)
    second_sum = hidden + product(active_low, full[11]) + full[12].astype(jnp.float32)
    result, second_pull = jax.vjp(
        norm_rows, second_sum, full[13].astype(jnp.float32), full[14].astype(jnp.float32)
    )
    layer_out = result.astype(jnp.bfloat16).reshape(tokens.shape)
    back = (
        lax.all_gather(shards[0], "wt", axis=0, tiled=True),
        lax.all_gather(shards[1], "wt", axis=0, tiled=True),
        lax.all_gather(shards[2], "wt", axis=0, tiled=True),
        lax.all_gather(shards[3], "wt", axis=0, tiled=True),
        lax.all_gather(shards[4], "wt", axis=0, tiled=True),
        lax.all_gather(shards[5], "wt", axis=0, tiled=True),
        lax.all_gather(shards[6], "wt", axis=0, tiled=True),
        lax.all_gather(shards[7], "wt", axis=0, tiled=True),
        lax.all_gather(shards[8], "wt", axis=0, tiled=True),
        lax.all_gather(shards[9], "wt", axis=0, tiled=True),
        lax.all_gather(shards[10], "wt", axis=0, tiled=True),
        lax.all_gather(shards[11], "wt", axis=0, tiled=True),
        lax.all_gather(shards[12], "wt", axis=0, tiled=True),
        lax.all_gather(shards[13], "wt", axis=0, tiled=True),
        lax.all_gather(shards[14], "wt", axis=0, tiled=True),
    )
    back_kv = (
        lax.all_gather(local_kv[0], "ctx", axis=1, tiled=True),
        lax.all_gather(local_kv[1], "ctx", axis=1, tiled=True),
    )
    back_keys = to_items(back_kv[0], groups)
    back_values = to_items(back_kv[1], groups)
    live = (segment_ids != 0).astype(jnp.float32).reshape(row_count, 1)
    grad_rows = cotangent.reshape(row_count, model_width).astype(jnp.float32) * live
    d_second, d_gain_two, d_shift_two = second_pull(grad_rows)
    d_outer = d_second.astype(jnp.bfloat16)
    g_w_outer = over_rows(active_low, d_outer)
    g_b_outer = jnp.sum(d_outer.astype(jnp.float32), axis=0)
    d_inner = gelu_pull(against(d_outer, back[11]))[0].astype(jnp.bfloat16)
    g_w_inner = over_rows(hidden_low, d_inner)
    g_b_inner = jnp.sum(d_inner.astype(jnp.float32), axis=0)
    d_hidden = d_second + against(d_inner, back[9])
    d_first, d_gain_one, d_shift_one = first_pull(d_hidden)
    d_proj = d_first.astype(jnp.bfloat16)
    g_w_attn = over_rows(attn, d_proj)
    g_b_attn = jnp.sum(d_proj.astype(jnp.float32), axis=0)
    d_attn = against(d_proj, back[5]).astype(jnp.bfloat16)
    d_attn_seq = d_attn.reshape(seq_count, shard_len, model_width)
    d_items = to_items(d_attn_seq, groups)

    def attend_back(item):
        head_q, head_k, head_v, q_seg, k_seg, log_sum, head_d = item
        scores = masked_scores(head_q, head_k, q_seg, k_seg, factor)
        probs = jnp.exp(scores - log_sum[..., None])
        d_probs = jnp.einsum("hqd,hkd->hqk", head_d, head_v, preferred_element_type=jnp.float32)
        center = jnp.sum(probs * d_probs, axis=-1, keepdims=True)
        d_scores = (probs * (d_probs - center)).astype(jnp.bfloat16)
        d_vals = jnp.einsum(
            "hqk,hqd->hkd", probs.astype(jnp.bfloat16), head_d, preferred_element_type=jnp.float32
        )
        d_q = (
            jnp.einsum("hqk,hkd->hqd", d_scores, head_k, preferred_element_type=jnp.float32)
            * factor
        )
        d_k = (
            jnp.einsum("hqk,hqd->hkd", d_scores, head_q, preferred_element_type=jnp.float32)
            * factor
        )
        return (d_q, d_k, d_vals)

    dq_items, dk_items, dv_items = lax.map(
        attend_back, (query_items, back_keys, back_values, query_segs, key_segs, log_sums, d_items)
    )
    d_query = from_items(dq_items, seq_count).reshape(row_count, model_width).astype(jnp.bfloat16)
    partial_kv = (from_items(dk_items, seq_count), from_items(dv_items, seq_count))
    own_kv = (
        lax.psum_scatter(
            partial_kv[0].astype(jnp.bfloat16), "ctx", scatter_dimension=1, tiled=True
        ).astype(jnp.float32),
        lax.psum_scatter(
            partial_kv[1].astype(jnp.bfloat16), "ctx", scatter_dimension=1, tiled=True
        ).astype(jnp.float32),
    )
    d_key = own_kv[0].reshape(row_count, model_width).astype(jnp.bfloat16)
    d_value = own_kv[1].reshape(row_count, model_width).astype(jnp.bfloat16)
    g_w_query = over_rows(rows, d_query)
    g_b_query = jnp.sum(d_query.astype(jnp.float32), axis=0)
    g_w_key = over_rows(rows, d_key)
    g_w_value = over_rows(rows, d_value)
    g_b_value = jnp.sum(d_value.astype(jnp.float32), axis=0)
    input_sum = (
        d_first + against(d_query, back[0]) + against(d_key, back[2]) + against(d_value, back[3])
    )
    grad_input = input_sum.astype(jnp.bfloat16).reshape(tokens.shape)
    grads = (
        g_w_query,
        g_b_query,
        g_w_key,
        g_w_value,
        g_b_value,
        g_w_attn,
        g_b_attn,
        d_gain_one,
        d_shift_one,
        g_w_inner,
        g_b_inner,
        g_w_outer,
        g_b_outer,
        d_gain_two,
        d_shift_two,
    )
    shares = (
        lax.psum_scatter(
            grads[0].astype(jnp.bfloat16), "wt", scatter_dimension=0, tiled=True
        ).astype(jnp.float32),
        lax.psum_scatter(
            grads[1].astype(jnp.bfloat16), "wt", scatter_dimension=0, tiled=True
        ).astype(jnp.float32),
        lax.psum_scatter(
            grads[2].astype(jnp.bfloat16), "wt", scatter_dimension=0, tiled=True
        ).astype(jnp.float32),
        lax.psum_scatter(
            grads[3].astype(jnp.bfloat16), "wt", scatter_dimension=0, tiled=True
        ).astype(jnp.float32),
        lax.psum_scatter(
            grads[4].astype(jnp.bfloat16), "wt", scatter_dimension=0, tiled=True
        ).astype(jnp.float32),
        lax.psum_scatter(
            grads[5].astype(jnp.bfloat16), "wt", scatter_dimension=0, tiled=True
        ).astype(jnp.float32),
        lax.psum_scatter(
            grads[6].astype(jnp.bfloat16), "wt", scatter_dimension=0, tiled=True
        ).astype(jnp.float32),
        lax.psum_scatter(
            grads[7].astype(jnp.bfloat16), "wt", scatter_dimension=0, tiled=True
        ).astype(jnp.float32),
        lax.psum_scatter(
            grads[8].astype(jnp.bfloat16), "wt", scatter_dimension=0, tiled=True
        ).astype(jnp.float32),
        lax.psum_scatter(
            grads[9].astype(jnp.bfloat16), "wt", scatter_dimension=0, tiled=True
        ).astype(jnp.float32),
        lax.psum_scatter(
            grads[10].astype(jnp.bfloat16), "wt", scatter_dimension=0, tiled=True
        ).astype(jnp.float32),
        lax.psum_scatter(
            grads[11].astype(jnp.bfloat16), "wt", scatter_dimension=0, tiled=True
        ).astype(jnp.float32),
        lax.psum_scatter(
            grads[12].astype(jnp.bfloat16), "wt", scatter_dimension=0, tiled=True
        ).astype(jnp.float32),
        lax.psum_scatter(
            grads[13].astype(jnp.bfloat16), "wt", scatter_dimension=0, tiled=True
        ).astype(jnp.float32),
        lax.psum_scatter(
            grads[14].astype(jnp.bfloat16), "wt", scatter_dimension=0, tiled=True
        ).astype(jnp.float32),
    )
    summed = (
        lax.psum(shares[0].astype(jnp.bfloat16), ("seq", "ctx")).astype(jnp.float32),
        lax.psum(shares[1].astype(jnp.bfloat16), ("seq", "ctx")).astype(jnp.float32),
        lax.psum(shares[2].astype(jnp.bfloat16), ("seq", "ctx")).astype(jnp.float32),
        lax.psum(shares[3].astype(jnp.bfloat16), ("seq", "ctx")).astype(jnp.float32),
        lax.psum(shares[4].astype(jnp.bfloat16), ("seq", "ctx")).astype(jnp.float32),
        lax.psum(shares[5].astype(jnp.bfloat16), ("seq", "ctx")).astype(jnp.float32),
        lax.psum(shares[6].astype(jnp.bfloat16), ("seq", "ctx")).astype(jnp.float32),
        lax.psum(shares[7].astype(jnp.bfloat16), ("seq", "ctx")).astype(jnp.float32),
        lax.psum(shares[8].astype(jnp.bfloat16), ("seq", "ctx")).astype(jnp.float32),
        lax.psum(shares[9].astype(jnp.bfloat16), ("seq", "ctx")).astype(jnp.float32),
        lax.psum(shares[10].astype(jnp.bfloat16), ("seq", "ctx")).astype(jnp.float32),
        lax.psum(shares[11].astype(jnp.bfloat16), ("seq", "ctx")).astype(jnp.float32),
        lax.psum(shares[12].astype(jnp.bfloat16), ("seq", "ctx")).astype(jnp.float32),
        lax.psum(shares[13].astype(jnp.bfloat16), ("seq", "ctx")).astype(jnp.float32),
        lax.psum(shares[14].astype(jnp.bfloat16), ("seq", "ctx")).astype(jnp.float32),
    )
    return (layer_out, grad_input) + tuple(summed)


def solution(mesh):
    in_specs = (
        P(("seq", "wt"), "ctx", None),
        P(("seq", "wt"), "ctx", None),
        P(("seq", "wt"), "ctx"),
        P(("seq", "wt"), None),
        P("wt", None),
        P("wt"),
        P("wt", None),
        P("wt", None),
        P("wt"),
        P("wt", None),
        P("wt"),
        P("wt"),
        P("wt"),
        P("wt", None),
        P("wt"),
        P("wt", None),
        P("wt"),
        P("wt"),
        P("wt"),
    )
    out_specs = (
        P(("seq", "wt"), "ctx", None),
        P(("seq", "wt"), "ctx", None),
        P("wt", None),
        P("wt"),
        P("wt", None),
        P("wt", None),
        P("wt"),
        P("wt", None),
        P("wt"),
        P("wt"),
        P("wt"),
        P("wt", None),
        P("wt"),
        P("wt", None),
        P("wt"),
        P("wt"),
        P("wt"),
    )
    return jax.shard_map(body, mesh=mesh, in_specs=in_specs, out_specs=out_specs, check_vma=False)
```

profile of v0, /device:TPU:0, one launch (start us, length us, event | category | flops | bytes accessed | tf_op | source)
XLA Modules:
  0.0 968.9 jit_solution(11220610871833606484)
XLA Ops:
  17.3 21.1 %all-reduce.20 = (bf16[768]{0:T(1024)(128)(2,1)S(1)}, bf16[768]{0:T(1024)(128)(2,1)S(1)}, bf16[768]{0:T(1024)(128)(2,1)S(1)}, bf16[768]{0:T(1024)(128)(2,1)S(1)}...) all-reduce(bf16[768]{0:T(1024)(128)(2,1)S(1)} %dynamic-update-slice, ...), channel_id=1, replica_groups=mesh['seq'=2,'ctx'=4,'wt'=4] {'wt'}, use_global_device_ids=true, to_apply=%add | all-reduce | flops 5376 | bytes 21504
  38.4 4.9 all-gather.16.cloned.1.call-done
  43.3 2.4 add_convert_fusion.3
  46.9 27.5 %all-gather.12.cloned.1.call-done = bf16[768,768]{1,0:T(8,128)(2,1)} async-done(((bf16[192,768]{1,0:T(8,128)(2,1)}), bf16[768,768]{1,0:T(8,128)(2,1)}) %all-gather.12.cloned.1.call-update) | async-done | bytes 1179664 | tf_op jit(solution)/shard_map/all_gather | solution.py:117
  81.1 13.8 %all-gather = bf16[4,1,768]{2,1,0:T(2,128)(2,1)S(1)} all-gather(bf16[1,1,768]{2,1,0:T(2,128)(2,1)S(1)} %reshape.309), channel_id=1, replica_groups=mesh['seq'=2,'ctx'=4,'wt'=4] {'wt'}, dimensions={0}, use_global_device_ids=true | all-gather | bytes 7680 | tf_op jit(solution)/shard_map/all_gather | solution.py:125
  95.0 10.8 %all-gather.10.cloned.1.call-done = bf16[768,768]{1,0:T(8,128)(2,1)} async-done(((bf16[192,768]{1,0:T(8,128)(2,1)}), bf16[768,768]{1,0:T(8,128)(2,1)}) %all-gather.10.cloned.1.call-update) | async-done | bytes 1179664 | tf_op jit(solution)/shard_map/all_gather | solution.py:115
  108.4 27.4 %all-gather.18.cloned.1.call-done = bf16[2,1024,768]{1,2,0:T(8,128)(2,1)} async-done(((bf16[2,256,768]{1,2,0:T(8,128)(2,1)}), bf16[2,1024,768]{1,2,0:T(8,128)(2,1)}) %all-gather.18.cloned.1.call-update) | async-done | bytes 3145744 | tf_op jit(solution)/shard_map/all_gather | solution.py:141
  135.8 30.9 %all-gather.14.cloned.1.call-done = bf16[2,1024,768]{1,2,0:T(8,128)(2,1)} async-done(((bf16[2,256,768]{1,2,0:T(8,128)(2,1)}), bf16[2,1024,768]{1,2,0:T(8,128)(2,1)}) %all-gather.14.cloned.1.call-update) | async-done | bytes 3145744 | tf_op jit(solution)/shard_map/all_gather | solution.py:140
  166.9 34.3 %while.26 = (s32[]{:T(128)}, bf16[6,4,256,64]{2,3,1,0:T(8,128)(2,1)S(1)}, f32[6,4,256]{2,1,0:T(4,128)S(1)}, s32[6,256]{1,0:T(8,128)S(1)}, s32[6,1024]{1,0:T(8,12...) while((s32[]{:T(128)}, ...), condition=%wide.region_5.6_spmd, body=%wide.region_2.5_spmd.sunk | while | flops 280230912 | bytes 15123561 | solution.py:160
  176.1 2.2 fusion.134
  202.2 2.7 fusion.77
  205.2 83.6 %all-gather.22.cloned.1.call-done = bf16[768,3072]{1,0:T(8,128)(2,1)} async-done(((bf16[192,3072]{1,0:T(8,128)(2,1)}), bf16[768,3072]{1,0:T(8,128)(2,1)}) %all-gather.22.cloned.1.call-update) | async-done | bytes 4718608 | tf_op jit(solution)/shard_map/all_gather | solution.py:124
  288.8 19.8 %multiply_convert_fusion.1 = (bf16[512,3072]{1,0:T(8,128)(2,1)}, f32[512,3072]{1,0:T(8,128)}, f32[512,3072]{1,0:T(8,128)}) fusion(f32[3072]{0:T(1024)S(1)} %bitcast.251, bf16[768,3072]{1,0:T(8,128)(2,1)} %all-gather.22.cloned.1.call-done, f32[512,768]{1,0:T(8,128)S(1)} %get-tuple-element.307, f32[768]{0:T(1024)S(1)} %convert_element_type.289, ...), kind=kOutput, calls=%fused_computation.68 | convolution fusion | flops 2521694208 | bytes 22042624 | tf_op jit(solution)/shard_map/dot_general | solution.py:17
  308.6 69.7 %all-gather.24.cloned.1.call-done = bf16[3072,768]{1,0:T(8,128)(2,1)} async-done(((bf16[768,768]{1,0:T(8,128)(2,1)}), bf16[3072,768]{1,0:T(8,128)(2,1)}) %all-gather.24.cloned.1.call-update) | async-done | bytes 4718608 | tf_op jit(solution)/shard_map/all_gather | solution.py:126
  378.3 6.1 fusion.78
  388.1 7.9 fusion.71
  396.1 3.1 multiply_reduce_fusion.3
  404.2 2.3 copy.87
  406.5 2.9 reshape_reshape.9
  412.5 83.5 %while.27 = (s32[]{:T(128)}, bf16[6,4,256,64]{2,3,1,0:T(8,128)(2,1)}, bf16[6,4,1024,64]{2,3,1,0:T(8,128)(2,1)}, bf16[6,4,1024,64]{2,3,1,0:T(8,128)(2,1)}, s32[6,...) while((s32[]{:T(128)}, ...), condition=%wide.region_16.17_spmd, body=%wide.region_14.16_spmd.sunk | while | flops 687406080 | bytes 37011584 | solution.py:238
  414.9 2.8 multiply_reduce_fusion.9
  419.0 2.2 fusion.145
  421.2 2.5 fusion.144
  423.6 3.0 fusion.146
  428.8 2.8 multiply_reduce_fusion.9
  435.0 2.5 fusion.144
  437.5 3.0 fusion.146
  442.6 2.8 multiply_reduce_fusion.9
  448.9 2.5 fusion.144
  451.4 3.0 fusion.146
  456.5 2.8 multiply_reduce_fusion.9
  462.8 2.5 fusion.144
  465.3 3.0 fusion.146
  470.4 2.8 multiply_reduce_fusion.9
  476.7 2.5 fusion.144
  479.1 3.0 fusion.146
  484.2 2.8 multiply_reduce_fusion.9
  490.5 2.5 fusion.144
  493.0 3.0 fusion.146
  501.5 2.6 copy.95
  504.2 28.4 %reduce-scatter.17.cloned.1.call-done = bf16[2,256,768]{1,2,0:T(8,128)(2,1)} async-done(((bf16[2,1024,768]{1,2,0:T(8,128)(2,1)}), bf16[2,256,768]{1,2,0:T(8,128)(2,1)}) %reduce-scatter.17.cloned.1.call-update) | async-done | bytes 786448 | tf_op jit(solution)/shard_map/reduce_scatter | solution.py:247
  532.6 3.2 fusion.62
  535.7 2.4 copy.99
  538.2 34.9 %reduce-scatter.15.cloned.1.call-done = bf16[2,256,768]{1,2,0:T(8,128)(2,1)} async-done(((bf16[2,1024,768]{1,2,0:T(8,128)(2,1)}), bf16[2,256,768]{1,2,0:T(8,128)(2,1)}) %reduce-scatter.15.cloned.1.call-update) | async-done | bytes 786448 | tf_op jit(solution)/shard_map/reduce_scatter | solution.py:244
  573.1 3.2 fusion.61
  576.3 2.4 copy.97
  578.7 3.2 convolution_convert_fusion.2
  582.2 7.4 convolution_convert_fusion.1
  589.6 6.9 convolution_convert_fusion
  598.2 6.5 reduce-scatter.25.cloned.1.call-done
  606.5 28.2 %reduce-scatter.29.cloned.1.call-done = bf16[192,768]{1,0:T(8,128)(2,1)} async-done(((bf16[768,768]{1,0:T(8,128)(2,1)}), bf16[192,768]{1,0:T(8,128)(2,1)}) %reduce-scatter.29.cloned.1.call-update) | async-done | bytes 294928
  636.6 28.4 %reduce-scatter.27.cloned.1.call-done = bf16[192,768]{1,0:T(8,128)(2,1)} async-done(((bf16[768,768]{1,0:T(8,128)(2,1)}), bf16[192,768]{1,0:T(8,128)(2,1)}) %reduce-scatter.27.cloned.1.call-update) | async-done | bytes 294928
  666.8 28.8 %reduce-scatter.19.cloned.1.call-done = bf16[192,768]{1,0:T(8,128)(2,1)} async-done(((bf16[768,768]{1,0:T(8,128)(2,1)}), bf16[192,768]{1,0:T(8,128)(2,1)}) %reduce-scatter.19.cloned.1.call-update) | async-done | bytes 294928 | tf_op jit(solution)/shard_map/reduce_scatter | solution.py:295
  695.6 86.2 %reduce-scatter.21.cloned.1.call-done = bf16[192,3072]{1,0:T(8,128)(2,1)} async-done(((bf16[768,3072]{1,0:T(8,128)(2,1)}), bf16[192,3072]{1,0:T(8,128)(2,1)}) %reduce-scatter.21.cloned.1.call-update) | async-done | bytes 1179664 | tf_op jit(solution)/shard_map/reduce_scatter | solution.py:307
  781.8 88.0 %reduce-scatter.23.cloned.1.call-done = bf16[768,768]{1,0:T(8,128)(2,1)} async-done(((bf16[3072,768]{1,0:T(8,128)(2,1)}), bf16[768,768]{1,0:T(8,128)(2,1)}) %reduce-scatter.23.cloned.1.call-update) | async-done | bytes 1179664 | tf_op jit(solution)/shard_map/reduce_scatter | solution.py:313
  871.2 3.0 bitcast_reduce_fusion
  874.3 3.5 fusion.79
  879.1 18.2 %all-reduce.19 = (bf16[768]{0:T(1024)(128)(2,1)S(1)}, bf16[768]{0:T(1024)(128)(2,1)S(1)}, bf16[768]{0:T(1024)(128)(2,1)S(1)}, bf16[768]{0:T(1024)(128)(2,1)S(1)}...) all-reduce(bf16[768]{0:T(1024)(128)(2,1)S(1)} %dynamic-update-slice, ...), channel_id=1, replica_groups=mesh['seq'=2,'ctx'=4,'wt'=4] {'wt'}, use_global_device_ids=true, to_apply=%add.7 | all-reduce | flops 9984 | bytes 39936
  898.0 12.6 %all-reduce.17 = (bf16[192]{0:T(256)(128)(2,1)S(1)}, bf16[192]{0:T(256)(128)(2,1)S(1)}, bf16[192]{0:T(256)(128)(2,1)S(1)}, bf16[192]{0:T(256)(128)(2,1)S(1)}, bf...) all-reduce(bf16[192]{0:T(256)(128)(2,1)S(1)} %dynamic-slice.9, ...), channel_id=1, replica_groups=mesh['seq'=2,'ctx'=4,'wt'=4] {'seq','ctx'}, use_global_device_ids=true, to_apply=%region_23.24 | all-reduce | flops 2304 | bytes 9216 | tf_op jit(solution)/shard_map/psum | solution.py:328
  915.7 2.3 copy.90
  918.0 2.3 copy.91
  921.5 2.6 fusion.80
  925.9 27.5 %all-reduce.23.cloned.1.call-done = (bf16[192,768]{0,1:T(8,128)(2,1)}, bf16[192,768]{0,1:T(8,128)(2,1)}, bf16[192,768]{0,1:T(8,128)(2,1)}, bf16[192,768]{1,0:T(8...) async-done(((bf16[192,768]{0,1:T(8,128)(2,1)}, bf16[192,768]{0,1:T(8,128)(2,1)}, bf16[192,768]{0,1:T(8,128)(2,1)}, bf16[192,768]{1,0:T(8,128)(2,1)}, ...) | async-done | bytes 3538960 | tf_op jit(solution)/shard_map/psum | solution.py:327
  953.4 3.1 convert_element_type.338
  (274 shorter events, 124.7 us)
Async XLA Ops:
  7.2 36.1 %all-gather.16.cloned.1.call-start = ((), (), s32[]{:S(2)}) async-start(), calls=%async_computation.11 | async-start | bytes 1474560 | tf_op jit(solution)/shard_map/all_gather | solution.py:118
  7.9 66.5 %all-gather.12.cloned.1.call-start = ((), (), s32[]{:S(2)}) async-start(), calls=%async_computation.9 | async-start | bytes 1474560 | tf_op jit(solution)/shard_map/all_gather | solution.py:117
  8.7 97.1 %all-gather.10.cloned.1.call-start = ((), (), s32[]{:S(2)}) async-start(), calls=%async_computation.8 | async-start | bytes 1474560 | tf_op jit(solution)/shard_map/all_gather | solution.py:115
  9.4 126.4 %all-gather.18.cloned.1.call-start = ((), (), s32[]{:S(2)}) async-start(), calls=%async_computation.12 | async-start | bytes 3932160 | tf_op jit(solution)/shard_map/all_gather | solution.py:141
  43.3 31.1 %copy-start.21 = (bf16[2,256,768]{2,1,0:T(8,128)(2,1)S(1)}, bf16[2,256,768]{2,1,0:T(8,128)(2,1)}, u32[]{:S(2)}) copy-start(bf16[2,256,768]{2,1,0:T(8,128)(2,1)} %param.23) | copy-start | bytes 2359300
  46.9 119.9 %all-gather.14.cloned.1.call-start = ((), (), s32[]{:S(2)}) async-start(), calls=%async_computation.10 | async-start | bytes 3932160 | tf_op jit(solution)/shard_map/all_gather | solution.py:140
  76.5 3.3 copy-start.18
  76.5 3.9 copy-start.16
  76.5 4.6 copy-start.17
  77.7 124.5 %all-gather.20.cloned.1.call-start = ((), (), s32[]{:S(2)}) async-start(), calls=%async_computation.13 | async-start | bytes 1474560 | tf_op jit(solution)/shard_map/all_gather | solution.py:120
  78.3 210.5 %all-gather.22.cloned.1.call-start = ((), (), s32[]{:S(2)}) async-start(), calls=%async_computation.14 | async-start | bytes 5898240 | tf_op jit(solution)/shard_map/all_gather | solution.py:124
  79.1 299.3 %all-gather.24.cloned.1.call-start = ((), (), s32[]{:S(2)}) async-start(), calls=%async_computation.15 | async-start | bytes 5898240 | tf_op jit(solution)/shard_map/all_gather | solution.py:126
  79.8 452.8 %reduce-scatter.17.cloned.1.call-start = ((), (), s32[]{:S(2)}) async-start(), calls=%async_computation.17 | async-start | bytes 3932160 | tf_op jit(solution)/shard_map/reduce_scatter | solution.py:247
  201.2 3.7 copy-start
  202.2 3.0 copy-start.7
  204.9 191.1 %copy-start.2 = (f32[512,768]{1,0:T(8,128)}, f32[512,768]{1,0:T(8,128)S(1)}, u32[]{:S(2)}) copy-start(f32[512,768]{1,0:T(8,128)S(1)} %get-tuple-element.307) | copy-start | bytes 4718596
  378.3 6.4 copy-start.1
  385.5 2.6 copy-start.19
  386.2 9.8 %slice-start = ((s8[4718592]{0:T(1024)(128)(4,1)}), s8[4194304]{0:T(1024)(128)(4,1)S(1)}, s32[]{:S(2)}) async-start(s8[4718592]{0:T(1024)(128)(4,1)} %bitcast.253), calls=%async_computation.25 | async-start | bytes 8388608
  386.4 9.6 copy-start.9
  388.1 8.0 slice-start.1
  396.0 3.2 copy-start.24
  399.2 3.3 copy-start.20
  401.6 0.9 copy-start.10
  496.0 77.1 %reduce-scatter.15.cloned.1.call-start = ((), (), s32[]{:S(2)}) async-start(), calls=%async_computation.16 | async-start | bytes 3932160 | tf_op jit(solution)/shard_map/reduce_scatter | solution.py:244
  496.6 108.0 %reduce-scatter.25.cloned.1.call-start = ((), (), s32[]{:S(2)}) async-start(), calls=%async_computation.21 | async-start | bytes 1474560
  496.7 3.1 copy-start.22
  498.9 0.9 copy-start.8
  504.1 130.6 %reduce-scatter.29.cloned.1.call-start = ((), (), s32[]{:S(2)}) async-start(), calls=%async_computation.23 | async-start | bytes 1474560
  538.1 126.8 %reduce-scatter.27.cloned.1.call-start = ((), (), s32[]{:S(2)}) async-start(), calls=%async_computation.22 | async-start | bytes 1474560
  578.6 117.0 %reduce-scatter.19.cloned.1.call-start = ((), (), s32[]{:S(2)}) async-start(), calls=%async_computation.18 | async-start | bytes 1474560 | tf_op jit(solution)/shard_map/reduce_scatter | solution.py:295
  581.9 199.9 %reduce-scatter.21.cloned.1.call-start = ((), (), s32[]{:S(2)}) async-start(), calls=%async_computation.19 | async-start | bytes 5898240 | tf_op jit(solution)/shard_map/reduce_scatter | solution.py:307
  589.6 280.2 %reduce-scatter.23.cloned.1.call-start = ((), (), s32[]{:S(2)}) async-start(), calls=%async_computation.20 | async-start | bytes 5898240 | tf_op jit(solution)/shard_map/reduce_scatter | solution.py:313
  596.6 1.4 copy-start.23
  596.6 273.2 %copy-start.15 = (f32[2,256]{1,0:T(2,128)S(1)}, f32[2,256]{1,0:T(2,128)}, u32[]{:S(2)}) copy-start(f32[2,256]{1,0:T(2,128)} %get-tuple-element.302) | copy-start | bytes 6148
  596.6 356.8 %all-reduce.23.cloned.1.call-start = ((), (), s32[]{:S(2)}) async-start(), calls=%async_computation.24 | async-start | bytes 7667712 | tf_op jit(solution)/shard_map/psum | solution.py:327
  920.3 3.8 copy-start.3
  920.3 3.8 copy-start.4
  920.3 3.8 copy-start.6
  953.4 3.1 copy-start.5
  953.4 4.7 copy-start.14
  953.4 5.5 copy-start.13
  956.5 3.4 copy-start.12
  956.5 4.4 copy-start.11
Sparse Core Ops, SparseCore 0:
  9.6 33.6 all-gather.15
  44.9 29.5 all-gather.11
  76.0 29.7 all-gather.9
  107.8 28.0 all-gather.17
  137.8 28.9 all-gather.13
  168.2 30.4 all-gather.19
  200.3 88.5 all-gather.21
  290.4 87.8 all-gather.23
  496.1 36.3 reduce-scatter.16
  535.1 37.9 reduce-scatter.14
  575.4 29.1 reduce-scatter.24
  606.8 27.8 reduce-scatter.28
  637.0 27.8 reduce-scatter.26
  667.7 27.8 reduce-scatter.18
  697.8 83.9 reduce-scatter.20
  784.0 85.7 reduce-scatter.22
  874.3 79.0 all-reduce.22
where the time goes:
time: 975 us; the launch traced here: 969 us
  waiting for transfers between devices  616 us (63%)
  matrix products  180 us (18%)
  blocking collectives  65.7 us (7%)
  local copies, waits for them, and re-layouts  47.2 us (5%)
  other arithmetic  40.5 us (4%)
  between operations  17 us (2%)
    reduce_scatter x1, waiting for transfers between devices, body(): lax.psum_scatter(grads[11].astype(jnp.bfloat16), 'wt', scatter_dimension=...  88 us
    reduce_scatter x1, waiting for transfers between devices, body(): lax.psum_scatter(grads[9].astype(jnp.bfloat16), 'wt', scatter_dimension=0...  86.2 us
    all_gather x1, waiting for transfers between devices, body(): lax.all_gather(shards[9], 'wt', axis=0, tiled=True)  83.6 us
    all_gather x1, waiting for transfers between devices, body(): lax.all_gather(shards[11], 'wt', axis=0, tiled=True)  69.7 us
    unnamed x20, waiting for transfers between devices  67.7 us
    unnamed x2, blocking collectives  39.3 us
    dot_general x6, matrix products, product(): return jnp.dot(former, latter, preferred_element_type=jnp.float32)  35 us
    reduce_scatter x1, waiting for transfers between devices, body(): lax.psum_scatter(partial_kv[0].astype(jnp.bfloat16), 'ctx', scatter_dimen...  34.9 us
  transfers between devices with their start and end apart: 17, of which 16 were waited for; matrix products, arithmetic and copies ran while one was open for 15% of the time, Pallas kernels for 0%

commit v1 on v0

v1 whole, which is shorter than its diff:
```python
import functools
import math

import jax
import jax.numpy as jnp
from jax import lax
from jax.experimental import pallas as pl
from jax.experimental.pallas import tpu as pltpu
from jax.sharding import Mesh
from jax.sharding import PartitionSpec as P

H = 12
HD = 64
NEG = -1000000000.0
EPS = 1e-05
BF = jnp.bfloat16
F32 = jnp.float32
AX = ("seq", "pg", "x", "core", "wt")
VM = pl.BlockSpec(memory_space=pltpu.VMEM)
SM = pl.BlockSpec(memory_space=pltpu.SMEM)
ANY = pl.BlockSpec(memory_space=pl.ANY)
OFFS = (0, 2, 1, 3)
VMEM_LIMIT = 62 * 2**20


def mm(a, b):
    return jnp.dot(a, b, preferred_element_type=F32)


def mm_nt(a, b):
    return lax.dot_general(a, b, (((1,), (1,)), ((), ())), preferred_element_type=F32)


def mm_tn(a, b):
    return lax.dot_general(a, b, (((0,), (0,)), ((), ())), preferred_element_type=F32)


def span(bounds, s, first, last):
    low = jnp.int32(0)
    high = bounds[s, 5]
    for d in range(1, 5):
        low = jnp.where(bounds[s, d] <= first, bounds[s, d], low)
        e = 5 - d
        high = jnp.where(bounds[s, e] > last, bounds[s, e], high)
    return low, high


def attn_fwd_kernel(pg, bounds, idx, qa, qb, o_ref, q_out, k_out, v_out, m_s, acc_s):
    c, mine = idx[0], idx[1]
    T = qa.shape[3]
    lane = lax.broadcasted_iota(jnp.int32, (T, 128), 1)
    row = lax.broadcasted_iota(jnp.int32, (T, 128), 0)
    lower = lane < 64

    def per_seq(s, _):
        for g in range(pg):
            for n, off in enumerate(OFFS):
                src = qa if n < 2 else qb
                tile = g * 4 + (c ^ off)
                place = pl.multiple_of(tile * T, T)
                pos = row + place
                seg = jnp.zeros((T, 128), jnp.int32)
                for d in range(1, 5):
                    seg = seg + (pos >= bounds[s, d]).astype(jnp.int32)
                rel = lane & 63
                hot = rel == seg
                q_aug = jnp.where(hot, 1.0, 0.0)
                k_aug = jnp.where(rel < 5, jnp.where(hot, 0.0, NEG), jnp.where(rel < 11, 1.0, 0.0))

                def part(i):
                    return src[g, n % 2, s, :, i * 128 : (i + 1) * 128].astype(F32)

                q01, k01, v01, v2q2, k2 = (part(i) for i in range(5))
                keep = (lower, ~lower, ~lower)
                for h, (q, k) in enumerate(((q01, k01), (q01, k01), (v2q2, k2))):
                    k_out[s, h, pl.ds(place, T)] = jnp.where(keep[h], k, k_aug).astype(BF)
                    v = v01 if h < 2 else v2q2
                    kv = lower if h != 1 else ~lower
                    v_out[s, h, pl.ds(place, T)] = jnp.where(kv, v, 1.0).astype(BF)

                @pl.when(mine == g)
                def _():
                    own = pl.multiple_of((c ^ off) * T, T)
                    for h, q in enumerate((q01, q01, v2q2)):
                        q_out[s, h, pl.ds(own, T)] = jnp.where(keep[h], q * 0.125, q_aug).astype(BF)

        def per_tile(i, _):
            here = pl.multiple_of(i * T, T)
            first = (mine * 4 + i) * T
            low, high = span(bounds, s, first, first + T - 1)
            for h in range(3):
                m_s[h] = jnp.full((T, 128), -jnp.inf, F32)
                acc_s[h] = jnp.zeros((T, 128), F32)

            def step(kt, _):
                at = pl.multiple_of(kt * T, T)
                for h in range(3):
                    sc = mm_nt(q_out[s, h, pl.ds(here, T)], k_out[s, h, pl.ds(at, T)])
                    old = m_s[h]
                    new = jnp.maximum(old, jnp.max(sc, axis=1, keepdims=True))
                    p = jnp.exp(sc - new[:, :1])
                    acc_s[h] = acc_s[h] * jnp.exp(old - new) + mm(
                        p.astype(BF), v_out[s, h, pl.ds(at, T)]
                    )
                    m_s[h] = new
                return 0

            lax.fori_loop(low // T, (high + T - 1) // T, step, 0)
            outs = []
            for h in range(3):
                acc = acc_s[h]
                other = pltpu.roll(acc, 64, 1)
                data = lower if h != 1 else ~lower
                total = jnp.where(data, other, acc)
                outs.append(acc / total)
                lse = m_s[h] + jnp.log(total)
                l1 = lse.astype(BF).astype(F32)
                l2 = (lse - l1).astype(BF).astype(F32)
                l3 = lse - l1 - l2
                rel = lane if h > 0 else lane - 64
                q = q_out[s, h, pl.ds(here, T)].astype(F32)
                q = jnp.where(rel == 8, -l1, jnp.where(rel == 9, -l2, jnp.where(rel == 10, -l3, q)))
                q_out[s, h, pl.ds(here, T)] = q.astype(BF)
            o_ref[i, s, :, 0:128] = jnp.where(lower, outs[0], outs[1]).astype(BF)
            o_ref[i, s, :, 128:192] = outs[2][:, 0:64].astype(BF)
            return 0

        lax.fori_loop(0, 4, per_tile, 0)
        return 0

    lax.fori_loop(0, 2, per_seq, 0)


def attn_bwd_kernel(pg, bounds, idx, q_ref, k_ref, v_ref, o_ref, do_ref, d_ref, dq_s, dk_s, dv_s, do_s):
    c, mine = idx[0], idx[1]
    T = o_ref.shape[2]
    lane = lax.broadcasted_iota(jnp.int32, (T, 128), 1)
    lower = lane < 64

    def per_seq(s, _):
        dk_s[...] = jnp.zeros_like(dk_s)
        dv_s[...] = jnp.zeros_like(dv_s)
        dq_s[...] = jnp.zeros_like(dq_s)
        live = bounds[s, 4]

        def per_tile(i, _):
            here = pl.multiple_of(i * T, T)
            first = (mine * 4 + i) * T
            low, high = span(bounds, s, first, first + T - 1)
            high = jnp.minimum(high, live)
            pair = do_ref[i, s, :, 0:128].astype(F32)
            last = do_ref[i, s, :, 128:192].astype(F32)
            last = jnp.concatenate([last, jnp.zeros_like(last)], axis=1)
            o_last = o_ref[i, s, :, 128:192].astype(F32)
            o_last = jnp.concatenate([o_last, jnp.zeros_like(o_last)], axis=1)
            prod = pair * o_ref[i, s, :, 0:128].astype(F32)
            zero = jnp.zeros_like(prod)
            for h in range(3):
                data = lower if h != 1 else ~lower
                full = prod if h < 2 else last * o_last
                delta = jnp.sum(jnp.where(data, full, zero), axis=1, keepdims=True)
                d1 = delta.astype(BF).astype(F32)
                d2 = (delta - d1).astype(BF).astype(F32)
                d3 = delta - d1 - d2
                rel = lane if h == 1 else lane - 64
                aug = jnp.where(rel == 8, -d1, jnp.where(rel == 9, -d2, jnp.where(rel == 10, -d3, zero)))
                do_s[h] = jnp.where(data, pair if h < 2 else last, aug).astype(BF)

            def step(kt, _):
                at = pl.multiple_of(kt * T, T)
                for h in range(3):
                    q = q_ref[s, h, pl.ds(here, T)]
                    k = k_ref[s, h, pl.ds(at, T)]
                    d = do_s[h]
                    pt = jnp.exp(mm_nt(k, q))
                    ds = (pt * mm_nt(v_ref[s, h, pl.ds(at, T)], d)).astype(BF)
                    dv_s[h, pl.ds(at, T)] += mm(pt.astype(BF), d)
                    dk_s[h, pl.ds(at, T)] += mm(ds, q)
                    dq_s[h, pl.ds(here, T)] += mm_tn(ds, k)
                return 0

            lax.fori_loop(low // T, (high + T - 1) // T, step, 0)
            return 0

        lax.fori_loop(0, 4, per_tile, 0)
        for g in range(pg):
            for n, off in enumerate(OFFS):
                at = pl.multiple_of((g * 4 + (c ^ off)) * T, T)
                own = pl.multiple_of((c ^ off) * T, T)
                keep = jnp.where(mine == g, 0.125, 0.0)
                dq = [dq_s[h, pl.ds(own, T)] * keep for h in range(3)]
                dk = [dk_s[h, pl.ds(at, T)] for h in range(3)]
                dv = [dv_s[h, pl.ds(at, T)] for h in range(3)]
                d_ref[g, n, s, :, 0:128] = jnp.where(lower, dq[0], dq[1]).astype(BF)
                d_ref[g, n, s, :, 128:256] = jnp.where(lower, dk[0], dk[1]).astype(BF)
                d_ref[g, n, s, :, 256:384] = jnp.where(lower, dv[0], dv[1]).astype(BF)
                d_ref[g, n, s, :, 384:512] = jnp.where(lower, dv[2], dq[2]).astype(BF)
                d_ref[g, n, s, :, 512:640] = jnp.where(lower, 0.0, dk[2]).astype(BF)
        return 0

    lax.fori_loop(0, 2, per_seq, 0)


def gelu_parts(u):
    t = 1.0 / (1.0 + (0.3275911 * 0.7071067811865476) * jnp.abs(u))
    e = jnp.exp(-0.5 * u * u)
    poly = t * (
        0.127414796
        + t * (-0.142248368 + t * (0.7107068705 + t * (-0.7265760135 + t * 0.5307027145)))
    )
    tail = poly * e
    cdf = jnp.where(u >= 0, 1.0 - tail, tail)
    return u * cdf, cdf + u * e * 0.3989422804014327


def fold8(v):
    return jnp.sum(v.reshape(v.shape[0] // 8, 8, v.shape[1]), axis=0)


def ffn_kernel(
    idx, attn, tok, cot, live, vec, b1,
    s1a, r2a, c1a, c2a, s1b, r2b, c1b, c2b,
    out, dfirst, dattn, g1o, g1x, g2o, g2x, small, gb1,
    w1, w2, wa, hid, hlow, xhat, rstd, acc, act, gp, din, dlow, sums, g2s, sem,
):
    c = idx[0]
    R, D = tok.shape
    FB = b1.shape[2]
    TR = 128
    copies = []
    for n, ref in enumerate((s1a, r2a, c1a, c2a)):
        for k in range(2):
            p = idx[2 + 2 * n + k]
            copies.append((ref.at[k, :, 0:192], w1.at[:, :, pl.ds(pl.multiple_of(p * FB, 128), FB)]))
            q, half = p // 2, p % 2
            copies.append((
                ref.at[k, :, 192:240],
                wa.at[:, pl.ds(pl.multiple_of(q * 48, 16), 48), pl.ds(pl.multiple_of(half * FB, 128), FB)],
            ))
    for n, ref in enumerate((s1b, r2b, c1b, c2b)):
        for k in range(2):
            p = idx[2 + 2 * n + k]
            copies.append((ref.at[k], w2.at[:, pl.ds(pl.multiple_of(p * 96, 16), 96)]))
    copies = [pltpu.make_async_copy(a, b, sem.at[i]) for i, (a, b) in enumerate(copies)]
    for cp in copies:
        cp.start()
    for cp in copies:
        cp.wait()

    b_attn, g1v, s1v, b_out, g2v, s2v = (vec[i : i + 1, :] for i in range(6))
    sums[...] = jnp.zeros_like(sums)

    def first(r, _):
        rows = pl.ds(pl.multiple_of(r * TR, TR), TR)
        v = tok[rows, :].astype(F32) + b_attn
        for g in range(4):
            v = v + mm(attn[g, rows, :], wa[g])
        mean = jnp.mean(v, axis=-1, keepdims=True)
        v = v - mean
        rs = lax.rsqrt(jnp.mean(v * v, axis=-1, keepdims=True) + EPS)
        xh = v * rs
        xhat[rows, :] = xh
        rstd[rows, :] = jnp.broadcast_to(rs, (TR, 128))
        h = xh * g1v + s1v
        hid[rows, :] = h
        hlow[rows, :] = h.astype(BF)
        acc[rows, :] = h + b_out
        return 0

    lax.fori_loop(0, R // TR, first, 0)

    def block(z, half):
        return w2[z, half * FB : (half + 1) * FB, :]

    def forward(z, _):
        for half in range(2):
            j = z * 2 + half
            cols = pl.ds(pl.multiple_of(j * FB, 128), FB)
            w = w1[:, :, cols].reshape(D, FB)
            for r in range(R // TR):
                rows = slice(r * TR, (r + 1) * TR)
                u = mm(hlow[rows, :], w) + b1[j]
                a, d = gelu_parts(u)
                a = a.astype(BF)
                act[j, rows, :] = a
                gp[j, rows, :] = d.astype(BF)
                acc[rows, :] += mm(a, block(z, half))
        return 0

    lax.fori_loop(0, 4, forward, 0)

    def second(r, _):
        rows = pl.ds(pl.multiple_of(r * TR, TR), TR)
        v = acc[rows, :]
        mean = jnp.mean(v, axis=-1, keepdims=True)
        v = v - mean
        rs = lax.rsqrt(jnp.mean(v * v, axis=-1, keepdims=True) + EPS)
        xh = v * rs
        out[rows, :] = (xh * g2v + s2v).astype(BF)
        dy = cot[rows, :].astype(F32) * live[rows, :]
        sums[4] += fold8(dy * xh)
        sums[5] += fold8(dy)
        dx = dy * g2v
        m1 = jnp.mean(dx, axis=-1, keepdims=True)
        m2 = jnp.mean(dx * xh, axis=-1, keepdims=True)
        ds = rs * (dx - m1 - xh * m2)
        low = ds.astype(BF)
        dlow[rows, :] = low
        sums[3] += fold8(low.astype(F32))
        acc[rows, :] = ds
        return 0

    lax.fori_loop(0, R // TR, second, 0)

    def backward(yx, _):
        for o in range(2):
            half = c if o == 0 else 1 - c
            j = yx * 2 + half
            cols = pl.ds(pl.multiple_of(j * FB, 128), FB)
            w2j = w2[yx, pl.ds(pl.multiple_of(half * FB, 128), FB), :]
            w1j = w1[:, :, cols].reshape(D, FB)
            g2s[...] = mm_tn(act[j], dlow[...]).astype(BF)
            for xx in range(2):
                for o2, ref in ((0, g2o), (1, g2x)):
                    cc = c if o2 == 0 else 1 - c
                    at = pl.multiple_of((xx * 2 + cc) * 96, 16)
                    ref[half * 2 + xx, yx] = g2s[pl.ds(at, 96), :]
            gsum = jnp.zeros((8, FB), F32)
            for r in range(R // TR):
                rows = slice(r * TR, (r + 1) * TR)
                di = (mm_nt(dlow[rows, :], w2j) * gp[j, rows, :].astype(F32)).astype(BF)
                din[rows, :] = di
                gsum = gsum + fold8(di.astype(F32))
                acc[rows, :] += mm_nt(di, w1j)
            gb1[j] = gsum
            g1 = mm_tn(hlow[...], din[...]).astype(BF)
            ref = g1o if o == 0 else g1x
            for z in range(4):
                ref[yx, z, 0:192, :] = g1[z * 192 : (z + 1) * 192, :]
        return 0

    lax.fori_loop(0, 4, backward, 0)

    def last(r, _):
        rows = pl.ds(pl.multiple_of(r * TR, TR), TR)
        dy = acc[rows, :]
        xh = xhat[rows, :]
        sums[1] += fold8(dy * xh)
        sums[2] += fold8(dy)
        dx = dy * g1v
        m1 = jnp.mean(dx, axis=-1, keepdims=True)
        m2 = jnp.mean(dx * xh, axis=-1, keepdims=True)
        df = rstd[rows, :1] * (dx - m1 - xh * m2)
        dfirst[rows, :] = df
        low = df.astype(BF)
        dlow[rows, :] = low
        sums[0] += fold8(low.astype(F32))
        for g in range(4):
            dattn[g, rows, :] = mm_nt(low, wa[g]).astype(BF)
        return 0

    lax.fori_loop(0, R // TR, last, 0)
    for g in range(4):
        ga = mm_tn(attn[g], dlow[...]).astype(BF)
        for q in range(4):
            for o, ref in ((0, g1o), (1, g1x)):
                cc = c if o == 0 else 1 - c
                left, right = ga[q * 48 : (q + 1) * 48, :FB], ga[q * 48 : (q + 1) * 48, FB:]
                ref[q, g, 192:240, :] = jnp.where(cc == 0, left.astype(F32), right.astype(F32)).astype(BF)
    for i in range(6):
        small[i : i + 1, :] = jnp.sum(sums[i], axis=0, keepdims=True)


def bcast_a2a(a, axes, n):
    return lax.all_to_all(jnp.broadcast_to(a[None], (n,) + a.shape), axes, 0, 0, tiled=True)


def make_body(sizes):
    pg = sizes["pg"]
    order = [sizes[a] for a in AX]

    def send(a, fn):
        pairs = []
        for flat in range(math.prod(order)):
            at, rest = [], flat
            for n in reversed(order):
                at.append(rest % n)
                rest //= n
            to = fn(*reversed(at))
            dest = 0
            for n, v in zip(order, to):
                dest = dest * n + v
            pairs.append((flat, dest))
        return lax.ppermute(a, AX, pairs)

    to_x = functools.partial(send, fn=lambda s, g, x, c, z: (s, g, 1 - x, c, z))
    to_core = functools.partial(send, fn=lambda s, g, x, c, z: (s, g, x, 1 - c, z))
    mix_a = functools.partial(send, fn=lambda s, g, x, c, z: (s, g, 1 - x, c, z) if c == 0 else (1 - s, g, x, c, z))
    mix_b = functools.partial(send, fn=lambda s, g, x, c, z: (1 - s, g, x, c, z) if c == 0 else (s, g, 1 - x, c, z))

    def spread(own):
        s1 = jnp.stack([own, mix_a(own)])
        r2 = mix_b(s1)
        return s1, r2, to_core(s1), to_core(r2)

    def body(
        tokens, cotangent, segment_ids, lengths, w_query, b_query, w_key, w_value, b_value, w_attn, b_attn,
        ln1_gain, ln1_shift, w_inner, b_inner, w_outer, b_outer, ln2_gain, ln2_shift,
    ):
        S, T, D = tokens.shape
        R = S * T
        y, x, c = (lax.axis_index(a) for a in ("seq", "x", "core"))
        mine, z = lax.axis_index("pg"), lax.axis_index("wt")
        h = x * 2 + c
        p = y * 4 + h
        L = 4 * pg * T
        FB = w_inner.shape[1] // 8

        tok_a = jnp.stack([tokens, to_x(tokens)])
        tok_b = to_core(tok_a)

        def cols(w):
            return lax.dynamic_slice_in_dim(w, h * 192, 192, 1)

        wq, wk, wv = cols(w_query), cols(w_key), cols(w_value)
        pack = jnp.concatenate([wq[:, :128], wk[:, :128], wv[:, :128], wv[:, 128:], wq[:, 128:], wk[:, 128:]], axis=1)
        smalls = jnp.concatenate([b_query, b_value, b_attn, ln1_gain, ln1_shift, b_outer, ln2_gain, ln2_shift, b_inner])
        pack = jnp.concatenate([pack, smalls.reshape(4, 576), jnp.zeros((12, 576), BF)], axis=0)
        got = bcast_a2a(pack, "wt", 4)
        w_qkv = got[:, :192].reshape(D, 576)
        w_qkv = jnp.concatenate([w_qkv[:, :512], jnp.zeros((D, 64), BF), w_qkv[:, 512:]], axis=1)
        small_in = got[:, 192:196].reshape(4, 2304).astype(F32)
        vec = small_in[:, 384:1536].reshape(4, 6, 192).transpose(1, 0, 2).reshape(6, D)
        vec = jnp.concatenate([vec, jnp.zeros((2, D), F32)], axis=0)
        b1 = small_in[:, 1536:].reshape(8, 1, FB)
        mine_small = lax.dynamic_slice_in_dim(small_in, h, 1, 0)[0]
        bq, bv = mine_small[:192], mine_small[192:384]
        zero = jnp.zeros((128,), F32)
        b_qkv = jnp.concatenate([bq[:128], zero, bv[:128], bv[128:], bq[128:], zero])

        own1 = lax.dynamic_slice_in_dim(w_inner, p * FB, FB, 1)
        own_a = lax.dynamic_slice(w_attn, ((p // 2) * 48, c * FB), (48, FB))
        own2 = lax.dynamic_slice_in_dim(w_outer, p * 96, 96, 0)
        piece1 = bcast_a2a(jnp.concatenate([own1, own_a], axis=0), "wt", 4)
        piece2 = bcast_a2a(own2, "wt", 4)
        one = spread(piece1)
        two = spread(piece2)

        def project(t):
            v = jnp.dot(t.reshape(-1, D), w_qkv, preferred_element_type=F32) + b_qkv
            return v.astype(BF).reshape(1, 2, S, T, 640)

        qkv_a, qkv_b = project(tok_a), project(tok_b)
        if pg > 1:
            qkv_a = lax.all_gather(qkv_a, "pg", axis=0, tiled=True)
            qkv_b = lax.all_gather(qkv_b, "pg", axis=0, tiled=True)
        ends = [lengths[:, :1]]
        for d in range(1, 4):
            ends.append(ends[-1] + lengths[:, d : d + 1])
        bounds = jnp.concatenate(
            [jnp.zeros_like(ends[0])] + ends + [jnp.full_like(ends[0], L), jnp.zeros((S, 2), jnp.int32)], axis=1
        ).astype(jnp.int32)
        a_of = jnp.where(c == 0, 2, 4)
        mates = [p, p ^ a_of, p ^ (6 - a_of), p ^ 6]
        other = p ^ 1
        mates += [other, other ^ (6 - a_of), other ^ a_of, other ^ 6]
        idx = jnp.stack([h, mine] + mates).astype(jnp.int32)
        idx_f = jnp.stack([c, mine] + mates).astype(jnp.int32)
        head = (S, 3, L, 128)
        own_head = (S, 3, 4 * T, 128)
        params = pltpu.CompilerParams(vmem_limit_bytes=VMEM_LIMIT)
        o, q_aug, k_aug, v_aug = pl.pallas_call(
            functools.partial(attn_fwd_kernel, pg),
            out_shape=(
                jax.ShapeDtypeStruct((4, S, T, 192), BF),
                jax.ShapeDtypeStruct(own_head, BF),
                jax.ShapeDtypeStruct(head, BF),
                jax.ShapeDtypeStruct(head, BF),
            ),
            in_specs=[SM, SM, VM, VM],
            out_specs=(VM,) * 4,
            scratch_shapes=[pltpu.VMEM((3, T, 128), F32), pltpu.VMEM((3, T, 128), F32)],
            compiler_params=params,
            cost_estimate=pl.CostEstimate(flops=30 * 10**9, bytes_accessed=10 * 2**20, transcendentals=0),
            name="attn_fwd",
        )(bounds, idx, qkv_a, qkv_b)
        attn = lax.all_to_all(o, ("x", "core"), 0, 0, tiled=True)

        live = (segment_ids != 0).astype(F32).reshape(R, 1)
        res = pl.pallas_call(
            ffn_kernel,
            out_shape=(
                jax.ShapeDtypeStruct((R, D), BF),
                jax.ShapeDtypeStruct((R, D), F32),
                jax.ShapeDtypeStruct((4, R, 192), BF),
                jax.ShapeDtypeStruct((4, 4, 240, FB), BF),
                jax.ShapeDtypeStruct((4, 4, 240, FB), BF),
                jax.ShapeDtypeStruct((4, 4, 96, D), BF),
                jax.ShapeDtypeStruct((4, 4, 96, D), BF),
                jax.ShapeDtypeStruct((8, D), F32),
                jax.ShapeDtypeStruct((8, 8, FB), F32),
            ),
            in_specs=[SM] + [VM] * 6 + [ANY] * 8,
            out_specs=(VM,) * 9,
            scratch_shapes=[
                pltpu.VMEM((4, 192, 8 * FB), BF),
                pltpu.VMEM((4, 8 * FB // 4, D), BF),
                pltpu.VMEM((4, 192, D), BF),
                pltpu.VMEM((R, D), F32),
                pltpu.VMEM((R, D), BF),
                pltpu.VMEM((R, D), F32),
                pltpu.VMEM((R, 128), F32),
                pltpu.VMEM((R, D), F32),
                pltpu.VMEM((8, R, FB), BF),
                pltpu.VMEM((8, R, FB), BF),
                pltpu.VMEM((R, FB), BF),
                pltpu.VMEM((R, D), BF),
                pltpu.VMEM((8, 8, D), F32),
                pltpu.VMEM((FB, D), BF),
                pltpu.SemaphoreType.DMA((24,)),
            ],
            compiler_params=params,
            cost_estimate=pl.CostEstimate(flops=40 * 10**9, bytes_accessed=20 * 2**20, transcendentals=0),
            name="ffn",
        )(
            idx_f, attn.reshape(4, R, 192), tokens.reshape(R, D), cotangent.reshape(R, D), live, vec, b1,
            *one, *two,
        )
        layer_out, d_first, d_attn, g1o, g1x, g2o, g2x, small, gb1 = res

        def reduce(own, other):
            v = (own.astype(F32) + to_core(other).astype(F32)).astype(BF)
            v = lax.all_to_all(v, ("seq", "x"), 0, 0, tiled=True)
            v = jnp.sum(v.astype(F32), axis=0).astype(BF)
            v = lax.all_to_all(v, "wt", 0, 0, tiled=True)
            v = jnp.sum(v.astype(F32), axis=0)
            if pg > 1:
                v = lax.psum(v, "pg")
            return bcast_a2a(v.astype(BF), ("seq", "x", "core"), 8)

        g2 = reduce(g2o, g2x)
        g1 = reduce(g1o, g1x)
        small_sum = jnp.concatenate([small[:6].reshape(-1), jnp.sum(gb1, axis=1).reshape(-1)]).reshape(10, D)
        small_sum = lax.psum(small_sum, AX)

        d_o = lax.all_to_all(d_attn.reshape(4, S, T, 192), ("x", "core"), 0, 0, tiled=True)
        d = pl.pallas_call(
            functools.partial(attn_bwd_kernel, pg),
            out_shape=jax.ShapeDtypeStruct((pg, 4, S, T, 640), BF),
            in_specs=[SM, SM] + [VM] * 5,
            out_specs=VM,
            scratch_shapes=[
                pltpu.VMEM((3, 4 * T, 128), F32),
                pltpu.VMEM((3, L, 128), F32),
                pltpu.VMEM((3, L, 128), F32),
                pltpu.VMEM((3, T, 128), BF),
            ],
            compiler_params=params,
            cost_estimate=pl.CostEstimate(flops=40 * 10**9, bytes_accessed=10 * 2**20, transcendentals=0),
            name="attn_bwd",
        )(bounds, idx, q_aug, k_aug, v_aug, o, d_o)
        if pg > 1:
            d = lax.psum_scatter(d, "pg", scatter_dimension=0, tiled=True)
        d = d.reshape(4, R, 640)
        d_a, d_b = d[:2].reshape(2 * R, 640), d[2:].reshape(2 * R, 640)

        def back(v):
            return lax.dot_general(v, w_qkv, (((1,), (1,)), ((), ())), preferred_element_type=F32)

        def over_rows(a, b):
            return lax.dot_general(a, b, (((0,), (0,)), ((), ())), preferred_element_type=F32)

        gi_b = to_core(back(d_b).astype(BF))
        gi_a = back(d_a) + gi_b.astype(F32)
        gi_x = to_x(gi_a[R:].astype(BF))
        grad_input = (gi_a[:R] + gi_x.astype(F32) + d_first).astype(BF).reshape(tokens.shape)

        gq = over_rows(tok_a.reshape(2 * R, D), d_a) + over_rows(tok_b.reshape(2 * R, D), d_b)
        col = jnp.sum(d.astype(F32), axis=(0, 1))
        gq = jnp.concatenate([gq[:, :512], gq[:, 576:]], axis=1).astype(BF)
        if pg > 1:
            gq = lax.psum(gq, "pg")
        gq = lax.all_to_all(gq.reshape(8, 96, 576), ("wt", "seq"), 0, 0, tiled=True)
        gq = jnp.sum(gq.astype(F32), axis=0).astype(BF)
        gq = bcast_a2a(gq, ("seq", "x", "core"), 8).astype(F32).reshape(2, 4, 96, 576)

        def rows_of(*parts):
            return jnp.concatenate(parts, axis=-1).transpose(0, 2, 1, 3).reshape(192, D)

        g_wq = rows_of(gq[..., 0:128], gq[..., 448:512])
        g_wk = rows_of(gq[..., 128:256], gq[..., 512:576])
        g_wv = rows_of(gq[..., 256:384], gq[..., 384:448])
        bias = jnp.stack([jnp.concatenate([col[0:128], col[448:512]]), jnp.concatenate([col[256:384], col[384:448]])])
        wide = jnp.where((jnp.arange(4) == h)[None, :, None], bias[:, None, :], 0.0).reshape(2, D)
        bias_sum = lax.psum(wide, AX)

        def shard(v):
            n = v.shape[0] // 4
            return lax.dynamic_slice_in_dim(v, z * n, n, 0)

        g1 = g1.astype(F32)
        g_wi = g1[:, :192].transpose(1, 0, 2).reshape(192, 8 * FB)
        g_wa = g1[:, 192:].reshape(4, 2, 48, FB).transpose(0, 2, 1, 3).reshape(192, D)
        g_wo = g2.astype(F32).reshape(768, D)
        return (
            layer_out.reshape(tokens.shape), grad_input,
            g_wq, shard(bias_sum[0]), g_wk, g_wv, shard(bias_sum[1]),
            g_wa, shard(small_sum[0]), shard(small_sum[1]), shard(small_sum[2]),
            g_wi, shard(small_sum[6:].reshape(-1)), g_wo, shard(small_sum[3]),
            shard(small_sum[4]), shard(small_sum[5]),
        )

    return body


def solution(mesh):
    sizes = dict(mesh.shape)
    pg = sizes["ctx"] // 4
    fine = dict(zip(AX, (sizes["seq"], pg, 2, 2, sizes["wt"])))
    split = Mesh(mesh.devices.reshape(tuple(fine.values())), AX)
    rows = P(("seq", "wt"), ("pg", "x", "core"), None)
    mat, vec = P("wt", None), P("wt")
    in_specs = (
        rows, rows, P(("seq", "wt"), ("pg", "x", "core")), P(("seq", "wt"), None),
        mat, vec, mat, mat, vec, mat, vec, vec, vec, mat, vec, mat, vec, vec, vec,
    )
    out_specs = (rows, rows, mat, vec, mat, mat, vec, mat, vec, vec, vec, mat, vec, mat, vec, vec, vec)
    return jax.shard_map(make_body(fine), mesh=split, in_specs=in_specs, out_specs=out_specs, check_vma=False)
```

time: 975 us -> 521 us (0.53)
  waiting for transfers between devices: 616 us -> 184 us
  matrix products: 180 us -> 21.6 us
  Pallas kernels: 0 us -> 124 us
  starting transfers between devices: 0.93 us -> 63.7 us
  blocking collectives: 65.7 us -> 40.6 us
  between operations: 17 us -> 1.9 us
  other arithmetic: 40.5 us -> 30 us
    reduce_scatter x5 -> x0, waiting for transfers between devices: 266 us -> none  [the longest x1 88 us: body(): lax.psum_scatter(grads[11].astype(jnp.bfloat16), 'wt', scatter_dimension=...]
    all_gather x8 -> x0, waiting for transfers between devices: 255 us -> none  [the longest x1 83.6 us: body(): lax.all_gather(shards[9], 'wt', axis=0, tiled=True)]
    dot_general x60 -> x6, matrix products: 180 us -> 21.6 us  [the longest x2 7.73 us: project(): v = jnp.dot(t.reshape(-1, D), w_qkv, preferred_element_type=F32) + b_qkv]
    all_to_all x0 -> x13, waiting for transfers between devices: none -> 158 us  [the longest x6 55.9 us: bcast_a2a(): lax.all_to_all(jnp.broadcast_to(a[None], (n,) + a.shape), axes, 0, 0, til...]
    pallas_call x0 -> x3, Pallas kernels: none -> 124 us  [the longest x1 51.3 us: body(): pl.pallas_call(ffn_kernel, out_shape=(jax.ShapeDtypeStruct((R, D), BF), j...]
    unnamed x20 -> x0, waiting for transfers between devices: 67.7 us -> none
    all_to_all x0 -> x13, starting transfers between devices: none -> 52.7 us  [the longest x6 24.2 us: bcast_a2a(): lax.all_to_all(jnp.broadcast_to(a[None], (n,) + a.shape), axes, 0, 0, til...]
    unnamed x2 -> x0, blocking collectives: 39.3 us -> none
  transfers between devices with their start and end apart: 17 -> 27, of which waited for: 16 -> 15; matrix products, arithmetic and copies ran while one was open for 15% -> 17% of each run, Pallas kernels for 0% -> 14%
where the time goes in v1:
time: 521 us; the launch traced here: 513 us
  waiting for transfers between devices  184 us (35%)
  Pallas kernels  124 us (24%)
  starting transfers between devices  63.7 us (12%)
  local copies, waits for them, and re-layouts  47.1 us (9%)
  blocking collectives  40.6 us (8%)
  other arithmetic  30 us (6%)
  matrix products  21.6 us (4%)
    all_to_all x6, waiting for transfers between devices, bcast_a2a(): lax.all_to_all(jnp.broadcast_to(a[None], (n,) + a.shape), axes, 0, 0, til...  55.9 us
    all_to_all x2, waiting for transfers between devices, reduce(): v = lax.all_to_all(v, ('seq', 'x'), 0, 0, tiled=True)  53.2 us
    pallas_call x1, Pallas kernels, body(): pl.pallas_call(ffn_kernel, out_shape=(jax.ShapeDtypeStruct((R, D), BF), j...  51.3 us
    psum x1, blocking collectives, body(): bias_sum = lax.psum(wide, AX)  40.6 us
    pallas_call x1, Pallas kernels, body(): pl.pallas_call(functools.partial(attn_fwd_kernel, pg), out_shape=(jax.Sha...  38.7 us
    pallas_call x1, Pallas kernels, body(): pl.pallas_call(functools.partial(attn_bwd_kernel, pg), out_shape=jax.Shap...  34 us
    ppermute x14, waiting for transfers between devices, send(): return lax.ppermute(a, AX, pairs)  26 us
    all_to_all x1, waiting for transfers between devices, body(): gq = lax.all_to_all(gq.reshape(8, 96, 576), ('wt', 'seq'), 0, 0, tiled=True)  24.3 us
  transfers between devices with their start and end apart: 27, of which 15 were waited for; matrix products, arithmetic and copies ran while one was open for 17% of the time, Pallas kernels for 14%

profile of v1, /device:TPU:0, one launch (start us, length us, event | category | flops | bytes accessed | tf_op | source)
XLA Modules:
  0.0 513.4 jit_solution(11614016127010064115)
XLA Ops:
  0.7 1.2 copy-done
  2.8 6.3 %all-to-all-start.3 = ((bf16[4,96,768]{2,1,0:T(8,128)(2,1)}), bf16[4,96,768]{2,1,0:T(8,128)(2,1)S(1)}, u32[]{:S(2)}, u32[]{:S(2)}) async-start(bf16[4,96,768]{2,1,0:T(8,128)(2,1)} %broadcast_in_dim.81), calls=%async_computation.3 | async-start | bytes 1179648 | tf_op jit(solution)/shard_map/all_to_all | solution.py:375
  11.0 14.0 %all-to-all-done.3 = bf16[4,96,768]{2,1,0:T(8,128)(2,1)S(1)} async-done(((bf16[4,96,768]{2,1,0:T(8,128)(2,1)}), bf16[4,96,768]{2,1,0:T(8,128)(2,1)S(1)}, u32[]{:S(2)}, u32[]{:S(2)}) %all-to-all-start.3) | async-done | bytes 589856 | tf_op jit(solution)/shard_map/all_to_all | solution.py:375
  25.9 3.5 all-to-all-start.2
  29.4 1.6 collective-permute-start
  34.6 13.4 %all-to-all-done.2 = bf16[4,240,384]{2,1,0:T(8,128)(2,1)S(1)} async-done(((bf16[4,240,384]{2,1,0:T(8,128)(2,1)}), bf16[4,240,384]{2,1,0:T(8,128)(2,1)S(1)}, u32[]{:S(2)}, u32[]{:S(2)}) %all-to-all-start.2) | async-done | bytes 737312 | tf_op jit(solution)/shard_map/all_to_all | solution.py:375
  49.0 3.5 all-to-all-start
  52.6 1.6 collective-permute-start.2
  54.6 2.4 pad_maximum_fusion
  57.1 7.0 %collective-permute-done.2 = bf16[4,240,384]{2,1,0:T(8,128)(2,1)S(1)} collective-permute-done((bf16[4,240,384]{2,1,0:T(8,128)(2,1)S(1)}, bf16[4,240,384]{2,1,0:T(8,128)(2,1)S(1)}, u32[]{:S(2)}, u32[]{:S(2)}) %collective-permute-start.2) | collective-permute-done | bytes 737312 | tf_op jit(solution)/shard_map/ppermute | solution.py:394
  64.1 1.3 pad_maximum_fusion.1.s1a
  65.4 1.5 collective-permute-start.3
  66.9 7.5 %collective-permute-done.6 = bf16[4,96,768]{2,1,0:T(8,128)(2,1)S(1)} collective-permute-done((bf16[4,96,768]{2,1,0:T(8,128)(2,1)S(1)}, bf16[4,96,768]{2,1,0:T(8,128)(2,1)S(1)}, u32[]{:S(2)}, u32[]{:S(2)}) %collective-permute-start.6) | collective-permute-done | bytes 589856 | tf_op jit(solution)/shard_map/ppermute | solution.py:394
  75.5 1.5 collective-permute-start.7
  79.0 3.9 add_convert_fusion.3
  83.3 3.9 add_convert_fusion.2
  87.2 10.5 %collective-permute-done.7.r2b = bf16[2,4,96,768]{3,2,1,0:T(8,128)(2,1)} collective-permute-done((bf16[2,4,96,768]{3,2,1,0:T(8,128)(2,1)}, bf16[2,4,96,768]{3,2,1,0:T(8,128)(2,1)}, u32[]{:S(2)}, u32[]{:S(2)}) %collective-permute-start.7) | collective-permute-done | bytes 1179680 | tf_op jit(solution)/shard_map/ppermute | solution.py:394
  98.8 38.7 %attn_fwd.1 = (bf16[4,2,256,192]{3,2,1,0:T(8,128)(2,1)}, bf16[2,3,1024,128]{3,2,1,0:T(8,128)(2,1)}, bf16[2,3,1024,128]{3,2,1,0:T(8,128)(2,1)}, bf16[2,3,1024,128]{3,2,1,0:T(8,128)(2,1)}) custom-call(s32[2,8]{1,0:T(2,128)} %concatenate.52.bounds, s32[10]{0:T(128)} %stack.93.idx, bf16[1,2,2,256,640]{4,3,2,1,0:T(8,128)(2,1)} %bitcast.124, ...), custom_call_target="tpu_custom_call" | custom-call | flops 30000001024 | bytes 10485760 | tf_op jit(solution)/shard_map/attn_fwd/pallas_call | solution.py:472
  137.5 2.2 copy.68
  139.7 3.7 all-to-all-start.1
  146.4 8.6 %all-to-all-done.1 = bf16[4,2,256,192]{2,3,1,0:T(8,128)(2,1)S(1)} async-done(((bf16[4,2,256,192]{2,3,1,0:T(8,128)(2,1)}), bf16[4,2,256,192]{2,3,1,0:T(8,128)(2,1)S(1)}, u32[]{:S(2)}, u32[]{:S(2)}) %all-to-all-start.1) | async-done | bytes 786464 | tf_op jit(solution)/shard_map/all_to_all | solution.py:487
  155.0 1.3 copy.69
  156.3 51.3 %ffn.1 = (bf16[512,768]{1,0:T(8,128)(2,1)}, f32[512,768]{1,0:T(8,128)}, bf16[4,512,192]{2,1,0:T(8,128)(2,1)}, bf16[4,4,240,384]{3,2,1,0:T(8,128)(2,1)}, bf16[4,4...) custom-call(s32[10]{0:T(128)} %stack.91.idx, ...), custom_call_target="tpu_custom_call" | custom-call | flops 40000000000 | bytes 20971520 | tf_op jit(solution)/shard_map/ffn/pallas_call | solution.py:490
  207.7 2.2 copy.72
  209.9 3.7 all-to-all-start.4
  214.1 11.1 %all-to-all-done.4 = bf16[4,2,256,192]{2,3,1,0:T(8,128)(2,1)S(1)} async-done(((bf16[4,2,256,192]{2,3,1,0:T(8,128)(2,1)}), bf16[4,2,256,192]{2,3,1,0:T(8,128)(2,1)S(1)}, u32[]{:S(2)}, u32[]{:S(2)}) %all-to-all-start.4) | async-done | bytes 786464 | tf_op jit(solution)/shard_map/all_to_all | solution.py:546
  225.2 1.3 copy.73.do_ref
  226.5 34.0 %attn_bwd.1 = bf16[1,4,2,256,640]{4,3,2,1,0:T(8,128)(2,1)} custom-call(s32[2,8]{1,0:T(2,128)} %concatenate.52.bounds, s32[10]{0:T(128)} %stack.93.idx, bf16[2,3,1024,128]{3,2,1,0:T(8,128)(2,1)} %get-tuple-element.32.q_ref, bf16[2,3,1024,128]{3,2,1,0:T(8,128)(2,1)} %get-tuple-element.33.k_ref, bf16[2,3,1024,128]{3,2,1,0:T(8,128)(2,1)} %get-tuple-element.34.v_ref, ...), custom_call_target="tpu_custom_call" | custom-call | flops 40000000000 | bytes 10485760 | tf_op jit(solution)/shard_map/attn_bwd/pallas_call | solution.py:547
  260.5 2.0 fusion.5
  262.5 3.8 fusion.10
  266.4 2.9 add_convert_fusion.4
  270.4 5.9 %all-to-all-start.5 = ((bf16[8,96,576]{2,1,0:T(8,128)(2,1)}), bf16[8,96,576]{2,1,0:T(8,128)(2,1)S(1)}, u32[]{:S(2)}, u32[]{:S(2)}) async-start(bf16[8,96,576]{2,1,0:T(8,128)(2,1)} %pad_maximum_fusion.4), calls=%async_computation.5 | async-start | bytes 1966080 | tf_op jit(solution)/shard_map/all_to_all | solution.py:583
  276.4 24.3 %all-to-all-done.5 = bf16[8,96,576]{2,1,0:T(8,128)(2,1)S(1)} async-done(((bf16[8,96,576]{2,1,0:T(8,128)(2,1)}), bf16[8,96,576]{2,1,0:T(8,128)(2,1)S(1)}, u32[]{:S(2)}, u32[]{:S(2)}) %all-to-all-start.5) | async-done | bytes 884768 | tf_op jit(solution)/shard_map/all_to_all | solution.py:583
  301.8 3.7 all-to-all-start.6
  305.5 3.8 add_convert_fusion.1
  309.3 10.9 %all-to-all-done.6 = bf16[8,96,576]{2,1,0:T(8,128)(2,1)S(1)} async-done(((bf16[8,96,576]{2,1,0:T(8,128)(2,1)}), bf16[8,96,576]{2,1,0:T(8,128)(2,1)S(1)}, u32[]{:S(2)}, u32[]{:S(2)}) %all-to-all-start.6) | async-done | bytes 884768 | tf_op jit(solution)/shard_map/all_to_all | solution.py:375
  320.2 3.6 all-to-all-start.10
  323.8 5.0 add_convert_fusion
  328.8 21.9 %all-to-all-done.10 = bf16[4,4,96,768]{3,2,1,0:T(8,128)(2,1)S(1)} async-done(((bf16[4,4,96,768]{3,2,1,0:T(8,128)(2,1)}), bf16[4,4,96,768]{3,2,1,0:T(8,128)(2,1)S(1)}, u32[]{:S(2)}, u32[]{:S(2)}) %all-to-all-start.10) | async-done | bytes 2359328 | tf_op jit(solution)/shard_map/all_to_all | solution.py:533
  350.7 4.6 all-to-all-start.7
  355.4 1.3 reduce_sum.83
  356.7 31.3 %all-to-all-done.7 = bf16[4,4,240,384]{3,2,1,0:T(8,128)(2,1)} async-done(((bf16[4,4,240,384]{3,2,1,0:T(8,128)(2,1)}), bf16[4,4,240,384]{3,2,1,0:T(8,128)(2,1)}, u32[]{:S(2)}, u32[]{:S(2)}) %all-to-all-start.7) | async-done | bytes 2949152 | tf_op jit(solution)/shard_map/all_to_all | solution.py:533
  388.0 3.5 all-to-all-start.11
  391.8 2.4 convert_reduce_fusion
  394.4 3.7 convolution_convert_fusion
  398.1 3.3 reduce_sum.80
  401.4 5.4 %all-to-all-done.11 = bf16[4,96,768]{2,1,0:T(8,128)(2,1)S(1)} async-done(((bf16[4,96,768]{2,1,0:T(8,128)(2,1)}), bf16[4,96,768]{2,1,0:T(8,128)(2,1)S(1)}, u32[]{:S(2)}, u32[]{:S(2)}) %all-to-all-start.11) | async-done | bytes 589856 | tf_op jit(solution)/shard_map/all_to_all | solution.py:535
  406.8 3.5 all-to-all-start.8
  410.3 40.6 %all-reduce.1 = (f32[2,768]{1,0:T(2,128)S(1)}, f32[10,768]{1,0:T(8,128)S(1)}) all-reduce(f32[2,768]{1,0:T(2,128)S(1)} %broadcast_select_fusion, f32[10,768]{1,0:T(8,128)S(1)} %reshape.204), channel_id=1, replica_groups=mesh['seq'=2,'pg'=1,'x'=2,'core'=2,'wt'=4] {'seq','pg','x','core','wt'}, use_global_device_ids=true, to_apply=%region_2.3 | all-reduce | flops 9216 | bytes 73728 | tf_op jit(solution)/shard_map/psum | solution.py:595
  456.7 3.6 all-to-all-start.12
  461.5 3.5 convert_add_fusion
  465.0 1.6 copy-done.5
  467.6 2.2 collective-permute-start.11
  470.8 6.7 %all-to-all-done.12 = bf16[8,96,768]{2,1,0:T(8,128)(2,1)S(1)} async-done(((bf16[8,96,768]{2,1,0:T(8,128)(2,1)}), bf16[8,96,768]{2,1,0:T(8,128)(2,1)S(1)}, u32[]{:S(2)}, u32[]{:S(2)}) %all-to-all-start.12) | async-done | bytes 1179680 | tf_op jit(solution)/shard_map/all_to_all | solution.py:375
  477.5 1.4 broadcast_in_dim.89
  479.1 3.6 all-to-all-start.9
  483.5 1.4 convert.22
  485.5 1.3 reshape.198
  488.5 1.3 reshape.199
  491.4 1.3 reshape.197
  493.7 3.3 fusion.1
  497.0 1.7 bitcast_convert_fusion
  498.7 11.0 %all-to-all-done.9 = bf16[8,240,384]{2,1,0:T(8,128)(2,1)S(1)} async-done(((bf16[8,240,384]{2,1,0:T(8,128)(2,1)}), bf16[8,240,384]{2,1,0:T(8,128)(2,1)S(1)}, u32[]{:S(2)}, u32[]{:S(2)}) %all-to-all-start.9) | async-done | bytes 1474592 | tf_op jit(solution)/shard_map/all_to_all | solution.py:375
  510.0 1.7 copy.79
  (170 shorter events, 36.0 us)
Async XLA Ops:
  0.7 1.3 copy-start
  2.8 22.2 %all-to-all-start.3 = ((bf16[4,96,768]{2,1,0:T(8,128)(2,1)}), bf16[4,96,768]{2,1,0:T(8,128)(2,1)S(1)}, u32[]{:S(2)}, u32[]{:S(2)}) async-start(bf16[4,96,768]{2,1,0:T(8,128)(2,1)} %broadcast_in_dim.81), calls=%async_computation.3 | async-start | bytes 1179648 | tf_op jit(solution)/shard_map/all_to_all | solution.py:375
  9.1 20.3 %copy-start.11 = (bf16[2,256,768]{2,1,0:T(8,128)(2,1)S(1)}, bf16[2,256,768]{2,1,0:T(8,128)(2,1)}, u32[]{:S(2)}) copy-start(bf16[2,256,768]{2,1,0:T(8,128)(2,1)} %param.19) | copy-start | bytes 2359300
  10.9 23.1 %copy-start.18 = (bf16[768]{0:T(1024)(128)(2,1)S(1)}, bf16[768]{0:T(1024)(128)(2,1)}, u32[]{:S(2)}) copy-start(bf16[768]{0:T(1024)(128)(2,1)} %param.33) | copy-start | bytes 4612
  10.9 23.1 %copy-start.19 = (bf16[192]{0:T(256)(128)(2,1)S(1)}, bf16[192]{0:T(256)(128)(2,1)}, u32[]{:S(2)}) copy-start(bf16[192]{0:T(256)(128)(2,1)} %param.24) | copy-start | bytes 1156
  10.9 23.1 %copy-start.20 = (bf16[192]{0:T(256)(128)(2,1)S(1)}, bf16[192]{0:T(256)(128)(2,1)}, u32[]{:S(2)}) copy-start(bf16[192]{0:T(256)(128)(2,1)} %param.27) | copy-start | bytes 1156
  11.0 23.1 %copy-start.21 = (bf16[192]{0:T(256)(128)(2,1)S(1)}, bf16[192]{0:T(256)(128)(2,1)}, u32[]{:S(2)}) copy-start(bf16[192]{0:T(256)(128)(2,1)} %param.29) | copy-start | bytes 1156
  11.0 23.1 %copy-start.22 = (bf16[192]{0:T(256)(128)(2,1)S(1)}, bf16[192]{0:T(256)(128)(2,1)}, u32[]{:S(2)}) copy-start(bf16[192]{0:T(256)(128)(2,1)} %param.30) | copy-start | bytes 1156
  11.0 23.1 %copy-start.23 = (bf16[192]{0:T(256)(128)(2,1)S(1)}, bf16[192]{0:T(256)(128)(2,1)}, u32[]{:S(2)}) copy-start(bf16[192]{0:T(256)(128)(2,1)} %param.31) | copy-start | bytes 1156
  11.0 23.1 %copy-start.24 = (bf16[192]{0:T(256)(128)(2,1)S(1)}, bf16[192]{0:T(256)(128)(2,1)}, u32[]{:S(2)}) copy-start(bf16[192]{0:T(256)(128)(2,1)} %param.35) | copy-start | bytes 1156
  11.0 23.1 %copy-start.25 = (bf16[192]{0:T(256)(128)(2,1)S(1)}, bf16[192]{0:T(256)(128)(2,1)}, u32[]{:S(2)}) copy-start(bf16[192]{0:T(256)(128)(2,1)} %param.36) | copy-start | bytes 1156
  11.0 23.1 %copy-start.26 = (bf16[192]{0:T(256)(128)(2,1)S(1)}, bf16[192]{0:T(256)(128)(2,1)}, u32[]{:S(2)}) copy-start(bf16[192]{0:T(256)(128)(2,1)} %param.37) | copy-start | bytes 1156
  25.9 22.0 %all-to-all-start.2 = ((bf16[4,240,384]{2,1,0:T(8,128)(2,1)}), bf16[4,240,384]{2,1,0:T(8,128)(2,1)S(1)}, u32[]{:S(2)}, u32[]{:S(2)}) async-start(bf16[4,240,384]{2,1,0:T(8,128)(2,1)} %broadcast_in_dim.80), calls=%async_computation.2 | async-start | bytes 1474560 | tf_op jit(solution)/shard_map/all_to_all | solution.py:375
  29.4 25.2 %collective-permute-start = (bf16[2,256,768]{2,1,0:T(8,128)(2,1)S(1)}, bf16[2,256,768]{2,1,0:T(8,128)(2,1)}, u32[]{:S(2)}, u32[]{:S(2)}) collective-permute-start(bf16[2,256,768]{2,1,0:T(8,128)(2,1)S(1)} %copy-done.11), channel_id=1, source_target_pairs={{0,8},{1,9},{2,10},{3,11},{4,12},{5,13},{6,14},{7,15},{8,0},{9,1},... | collective-permute-start | bytes 2359304 | tf_op jit(solution)/shard_map/ppermute | solution.py:394
  49.0 29.4 %all-to-all-start = ((bf16[4,208,576]{2,1,0:T(8,128)(2,1)}), bf16[4,208,576]{2,1,0:T(8,128)(2,1)S(1)}, u32[]{:S(2)}, u32[]{:S(2)}) async-start(bf16[4,208,576]{2,1,0:T(8,128)(2,1)} %broadcast_in_dim.38), calls=%async_computation | async-start | bytes 2129920 | tf_op jit(solution)/shard_map/all_to_all | solution.py:375
  52.6 11.5 %collective-permute-start.2 = (bf16[4,240,384]{2,1,0:T(8,128)(2,1)S(1)}, bf16[4,240,384]{2,1,0:T(8,128)(2,1)S(1)}, u32[]{:S(2)}, u32[]{:S(2)}) collective-permute-start(bf16[4,240,384]{2,1,0:T(8,128)(2,1)S(1)} %all-to-all-done.2), channel_id=1, source_target_pairs={{0,8},{1,9},{2,10},{3,11},{4,20},{5,21},{6,22},{7,23},{8,0},{9,1},... | collective-permute-start | bytes 2211848 | tf_op jit(solution)/shard_map/ppermute | solution.py:394
  54.1 20.3 %collective-permute-start.6 = (bf16[4,96,768]{2,1,0:T(8,128)(2,1)S(1)}, bf16[4,96,768]{2,1,0:T(8,128)(2,1)S(1)}, u32[]{:S(2)}, u32[]{:S(2)}) collective-permute-start(bf16[4,96,768]{2,1,0:T(8,128)(2,1)S(1)} %all-to-all-done.3), channel_id=1, source_target_pairs={{0,8},{1,9},{2,10},{3,11},{4,20},{5,21},{6,22},{7,23},{8,0},{9,1},... | collective-permute-start | bytes 1769480 | tf_op jit(solution)/shard_map/ppermute | solution.py:394
  57.1 26.3 %collective-permute-start.1 = (bf16[2,2,256,768]{3,2,1,0:T(8,128)(2,1)}, bf16[2,2,256,768]{3,2,1,0:T(8,128)(2,1)}, u32[]{:S(2)}, u32[]{:S(2)}) collective-permute-start(bf16[2,2,256,768]{3,2,1,0:T(8,128)(2,1)} %pad_maximum_fusion), channel_id=1, source_target_pairs={{0,4},{1,5},{2,6},{3,7},{4,0},{5,1},{6,2},{7,3},{8,12},{9,13},{10,... | collective-permute-start | bytes 4718600 | tf_op jit(solution)/shard_map/ppermute | solution.py:394
  65.4 11.6 %copy-start.16 = (s32[2,4]{1,0:T(2,128)S(1)}, s32[2,4]{1,0:T(2,128)}, u32[]{:S(2)}) copy-start(s32[2,4]{1,0:T(2,128)} %param.22) | copy-start | bytes 100
  65.4 33.4 %collective-permute-start.3 = (bf16[2,4,240,384]{3,2,1,0:T(8,128)(2,1)}, bf16[2,4,240,384]{3,2,1,0:T(8,128)(2,1)}, u32[]{:S(2)}, u32[]{:S(2)}) collective-permute-start(bf16[2,4,240,384]{3,2,1,0:T(8,128)(2,1)} %pad_maximum_fusion.1.s1a), channel_id=1, source_target_pairs={{0,16},{1,17},{2,18},{3,19},{4,12},{5,13},{6,14},{7,15},{8,24},{9,... | collective-permute-start | bytes 4423688 | tf_op jit(solution)/shard_map/ppermute | solution.py:394
  75.5 22.2 %collective-permute-start.7 = (bf16[2,4,96,768]{3,2,1,0:T(8,128)(2,1)}, bf16[2,4,96,768]{3,2,1,0:T(8,128)(2,1)}, u32[]{:S(2)}, u32[]{:S(2)}) collective-permute-start(bf16[2,4,96,768]{3,2,1,0:T(8,128)(2,1)} %pad_maximum_fusion.2.s1b), channel_id=1, source_target_pairs={{0,16},{1,17},{2,18},{3,19},{4,12},{5,13},{6,14},{7,15},{8,24},{9,... | collective-permute-start | bytes 3538952 | tf_op jit(solution)/shard_map/ppermute | solution.py:394
  78.6 4.8 copy-start.10
  78.6 4.8 copy-start.12
  82.8 73.5 %collective-permute-start.8 = (bf16[2,4,96,768]{3,2,1,0:T(8,128)(2,1)}, bf16[2,4,96,768]{3,2,1,0:T(8,128)(2,1)}, u32[]{:S(2)}, u32[]{:S(2)}) collective-permute-start(bf16[2,4,96,768]{3,2,1,0:T(8,128)(2,1)} %pad_maximum_fusion.2.s1b), channel_id=1, source_target_pairs={{0,4},{1,5},{2,6},{3,7},{4,0},{5,1},{6,2},{7,3},{8,12},{9,13},{10,... | collective-permute-start | bytes 3538952 | tf_op jit(solution)/shard_map/ppermute | solution.py:394
  82.8 73.5 %collective-permute-start.4 = (bf16[2,4,240,384]{3,2,1,0:T(8,128)(2,1)}, bf16[2,4,240,384]{3,2,1,0:T(8,128)(2,1)}, u32[]{:S(2)}, u32[]{:S(2)}) collective-permute-start(bf16[2,4,240,384]{3,2,1,0:T(8,128)(2,1)} %pad_maximum_fusion.1.s1a), channel_id=1, source_target_pairs={{0,4},{1,5},{2,6},{3,7},{4,0},{5,1},{6,2},{7,3},{8,12},{9,13},{10,... | collective-permute-start | bytes 4423688 | tf_op jit(solution)/shard_map/ppermute | solution.py:394
  97.7 58.6 %collective-permute-start.9 = (bf16[2,4,96,768]{3,2,1,0:T(8,128)(2,1)}, bf16[2,4,96,768]{3,2,1,0:T(8,128)(2,1)}, u32[]{:S(2)}, u32[]{:S(2)}) collective-permute-start(bf16[2,4,96,768]{3,2,1,0:T(8,128)(2,1)} %collective-permute-done.7.r2b), channel_id=1, source_target_pairs={{0,4},{1,5},{2,6},{3,7},{4,0},{5,1},{6,2},{7,3},{8,12},{9,13},{10,... | collective-permute-start | bytes 3538952 | tf_op jit(solution)/shard_map/ppermute | solution.py:394
  98.8 57.5 %collective-permute-start.5 = (bf16[2,4,240,384]{3,2,1,0:T(8,128)(2,1)}, bf16[2,4,240,384]{3,2,1,0:T(8,128)(2,1)}, u32[]{:S(2)}, u32[]{:S(2)}) collective-permute-start(bf16[2,4,240,384]{3,2,1,0:T(8,128)(2,1)} %collective-permute-done.3.r2a), channel_id=1, source_target_pairs={{0,4},{1,5},{2,6},{3,7},{4,0},{5,1},{6,2},{7,3},{8,12},{9,13},{10,... | collective-permute-start | bytes 4423688 | tf_op jit(solution)/shard_map/ppermute | solution.py:394
  137.5 6.6 %copy-start.17 = (s32[2,256]{1,0:T(2,128)S(1)}, s32[2,256]{1,0:T(2,128)}, u32[]{:S(2)}) copy-start(s32[2,256]{1,0:T(2,128)} %param.21) | copy-start | bytes 6148
  139.7 15.3 %all-to-all-start.1 = ((bf16[4,2,256,192]{2,3,1,0:T(8,128)(2,1)}), bf16[4,2,256,192]{2,3,1,0:T(8,128)(2,1)S(1)}, u32[]{:S(2)}, u32[]{:S(2)}) async-start(bf16[4,2,256,192]{2,3,1,0:T(8,128)(2,1)} %copy.68), calls=%async_computation.1 | async-start | bytes 1572864 | tf_op jit(solution)/shard_map/all_to_all | solution.py:487
  209.9 15.3 %all-to-all-start.4 = ((bf16[4,2,256,192]{2,3,1,0:T(8,128)(2,1)}), bf16[4,2,256,192]{2,3,1,0:T(8,128)(2,1)S(1)}, u32[]{:S(2)}, u32[]{:S(2)}) async-start(bf16[4,2,256,192]{2,3,1,0:T(8,128)(2,1)} %copy.72), calls=%async_computation.4 | async-start | bytes 1572864 | tf_op jit(solution)/shard_map/all_to_all | solution.py:546
  213.6 91.9 %collective-permute-start.13 = (bf16[4,4,96,768]{3,2,1,0:T(8,128)(2,1)}, bf16[4,4,96,768]{3,2,1,0:T(8,128)(2,1)}, u32[]{:S(2)}, u32[]{:S(2)}) collective-permute-start(bf16[4,4,96,768]{3,2,1,0:T(8,128)(2,1)} %get-tuple-element.42), channel_id=1, source_target_pairs={{0,4},{1,5},{2,6},{3,7},{4,0},{5,1},{6,2},{7,3},{8,12},{9,13},{10,... | collective-permute-start | bytes 7077896 | tf_op jit(solution)/shard_map/ppermute | solution.py:394
  262.5 3.8 copy-start.8
  262.5 3.8 copy-start.7
  270.4 30.2 %all-to-all-start.5 = ((bf16[8,96,576]{2,1,0:T(8,128)(2,1)}), bf16[8,96,576]{2,1,0:T(8,128)(2,1)S(1)}, u32[]{:S(2)}, u32[]{:S(2)}) async-start(bf16[8,96,576]{2,1,0:T(8,128)(2,1)} %pad_maximum_fusion.4), calls=%async_computation.5 | async-start | bytes 1966080 | tf_op jit(solution)/shard_map/all_to_all | solution.py:583
  276.3 47.5 %collective-permute-start.12 = (bf16[4,4,240,384]{3,2,1,0:T(8,128)(2,1)}, bf16[4,4,240,384]{3,2,1,0:T(8,128)(2,1)}, u32[]{:S(2)}, u32[]{:S(2)}) collective-permute-start(bf16[4,4,240,384]{3,2,1,0:T(8,128)(2,1)} %get-tuple-element.38), channel_id=1, source_target_pairs={{0,4},{1,5},{2,6},{3,7},{4,0},{5,1},{6,2},{7,3},{8,12},{9,13},{10,... | collective-permute-start | bytes 8847368 | tf_op jit(solution)/shard_map/ppermute | solution.py:394
  300.8 4.7 copy-start.4
  301.8 18.3 %all-to-all-start.6 = ((bf16[8,96,576]{2,1,0:T(8,128)(2,1)}), bf16[8,96,576]{2,1,0:T(8,128)(2,1)S(1)}, u32[]{:S(2)}, u32[]{:S(2)}) async-start(bf16[8,96,576]{2,1,0:T(8,128)(2,1)} %broadcast_in_dim.82), calls=%async_computation.6 | async-start | bytes 1966080 | tf_op jit(solution)/shard_map/all_to_all | solution.py:375
  320.2 30.6 %all-to-all-start.10 = ((bf16[4,4,96,768]{3,2,1,0:T(8,128)(2,1)}), bf16[4,4,96,768]{3,2,1,0:T(8,128)(2,1)S(1)}, u32[]{:S(2)}, u32[]{:S(2)}) async-start(bf16[4,4,96,768]{3,2,1,0:T(8,128)(2,1)} %add_convert_fusion.1), calls=%async_computation.10 | async-start | bytes 4718592 | tf_op jit(solution)/shard_map/all_to_all | solution.py:533
  350.7 37.3 %all-to-all-start.7 = ((bf16[4,4,240,384]{3,2,1,0:T(8,128)(2,1)}), bf16[4,4,240,384]{3,2,1,0:T(8,128)(2,1)}, u32[]{:S(2)}, u32[]{:S(2)}) async-start(bf16[4,4,240,384]{3,2,1,0:T(8,128)(2,1)} %add_convert_fusion), calls=%async_computation.7 | async-start | bytes 5898240 | tf_op jit(solution)/shard_map/all_to_all | solution.py:533
  355.4 36.3 %copy-start.14 = (f32[8,8,384]{2,1,0:T(8,128)S(1)}, f32[8,8,384]{2,1,0:T(8,128)}, u32[]{:S(2)}) copy-start(f32[8,8,384]{2,1,0:T(8,128)} %get-tuple-element.40) | copy-start | bytes 294916
  355.4 36.4 %copy-start.15 = (f32[8,768]{1,0:T(8,128)S(1)}, f32[8,768]{1,0:T(8,128)}, u32[]{:S(2)}) copy-start(f32[8,768]{1,0:T(8,128)} %get-tuple-element.39) | copy-start | bytes 73732
  388.0 18.8 %all-to-all-start.11 = ((bf16[4,96,768]{2,1,0:T(8,128)(2,1)}), bf16[4,96,768]{2,1,0:T(8,128)(2,1)S(1)}, u32[]{:S(2)}, u32[]{:S(2)}) async-start(bf16[4,96,768]{2,1,0:T(8,128)(2,1)} %reduce_sum.83), calls=%async_computation.11 | async-start | bytes 1179648 | tf_op jit(solution)/shard_map/all_to_all | solution.py:535
  391.5 2.9 copy-start.9
  391.5 2.9 copy-start.13
  398.1 63.4 %collective-permute-start.10 = (bf16[1024,768]{1,0:T(8,128)(2,1)}, bf16[1024,768]{1,0:T(8,128)(2,1)}, u32[]{:S(2)}, u32[]{:S(2)}) collective-permute-start(bf16[1024,768]{1,0:T(8,128)(2,1)} %convolution_convert_fusion), channel_id=1, source_target_pairs={{0,4},{1,5},{2,6},{3,7},{4,0},{5,1},{6,2},{7,3},{8,12},{9,13},{10,... | collective-permute-start | bytes 4718600 | tf_op jit(solution)/shard_map/ppermute | solution.py:394
  406.8 48.8 %all-to-all-start.8 = ((bf16[4,240,384]{2,1,0:T(8,128)(2,1)}), bf16[4,240,384]{2,1,0:T(8,128)(2,1)S(1)}, u32[]{:S(2)}, u32[]{:S(2)}) async-start(bf16[4,240,384]{2,1,0:T(8,128)(2,1)} %reduce_sum.80), calls=%async_computation.8 | async-start | bytes 1474560 | tf_op jit(solution)/shard_map/all_to_all | solution.py:535
  456.7 20.8 %all-to-all-start.12 = ((bf16[8,96,768]{2,1,0:T(8,128)(2,1)}), bf16[8,96,768]{2,1,0:T(8,128)(2,1)S(1)}, u32[]{:S(2)}, u32[]{:S(2)}) async-start(bf16[8,96,768]{2,1,0:T(8,128)(2,1)} %broadcast_in_dim.90), calls=%async_computation.12 | async-start | bytes 2359296 | tf_op jit(solution)/shard_map/all_to_all | solution.py:375
  465.0 1.6 copy-start.5
  467.6 26.1 %collective-permute-start.11 = (bf16[512,768]{1,0:T(8,128)(2,1)}, bf16[512,768]{1,0:T(8,128)(2,1)}, u32[]{:S(2)}, u32[]{:S(2)}) collective-permute-start(bf16[512,768]{1,0:T(8,128)(2,1)} %slice.245), channel_id=1, source_target_pairs={{0,8},{1,9},{2,10},{3,11},{4,12},{5,13},{6,14},{7,15},{8,0},{9,1},... | collective-permute-start | bytes 2359304 | tf_op jit(solution)/shard_map/ppermute | solution.py:394
  477.5 1.6 copy-start.2
  479.1 30.6 %all-to-all-start.9 = ((bf16[8,240,384]{2,1,0:T(8,128)(2,1)}), bf16[8,240,384]{2,1,0:T(8,128)(2,1)S(1)}, u32[]{:S(2)}, u32[]{:S(2)}) async-start(bf16[8,240,384]{2,1,0:T(8,128)(2,1)} %broadcast_in_dim.89), calls=%async_computation.9 | async-start | bytes 2949120 | tf_op jit(solution)/shard_map/all_to_all | solution.py:375
  488.0 1.8 copy-start.6
  493.7 3.3 copy-start.3
  510.0 2.9 copy-start.1

commit v2 on v1

v2 whole, which is shorter than its diff:
```python
import functools
import math

import jax
import jax.numpy as jnp
from jax import lax
from jax.experimental import pallas as pl
from jax.experimental.pallas import tpu as pltpu
from jax.sharding import Mesh
from jax.sharding import PartitionSpec as P

NEG = -1000000000.0
EPS = 1e-05
BF = jnp.bfloat16
F32 = jnp.float32
AX = ("seq", "pg", "x", "core", "wt")
VM = pl.BlockSpec(memory_space=pltpu.VMEM)
SM = pl.BlockSpec(memory_space=pltpu.SMEM)
ANY = pl.BlockSpec(memory_space=pl.ANY)
OFFS = (0, 2, 1, 3)
VMEM_LIMIT = 60 * 2**20


def mm(a, b):
    return jnp.dot(a, b, preferred_element_type=F32)


def mm_nt(a, b):
    return lax.dot_general(a, b, (((1,), (1,)), ((), ())), preferred_element_type=F32)


def mm_tn(a, b):
    return lax.dot_general(a, b, (((0,), (0,)), ((), ())), preferred_element_type=F32)


def span(bounds, s, first, last):
    low = jnp.int32(0)
    high = bounds[s, 5]
    for d in range(1, 5):
        low = jnp.where(bounds[s, d] <= first, bounds[s, d], low)
        e = 5 - d
        high = jnp.where(bounds[s, e] > last, bounds[s, e], high)
    return low, high


def attn_fwd_kernel(pg, KC, bounds, idx, t0, t1, t2, t3, bias, w_own, w_z1, w_z2, w_z3, w_y,
                    o_ref, q_out, k_out, v_out, w, m_s, acc_s, sem):
    c, mine, y, z = (idx[i] for i in range(4))
    T = t0.shape[2]
    D = t0.shape[3]
    copies = [(w_own, w.at[z])]
    for k, ref in enumerate((w_z1, w_z2, w_z3)):
        copies.append((ref.at[0:96], w.at[z ^ (k + 1), pl.ds(pl.multiple_of(y * 96, 16), 96)]))
        copies.append((w_y.at[k, 0:96], w.at[z ^ (k + 1), pl.ds(pl.multiple_of((1 - y) * 96, 16), 96)]))
    copies = [pltpu.make_async_copy(a, b, sem.at[i]) for i, (a, b) in enumerate(copies)]
    for cp in copies:
        cp.start()
    for cp in copies:
        cp.wait()
    lane = lax.broadcasted_iota(jnp.int32, (T, 128), 1)
    row = lax.broadcasted_iota(jnp.int32, (T, 128), 0)
    lower = lane < 64
    rel = lane & 63
    zero64 = jnp.zeros((T, 64), F32)

    for g in range(pg):
        for n, src in enumerate((t0, t1, t2, t3)):
            off = OFFS[n]
            place = pl.multiple_of((g * 4 + (c ^ off)) * T, T)
            own = pl.multiple_of((c ^ off) * T, T)
            pos = row + place
            for s in range(2):
                qkv = mm(src[g, s], w[...].reshape(D, 576)) + bias[...]
                qkv = qkv.astype(BF).astype(F32)
                seg = jnp.zeros((T, 128), jnp.int32)
                for d in range(1, 5):
                    seg = seg + (pos >= bounds[s, d]).astype(jnp.int32)
                hot = rel == seg
                q_aug = jnp.where(hot, 1.0, 0.0)
                k_aug = jnp.where(rel < 5, jnp.where(hot, 0.0, NEG), jnp.where(rel < 11, 1.0, 0.0))
                q01, k01, v01, q2v2 = (qkv[:, j * 128 : (j + 1) * 128] for j in range(4))
                k2 = jnp.concatenate([qkv[:, 512:576], zero64], axis=1)
                for h, (k, v) in enumerate(((k01, v01), (k01, v01), (k2, q2v2))):
                    half = ~lower if h == 1 else lower
                    k_out[s, h, pl.ds(place, T)] = jnp.where(half, k, k_aug).astype(BF)
                    half = lower if h == 0 else ~lower
                    v_out[s, h, pl.ds(place, T)] = jnp.where(half, v, 1.0).astype(BF)

                def store_q():
                    for h, q in enumerate((q01, q01, q2v2)):
                        half = ~lower if h == 1 else lower
                        q_out[s, h, pl.ds(own, T)] = jnp.where(half, q * 0.125, q_aug).astype(BF)

                if pg == 1:
                    store_q()
                else:
                    pl.when(mine == g)(store_q)

    def per_tile(si, _):
        s, i = si // 4, si % 4
        here = pl.multiple_of(i * T, T)
        first = (mine * 4 + i) * T
        low, high = span(bounds, s, first, first + T - 1)
        for h in range(3):
            m_s[h] = jnp.full((T, 128), -jnp.inf, F32)
            acc_s[h] = jnp.zeros((T, 128), F32)

        def step(kt, _):
            at = pl.multiple_of(kt * KC, KC)
            for h in range(3):
                sc = mm_nt(q_out[s, h, pl.ds(here, T)], k_out[s, h, pl.ds(at, KC)])
                old = m_s[h]
                parts = [sc[:, j * 128 : (j + 1) * 128] for j in range(KC // 128)]
                top = functools.reduce(jnp.maximum, parts)
                new = jnp.maximum(old, jnp.broadcast_to(jnp.max(top, axis=1, keepdims=True), (T, 128)))
                p = jnp.concatenate([jnp.exp(v - new).astype(BF) for v in parts], axis=1)
                acc_s[h] = acc_s[h] * jnp.exp(old - new) + mm(p, v_out[s, h, pl.ds(at, KC)])
                m_s[h] = new
            return 0

        lax.fori_loop(low // KC, (high + KC - 1) // KC, step, 0)
        outs = []
        for h in range(3):
            acc = acc_s[h]
            turned = pltpu.roll(acc, 64, 1)
            data = lower if h == 0 else ~lower
            total = jnp.where(data, turned, acc)
            outs.append(acc / total)
            lse = m_s[h] + jnp.log(total)
            l1 = lse.astype(BF).astype(F32)
            l2 = (lse - l1).astype(BF).astype(F32)
            l3 = lse - l1 - l2
            at = lane if h == 1 else lane - 64
            q = q_out[s, h, pl.ds(here, T)].astype(F32)
            q = jnp.where(at == 8, -l1, jnp.where(at == 9, -l2, jnp.where(at == 10, -l3, q)))
            q_out[s, h, pl.ds(here, T)] = q.astype(BF)
        o_ref[i, :, pl.ds(pl.multiple_of(s * 128, 128), 128)] = jnp.where(lower, outs[0], outs[1]).astype(BF)

        @pl.when(s == 0)
        def _():
            o_ref[i, :, 256:384] = pltpu.roll(outs[2], 64, 1).astype(BF)

        @pl.when(s == 1)
        def _():
            o_ref[i, :, 256:384] = jnp.where(lower, o_ref[i, :, 256:384].astype(F32), outs[2]).astype(BF)

        return 0

    lax.fori_loop(0, 8, per_tile, 0)


def attn_bwd_kernel(pg, KC, bounds, idx, q_ref, k_ref, v_ref, o_ref, do_ref, d_ref, dq_s, dk_s, dv_s, do_s):
    c, mine = idx[0], idx[1]
    T = o_ref.shape[1]
    lane = lax.broadcasted_iota(jnp.int32, (T, 128), 1)
    lower = lane < 64
    zero = jnp.zeros((T, 128), F32)

    def per_seq(s, _):
        dk_s[...] = jnp.zeros_like(dk_s)
        dv_s[...] = jnp.zeros_like(dv_s)
        live = bounds[s, 4]
        cols = pl.ds(pl.multiple_of(s * 128, 128), 128)

        def per_tile(i, _):
            here = pl.multiple_of(i * T, T)
            first = (mine * 4 + i) * T
            low, high = span(bounds, s, first, first + T - 1)
            high = jnp.minimum(high, live)
            pair = do_ref[i, :, cols].astype(F32)
            third = do_ref[i, :, 256:384].astype(F32)
            third = jnp.where(s == 0, pltpu.roll(third, 64, 1), third)
            o_third = o_ref[i, :, 256:384].astype(F32)
            o_third = jnp.where(s == 0, pltpu.roll(o_third, 64, 1), o_third)
            prod = pair * o_ref[i, :, cols].astype(F32)
            for h in range(3):
                data = lower if h == 0 else ~lower
                full = prod if h < 2 else third * o_third
                delta = jnp.sum(jnp.where(data, full, zero), axis=1, keepdims=True)
                d1 = delta.astype(BF).astype(F32)
                d2 = (delta - d1).astype(BF).astype(F32)
                d3 = delta - d1 - d2
                at = lane - 64 if h == 0 else lane
                aug = jnp.where(at == 8, -d1, jnp.where(at == 9, -d2, jnp.where(at == 10, -d3, zero)))
                do_s[h] = jnp.where(data, pair if h < 2 else third, aug).astype(BF)
                dq_s[h, pl.ds(here, T)] = zero

            def step(kt, _):
                at = pl.multiple_of(kt * KC, KC)
                for h in range(3):
                    q = q_ref[s, h, pl.ds(here, T)]
                    k = k_ref[s, h, pl.ds(at, KC)]
                    d = do_s[h]
                    pt = jnp.exp(mm_nt(k, q))
                    ds = (pt * mm_nt(v_ref[s, h, pl.ds(at, KC)], d)).astype(BF)
                    dv_s[h, pl.ds(at, KC)] += mm(pt.astype(BF), d)
                    dk_s[h, pl.ds(at, KC)] += mm(ds, q)
                    dq_s[h, pl.ds(here, T)] += mm_tn(ds, k)
                return 0

            lax.fori_loop(low // KC, (high + KC - 1) // KC, step, 0)
            return 0

        lax.fori_loop(0, 4, per_tile, 0)
        for g in range(pg):
            for n, off in enumerate(OFFS):
                at = pl.multiple_of((g * 4 + (c ^ off)) * T, T)
                own = pl.multiple_of((c ^ off) * T, T)
                keep = 0.125 if pg == 1 else jnp.where(mine == g, 0.125, 0.0)
                dq = [dq_s[h, pl.ds(own, T)] * keep for h in range(3)]
                dk = [dk_s[h, pl.ds(at, T)] for h in range(3)]
                dv = [dv_s[h, pl.ds(at, T)] for h in range(3)]
                d_ref[g, n, s, :, 0:128] = jnp.where(lower, dq[0], dq[1]).astype(BF)
                d_ref[g, n, s, :, 128:256] = jnp.where(lower, dk[0], dk[1]).astype(BF)
                d_ref[g, n, s, :, 256:384] = jnp.where(lower, dv[0], dv[1]).astype(BF)
                d_ref[g, n, s, :, 384:512] = jnp.where(lower, dq[2], dv[2]).astype(BF)
                d_ref[g, n, s, :, 512:576] = dk[2][:, 0:64].astype(BF)
        return 0

    lax.fori_loop(0, 2, per_seq, 0)


def gelu_parts(u):
    t = 1.0 / (1.0 + (0.3275911 * 0.7071067811865476) * jnp.abs(u))
    e = jnp.exp(-0.5 * u * u)
    poly = t * (
        0.127414796
        + t * (-0.142248368 + t * (0.7107068705 + t * (-0.7265760135 + t * 0.5307027145)))
    )
    tail = poly * e
    cdf = jnp.where(u >= 0, 1.0 - tail, tail)
    return u * cdf, cdf + u * e * 0.3989422804014327


def fold8(v):
    return jnp.sum(v.reshape(v.shape[0] // 8, 8, v.shape[1]), axis=0)


def gather_heads(tiles):
    (pair0, third0), (pair1, third1) = tiles
    lower = lax.broadcasted_iota(jnp.int32, pair0.shape, 1) < 64
    turned = pltpu.roll(pair1, 64, 1)
    return pair0, jnp.where(lower, third0, turned), jnp.where(lower, turned, pltpu.roll(third1, 64, 1))


def ffn_kernel(
    idx, bounds, attn, tok, cot, vec, b1, w_in, w_at, w_out,
    s1a, r2a, c1a, c2a, s1b, r2b, c1b, c2b,
    out, dfirst, dattn, g1o, g1x, g2o, g2x, small, gb1,
    w1, w2, wa, att, hlow, xhat, rstd, acc, act, gp, din, dlow, sums, g1s, g2s, gas, sem, gsem,
):
    c, z, h, y, x, mine = (idx[i] for i in range(6))
    R, D = tok.shape
    T = attn.shape[1]
    FB = b1.shape[2]
    TR = 128
    first_copies = [(w_at, wa.at[z])]
    copies = [(w_in, w1.at[z]), (w_out, w2.at[z])]
    for n, (ra, rb) in enumerate(((s1a, s1b), (r2a, r2b), (c1a, c1b), (c2a, c2b))):
        for k in range(2):
            p = idx[6 + 2 * n + k]
            q, half = p // 2, p % 2
            for kz in range(3):
                zz = z ^ (kz + 1)
                at = pl.ds(pl.multiple_of(half * FB, 128), FB)
                first_copies.append((ra.at[k, kz, 192:240], wa.at[zz, pl.ds(pl.multiple_of(q * 48, 16), 48), at]))
                copies.append((ra.at[k, kz, 0:192], w1.at[zz, :, pl.ds(pl.multiple_of(p * FB, 128), FB)]))
                copies.append((rb.at[k, kz], w2.at[zz, pl.ds(pl.multiple_of(p * 96, 16), 96)]))
    many = len(first_copies)
    first_copies = [pltpu.make_async_copy(a, b, sem.at[i]) for i, (a, b) in enumerate(first_copies)]
    copies = [pltpu.make_async_copy(a, b, sem.at[many + i]) for i, (a, b) in enumerate(copies)]
    for cp in first_copies + copies:
        cp.start()

    b_attn, g1v, s1v, b_out, g2v, s2v = (vec[i : i + 1, :] for i in range(6))
    sums[...] = jnp.zeros_like(sums)

    lower = lax.broadcasted_iota(jnp.int32, (T, 128), 1) < 64
    for s in range(2):
        for g in range(0, 4, 2):
            tiles = []
            for n in (g, g + 1):
                third = attn[n, :, 256:384].astype(F32)
                tiles.append((
                    attn[n, :, s * 128 : (s + 1) * 128].astype(F32),
                    third if s == 0 else pltpu.roll(third, 64, 1),
                ))
            for j, tile in enumerate(gather_heads(tiles)):
                at = g * 192 + j * 128
                att[s * T : (s + 1) * T, at : at + 128] = tile.astype(BF)

    for cp in first_copies:
        cp.wait()

    acc[...] = mm(att[...], wa[...].reshape(D, D))

    def first(r, _):
        rows = pl.ds(pl.multiple_of(r * TR, TR), TR)
        v = acc[rows, :] + tok[rows, :].astype(F32) + b_attn
        mean = jnp.mean(v, axis=-1, keepdims=True)
        v = v - mean
        rs = lax.rsqrt(jnp.mean(v * v, axis=-1, keepdims=True) + EPS)
        xh = v * rs
        xhat[rows, :] = xh
        rstd[rows, :] = jnp.broadcast_to(rs, (TR, 128))
        hid = xh * g1v + s1v
        hlow[rows, :] = hid.astype(BF)
        acc[rows, :] = hid + b_out
        return 0

    lax.fori_loop(0, R // TR, first, 0)
    for cp in copies:
        cp.wait()

    def forward(zz, _):
        for half in range(2):
            j = zz * 2 + half
            w = w1[:, :, pl.ds(pl.multiple_of(j * FB, 128), FB)].reshape(D, FB)
            u = mm(hlow[...], w) + b1[j]
            for r in range(R // TR):
                rows = slice(r * TR, (r + 1) * TR)
                a, d = gelu_parts(u[rows])
                act[j, rows, :] = a.astype(BF)
                gp[j, rows, :] = d.astype(BF)
            acc[...] += mm(act[j], w2[zz, half * FB : (half + 1) * FB, :])
        return 0

    lax.fori_loop(0, 4, forward, 0)

    def second(r, _):
        rows = pl.ds(pl.multiple_of(r * TR, TR), TR)
        s = r // (T // TR)
        v = acc[rows, :]
        mean = jnp.mean(v, axis=-1, keepdims=True)
        v = v - mean
        rs = lax.rsqrt(jnp.mean(v * v, axis=-1, keepdims=True) + EPS)
        xh = v * rs
        out[rows, :] = (xh * g2v + s2v).astype(BF)
        place = (mine * 4 + h) * T + r * TR - s * T
        pos = lax.broadcasted_iota(jnp.int32, (TR, D), 0) + place
        dy = jnp.where(pos < bounds[s, 4], cot[rows, :].astype(F32), 0.0)
        sums[4] += fold8(dy * xh)
        sums[5] += fold8(dy)
        dx = dy * g2v
        m1 = jnp.mean(dx, axis=-1, keepdims=True)
        m2 = jnp.mean(dx * xh, axis=-1, keepdims=True)
        ds = rs * (dx - m1 - xh * m2)
        low = ds.astype(BF)
        dlow[rows, :] = low
        sums[3] += fold8(low.astype(F32))
        acc[rows, :] = ds
        return 0

    lax.fori_loop(0, R // TR, second, 0)

    def place_of(yy, xx, cc):
        dy, dx = yy ^ y, xx ^ x
        return jnp.where(cc == 0, dy, dx), jnp.where(cc == 0, dx, dy)

    def emit(src, own, other, cc, s):
        @pl.when(cc == c)
        def _():
            pltpu.make_async_copy(src, own, s).start()

        @pl.when(cc != c)
        def _():
            pltpu.make_async_copy(src, other, s).start()

    def wait_block(slot):
        pltpu.make_async_copy(g1s.at[slot], g1o.at[0, 0, :, 0:192], gsem.at[slot]).wait()
        for i in range(4):
            pltpu.make_async_copy(g2s.at[slot, i], g2o.at[0, 0, 0], gsem.at[2 + slot * 4 + i]).wait()

    def backward(zz, _):
        for half in range(2):
            j = zz * 2 + half

            @pl.when(zz > 0)
            def _():
                wait_block(half)

            w2j = w2[zz, half * FB : (half + 1) * FB, :]
            w1j = w1[:, :, pl.ds(pl.multiple_of(j * FB, 128), FB)].reshape(D, FB)
            g2s[half] = mm_tn(act[j], dlow[...]).astype(BF).reshape(4, 96, D)
            for i in range(4):
                u, v = place_of(half, i // 2, i % 2)
                emit(g2s.at[half, i], g2o.at[u, v, zz], g2x.at[u, v, zz], i % 2, gsem.at[2 + half * 4 + i])
            da = mm_nt(dlow[...], w2j)
            gsum = jnp.zeros((8, FB), F32)
            for r in range(R // TR):
                rows = slice(r * TR, (r + 1) * TR)
                di = (da[rows] * gp[j, rows, :].astype(F32)).astype(BF)
                din[rows, :] = di
                gsum = gsum + fold8(di.astype(F32))
            gb1[j] = gsum
            acc[...] += mm_nt(din[...], w1j)
            g1s[half] = mm_tn(hlow[...], din[...]).astype(BF).reshape(4, 192, FB)
            u, v = place_of(zz // 2, zz % 2, half)
            emit(g1s.at[half], g1o.at[u, v, :, 0:192], g1x.at[u, v, :, 0:192], half, gsem.at[half])
        return 0

    lax.fori_loop(0, 4, backward, 0)

    def last(r, _):
        rows = pl.ds(pl.multiple_of(r * TR, TR), TR)
        dy = acc[rows, :]
        xh = xhat[rows, :]
        sums[1] += fold8(dy * xh)
        sums[2] += fold8(dy)
        dx = dy * g1v
        m1 = jnp.mean(dx, axis=-1, keepdims=True)
        m2 = jnp.mean(dx * xh, axis=-1, keepdims=True)
        df = rstd[rows, :1] * (dx - m1 - xh * m2)
        dfirst[rows, :] = df
        low = df.astype(BF)
        dlow[rows, :] = low
        sums[0] += fold8(low.astype(F32))
        return 0

    lax.fori_loop(0, R // TR, last, 0)
    acc[...] = mm_nt(dlow[...], wa[...].reshape(D, D))
    for g in range(0, 4, 2):
        thirds = []
        for s in range(2):
            t0, t1, t2 = (acc[s * T : (s + 1) * T, g * 192 + j * 128 : g * 192 + (j + 1) * 128] for j in range(3))
            t1r, t2r = pltpu.roll(t1, 64, 1), pltpu.roll(t2, 64, 1)
            dattn[g, :, s * 128 : (s + 1) * 128] = t0.astype(BF)
            dattn[g + 1, :, s * 128 : (s + 1) * 128] = jnp.where(lower, t1r, t2r).astype(BF)
            thirds.append((t1, t1r, t2, t2r))
        (a1, _, _, a2r), (_, b1r, b2, _) = thirds
        dattn[g, :, 256:384] = jnp.where(lower, a1, b1r).astype(BF)
        dattn[g + 1, :, 256:384] = jnp.where(lower, a2r, b2).astype(BF)
    gas[...] = mm_tn(att[...], dlow[...]).astype(BF).reshape(4, 192, D)
    for p in range(8):
        q, cc = p // 2, p % 2
        u, v = place_of(q // 2, q % 2, cc)
        src = gas.at[:, q * 48 : (q + 1) * 48, cc * FB : (cc + 1) * FB]
        emit(src, g1o.at[u, v, :, 192:240], g1x.at[u, v, :, 192:240], cc, gsem.at[10 + p])
    for i in range(6):
        small[i : i + 1, :] = jnp.sum(sums[i], axis=0, keepdims=True)
    small[6:8, :] = jnp.zeros((2, D), F32)
    for half in range(2):
        wait_block(half)
    for p in range(8):
        cc = p % 2
        src = gas.at[:, (p // 2) * 48 : (p // 2 + 1) * 48, cc * FB : (cc + 1) * FB]
        pltpu.make_async_copy(src, g1o.at[0, 0, :, 192:240], gsem.at[10 + p]).wait()


def grad_qkv_kernel(idx, d, t0, t1, t2, t3, extra, gq, acc):
    h = idx[2]
    R = t0.shape[0]
    for n, t in enumerate((t0, t1, t2, t3)):
        part = mm_tn(t[...], d[n])
        if n == 0:
            acc[...] = part
        else:
            acc[...] += part
    col = jnp.zeros((8, 576), F32)
    for n in range(4):
        col = col + fold8(d[n].astype(F32))
    col = jnp.sum(col, axis=0, keepdims=True)
    top = lax.broadcasted_iota(jnp.int32, (8, 576), 0) == 0
    for z in range(4):
        tail = jnp.where(top & (h == z), col, extra[z])
        for yy in range(2):
            gq[z * 2 + yy, 0:96, :] = acc[z * 192 + yy * 96 : z * 192 + (yy + 1) * 96, :].astype(BF)
            gq[z * 2 + yy, 96:104, :] = tail.astype(BF)


def grad_in_kernel(d, w, dfirst, gi_own, gi_x, gi_b):
    gi_b[0] = mm_nt(d[2], w[...]).astype(BF)
    gi_b[1] = mm_nt(d[3], w[...]).astype(BF)
    gi_x[...] = mm_nt(d[1], w[...])
    gi_own[...] = mm_nt(d[0], w[...]) + dfirst[...]


def out_ffn_kernel(idx, s1a, r2a, c1a, c2a, s1b, r2b, c1b, c2b, g_wi, g_wa, g_wo):
    FB = s1a.shape[2]
    for n, (ra, rb) in enumerate(((s1a, s1b), (r2a, r2b), (c1a, c1b), (c2a, c2b))):
        for k in range(2):
            p = idx[6 + 2 * n + k]
            g_wi[:, pl.ds(pl.multiple_of(p * FB, 128), FB)] = ra[k, 0:192, :].astype(F32)
            rows = pl.ds(pl.multiple_of((p // 2) * 48, 16), 48)
            g_wa[rows, pl.ds(pl.multiple_of((p % 2) * FB, 128), FB)] = ra[k, 192:240, :].astype(F32)
            g_wo[pl.ds(pl.multiple_of(p * 96, 16), 96), :] = rb[k].astype(F32)


def out_qkv_kernel(idx, g, g_wq, g_wk, g_wv, tail):
    z = idx[1]
    lower = lax.broadcasted_iota(jnp.int32, (96, 128), 1) < 64
    for yy in range(2):
        rows = slice(yy * 96, (yy + 1) * 96)
        for h in range(0, 4, 2):
            a, b = g[yy * 4 + h], g[yy * 4 + h + 1]

            def tile(m, i):
                return m[0:96, i * 128 : (i + 1) * 128].astype(F32)

            k2 = [jnp.concatenate([m[0:96, 512:576], jnp.zeros((96, 64), BF)], axis=1).astype(F32) for m in (a, b)]
            q2v2 = [tile(a, 3), tile(b, 3)]
            thirds = (q2v2, k2, [pltpu.roll(v, 64, 1) for v in q2v2])
            for ref, i, (ta, tb) in zip((g_wq, g_wk, g_wv), range(3), thirds):
                turned = pltpu.roll(tile(b, i), 64, 1)
                at = h * 192
                ref[rows, at : at + 128] = tile(a, i)
                ref[rows, at + 128 : at + 256] = jnp.where(lower, ta, turned)
                ref[rows, at + 256 : at + 384] = jnp.where(lower, turned, pltpu.roll(tb, 64, 1))
    total = jnp.zeros((8, 576), F32)
    for h in range(4):
        total = total + g[h, 96:104, :].astype(F32)
    top = lax.broadcasted_iota(jnp.int32, (8, 576), 0) == 0
    tail[...] = jnp.where(top, g[z, 96:104, :].astype(F32), total)


def call(kernel, outs, in_specs, out_specs, scratch=(), flops=0, size=0, name=None):
    return pl.pallas_call(
        kernel,
        out_shape=outs,
        in_specs=in_specs,
        out_specs=out_specs,
        scratch_shapes=list(scratch),
        compiler_params=pltpu.CompilerParams(vmem_limit_bytes=VMEM_LIMIT),
        cost_estimate=pl.CostEstimate(flops=flops, bytes_accessed=size, transcendentals=0),
        name=name,
    )


def make_body(sizes):
    pg = sizes["pg"]
    order = [sizes[a] for a in AX]

    def send(fn, a):
        pairs = []
        for flat in range(math.prod(order)):
            at, rest = [], flat
            for n in reversed(order):
                at.append(rest % n)
                rest //= n
            dest = 0
            for n, v in zip(order, fn(*reversed(at))):
                dest = dest * n + v
            pairs.append((flat, dest))
        return lax.ppermute(a, AX, pairs)

    to_x = functools.partial(send, lambda s, g, x, c, z: (s, g, 1 - x, c, z))
    to_y = functools.partial(send, lambda s, g, x, c, z: (1 - s, g, x, c, z))
    to_core = functools.partial(send, lambda s, g, x, c, z: (s, g, x, 1 - c, z))
    to_z = [functools.partial(send, lambda s, g, x, c, z, k=k: (s, g, x, c, z ^ k)) for k in (1, 2, 3)]
    mix_a = functools.partial(send, lambda s, g, x, c, z: (s, g, 1 - x, c, z) if c == 0 else (1 - s, g, x, c, z))
    mix_b = functools.partial(send, lambda s, g, x, c, z: (1 - s, g, x, c, z) if c == 0 else (s, g, 1 - x, c, z))

    def spread(own):
        s1 = jnp.stack([own, mix_a(own)])
        r2 = mix_b(s1)
        return s1, r2, to_core(s1), to_core(r2)

    def body(
        tokens, cotangent, segment_ids, lengths, w_query, b_query, w_key, w_value, b_value, w_attn, b_attn,
        ln1_gain, ln1_shift, w_inner, b_inner, w_outer, b_outer, ln2_gain, ln2_shift,
    ):
        S, T, D = tokens.shape
        R = S * T
        y, x, c = (lax.axis_index(a) for a in ("seq", "x", "core"))
        mine, z = lax.axis_index("pg"), lax.axis_index("wt")
        h = x * 2 + c
        p = y * 4 + h
        L = 4 * pg * T
        FB = w_inner.shape[1] // 8

        ends = [lengths[:, :1]]
        for d in range(1, 4):
            ends.append(ends[-1] + lengths[:, d : d + 1])
        bounds = jnp.concatenate(
            [jnp.zeros_like(ends[0])] + ends + [jnp.full_like(ends[0], L), jnp.zeros((S, 2), jnp.int32)], axis=1
        ).astype(jnp.int32)
        a_of = jnp.where(c == 0, 2, 4)
        other = p ^ 1
        mates = [p, p ^ a_of, p ^ (6 - a_of), p ^ 6, other, other ^ (6 - a_of), other ^ a_of, other ^ 6]
        idx_a = jnp.stack([h, mine, y, z]).astype(jnp.int32)
        idx = jnp.stack([c, z, h, y, x, mine] + mates).astype(jnp.int32)

        def cols(w):
            return lax.dynamic_slice_in_dim(w, h * 192, 192, 1)

        wq, wk, wv = cols(w_query), cols(w_key), cols(w_value)
        w_own = jnp.concatenate([wq[:, :128], wk[:, :128], wv[:, :128], wq[:, 128:], wv[:, 128:], wk[:, 128:]], axis=1)
        none = jnp.zeros((128,), BF)
        rest = [b_attn, ln1_gain, ln1_shift, b_outer, ln2_gain, ln2_shift, b_inner, jnp.zeros((384 + 3 * 576,), BF)]
        smalls = jnp.concatenate(
            [b_query[:128], none, b_value[:128], b_query[128:], b_value[128:], none[:64]] + rest
        ).reshape(8, 576)
        pack = jnp.concatenate([lax.dynamic_slice_in_dim(w_own, y * 96, 96, 0), smalls], axis=0)
        w_z = [f(pack) for f in to_z]
        tok_x = to_x(tokens)
        tok_c = to_core(tokens)
        w_y = to_y(jnp.stack(w_z))
        tok_xc = to_core(tok_x)

        piece1 = jnp.concatenate(
            [lax.dynamic_slice_in_dim(w_inner, p * FB, FB, 1), lax.dynamic_slice(w_attn, ((p // 2) * 48, c * FB), (48, FB))],
            axis=0,
        )
        piece2 = lax.dynamic_slice_in_dim(w_outer, p * 96, 96, 0)
        one = spread(jnp.stack([f(piece1) for f in to_z]))
        two = spread(jnp.stack([f(piece2) for f in to_z]))

        sm = jnp.stack([smalls] + [v[96:] for v in w_z]).astype(F32).reshape(4, 8 * 576)
        sm = jnp.where((z & 1) == 0, sm, sm[jnp.array([1, 0, 3, 2])])
        sm = jnp.where((z & 2) == 0, sm, sm[jnp.array([2, 3, 0, 1])])
        bias = lax.dynamic_slice_in_dim(sm, h, 1, 0)[:, :576]
        vec = sm[:, 576:1728].reshape(4, 6, 192).transpose(1, 0, 2).reshape(6, D)
        vec = jnp.concatenate([vec, jnp.zeros((2, D), F32)], axis=0)
        b1 = sm[:, 1728:2496].reshape(8, 1, FB)

        toks = [tokens[None], tok_x[None], tok_c[None], tok_xc[None]]
        if pg > 1:
            toks = [lax.all_gather(t, "pg", axis=0, tiled=True) for t in toks]
        head = jax.ShapeDtypeStruct((S, 3, L, 128), BF)
        o, q_aug, k_aug, v_aug, w_qkv = call(
            functools.partial(attn_fwd_kernel, pg, 1024),
            (
                jax.ShapeDtypeStruct((4, T, 384), BF), jax.ShapeDtypeStruct((S, 3, 4 * T, 128), BF), head, head,
                jax.ShapeDtypeStruct((4, 192, 576), BF),
            ),
            [SM, SM] + [VM] * 5 + [ANY] * 5,
            (VM,) * 5,
            [pltpu.VMEM((3, T, 128), F32), pltpu.VMEM((3, T, 128), F32), pltpu.SemaphoreType.DMA((7,))],
            flops=20 * 10**9, size=10 * 2**20, name="attn_fwd",
        )(bounds, idx_a, *toks, bias, w_own, *w_z, w_y)
        w_qkv = w_qkv.reshape(D, 576)
        attn = lax.all_to_all(o, ("x", "core"), 0, 0, tiled=True)

        g1s = jax.ShapeDtypeStruct((2, 2, 4, 240, FB), BF)
        g2s = jax.ShapeDtypeStruct((2, 2, 4, 96, D), BF)
        layer_out, d_first, d_attn, g1o, g1x, g2o, g2x, small, gb1 = call(
            ffn_kernel,
            (
                jax.ShapeDtypeStruct((R, D), BF), jax.ShapeDtypeStruct((R, D), F32), jax.ShapeDtypeStruct((4, T, 384), BF),
                g1s, g1s, g2s, g2s, jax.ShapeDtypeStruct((8, D), F32), jax.ShapeDtypeStruct((8, 8, FB), F32),
            ),
            [SM, SM] + [VM] * 5 + [ANY] * 11,
            (VM, VM, VM, ANY, ANY, ANY, ANY, VM, VM),
            [
                pltpu.VMEM((4, 192, 8 * FB), BF),
                pltpu.VMEM((4, 2 * FB, D), BF),
                pltpu.VMEM((4, 192, D), BF),
                pltpu.VMEM((R, D), BF),
                pltpu.VMEM((R, D), BF),
                pltpu.VMEM((R, D), F32),
                pltpu.VMEM((R, 128), F32),
                pltpu.VMEM((R, D), F32),
                pltpu.VMEM((8, R, FB), BF),
                pltpu.VMEM((8, R, FB), BF),
                pltpu.VMEM((R, FB), BF),
                pltpu.VMEM((R, D), BF),
                pltpu.VMEM((8, 8, D), F32),
                pltpu.VMEM((2, 4, 192, FB), BF),
                pltpu.VMEM((2, 4, 96, D), BF),
                pltpu.VMEM((4, 192, D), BF),
                pltpu.SemaphoreType.DMA((75,)),
                pltpu.SemaphoreType.DMA((18,)),
            ],
            flops=30 * 10**9, size=20 * 2**20, name="ffn",
        )(
            idx, bounds, attn, tokens.reshape(R, D), cotangent.reshape(R, D), vec, b1, w_inner, w_attn, w_outer, *one, *two
        )

        d_o = lax.all_to_all(d_attn, ("x", "core"), 0, 0, tiled=True)

        def add(*parts):
            return sum(v.astype(F32) for v in parts)

        def reduce(own, other):
            got = to_core(other)
            first = mix_b(add(own[1], got[1]).astype(BF))
            second = mix_a(add(own[0, 1], got[0, 1], first[1]).astype(BF))

            def chunk(k):
                return add(*(lax.dynamic_index_in_dim(v, z ^ k, 0, False) for v in (own[0, 0], got[0, 0], first[0], second)))

            sent = [f(chunk(k + 1).astype(BF)) for k, f in enumerate(to_z)]
            v = add(chunk(0), *sent)
            if pg > 1:
                v = lax.psum(v, "pg")
            return spread(v.astype(BF))

        g2 = reduce(g2o, g2x)
        g1 = reduce(g1o, g1x)
        g_wi, g_wa, g_wo = call(
            out_ffn_kernel,
            (jax.ShapeDtypeStruct((192, 8 * FB), F32), jax.ShapeDtypeStruct((192, D), F32), jax.ShapeDtypeStruct((D, D), F32)),
            [SM] + [VM] * 8, (VM,) * 3, size=8 * 2**20, name="out_ffn",
        )(idx, *g1, *g2)

        d = call(
            functools.partial(attn_bwd_kernel, pg, 512),
            jax.ShapeDtypeStruct((pg, 4, S, T, 576), BF),
            [SM, SM] + [VM] * 5,
            VM,
            [pltpu.VMEM((3, 4 * T, 128), F32), pltpu.VMEM((3, L, 128), F32), pltpu.VMEM((3, L, 128), F32), pltpu.VMEM((3, T, 128), BF)],
            flops=25 * 10**9, size=10 * 2**20, name="attn_bwd",
        )(bounds, idx_a, q_aug, k_aug, v_aug, o, d_o)
        if pg > 1:
            d = lax.psum_scatter(d, "pg", scatter_dimension=0, tiled=True)
        d = d.reshape(4, R, 576)

        extra = jnp.concatenate(
            [
                small[:6].reshape(6, 4, 192).transpose(1, 0, 2).reshape(4, 6 * 192),
                jnp.sum(gb1, axis=1).reshape(4, 2 * FB),
                jnp.zeros((4, 384 + 3 * 576), F32),
            ],
            axis=1,
        ).reshape(4, 7, 576)
        extra = jnp.concatenate([jnp.zeros((4, 1, 576), F32), extra], axis=1)
        gq = call(
            grad_qkv_kernel, jax.ShapeDtypeStruct((8, 104, 576), BF), [SM] + [VM] * 6, VM,
            [pltpu.VMEM((D, 576), F32)], flops=2 * 10**9, size=6 * 2**20, name="grad_qkv",
        )(idx, d, *(t.reshape(R, D) for t in (tokens, tok_x, tok_c, tok_xc)), extra)
        gi_own, gi_x, gi_b = call(
            grad_in_kernel,
            (jax.ShapeDtypeStruct((R, D), F32), jax.ShapeDtypeStruct((R, D), F32), jax.ShapeDtypeStruct((2, R, D), BF)),
            [VM] * 3, (VM,) * 3, flops=2 * 10**9, size=10 * 2**20, name="grad_in",
        )(d, w_qkv, d_first)
        if pg > 1:
            gq = lax.psum(gq, "pg")
        gq = lax.all_to_all(gq, ("wt", "seq"), 0, 0, tiled=True)
        gi_b = to_core(gi_b)
        gi_x = to_x(add(gi_x, gi_b[1]).astype(BF))
        grad_input = add(gi_own, gi_b[0], gi_x).astype(BF).reshape(tokens.shape)
        gq = jnp.sum(gq.astype(F32), axis=0).astype(BF)
        gq = lax.all_to_all(jnp.broadcast_to(gq[None], (8, 104, 576)), ("seq", "x", "core"), 0, 0, tiled=True)
        mat = jax.ShapeDtypeStruct((192, D), F32)
        g_wq, g_wk, g_wv, tail = call(
            out_qkv_kernel, (mat, mat, mat, jax.ShapeDtypeStruct((8, 576), F32)), [SM, VM], (VM,) * 4,
            size=3 * 2**20, name="out_qkv",
        )(idx, gq)
        g_bq = jnp.concatenate([tail[0, 0:128], tail[0, 384:448]])
        g_bv = jnp.concatenate([tail[0, 256:384], tail[0, 448:512]])
        t = tail[1:].reshape(-1)
        six = [t[i * 192 : (i + 1) * 192] for i in range(6)]
        return (
            layer_out.reshape(tokens.shape), grad_input,
            g_wq, g_bq, g_wk, g_wv, g_bv, g_wa, six[0], six[1], six[2], g_wi, t[1152 : 1152 + 2 * FB], g_wo, six[3],
            six[4], six[5],
        )

    return body


def solution(mesh):
    sizes = dict(mesh.shape)
    pg = sizes["ctx"] // 4
    fine = dict(zip(AX, (sizes["seq"], pg, 2, 2, sizes["wt"])))
    split = Mesh(mesh.devices.reshape(tuple(fine.values())), AX)
    rows = P(("seq", "wt"), ("pg", "x", "core"), None)
    mat, vec = P("wt", None), P("wt")
    in_specs = (
        rows, rows, P(("seq", "wt"), ("pg", "x", "core")), P(("seq", "wt"), None),
        mat, vec, mat, mat, vec, mat, vec, vec, vec, mat, vec, mat, vec, vec, vec,
    )
    out_specs = (rows, rows, mat, vec, mat, mat, vec, mat, vec, vec, vec, mat, vec, mat, vec, vec, vec)
    return jax.shard_map(make_body(fine), mesh=split, in_specs=in_specs, out_specs=out_specs, check_vma=False)
```

time: 521 us -> 349 us (0.67)
  waiting for transfers between devices: 184 us -> 107 us
  blocking collectives: 40.6 us -> 0 us
  matrix products: 21.6 us -> 0 us
  Pallas kernels: 124 us -> 112 us
  local copies, waits for them, and re-layouts: 47.1 us -> 36.1 us
    all_to_all x12 -> x3, waiting for transfers between devices: 150 us -> 12.2 us  [the longest x1 10.5 us: body(): d_o = lax.all_to_all(d_attn, ('x', 'core'), 0, 0, tiled=True)]
    ppermute x14 -> x43, waiting for transfers between devices: 26 us -> 85.4 us  [send(): return lax.ppermute(a, AX, pairs)]
    psum x1 -> x0, blocking collectives: 40.6 us -> none  [body(): bias_sum = lax.psum(wide, AX)]
    all_to_all x12 -> x3, starting transfers between devices: 49 us -> 11.2 us  [the longest x1 3.86 us: body(): d_o = lax.all_to_all(d_attn, ('x', 'core'), 0, 0, tiled=True)]
    ppermute x14 -> x43, starting transfers between devices: 11 us -> 47.6 us  [send(): return lax.ppermute(a, AX, pairs)]
    dot_general x6 -> x0, matrix products: 21.6 us -> none  [the longest x2 7.73 us: project(): v = jnp.dot(t.reshape(-1, D), w_qkv, preferred_element_type=F32) + b_qkv]
    pallas_call x3 -> x7, Pallas kernels: 124 us -> 112 us  [the longest x1 41 us: body(): call(ffn_kernel, (jax.ShapeDtypeStruct((R, D), BF), jax.ShapeDtypeStruct(...]
    convert_element_type x5 -> x11, other arithmetic: 12.3 us -> 21.7 us  [the longest x2 5.45 us: reduce(): first = mix_b(add(own[1], got[1]).astype(BF))]
  transfers between devices with their start and end apart: 27 -> 47, of which waited for: 15 -> 16; matrix products, arithmetic and copies ran while one was open for 17% -> 16% of each run, Pallas kernels for 14% -> 19%
where the time goes in v2:
time: 349 us; the launch traced here: 345 us
  Pallas kernels  112 us (32%)
  waiting for transfers between devices  107 us (31%)
  starting transfers between devices  62.5 us (18%)
  local copies, waits for them, and re-layouts  36.1 us (10%)
  other arithmetic  27 us (8%)
    ppermute x43, waiting for transfers between devices, send(): return lax.ppermute(a, AX, pairs)  85.4 us
    ppermute x43, starting transfers between devices, send(): return lax.ppermute(a, AX, pairs)  47.6 us
    pallas_call x1, Pallas kernels, body(): call(ffn_kernel, (jax.ShapeDtypeStruct((R, D), BF), jax.ShapeDtypeStruct(...  41 us
    pallas_call x1, Pallas kernels, body(): call(functools.partial(attn_bwd_kernel, pg, 512), jax.ShapeDtypeStruct((p...  25.7 us
    pallas_call x1, Pallas kernels, body(): call(functools.partial(attn_fwd_kernel, pg, 1024), (jax.ShapeDtypeStruct(...  24.1 us
    all_to_all x1, waiting for transfers between devices, body(): d_o = lax.all_to_all(d_attn, ('x', 'core'), 0, 0, tiled=True)  10.5 us
    all_to_all x1, waiting for transfers between devices, body(): attn = lax.all_to_all(o, ('x', 'core'), 0, 0, tiled=True)  9.16 us
    pallas_call x1, Pallas kernels, body(): call(grad_in_kernel, (jax.ShapeDtypeStruct((R, D), F32), jax.ShapeDtypeSt...  7.06 us
  transfers between devices with their start and end apart: 47, of which 16 were waited for; matrix products, arithmetic and copies ran while one was open for 16% of the time, Pallas kernels for 19%

profile of v2, /device:TPU:0, one launch (start us, length us, event | category | flops | bytes accessed | tf_op | source)
XLA Modules:
  0.0 345.5 jit_solution(5441070429608930211)
XLA Ops:
  2.5 3.1 collective-permute-start.7
  5.5 2.6 collective-permute-start.8
  13.3 6.1 %concatenate.32 = bf16[4608]{0:T(1024)(128)(2,1)S(1)} concatenate(bf16[128]{0:T(256)(128)(2,1)} %bitcast.171, bf16[128]{0:T(256)(128)(2,1)S(1)} %broadcast_in_dim.39, bf16[128]{0:T(256)(128)(2,1)} %bitcast.172, bf16[64]{0:T(256)(128)(2,1)S(1)} %slice.180, bf16[64]{0:T(256)(128)(2,1)S(1)} %slice.181, bf16[64]{0:T(256)(128)(2,1)S(1)} %slice.182, bf16[192]{0:T(256)(128)(2,1)} %param.30, ...), dimensions={0} | concatenate | bytes 18432 | tf_op jit(solution)/shard_map/concatenate | solution.py:590
  20.2 3.9 %collective-permute-start.5 = (bf16[104,576]{1,0:T(8,128)(2,1)S(1)}, bf16[104,576]{1,0:T(8,128)(2,1)S(1)}, u32[]{:S(2)}, u32[]{:S(2)}) collective-permute-start(bf16[104,576]{1,0:T(8,128)(2,1)S(1)} %pad_maximum_fusion.8), channel_id=1, source_target_pairs={{0,3},{1,2},{2,1},{3,0},{4,7},{5,6},{6,5},{7,4},{8,11},{9,10},{10,... | collective-permute-start | bytes 359432 | tf_op jit(solution)/shard_map/ppermute | solution.py:544
  26.8 6.6 %collective-permute-done.4.w_z2 = bf16[104,576]{1,0:T(8,128)(2,1)S(1)} collective-permute-done((bf16[104,576]{1,0:T(8,128)(2,1)S(1)}, bf16[104,576]{1,0:T(8,128)(2,1)S(1)}, u32[]{:S(2)}, u32[]{:S(2)}) %collective-permute-start.4) | collective-permute-done | bytes 119840 | tf_op jit(solution)/shard_map/ppermute | solution.py:544
  33.6 1.0 collective-permute-start.16
  34.8 2.9 collective-permute-start.9
  39.1 10.0 %collective-permute-done.15 = bf16[96,768]{1,0:T(8,128)(2,1)S(1)} collective-permute-done((bf16[96,768]{1,0:T(8,128)(2,1)S(1)}, bf16[96,768]{1,0:T(8,128)(2,1)S(1)}, u32[]{:S(2)}, u32[]{:S(2)}) %collective-permute-start.15) | collective-permute-done | bytes 147488 | tf_op jit(solution)/shard_map/ppermute | solution.py:544
  49.1 1.5 collective-permute-start
  50.7 1.6 collective-permute-start.6
  53.0 1.6 collective-permute-start.10
  55.2 15.4 %collective-permute-done.17 = bf16[3,96,768]{2,1,0:T(8,128)(2,1)S(1)} collective-permute-done((bf16[3,96,768]{2,1,0:T(8,128)(2,1)S(1)}, bf16[3,96,768]{2,1,0:T(8,128)(2,1)S(1)}, u32[]{:S(2)}, u32[]{:S(2)}) %collective-permute-start.17) | collective-permute-done | bytes 442400 | tf_op jit(solution)/shard_map/ppermute | solution.py:544
  71.4 1.1 pad_maximum_fusion.1.s1b
  72.5 1.6 collective-permute-start.18
  74.1 6.9 %collective-permute-done.10 = bf16[3,240,384]{2,1,0:T(8,128)(2,1)S(1)} collective-permute-done((bf16[3,240,384]{2,1,0:T(8,128)(2,1)S(1)}, bf16[3,240,384]{2,1,0:T(8,128)(2,1)S(1)}, u32[]{:S(2)}, u32[]{:S(2)}) %collective-permute-start.10) | collective-permute-done | bytes 552992 | tf_op jit(solution)/shard_map/ppermute | solution.py:544
  81.2 1.6 collective-permute-start.11
  84.0 1.7 collective-permute-done.18.r2b
  86.3 11.3 %collective-permute-done.11.r2a = bf16[2,3,240,384]{3,2,1,0:T(8,128)(2,1)} collective-permute-done((bf16[2,3,240,384]{3,2,1,0:T(8,128)(2,1)S(1)}, bf16[2,3,240,384]{3,2,1,0:T(8,128)(2,1)}, u32[]{:S(2)}, u32[]{:S(2)}) %collective-permute-start.11) | collective-permute-done | bytes 1105952 | tf_op jit(solution)/shard_map/ppermute | solution.py:544
  97.8 24.1 %attn_fwd.1 = (bf16[4,256,384]{2,1,0:T(8,128)(2,1)}, bf16[2,3,1024,128]{3,2,1,0:T(8,128)(2,1)}, bf16[2,3,1024,128]{3,2,1,0:T(8,128)(2,1)}, bf16[2,3,1024,128]{3,2,1,0:T(8,128)(2,1)}, bf16[4,192,576]{2,1,0:T(8,128)(2,1)}) custom-call(s32[2,8]{1,0:T(2,128)} %concatenate.31.bounds, s32[4]{0:T(128)} %pad_add_fusion.idx, bf16[1,2,256,768]{3,2,1,0:T(8,128)(2,1)} %bitcast.13.t0, ...), custom_call_target="tpu_custom_call" | custom-call | flops 20000000000 | bytes 10485760 | tf_op jit(solution)/shard_map/attn_fwd/pallas_call | solution.py:620
  121.9 3.7 %all-to-all-start = ((bf16[4,256,384]{2,1,0:T(8,128)(2,1)}), bf16[4,256,384]{2,1,0:T(8,128)(2,1)S(1)}, u32[]{:S(2)}, u32[]{:S(2)}) async-start(bf16[4,256,384]{2,1,0:T(8,128)(2,1)} %get-tuple-element.41.o_ref), calls=%async_computation | async-start | bytes 1572864 | tf_op jit(solution)/shard_map/all_to_all | solution.py:632
  127.9 9.2 %all-to-all-done.attn = bf16[4,256,384]{2,1,0:T(8,128)(2,1)S(1)} async-done(((bf16[4,256,384]{2,1,0:T(8,128)(2,1)}), bf16[4,256,384]{2,1,0:T(8,128)(2,1)S(1)}, u32[]{:S(2)}, u32[]{:S(2)}) %all-to-all-start) | async-done | bytes 786464 | tf_op jit(solution)/shard_map/all_to_all | solution.py:632
  137.9 41.0 %ffn.1 = (bf16[512,768]{1,0:T(8,128)(2,1)}, f32[512,768]{1,0:T(8,128)}, bf16[4,256,384]{2,1,0:T(8,128)(2,1)}, bf16[2,2,4,240,384]{4,3,2,1,0:T(8,128)(2,1)}, bf16...) custom-call(s32[14]{0:T(128)} %stack.149.idx, ...), custom_call_target="tpu_custom_call" | custom-call | flops 30000001024 | bytes 20971520 | tf_op jit(solution)/shard_map/ffn/pallas_call | solution.py:636
  179.0 3.9 %all-to-all-start.1 = ((bf16[4,256,384]{2,1,0:T(8,128)(2,1)}), bf16[4,256,384]{2,1,0:T(8,128)(2,1)S(1)}, u32[]{:S(2)}, u32[]{:S(2)}) async-start(bf16[4,256,384]{2,1,0:T(8,128)(2,1)} %get-tuple-element.46), calls=%async_computation.1 | async-start | bytes 1572864 | tf_op jit(solution)/shard_map/all_to_all | solution.py:669
  183.7 10.5 %all-to-all-done.1.do_ref = bf16[4,256,384]{2,1,0:T(8,128)(2,1)S(1)} async-done(((bf16[4,256,384]{2,1,0:T(8,128)(2,1)}), bf16[4,256,384]{2,1,0:T(8,128)(2,1)S(1)}, u32[]{:S(2)}, u32[]{:S(2)}) %all-to-all-start.1) | async-done | bytes 786464 | tf_op jit(solution)/shard_map/all_to_all | solution.py:669
  195.2 25.7 %attn_bwd.1 = bf16[1,4,2,256,576]{4,3,2,1,0:T(8,128)(2,1)} custom-call(s32[2,8]{1,0:T(2,128)} %concatenate.31.bounds, s32[4]{0:T(128)} %pad_add_fusion.idx, bf16[2,3,1024,128]{3,2,1,0:T(8,128)(2,1)} %get-tuple-element.43.q_ref, bf16[2,3,1024,128]{3,2,1,0:T(8,128)(2,1)} %get-tuple-element.44.k_ref, bf16[2,3,1024,128]{3,2,1,0:T(8,128)(2,1)} %get-tuple-element.45.v_ref, ...), custom_call_target="tpu_custom_call" | custom-call | flops 24999999488 | bytes 10485760 | tf_op jit(solution)/shard_map/attn_bwd/pallas_call | solution.py:696
  220.9 7.1 %grad_in.1 = (f32[512,768]{1,0:T(8,128)}, f32[512,768]{1,0:T(8,128)}, bf16[2,512,768]{2,1,0:T(8,128)(2,1)}) custom-call(bf16[4,512,576]{2,1,0:T(8,128)(2,1)} %bitcast.174, bf16[768,576]{1,0:T(8,128)(2,1)} %bitcast.176, f32[512,768]{1,0:T(8,128)} %get-tuple-element.48.dfirst), custom_call_target="tpu_custom_call" | custom-call | flops 2000000000 | bytes 10485760 | tf_op jit(solution)/shard_map/grad_in/pallas_call | solution.py:721
  228.0 2.9 fusion.3
  230.8 1.5 collective-permute-start.24
  233.1 6.8 %grad_qkv.1 = bf16[8,104,576]{2,1,0:T(8,128)(2,1)} custom-call(s32[14]{0:T(128)} %stack.149.idx, bf16[4,512,576]{2,1,0:T(8,128)(2,1)} %bitcast.175, bf16[512,768]{1,0:T(8,128)(2,1)} %bitcast.20.tok.t0, bf16[512,768]{1,0:T(8,128)(2,1)} %bitcast.39.t1, bf16[512,768]{1,0:T(8,128)(2,1)} %bitcast.40.t2, bf16[512,768]{1,0:T(8,128)(2,1)} %bitcast.41.t3, ...), custom_call_target="tpu_custom_call" | custom-call | flops 2000000000 | bytes 6291456 | tf_op jit(solution)/shard_map/grad_qkv/pallas_call | solution.py:717
  240.0 3.6 %all-to-all-start.2 = ((bf16[8,104,576]{2,1,0:T(8,128)(2,1)}), bf16[8,104,576]{2,1,0:T(8,128)(2,1)S(1)}, u32[]{:S(2)}, u32[]{:S(2)}) async-start(bf16[8,104,576]{2,1,0:T(8,128)(2,1)} %grad_qkv.1), calls=%async_computation.2 | async-start | bytes 2129920 | tf_op jit(solution)/shard_map/all_to_all | solution.py:728
  243.6 2.6 fusion.5
  246.1 1.9 collective-permute-start.34
  248.0 12.6 %collective-permute-done.24 = bf16[2,4,240,384]{3,2,1,0:T(8,128)(2,1)} collective-permute-done((bf16[2,4,240,384]{3,2,1,0:T(8,128)(2,1)}, bf16[2,4,240,384]{3,2,1,0:T(8,128)(2,1)}, u32[]{:S(2)}, u32[]{:S(2)}) %collective-permute-start.24) | collective-permute-done | bytes 1474592 | tf_op jit(solution)/shard_map/ppermute | solution.py:544
  260.6 2.7 fusion.4
  263.3 2.2 fusion
  265.6 2.0 collective-permute-start.22
  267.6 1.7 all-to-all-done.2
  270.1 2.0 broadcast_in_dim.44
  272.1 3.8 %all-to-all-start.3 = ((bf16[8,104,576]{2,1,0:T(8,128)(2,1)}), bf16[8,104,576]{2,1,0:T(8,128)(2,1)S(1)}, u32[]{:S(2)}, u32[]{:S(2)}) async-start(bf16[8,104,576]{2,1,0:T(8,128)(2,1)} %broadcast_in_dim.44), calls=%async_computation.3 | async-start | bytes 2129920 | tf_op jit(solution)/shard_map/all_to_all | solution.py:733
  275.9 11.9 %collective-permute-done.34 = bf16[2,4,96,768]{3,2,1,0:T(8,128)(2,1)} collective-permute-done((bf16[2,4,96,768]{3,2,1,0:T(8,128)(2,1)}, bf16[2,4,96,768]{3,2,1,0:T(8,128)(2,1)}, u32[]{:S(2)}, u32[]{:S(2)}) %collective-permute-start.34) | collective-permute-done | bytes 1179680 | tf_op jit(solution)/shard_map/ppermute | solution.py:544
  287.8 2.3 fusion.6
  291.2 1.2 slice.202
  292.4 1.9 slice.242
  294.3 1.2 slice.237
  295.5 1.2 slice.239
  296.7 2.2 fusion.9
  300.1 3.2 collective-permute-start.28
  303.3 2.5 fusion.2
  306.9 2.8 out_qkv.1
  309.6 1.1 slice.244
  310.7 1.6 fusion.16
  312.4 1.1 collective-permute-start.37
  313.6 3.2 collective-permute-start.38
  316.8 1.4 fusion.13
  318.2 1.9 collective-permute-start.29
  320.1 3.0 collective-permute-done.37
  323.1 1.2 fusion.20
  324.3 2.0 collective-permute-start.39
  326.4 2.6 collective-permute-start.30
  329.0 2.1 collective-permute-done.39
  331.1 1.4 collective-permute-start.40
  332.7 1.8 collective-permute-done.30.r2a
  336.3 1.7 collective-permute-done.40.r2b
  341.1 4.4 %out_ffn.1 = (f32[192,3072]{1,0:T(8,128)}, f32[192,768]{1,0:T(8,128)}, f32[768,768]{1,0:T(8,128)}) custom-call(s32[14]{0:T(128)} %stack.149.idx, bf16[2,240,384]{2,1,0:T(8,128)(2,1)} %copy-done.5, bf16[2,240,384]{2,1,0:T(8,128)(2,1)} %copy-done.13, bf16[2,240,384]{2,1,0:T(8,128)(2,1)} %copy-done.14, bf16[2,240,384]{2,1,0:T(8,128)(2,1)} %copy-done.15, ...), custom_call_target="tpu_custom_call" | custom-call | bytes 8388608 | tf_op jit(solution)/shard_map/out_ffn/pallas_call | solution.py:690
  (183 shorter events, 31.2 us)
Async XLA Ops:
  0.7 23.5 %copy-start.27 = (s32[4]{0:T(128)S(1)}, s32[4]{0:T(128)}, u32[]{:S(2)}) copy-start(s32[4]{0:T(128)} %constant.184) | copy-start | bytes 52
  0.7 23.5 %copy-start.26 = (s32[4]{0:T(128)S(1)}, s32[4]{0:T(128)}, u32[]{:S(2)}) copy-start(s32[4]{0:T(128)} %constant.185) | copy-start | bytes 52
  0.7 23.5 %copy-start.25 = (s32[2,4]{1,0:T(2,128)S(1)}, s32[2,4]{1,0:T(2,128)}, u32[]{:S(2)}) copy-start(s32[2,4]{1,0:T(2,128)} %param.23) | copy-start | bytes 100
  2.5 48.2 %collective-permute-start.7 = (bf16[240,384]{1,0:T(8,128)(2,1)S(1)}, bf16[240,384]{1,0:T(8,128)(2,1)S(1)}, u32[]{:S(2)}, u32[]{:S(2)}) collective-permute-start(bf16[240,384]{1,0:T(8,128)(2,1)S(1)} %pad_maximum_fusion.7), channel_id=1, source_target_pairs={{0,1},{1,0},{2,3},{3,2},{4,5},{5,4},{6,7},{7,6},{8,9},{9,8},{10,11... | collective-permute-start | bytes 552968 | tf_op jit(solution)/shard_map/ppermute | solution.py:544
  5.5 46.8 %collective-permute-start.8 = (bf16[240,384]{1,0:T(8,128)(2,1)S(1)}, bf16[240,384]{1,0:T(8,128)(2,1)S(1)}, u32[]{:S(2)}, u32[]{:S(2)}) collective-permute-start(bf16[240,384]{1,0:T(8,128)(2,1)S(1)} %pad_maximum_fusion.7), channel_id=1, source_target_pairs={{0,2},{1,3},{2,0},{3,1},{4,6},{5,7},{6,4},{7,5},{8,10},{9,11},{10,... | collective-permute-start | bytes 552968 | tf_op jit(solution)/shard_map/ppermute | solution.py:544
  19.7 31.0 %copy-start.11 = (bf16[192,576]{1,0:T(8,128)(2,1)}, bf16[192,576]{1,0:T(8,128)(2,1)S(1)}, u32[]{:S(2)}) copy-start(bf16[192,576]{1,0:T(8,128)(2,1)S(1)} %concatenate.33.w_own) | copy-start | bytes 663556
  19.7 6.8 %collective-permute-start.3 = (bf16[104,576]{1,0:T(8,128)(2,1)S(1)}, bf16[104,576]{1,0:T(8,128)(2,1)S(1)}, u32[]{:S(2)}, u32[]{:S(2)}) collective-permute-start(bf16[104,576]{1,0:T(8,128)(2,1)S(1)} %pad_maximum_fusion.8), channel_id=1, source_target_pairs={{0,1},{1,0},{2,3},{3,2},{4,5},{5,4},{6,7},{7,6},{8,9},{9,8},{10,11... | collective-permute-start | bytes 359432 | tf_op jit(solution)/shard_map/ppermute | solution.py:544
  20.2 13.2 %collective-permute-start.4 = (bf16[104,576]{1,0:T(8,128)(2,1)S(1)}, bf16[104,576]{1,0:T(8,128)(2,1)S(1)}, u32[]{:S(2)}, u32[]{:S(2)}) collective-permute-start(bf16[104,576]{1,0:T(8,128)(2,1)S(1)} %pad_maximum_fusion.8), channel_id=1, source_target_pairs={{0,2},{1,3},{2,0},{3,1},{4,6},{5,7},{6,4},{7,5},{8,10},{9,11},{10,... | collective-permute-start | bytes 359432 | tf_op jit(solution)/shard_map/ppermute | solution.py:544
  20.2 13.3 %collective-permute-start.5 = (bf16[104,576]{1,0:T(8,128)(2,1)S(1)}, bf16[104,576]{1,0:T(8,128)(2,1)S(1)}, u32[]{:S(2)}, u32[]{:S(2)}) collective-permute-start(bf16[104,576]{1,0:T(8,128)(2,1)S(1)} %pad_maximum_fusion.8), channel_id=1, source_target_pairs={{0,3},{1,2},{2,1},{3,0},{4,7},{5,6},{6,5},{7,4},{8,11},{9,10},{10,... | collective-permute-start | bytes 359432 | tf_op jit(solution)/shard_map/ppermute | solution.py:544
  26.6 24.0 %copy-start.19 = (bf16[104,576]{1,0:T(8,128)(2,1)}, bf16[104,576]{1,0:T(8,128)(2,1)S(1)}, u32[]{:S(2)}) copy-start(bf16[104,576]{1,0:T(8,128)(2,1)S(1)} %collective-permute-done.3.w_z1) | copy-start | bytes 359428
  26.6 8.2 %collective-permute-start.14 = (bf16[96,768]{1,0:T(8,128)(2,1)S(1)}, bf16[96,768]{1,0:T(8,128)(2,1)S(1)}, u32[]{:S(2)}, u32[]{:S(2)}) collective-permute-start(bf16[96,768]{1,0:T(8,128)(2,1)S(1)} %constant_dynamic-slice_fusion.3), channel_id=1, source_target_pairs={{0,1},{1,0},{2,3},{3,2},{4,5},{5,4},{6,7},{7,6},{8,9},{9,8},{10,11... | collective-permute-start | bytes 442376 | tf_op jit(solution)/shard_map/ppermute | solution.py:544
  33.4 17.2 %copy-start.20 = (bf16[104,576]{1,0:T(8,128)(2,1)}, bf16[104,576]{1,0:T(8,128)(2,1)S(1)}, u32[]{:S(2)}) copy-start(bf16[104,576]{1,0:T(8,128)(2,1)S(1)} %collective-permute-done.4.w_z2) | copy-start | bytes 359428
  33.4 15.7 %collective-permute-start.15 = (bf16[96,768]{1,0:T(8,128)(2,1)S(1)}, bf16[96,768]{1,0:T(8,128)(2,1)S(1)}, u32[]{:S(2)}, u32[]{:S(2)}) collective-permute-start(bf16[96,768]{1,0:T(8,128)(2,1)S(1)} %constant_dynamic-slice_fusion.3), channel_id=1, source_target_pairs={{0,2},{1,3},{2,0},{3,1},{4,6},{5,7},{6,4},{7,5},{8,10},{9,11},{10,... | collective-permute-start | bytes 442376 | tf_op jit(solution)/shard_map/ppermute | solution.py:544
  33.6 19.3 %copy-start.21 = (bf16[104,576]{1,0:T(8,128)(2,1)}, bf16[104,576]{1,0:T(8,128)(2,1)S(1)}, u32[]{:S(2)}) copy-start(bf16[104,576]{1,0:T(8,128)(2,1)S(1)} %collective-permute-done.5.w_z3) | copy-start | bytes 359428
  33.6 17.0 %collective-permute-start.16 = (bf16[96,768]{1,0:T(8,128)(2,1)S(1)}, bf16[96,768]{1,0:T(8,128)(2,1)S(1)}, u32[]{:S(2)}, u32[]{:S(2)}) collective-permute-start(bf16[96,768]{1,0:T(8,128)(2,1)S(1)} %constant_dynamic-slice_fusion.3), channel_id=1, source_target_pairs={{0,3},{1,2},{2,1},{3,0},{4,7},{5,6},{6,5},{7,4},{8,11},{9,10},{10,... | collective-permute-start | bytes 442376 | tf_op jit(solution)/shard_map/ppermute | solution.py:544
  34.8 18.0 %collective-permute-start.9 = (bf16[240,384]{1,0:T(8,128)(2,1)S(1)}, bf16[240,384]{1,0:T(8,128)(2,1)S(1)}, u32[]{:S(2)}, u32[]{:S(2)}) collective-permute-start(bf16[240,384]{1,0:T(8,128)(2,1)S(1)} %pad_maximum_fusion.7), channel_id=1, source_target_pairs={{0,3},{1,2},{2,1},{3,0},{4,7},{5,6},{6,5},{7,4},{8,11},{9,10},{10,... | collective-permute-start | bytes 552968 | tf_op jit(solution)/shard_map/ppermute | solution.py:544
  49.1 33.7 %collective-permute-start = (bf16[2,256,768]{2,1,0:T(8,128)(2,1)}, bf16[2,256,768]{2,1,0:T(8,128)(2,1)}, u32[]{:S(2)}, u32[]{:S(2)}) collective-permute-start(bf16[2,256,768]{2,1,0:T(8,128)(2,1)} %param.21), channel_id=1, source_target_pairs={{0,8},{1,9},{2,10},{3,11},{4,12},{5,13},{6,14},{7,15},{8,0},{9,1},... | collective-permute-start | bytes 2359304 | tf_op jit(solution)/shard_map/ppermute | solution.py:544
  50.6 33.4 %collective-permute-start.1 = (bf16[2,256,768]{2,1,0:T(8,128)(2,1)}, bf16[2,256,768]{2,1,0:T(8,128)(2,1)}, u32[]{:S(2)}, u32[]{:S(2)}) collective-permute-start(bf16[2,256,768]{2,1,0:T(8,128)(2,1)} %param.21), channel_id=1, source_target_pairs={{0,4},{1,5},{2,6},{3,7},{4,0},{5,1},{6,2},{7,3},{8,12},{9,13},{10,... | collective-permute-start | bytes 2359304 | tf_op jit(solution)/shard_map/ppermute | solution.py:544
  50.7 32.8 %collective-permute-start.6 = (bf16[3,104,576]{2,1,0:T(8,128)(2,1)}, bf16[3,104,576]{2,1,0:T(8,128)(2,1)}, u32[]{:S(2)}, u32[]{:S(2)}) collective-permute-start(bf16[3,104,576]{2,1,0:T(8,128)(2,1)} %pad_maximum_fusion.4), channel_id=1, source_target_pairs={{0,16},{1,17},{2,18},{3,19},{4,20},{5,21},{6,22},{7,23},{8,24},{9,... | collective-permute-start | bytes 1078280 | tf_op jit(solution)/shard_map/ppermute | solution.py:544
  52.3 18.3 %collective-permute-start.17 = (bf16[3,96,768]{2,1,0:T(8,128)(2,1)S(1)}, bf16[3,96,768]{2,1,0:T(8,128)(2,1)S(1)}, u32[]{:S(2)}, u32[]{:S(2)}) collective-permute-start(bf16[3,96,768]{2,1,0:T(8,128)(2,1)S(1)} %get-tuple-element.77), channel_id=1, source_target_pairs={{0,8},{1,9},{2,10},{3,11},{4,20},{5,21},{6,22},{7,23},{8,0},{9,1},... | collective-permute-start | bytes 1327112 | tf_op jit(solution)/shard_map/ppermute | solution.py:544
  53.0 28.1 %collective-permute-start.10 = (bf16[3,240,384]{2,1,0:T(8,128)(2,1)S(1)}, bf16[3,240,384]{2,1,0:T(8,128)(2,1)S(1)}, u32[]{:S(2)}, u32[]{:S(2)}) collective-permute-start(bf16[3,240,384]{2,1,0:T(8,128)(2,1)S(1)} %get-tuple-element.75), channel_id=1, source_target_pairs={{0,8},{1,9},{2,10},{3,11},{4,20},{5,21},{6,22},{7,23},{8,0},{9,1},... | collective-permute-start | bytes 1658888 | tf_op jit(solution)/shard_map/ppermute | solution.py:544
  72.5 49.4 %copy-start.8 = (bf16[2,3,96,768]{3,2,1,0:T(8,128)(2,1)}, bf16[2,3,96,768]{3,2,1,0:T(8,128)(2,1)S(1)}, u32[]{:S(2)}) copy-start(bf16[2,3,96,768]{3,2,1,0:T(8,128)(2,1)S(1)} %pad_maximum_fusion.1.s1b) | copy-start | bytes 2654212
  72.5 13.2 %collective-permute-start.18 = (bf16[2,3,96,768]{3,2,1,0:T(8,128)(2,1)S(1)}, bf16[2,3,96,768]{3,2,1,0:T(8,128)(2,1)}, u32[]{:S(2)}, u32[]{:S(2)}) collective-permute-start(bf16[2,3,96,768]{3,2,1,0:T(8,128)(2,1)S(1)} %pad_maximum_fusion.1.s1b), channel_id=1, source_target_pairs={{0,16},{1,17},{2,18},{3,19},{4,12},{5,13},{6,14},{7,15},{8,24},{9,... | collective-permute-start | bytes 2654216 | tf_op jit(solution)/shard_map/ppermute | solution.py:544
  81.2 40.7 %copy-start.7 = (bf16[2,3,240,384]{3,2,1,0:T(8,128)(2,1)}, bf16[2,3,240,384]{3,2,1,0:T(8,128)(2,1)S(1)}, u32[]{:S(2)}) copy-start(bf16[2,3,240,384]{3,2,1,0:T(8,128)(2,1)S(1)} %pad_maximum_fusion.s1a) | copy-start | bytes 3317764
  81.2 16.4 %collective-permute-start.11 = (bf16[2,3,240,384]{3,2,1,0:T(8,128)(2,1)S(1)}, bf16[2,3,240,384]{3,2,1,0:T(8,128)(2,1)}, u32[]{:S(2)}, u32[]{:S(2)}) collective-permute-start(bf16[2,3,240,384]{3,2,1,0:T(8,128)(2,1)S(1)} %pad_maximum_fusion.s1a), channel_id=1, source_target_pairs={{0,16},{1,17},{2,18},{3,19},{4,12},{5,13},{6,14},{7,15},{8,24},{9,... | collective-permute-start | bytes 3317768 | tf_op jit(solution)/shard_map/ppermute | solution.py:544
  82.8 15.1 %collective-permute-start.2 = (bf16[2,256,768]{2,1,0:T(8,128)(2,1)}, bf16[2,256,768]{2,1,0:T(8,128)(2,1)}, u32[]{:S(2)}, u32[]{:S(2)}) collective-permute-start(bf16[2,256,768]{2,1,0:T(8,128)(2,1)} %collective-permute-done), channel_id=1, source_target_pairs={{0,4},{1,5},{2,6},{3,7},{4,0},{5,1},{6,2},{7,3},{8,12},{9,13},{10,... | collective-permute-start | bytes 2359304 | tf_op jit(solution)/shard_map/ppermute | solution.py:544
  83.5 44.4 %collective-permute-start.19 = (bf16[2,3,96,768]{3,2,1,0:T(8,128)(2,1)S(1)}, bf16[2,3,96,768]{3,2,1,0:T(8,128)(2,1)}, u32[]{:S(2)}, u32[]{:S(2)}) collective-permute-start(bf16[2,3,96,768]{3,2,1,0:T(8,128)(2,1)S(1)} %pad_maximum_fusion.1.s1b), channel_id=1, source_target_pairs={{0,4},{1,5},{2,6},{3,7},{4,0},{5,1},{6,2},{7,3},{8,12},{9,13},{10,... | collective-permute-start | bytes 2654216 | tf_op jit(solution)/shard_map/ppermute | solution.py:544
  84.0 43.9 %collective-permute-start.12 = (bf16[2,3,240,384]{3,2,1,0:T(8,128)(2,1)S(1)}, bf16[2,3,240,384]{3,2,1,0:T(8,128)(2,1)}, u32[]{:S(2)}, u32[]{:S(2)}) collective-permute-start(bf16[2,3,240,384]{3,2,1,0:T(8,128)(2,1)S(1)} %pad_maximum_fusion.s1a), channel_id=1, source_target_pairs={{0,4},{1,5},{2,6},{3,7},{4,0},{5,1},{6,2},{7,3},{8,12},{9,13},{10,... | collective-permute-start | bytes 3317768 | tf_op jit(solution)/shard_map/ppermute | solution.py:544
  85.7 51.3 %collective-permute-start.20 = (bf16[2,3,96,768]{3,2,1,0:T(8,128)(2,1)}, bf16[2,3,96,768]{3,2,1,0:T(8,128)(2,1)}, u32[]{:S(2)}, u32[]{:S(2)}) collective-permute-start(bf16[2,3,96,768]{3,2,1,0:T(8,128)(2,1)} %collective-permute-done.18.r2b), channel_id=1, source_target_pairs={{0,4},{1,5},{2,6},{3,7},{4,0},{5,1},{6,2},{7,3},{8,12},{9,13},{10,... | collective-permute-start | bytes 2654216 | tf_op jit(solution)/shard_map/ppermute | solution.py:544
  97.6 39.5 %collective-permute-start.13 = (bf16[2,3,240,384]{3,2,1,0:T(8,128)(2,1)}, bf16[2,3,240,384]{3,2,1,0:T(8,128)(2,1)}, u32[]{:S(2)}, u32[]{:S(2)}) collective-permute-start(bf16[2,3,240,384]{3,2,1,0:T(8,128)(2,1)} %collective-permute-done.11.r2a), channel_id=1, source_target_pairs={{0,4},{1,5},{2,6},{3,7},{4,0},{5,1},{6,2},{7,3},{8,12},{9,13},{10,... | collective-permute-start | bytes 3317768 | tf_op jit(solution)/shard_map/ppermute | solution.py:544
  121.9 15.1 %all-to-all-start = ((bf16[4,256,384]{2,1,0:T(8,128)(2,1)}), bf16[4,256,384]{2,1,0:T(8,128)(2,1)S(1)}, u32[]{:S(2)}, u32[]{:S(2)}) async-start(bf16[4,256,384]{2,1,0:T(8,128)(2,1)} %get-tuple-element.41.o_ref), calls=%async_computation | async-start | bytes 1572864 | tf_op jit(solution)/shard_map/all_to_all | solution.py:632
  179.0 15.3 %all-to-all-start.1 = ((bf16[4,256,384]{2,1,0:T(8,128)(2,1)}), bf16[4,256,384]{2,1,0:T(8,128)(2,1)S(1)}, u32[]{:S(2)}, u32[]{:S(2)}) async-start(bf16[4,256,384]{2,1,0:T(8,128)(2,1)} %get-tuple-element.46), calls=%async_computation.1 | async-start | bytes 1572864 | tf_op jit(solution)/shard_map/all_to_all | solution.py:669
  182.8 45.1 %collective-permute-start.23 = (bf16[2,2,4,240,384]{4,3,2,1,0:T(8,128)(2,1)}, bf16[2,2,4,240,384]{4,3,2,1,0:T(8,128)(2,1)}, u32[]{:S(2)}, u32[]{:S(2)}) collective-permute-start(bf16[2,2,4,240,384]{4,3,2,1,0:T(8,128)(2,1)} %get-tuple-element.59), channel_id=1, source_target_pairs={{0,4},{1,5},{2,6},{3,7},{4,0},{5,1},{6,2},{7,3},{8,12},{9,13},{10,... | collective-permute-start | bytes 8847368 | tf_op jit(solution)/shard_map/ppermute | solution.py:544
  183.1 60.5 %collective-permute-start.33 = (bf16[2,2,4,96,768]{4,3,2,1,0:T(8,128)(2,1)}, bf16[2,2,4,96,768]{4,3,2,1,0:T(8,128)(2,1)}, u32[]{:S(2)}, u32[]{:S(2)}) collective-permute-start(bf16[2,2,4,96,768]{4,3,2,1,0:T(8,128)(2,1)} %get-tuple-element.61), channel_id=1, source_target_pairs={{0,4},{1,5},{2,6},{3,7},{4,0},{5,1},{6,2},{7,3},{8,12},{9,13},{10,... | collective-permute-start | bytes 7077896 | tf_op jit(solution)/shard_map/ppermute | solution.py:544
  220.9 7.1 %copy-start.1 = (bf16[2,2,4,240,384]{4,3,2,1,0:T(8,128)(2,1)S(1)}, bf16[2,2,4,240,384]{4,3,2,1,0:T(8,128)(2,1)}, u32[]{:S(2)}) copy-start(bf16[2,2,4,240,384]{4,3,2,1,0:T(8,128)(2,1)} %get-tuple-element.58) | copy-start | bytes 8847364
  227.9 35.4 %collective-permute-start.21 = (bf16[2,512,768]{2,1,0:T(8,128)(2,1)}, bf16[2,512,768]{2,1,0:T(8,128)(2,1)}, u32[]{:S(2)}, u32[]{:S(2)}) collective-permute-start(bf16[2,512,768]{2,1,0:T(8,128)(2,1)} %get-tuple-element.50), channel_id=1, source_target_pairs={{0,4},{1,5},{2,6},{3,7},{4,0},{5,1},{6,2},{7,3},{8,12},{9,13},{10,... | collective-permute-start | bytes 4718600 | tf_op jit(solution)/shard_map/ppermute | solution.py:544
  230.8 29.8 %collective-permute-start.24 = (bf16[2,4,240,384]{3,2,1,0:T(8,128)(2,1)}, bf16[2,4,240,384]{3,2,1,0:T(8,128)(2,1)}, u32[]{:S(2)}, u32[]{:S(2)}) collective-permute-start(bf16[2,4,240,384]{3,2,1,0:T(8,128)(2,1)} %fusion.3), channel_id=1, source_target_pairs={{0,16},{1,17},{2,18},{3,19},{4,12},{5,13},{6,14},{7,15},{8,24},{9,... | collective-permute-start | bytes 4423688 | tf_op jit(solution)/shard_map/ppermute | solution.py:544
  233.1 10.4 %copy-start.2 = (bf16[2,2,4,96,768]{4,3,2,1,0:T(8,128)(2,1)S(1)}, bf16[2,2,4,96,768]{4,3,2,1,0:T(8,128)(2,1)}, u32[]{:S(2)}) copy-start(bf16[2,2,4,96,768]{4,3,2,1,0:T(8,128)(2,1)} %get-tuple-element.60) | copy-start | bytes 7077892
  240.0 29.3 %all-to-all-start.2 = ((bf16[8,104,576]{2,1,0:T(8,128)(2,1)}), bf16[8,104,576]{2,1,0:T(8,128)(2,1)S(1)}, u32[]{:S(2)}, u32[]{:S(2)}) async-start(bf16[8,104,576]{2,1,0:T(8,128)(2,1)} %grad_qkv.1), calls=%async_computation.2 | async-start | bytes 2129920 | tf_op jit(solution)/shard_map/all_to_all | solution.py:728
  246.1 17.2 %copy-start.3 = (f32[512,768]{1,0:T(8,128)S(1)}, f32[512,768]{1,0:T(8,128)}, u32[]{:S(2)}) copy-start(f32[512,768]{1,0:T(8,128)} %get-tuple-element.51) | copy-start | bytes 4718596
  246.1 41.7 %collective-permute-start.34 = (bf16[2,4,96,768]{3,2,1,0:T(8,128)(2,1)}, bf16[2,4,96,768]{3,2,1,0:T(8,128)(2,1)}, u32[]{:S(2)}, u32[]{:S(2)}) collective-permute-start(bf16[2,4,96,768]{3,2,1,0:T(8,128)(2,1)} %fusion.5), channel_id=1, source_target_pairs={{0,16},{1,17},{2,18},{3,19},{4,12},{5,13},{6,14},{7,15},{8,24},{9,... | collective-permute-start | bytes 3538952 | tf_op jit(solution)/shard_map/ppermute | solution.py:544
  263.3 33.4 %collective-permute-start.25 = (bf16[4,240,384]{2,1,0:T(8,128)(2,1)}, bf16[4,240,384]{2,1,0:T(8,128)(2,1)}, u32[]{:S(2)}, u32[]{:S(2)}) collective-permute-start(bf16[4,240,384]{2,1,0:T(8,128)(2,1)} %fusion.4), channel_id=1, source_target_pairs={{0,8},{1,9},{2,10},{3,11},{4,20},{5,21},{6,22},{7,23},{8,0},{9,1},... | collective-permute-start | bytes 2211848 | tf_op jit(solution)/shard_map/ppermute | solution.py:544
  265.6 37.8 %collective-permute-start.22 = (bf16[512,768]{1,0:T(8,128)(2,1)}, bf16[512,768]{1,0:T(8,128)(2,1)}, u32[]{:S(2)}, u32[]{:S(2)}) collective-permute-start(bf16[512,768]{1,0:T(8,128)(2,1)} %fusion), channel_id=1, source_target_pairs={{0,8},{1,9},{2,10},{3,11},{4,12},{5,13},{6,14},{7,15},{8,0},{9,1},... | collective-permute-start | bytes 2359304 | tf_op jit(solution)/shard_map/ppermute | solution.py:544
  272.1 33.8 %all-to-all-start.3 = ((bf16[8,104,576]{2,1,0:T(8,128)(2,1)}), bf16[8,104,576]{2,1,0:T(8,128)(2,1)S(1)}, u32[]{:S(2)}, u32[]{:S(2)}) async-start(bf16[8,104,576]{2,1,0:T(8,128)(2,1)} %broadcast_in_dim.44), calls=%async_computation.3 | async-start | bytes 2129920 | tf_op jit(solution)/shard_map/all_to_all | solution.py:733
  290.1 20.7 %collective-permute-start.35 = (bf16[4,96,768]{2,1,0:T(8,128)(2,1)}, bf16[4,96,768]{2,1,0:T(8,128)(2,1)}, u32[]{:S(2)}, u32[]{:S(2)}) collective-permute-start(bf16[4,96,768]{2,1,0:T(8,128)(2,1)} %fusion.6), channel_id=1, source_target_pairs={{0,8},{1,9},{2,10},{3,11},{4,20},{5,21},{6,22},{7,23},{8,0},{9,1},... | collective-permute-start | bytes 1769480 | tf_op jit(solution)/shard_map/ppermute | solution.py:544
  296.7 6.7 %copy-start.4 = (f32[512,768]{1,0:T(8,128)S(1)}, f32[512,768]{1,0:T(8,128)}, u32[]{:S(2)}) copy-start(f32[512,768]{1,0:T(8,128)} %get-tuple-element.49) | copy-start | bytes 4718596
  298.9 14.6 %collective-permute-start.26 = (bf16[240,384]{1,0:T(8,128)(2,1)}, bf16[240,384]{1,0:T(8,128)(2,1)}, u32[]{:S(2)}, u32[]{:S(2)}) collective-permute-start(bf16[240,384]{1,0:T(8,128)(2,1)} %get-tuple-element.68), channel_id=1, source_target_pairs={{0,1},{1,0},{2,3},{3,2},{4,5},{5,4},{6,7},{7,6},{8,9},{9,8},{10,11... | collective-permute-start | bytes 552968 | tf_op jit(solution)/shard_map/ppermute | solution.py:544
  299.4 17.4 %collective-permute-start.27 = (bf16[240,384]{1,0:T(8,128)(2,1)}, bf16[240,384]{1,0:T(8,128)(2,1)}, u32[]{:S(2)}, u32[]{:S(2)}) collective-permute-start(bf16[240,384]{1,0:T(8,128)(2,1)} %get-tuple-element.70), channel_id=1, source_target_pairs={{0,2},{1,3},{2,0},{3,1},{4,6},{5,7},{6,4},{7,5},{8,10},{9,11},{10,... | collective-permute-start | bytes 552968 | tf_op jit(solution)/shard_map/ppermute | solution.py:544
  300.1 16.7 %collective-permute-start.28 = (bf16[240,384]{1,0:T(8,128)(2,1)}, bf16[240,384]{1,0:T(8,128)(2,1)}, u32[]{:S(2)}, u32[]{:S(2)}) collective-permute-start(bf16[240,384]{1,0:T(8,128)(2,1)} %get-tuple-element.69), channel_id=1, source_target_pairs={{0,3},{1,2},{2,1},{3,0},{4,7},{5,6},{6,5},{7,4},{8,11},{9,10},{10,... | collective-permute-start | bytes 552968 | tf_op jit(solution)/shard_map/ppermute | solution.py:544
  312.4 7.7 %collective-permute-start.36 = (bf16[96,768]{1,0:T(8,128)(2,1)S(1)}, bf16[96,768]{1,0:T(8,128)(2,1)S(1)}, u32[]{:S(2)}, u32[]{:S(2)}) collective-permute-start(bf16[96,768]{1,0:T(8,128)(2,1)S(1)} %get-tuple-element.71), channel_id=1, source_target_pairs={{0,1},{1,0},{2,3},{3,2},{4,5},{5,4},{6,7},{7,6},{8,9},{9,8},{10,11... | collective-permute-start | bytes 442376 | tf_op jit(solution)/shard_map/ppermute | solution.py:544
  312.4 10.6 %collective-permute-start.37 = (bf16[96,768]{1,0:T(8,128)(2,1)S(1)}, bf16[96,768]{1,0:T(8,128)(2,1)S(1)}, u32[]{:S(2)}, u32[]{:S(2)}) collective-permute-start(bf16[96,768]{1,0:T(8,128)(2,1)S(1)} %get-tuple-element.73), channel_id=1, source_target_pairs={{0,2},{1,3},{2,0},{3,1},{4,6},{5,7},{6,4},{7,5},{8,10},{9,11},{10,... | collective-permute-start | bytes 442376 | tf_op jit(solution)/shard_map/ppermute | solution.py:544
  313.6 15.4 %copy-start.23 = (f32[8,576]{1,0:T(8,128)S(1)}, f32[8,576]{1,0:T(8,128)}, u32[]{:S(2)}) copy-start(f32[8,576]{1,0:T(8,128)} %get-tuple-element.55) | copy-start | bytes 55300
  313.6 9.5 %collective-permute-start.38 = (bf16[96,768]{1,0:T(8,128)(2,1)S(1)}, bf16[96,768]{1,0:T(8,128)(2,1)S(1)}, u32[]{:S(2)}, u32[]{:S(2)}) collective-permute-start(bf16[96,768]{1,0:T(8,128)(2,1)S(1)} %get-tuple-element.72), channel_id=1, source_target_pairs={{0,3},{1,2},{2,1},{3,0},{4,7},{5,6},{6,5},{7,4},{8,11},{9,10},{10,... | collective-permute-start | bytes 442376 | tf_op jit(solution)/shard_map/ppermute | solution.py:544
  318.2 8.1 %collective-permute-start.29 = (bf16[240,384]{1,0:T(8,128)(2,1)S(1)}, bf16[240,384]{1,0:T(8,128)(2,1)S(1)}, u32[]{:S(2)}, u32[]{:S(2)}) collective-permute-start(bf16[240,384]{1,0:T(8,128)(2,1)S(1)} %fusion.13), channel_id=1, source_target_pairs={{0,8},{1,9},{2,10},{3,11},{4,20},{5,21},{6,22},{7,23},{8,0},{9,1},... | collective-permute-start | bytes 552968 | tf_op jit(solution)/shard_map/ppermute | solution.py:544
  324.3 6.9 %collective-permute-start.39 = (bf16[96,768]{1,0:T(8,128)(2,1)S(1)}, bf16[96,768]{1,0:T(8,128)(2,1)S(1)}, u32[]{:S(2)}, u32[]{:S(2)}) collective-permute-start(bf16[96,768]{1,0:T(8,128)(2,1)S(1)} %fusion.20), channel_id=1, source_target_pairs={{0,8},{1,9},{2,10},{3,11},{4,20},{5,21},{6,22},{7,23},{8,0},{9,1},... | collective-permute-start | bytes 442376 | tf_op jit(solution)/shard_map/ppermute | solution.py:544
  326.3 13.2 %copy-start.5 = (bf16[2,240,384]{2,1,0:T(8,128)(2,1)}, bf16[2,240,384]{2,1,0:T(8,128)(2,1)S(1)}, u32[]{:S(2)}) copy-start(bf16[2,240,384]{2,1,0:T(8,128)(2,1)S(1)} %pad_maximum_fusion.5.s1a) | copy-start | bytes 1105924
  326.4 8.1 %collective-permute-start.30 = (bf16[2,240,384]{2,1,0:T(8,128)(2,1)S(1)}, bf16[2,240,384]{2,1,0:T(8,128)(2,1)S(1)}, u32[]{:S(2)}, u32[]{:S(2)}) collective-permute-start(bf16[2,240,384]{2,1,0:T(8,128)(2,1)S(1)} %pad_maximum_fusion.5.s1a), channel_id=1, source_target_pairs={{0,16},{1,17},{2,18},{3,19},{4,12},{5,13},{6,14},{7,15},{8,24},{9,... | collective-permute-start | bytes 1105928 | tf_op jit(solution)/shard_map/ppermute | solution.py:544
  331.1 8.4 %copy-start.6 = (bf16[2,96,768]{2,1,0:T(8,128)(2,1)}, bf16[2,96,768]{2,1,0:T(8,128)(2,1)S(1)}, u32[]{:S(2)}) copy-start(bf16[2,96,768]{2,1,0:T(8,128)(2,1)S(1)} %pad_maximum_fusion.6.s1b) | copy-start | bytes 884740
  331.1 6.8 %collective-permute-start.40 = (bf16[2,96,768]{2,1,0:T(8,128)(2,1)S(1)}, bf16[2,96,768]{2,1,0:T(8,128)(2,1)S(1)}, u32[]{:S(2)}, u32[]{:S(2)}) collective-permute-start(bf16[2,96,768]{2,1,0:T(8,128)(2,1)S(1)} %pad_maximum_fusion.6.s1b), channel_id=1, source_target_pairs={{0,16},{1,17},{2,18},{3,19},{4,12},{5,13},{6,14},{7,15},{8,24},{9,... | collective-permute-start | bytes 884744 | tf_op jit(solution)/shard_map/ppermute | solution.py:544
  332.7 6.9 %collective-permute-start.31 = (bf16[2,240,384]{2,1,0:T(8,128)(2,1)S(1)}, bf16[2,240,384]{2,1,0:T(8,128)(2,1)S(1)}, u32[]{:S(2)}, u32[]{:S(2)}) collective-permute-start(bf16[2,240,384]{2,1,0:T(8,128)(2,1)S(1)} %pad_maximum_fusion.5.s1a), channel_id=1, source_target_pairs={{0,4},{1,5},{2,6},{3,7},{4,0},{5,1},{6,2},{7,3},{8,12},{9,13},{10,... | collective-permute-start | bytes 1105928 | tf_op jit(solution)/shard_map/ppermute | solution.py:544
  334.5 5.1 %copy-start.13 = (bf16[2,240,384]{2,1,0:T(8,128)(2,1)}, bf16[2,240,384]{2,1,0:T(8,128)(2,1)S(1)}, u32[]{:S(2)}) copy-start(bf16[2,240,384]{2,1,0:T(8,128)(2,1)S(1)} %collective-permute-done.30.r2a) | copy-start | bytes 1105924
  334.5 5.0 %collective-permute-start.32 = (bf16[2,240,384]{2,1,0:T(8,128)(2,1)S(1)}, bf16[2,240,384]{2,1,0:T(8,128)(2,1)S(1)}, u32[]{:S(2)}, u32[]{:S(2)}) collective-permute-start(bf16[2,240,384]{2,1,0:T(8,128)(2,1)S(1)} %collective-permute-done.30.r2a), channel_id=1, source_target_pairs={{0,4},{1,5},{2,6},{3,7},{4,0},{5,1},{6,2},{7,3},{8,12},{9,13},{10,... | collective-permute-start | bytes 1105928 | tf_op jit(solution)/shard_map/ppermute | solution.py:544
  335.8 3.4 collective-permute-start.41
  337.9 1.6 collective-permute-start.42
  (11 other events, 17.5 us)

commit v3 on v2

v3 whole, which is shorter than its diff:
```python
import functools
import math

import jax
import jax.numpy as jnp
from jax import lax
from jax.experimental import pallas as pl
from jax.experimental.pallas import tpu as pltpu
from jax.sharding import Mesh
from jax.sharding import PartitionSpec as P

NEG = -1000000000.0
EPS = 1e-05
BF = jnp.bfloat16
F32 = jnp.float32
AX = ("seq", "pg", "x", "core", "wt")
VM = pl.BlockSpec(memory_space=pltpu.VMEM)
SM = pl.BlockSpec(memory_space=pltpu.SMEM)
ANY = pl.BlockSpec(memory_space=pl.ANY)
OFFS = (0, 2, 1, 3)
VMEM_LIMIT = 60 * 2**20


def mm(a, b):
    return jnp.dot(a, b, preferred_element_type=F32)


def mm_nt(a, b):
    return lax.dot_general(a, b, (((1,), (1,)), ((), ())), preferred_element_type=F32)


def mm_tn(a, b):
    return lax.dot_general(a, b, (((0,), (0,)), ((), ())), preferred_element_type=F32)


def fold8(v):
    return jnp.sum(v.reshape(v.shape[0] // 8, 8, v.shape[1]), axis=0)


def limits(lengths, s, length):
    out = [jnp.int32(0)]
    for d in range(4):
        out.append(out[-1] + lengths[s, d])
    return out + [jnp.int32(length)]


def span(bounds, first, last):
    low, high = bounds[0], bounds[5]
    for d in range(1, 5):
        low = jnp.where(bounds[d] <= first, bounds[d], low)
        high = jnp.where(bounds[5 - d] > last, bounds[5 - d], high)
    return low, high


def prep_kernel(idx, wq, wk, wv, w_at, w_in, w_out, *rest):
    vecs, (w_own, pack, piece1, piece2) = rest[:9], rest[9:]
    c, h, y = idx[0], idx[2], idx[3]
    p = y * 4 + h
    FB = piece1.shape[1]
    for head in range(4):

        @pl.when(h == head)
        def _():
            a = head * 192
            for i, w in enumerate((wq, wk, wv)):
                w_own[0:192, i * 128 : (i + 1) * 128] = w[:, a : a + 128]
            w_own[0:192, 384:448] = wq[:, a + 128 : a + 192]
            w_own[0:192, 448:512] = wv[:, a + 128 : a + 192]
            w_own[0:192, 512:576] = wk[:, a + 128 : a + 192]

    bq, bv = (v[...].reshape(1, 192) for v in vecs[:2])
    w_own[192:200, :] = jnp.zeros((8, 576), BF)
    w_own[192:193, 0:128] = bq[:, 0:128]
    w_own[192:193, 256:384] = bv[:, 0:128]
    w_own[192:193, 384:448] = bq[:, 128:192]
    w_own[192:193, 448:512] = bv[:, 128:192]
    pack[0:96, :] = w_own[pl.ds(pl.multiple_of(y * 96, 16), 96), :]
    pack[96:104, :] = w_own[192:200, :]
    piece1[0:192, :] = w_in[:, pl.ds(pl.multiple_of(p * FB, 128), FB)]
    piece1[192:240, :] = w_at[pl.ds(pl.multiple_of((p // 2) * 48, 16), 48), pl.ds(pl.multiple_of(c * FB, 128), FB)]
    piece1[240:256, :] = jnp.zeros((16, FB), BF)
    for i, v in enumerate(vecs[:8]):
        piece1[240 + i : 241 + i, 0:192] = v[...].reshape(1, 192)
    for i in range(4):
        piece1[248 + i : 249 + i, 0:192] = vecs[8][i * 192 : (i + 1) * 192].reshape(1, 192)
    piece2[...] = w_out[pl.ds(pl.multiple_of(c * FB + (p // 2) * 96, 16), 96), :]


def qkv_kernel(pg, lengths, idx, *refs):
    toks, (w_own, w_z1, w_z2, w_z3, w_y, q_out, k_out, v_out, w, bs, sem) = refs[:4], refs[4:]
    z, c, y, mine = idx[1], idx[2], idx[3], idx[5]
    T, D = toks[0].shape[2:]
    copies = [(w_own.at[0:192], w.at[z]), (w_own.at[192:200], bs.at[0])]
    for k, ref in enumerate((w_z1, w_z2, w_z3)):
        copies.append((ref.at[0:96], w.at[z ^ (k + 1), pl.ds(pl.multiple_of(y * 96, 16), 96)]))
        copies.append((ref.at[96:104], bs.at[k + 1]))
        copies.append((w_y.at[k, 0:96], w.at[z ^ (k + 1), pl.ds(pl.multiple_of((1 - y) * 96, 16), 96)]))
    copies = [pltpu.make_async_copy(a, b, sem.at[i]) for i, (a, b) in enumerate(copies)]
    for cp in copies:
        cp.start()
    for cp in copies:
        cp.wait()
    lane = lax.broadcasted_iota(jnp.int32, (T, 128), 1)
    row = lax.broadcasted_iota(jnp.int32, (T, 128), 0)
    lower = lane < 64
    rel = lane & 63
    zero64 = jnp.zeros((T, 64), F32)

    bias = bs[c ^ z, 0:1, :].astype(F32)
    for g in range(pg):
        for n, off in enumerate(OFFS):
            place = pl.multiple_of((g * 4 + (c ^ off)) * T, T)
            own = pl.multiple_of((c ^ off) * T, T)
            pos = row + place
            for s in range(2):
                qkv = mm(toks[n][g, s], w[...].reshape(D, 576)) + bias
                qkv = qkv.astype(BF).astype(F32)
                seg = jnp.zeros((T, 128), jnp.int32)
                for start in limits(lengths, s, 0)[1:5]:
                    seg = seg + (pos >= start).astype(jnp.int32)
                hot = rel == seg
                q_aug = jnp.where(hot, 1.0, 0.0)
                k_aug = jnp.where(rel < 5, jnp.where(hot, 0.0, NEG), jnp.where(rel < 11, 1.0, 0.0))
                q01, k01, v01, q2v2 = (qkv[:, j * 128 : (j + 1) * 128] for j in range(4))
                k2 = jnp.concatenate([qkv[:, 512:576], zero64], axis=1)
                for h, (k, v) in enumerate(((k01, v01), (k01, v01), (k2, q2v2))):
                    half = ~lower if h == 1 else lower
                    k_out[s, h, pl.ds(place, T)] = jnp.where(half, k, k_aug).astype(BF)
                    half = lower if h == 0 else ~lower
                    v_out[s, h, pl.ds(place, T)] = jnp.where(half, v, 1.0).astype(BF)

                def store_q():
                    for h, q in enumerate((q01, q01, q2v2)):
                        half = ~lower if h == 1 else lower
                        q_out[s, h, pl.ds(own, T)] = jnp.where(half, q * 0.125, q_aug).astype(BF)

                if pg == 1:
                    store_q()
                else:
                    pl.when(mine == g)(store_q)


def attn_fwd_kernel(KC, lengths, idx, q_ref, k_ref, v_ref, o_ref, q_out, m_s, acc_s):
    mine = idx[5]
    T, L = o_ref.shape[1], k_ref.shape[2]
    lane = lax.broadcasted_iota(jnp.int32, (T, 128), 1)
    lower = lane < 64

    def per_tile(si, _):
        s, i = si // 4, si % 4
        here = pl.multiple_of(i * T, T)
        first = (mine * 4 + i) * T
        low, high = span(limits(lengths, s, L), first, first + T - 1)
        for h in range(3):
            m_s[h] = jnp.full((T, 128), -jnp.inf, F32)
            acc_s[h] = jnp.zeros((T, 128), F32)

        def step(kt, _):
            at = pl.multiple_of(kt * KC, KC)
            for h in range(3):
                sc = mm_nt(q_ref[s, h, pl.ds(here, T)], k_ref[s, h, pl.ds(at, KC)])
                old = m_s[h]
                parts = [sc[:, j * 128 : (j + 1) * 128] for j in range(KC // 128)]
                top = functools.reduce(jnp.maximum, parts)
                new = jnp.maximum(old, jnp.broadcast_to(jnp.max(top, axis=1, keepdims=True), (T, 128)))
                p = jnp.concatenate([jnp.exp(v - new).astype(BF) for v in parts], axis=1)
                acc_s[h] = acc_s[h] * jnp.exp(old - new) + mm(p, v_ref[s, h, pl.ds(at, KC)])
                m_s[h] = new
            return 0

        lax.fori_loop(low // KC, (high + KC - 1) // KC, step, 0)
        outs = []
        for h in range(3):
            acc = acc_s[h]
            turned = pltpu.roll(acc, 64, 1)
            data = lower if h == 0 else ~lower
            total = jnp.where(data, turned, acc)
            outs.append(acc / total)
            lse = m_s[h] + jnp.log(total)
            l1 = lse.astype(BF).astype(F32)
            l2 = (lse - l1).astype(BF).astype(F32)
            l3 = lse - l1 - l2
            at = lane if h == 1 else lane - 64
            q = q_ref[s, h, pl.ds(here, T)].astype(F32)
            q = jnp.where(at == 8, -l1, jnp.where(at == 9, -l2, jnp.where(at == 10, -l3, q)))
            q_out[s, h, pl.ds(here, T)] = q.astype(BF)
        o_ref[i, :, pl.ds(pl.multiple_of(s * 128, 128), 128)] = jnp.where(lower, outs[0], outs[1]).astype(BF)

        @pl.when(s == 0)
        def _():
            o_ref[i, :, 256:384] = pltpu.roll(outs[2], 64, 1).astype(BF)

        @pl.when(s == 1)
        def _():
            o_ref[i, :, 256:384] = jnp.where(lower, o_ref[i, :, 256:384].astype(F32), outs[2]).astype(BF)

        return 0

    lax.fori_loop(0, 8, per_tile, 0)


def attn_bwd_kernel(pg, KC, s, lengths, idx, q_ref, k_ref, v_ref, o_ref, do_ref, *rest):
    *rest, dq_s, dk_s, dv_s, do_s, d_ref, gq_s = rest
    if s == 1:
        rest = (*rest, gq_s)
    if pg > 1:
        d_ref = rest[0]
    c, mine = idx[2], idx[5]
    T, L = o_ref.shape[1], k_ref.shape[2]
    bounds = limits(lengths, s, L)
    lane = lax.broadcasted_iota(jnp.int32, (T, 128), 1)
    lower = lane < 64
    zero = jnp.zeros((T, 128), F32)

    dk_s[...] = jnp.zeros_like(dk_s)
    dv_s[...] = jnp.zeros_like(dv_s)
    live = bounds[4]
    cols = slice(s * 128, (s + 1) * 128)

    def per_tile(i, _):
        here = pl.multiple_of(i * T, T)
        first = (mine * 4 + i) * T
        low, high = span(bounds, first, first + T - 1)
        high = jnp.minimum(high, live)
        pair = do_ref[i, :, cols].astype(F32)
        third = do_ref[i, :, 256:384].astype(F32)
        if s == 0:
            third = pltpu.roll(third, 64, 1)
        o_third = o_ref[i, :, 256:384].astype(F32)
        if s == 0:
            o_third = pltpu.roll(o_third, 64, 1)
        prod = pair * o_ref[i, :, cols].astype(F32)
        for h in range(3):
            data = lower if h == 0 else ~lower
            full = prod if h < 2 else third * o_third
            delta = jnp.sum(jnp.where(data, full, zero), axis=1, keepdims=True)
            d1 = delta.astype(BF).astype(F32)
            d2 = (delta - d1).astype(BF).astype(F32)
            d3 = delta - d1 - d2
            at = lane - 64 if h == 0 else lane
            aug = jnp.where(at == 8, -d1, jnp.where(at == 9, -d2, jnp.where(at == 10, -d3, zero)))
            do_s[h] = jnp.where(data, pair if h < 2 else third, aug).astype(BF)
            dq_s[h, pl.ds(here, T)] = zero

        def step(kt, _):
            at = pl.multiple_of(kt * KC, KC)
            for h in range(3):
                q = q_ref[0, h, pl.ds(here, T)]
                k = k_ref[0, h, pl.ds(at, KC)]
                d = do_s[h]
                pt = jnp.exp(mm_nt(k, q))
                ds = (pt * mm_nt(v_ref[0, h, pl.ds(at, KC)], d)).astype(BF)
                dv_s[h, pl.ds(at, KC)] += mm(pt.astype(BF), d)
                dk_s[h, pl.ds(at, KC)] += mm(ds, q)
                dq_s[h, pl.ds(here, T)] += mm_tn(ds, k)
            return 0

        lax.fori_loop(low // KC, (high + KC - 1) // KC, step, 0)
        return 0

    lax.fori_loop(0, 4, per_tile, 0)
    for g in range(pg):
        for n, off in enumerate(OFFS):
            at = pl.multiple_of((g * 4 + (c ^ off)) * T, T)
            own = pl.multiple_of((c ^ off) * T, T)
            keep = 0.125 if pg == 1 else jnp.where(mine == g, 0.125, 0.0)
            dq = [dq_s[h, pl.ds(own, T)] * keep for h in range(3)]
            dk = [dk_s[h, pl.ds(at, T)] for h in range(3)]
            dv = [dv_s[h, pl.ds(at, T)] for h in range(3)]
            d_ref[g, n, :, 0:128] = jnp.where(lower, dq[0], dq[1]).astype(BF)
            d_ref[g, n, :, 128:256] = jnp.where(lower, dk[0], dk[1]).astype(BF)
            d_ref[g, n, :, 256:384] = jnp.where(lower, dv[0], dv[1]).astype(BF)
            d_ref[g, n, :, 384:512] = jnp.where(lower, dq[2], dv[2]).astype(BF)
            d_ref[g, n, :, 512:576] = dk[2][:, 0:64].astype(BF)
    if pg == 1:
        products(s, idx, d_ref, *rest)


def products(s, idx, d, w, dfirst, t0, t1, t2, t3, *rest):
    if s == 0:
        gq, gi_own, gi_x, gi_b = rest
    else:
        prev, extra, gq_own, gq_other, gi_own, gi_x, gi_b, gq = rest
    zw, h, y = idx[1], idx[2], idx[3]
    D = w.shape[0]
    for n in range(2):
        gi_b[n] = mm_nt(d[0, n + 2], w[...]).astype(BF)
    gi_x[...] = mm_nt(d[0, 1], w[...])
    gi_own[...] = mm_nt(d[0, 0], w[...]) + dfirst[...]
    toks = (t0, t1, t2, t3)
    acc = sum(mm_tn(t[0], d[0, n]) for n, t in enumerate(toks))
    col = sum(fold8(d[0, n].astype(F32)) for n in range(4))
    if s == 0:
        gq[0:D, :] = acc
        gq[D : D + 8, :] = col
        return
    gq[0:D, :] = acc + prev[0:D, :]
    col = jnp.sum(col + prev[D : D + 8, :], axis=0, keepdims=True)
    top = lax.broadcasted_iota(jnp.int32, (8, 576), 0) == 0
    for k in range(4):
        z = zw ^ k
        tail = jnp.where(top & (h == z), col, extra[z]).astype(BF)
        for ref, yy in ((gq_own, y), (gq_other, 1 - y)):
            ref[k, 0:96, :] = gq[pl.ds(pl.multiple_of(z * 192 + yy * 96, 8), 96), :].astype(BF)
            ref[k, 96:104, :] = tail


def gelu_parts(u):
    t = 1.0 / (1.0 + (0.3275911 * 0.7071067811865476) * jnp.abs(u))
    e = jnp.exp(-0.5 * u * u)
    poly = t * (
        0.127414796
        + t * (-0.142248368 + t * (0.7107068705 + t * (-0.7265760135 + t * 0.5307027145)))
    )
    tail = poly * e
    cdf = jnp.where(u >= 0, 1.0 - tail, tail)
    return u * cdf, cdf + u * e * 0.3989422804014327


def gather_heads(tiles):
    (pair0, third0), (pair1, third1) = tiles
    lower = lax.broadcasted_iota(jnp.int32, pair0.shape, 1) < 64
    turned = pltpu.roll(pair1, 64, 1)
    return pair0, jnp.where(lower, third0, turned), jnp.where(lower, turned, pltpu.roll(third1, 64, 1))


def ffn_kernel(
    idx, lengths, attn, tok, cot, sm_own, w_in, w_at, w_out,
    s1a, r2a, c1a, c2a, s1b, r2b, c1b, c2b,
    out, dfirst, dattn, sent, kept, extra,
    w1, w2, wa, sm, b1, att, hlow, xhat, rstd, acc, act, gp, dlow, sums, sem, osem,
):
    c, z, h, y, x, mine = (idx[i] for i in range(6))
    R, D = tok.shape
    T = attn.shape[1]
    FB = w_in.shape[1] // 8
    TR = 128
    first_copies = [(w_at, wa.at[z]), (sm_own.at[240:256], sm.at[0])]
    first_copies += [(s1a.at[0, k, 240:256], sm.at[k + 1]) for k in range(3)]
    copies = [(w_in, w1.at[z]), (w_out, w2.at[z])]
    for n, (ra, rb) in enumerate(((s1a, s1b), (r2a, r2b), (c1a, c1b), (c2a, c2b))):
        for k in range(2):
            p = idx[6 + 2 * n + k]
            q, half = p // 2, p % 2
            for kz in range(3):
                zz = z ^ (kz + 1)
                at = pl.ds(pl.multiple_of(half * FB, 128), FB)
                first_copies.append((ra.at[k, kz, 192:240], wa.at[zz, pl.ds(pl.multiple_of(q * 48, 16), 48), at]))
                copies.append((ra.at[k, kz, 0:192], w1.at[zz, :, pl.ds(pl.multiple_of(p * FB, 128), FB)]))
                copies.append((rb.at[k, kz], w2.at[zz, pl.ds(pl.multiple_of(half * FB + q * 96, 16), 96)]))
    many = len(first_copies)
    first_copies = [pltpu.make_async_copy(a, b, sem.at[i]) for i, (a, b) in enumerate(first_copies)]
    copies = [pltpu.make_async_copy(a, b, sem.at[many + i]) for i, (a, b) in enumerate(copies)]
    for cp in first_copies + copies:
        cp.start()

    sums[...] = jnp.zeros_like(sums)
    extra[...] = jnp.zeros_like(extra)

    lower = lax.broadcasted_iota(jnp.int32, (T, 128), 1) < 64
    for s in range(2):
        for g in range(0, 4, 2):
            tiles = []
            for n in (g, g + 1):
                third = attn[n, :, 256:384].astype(F32)
                tiles.append((
                    attn[n, :, s * 128 : (s + 1) * 128].astype(F32),
                    third if s == 0 else pltpu.roll(third, 64, 1),
                ))
            for j, tile in enumerate(gather_heads(tiles)):
                at = g * 192 + j * 128
                att[s * T : (s + 1) * T, at : at + 128] = tile.astype(BF)

    for cp in first_copies:
        cp.wait()

    def whole(i):
        return jnp.concatenate([sm[k ^ z, i : i + 1, 0:192].astype(F32) for k in range(4)], axis=1)

    b_attn, g1v, s1v, b_out, g2v, s2v = (whole(i) for i in range(2, 8))
    for k in range(4):
        row = jnp.concatenate([sm[k ^ z, i : i + 1, 0:192].astype(F32) for i in range(8, 12)], axis=1)
        for half in range(2):
            b1[2 * k + half, 0:1, :] = row[:, half * FB : (half + 1) * FB]

    acc[...] = mm(att[...], wa[...].reshape(D, D))

    def first(r, _):
        rows = pl.ds(pl.multiple_of(r * TR, TR), TR)
        v = acc[rows, :] + tok[rows, :].astype(F32) + b_attn
        mean = jnp.mean(v, axis=-1, keepdims=True)
        v = v - mean
        rs = lax.rsqrt(jnp.mean(v * v, axis=-1, keepdims=True) + EPS)
        xh = v * rs
        xhat[rows, :] = xh
        rstd[rows, :] = jnp.broadcast_to(rs, (TR, 128))
        hid = xh * g1v + s1v
        hlow[rows, :] = hid.astype(BF)
        acc[rows, :] = hid + b_out
        return 0

    lax.fori_loop(0, R // TR, first, 0)
    for cp in copies:
        cp.wait()

    def keep(src, i, cc, at):
        to = pl.ds(pl.multiple_of(i * FB, 128), FB)

        @pl.when(c == cc)
        def _():
            pltpu.make_async_copy(src, kept.at[:, to], osem.at[at]).start()

        @pl.when(c != cc)
        def _():
            pltpu.make_async_copy(src, sent.at[:, to], osem.at[at]).start()

    def kept_all(first, count):
        for i in range(first, first + count):
            pltpu.make_async_copy(act.at[:, 0:FB], kept.at[:, 0:FB], osem.at[i]).wait()

    def forward(zz, _):
        cols = pl.ds(pl.multiple_of(zz * D, 128), D)
        u = mm(hlow[...], w1[:, :, cols].reshape(D, D)) + jnp.concatenate([b1[2 * zz, 0:1, :], b1[2 * zz + 1, 0:1, :]], axis=1)
        for r in range(R // TR):
            rows = slice(r * TR, (r + 1) * TR)
            a, d = gelu_parts(u[rows])
            act[rows, cols] = a.astype(BF)
            gp[rows, cols] = d.astype(BF)
        acc[...] += mm(act[:, cols], w2[zz])
        for half in range(2):
            src = act.at[:, pl.ds(pl.multiple_of(zz * D + half * FB, 128), FB)]
            keep(src, zz, half, 2 * zz + half)
        return 0

    lax.fori_loop(0, 4, forward, 0)

    def second(r, _):
        rows = pl.ds(pl.multiple_of(r * TR, TR), TR)
        s = r // (T // TR)
        v = acc[rows, :]
        mean = jnp.mean(v, axis=-1, keepdims=True)
        v = v - mean
        rs = lax.rsqrt(jnp.mean(v * v, axis=-1, keepdims=True) + EPS)
        xh = v * rs
        out[rows, :] = (xh * g2v + s2v).astype(BF)
        place = (mine * 4 + h) * T + r * TR - s * T
        pos = lax.broadcasted_iota(jnp.int32, (TR, D), 0) + place
        dy = jnp.where(pos < limits(lengths, s, 0)[4], cot[rows, :].astype(F32), 0.0)
        sums[4] += fold8(dy * xh)
        sums[5] += fold8(dy)
        dx = dy * g2v
        m1 = jnp.mean(dx, axis=-1, keepdims=True)
        m2 = jnp.mean(dx * xh, axis=-1, keepdims=True)
        ds = rs * (dx - m1 - xh * m2)
        low = ds.astype(BF)
        dlow[rows, :] = low
        sums[3] += fold8(low.astype(F32))
        acc[rows, :] = ds
        return 0

    lax.fori_loop(0, R // TR, second, 0)

    kept_all(0, 8)
    shared = [(att, 9), (hlow, 11), (dlow, 13)]
    shared = [pltpu.make_async_copy(v, sent.at[:, i * FB : (i + 2) * FB], osem.at[n + 16]) for n, (v, i) in enumerate(shared)]
    for cp in shared:
        cp.start()

    def backward(zz, _):
        cols = pl.ds(pl.multiple_of(zz * D, 128), D)
        da = mm_nt(dlow[...], w2[zz])
        gsum = jnp.zeros((8, D), F32)
        for r in range(R // TR):
            rows = slice(r * TR, (r + 1) * TR)
            di = (da[rows] * gp[rows, cols].astype(F32)).astype(BF)
            act[rows, cols] = di
            gsum = gsum + fold8(di.astype(F32))
        acc[...] += mm_nt(act[:, cols], w1[:, :, cols].reshape(D, D))
        for half in range(2):
            src = act.at[:, pl.ds(pl.multiple_of(zz * D + half * FB, 128), FB)]
            keep(src, 4 + zz, half, 8 + 2 * zz + half)
        gsum = jnp.sum(gsum, axis=0, keepdims=True)
        extra[zz, 3:4, :] = gsum[:, 0:576]
        extra[zz, 4:5, 0:192] = gsum[:, 576:768]
        return 0

    lax.fori_loop(0, 4, backward, 0)
    for cp in shared:
        cp.wait()

    def last(r, _):
        rows = pl.ds(pl.multiple_of(r * TR, TR), TR)
        dy = acc[rows, :]
        xh = xhat[rows, :]
        sums[1] += fold8(dy * xh)
        sums[2] += fold8(dy)
        dx = dy * g1v
        m1 = jnp.mean(dx, axis=-1, keepdims=True)
        m2 = jnp.mean(dx * xh, axis=-1, keepdims=True)
        df = rstd[rows, :1] * (dx - m1 - xh * m2)
        dfirst[rows, :] = df
        low = df.astype(BF)
        dlow[rows, :] = low
        sums[0] += fold8(low.astype(F32))
        return 0

    lax.fori_loop(0, R // TR, last, 0)
    acc[...] = mm_nt(dlow[...], wa[...].reshape(D, D))
    for g in range(0, 4, 2):
        thirds = []
        for s in range(2):
            t0, t1, t2 = (acc[s * T : (s + 1) * T, g * 192 + j * 128 : g * 192 + (j + 1) * 128] for j in range(3))
            t1r, t2r = pltpu.roll(t1, 64, 1), pltpu.roll(t2, 64, 1)
            dattn[g, :, s * 128 : (s + 1) * 128] = t0.astype(BF)
            dattn[g + 1, :, s * 128 : (s + 1) * 128] = jnp.where(lower, t1r, t2r).astype(BF)
            thirds.append((t1, t1r, t2, t2r))
        (a1, _, _, a2r), (_, b1r, b2, _) = thirds
        dattn[g, :, 256:384] = jnp.where(lower, a1, b1r).astype(BF)
        dattn[g + 1, :, 256:384] = jnp.where(lower, a2r, b2).astype(BF)
    for half in range(2):
        keep(dlow.at[:, half * FB : (half + 1) * FB], 8, half, 19 + half)
    for i in range(6):
        row = jnp.sum(sums[i], axis=0, keepdims=True)
        for k in range(4):
            at = (i % 3) * 192
            extra[k, 1 + i // 3 : 2 + i // 3, at : at + 192] = row[:, k * 192 : (k + 1) * 192]
    kept_all(8, 8)
    kept_all(19, 2)


def weight_kernel(idx, kept, mate, sent, plane, mine, *rest):
    outs, (units, shared, units2, shared2, sem) = rest[:6], rest[6:]
    z = idx[1]
    D = shared.shape[1] // 3
    FB = D // 2
    wide = 4 * FB
    copies = []
    for refs, us, sh in (((kept, sent), units, shared), ((mate, mate), units2, shared2)):
        for at, size in ((wide, wide), (0, wide), (2 * wide, FB)):
            copies.append((refs[0].at[:, at : at + size], us.at[:, at : at + size]))
        for at in (D, 2 * D, 0):
            copies.append((refs[1].at[:, 9 * FB + at : 9 * FB + at + D], sh.at[:, at : at + D]))
    order = (0, 3, 6, 9, 1, 4, 7, 10, 2, 5, 8, 11)
    copies = [pltpu.make_async_copy(*copies[n], sem.at[n]) for n in order]
    for cp in copies:
        cp.start()
    for cp in copies[:4]:
        cp.wait()
    for n in range(2):
        cols = slice(wide + n * D, wide + (n + 1) * D)
        v = mm_tn(shared[:, D : 2 * D], units[:, cols]) + mm_tn(shared2[:, D : 2 * D], units2[:, cols])
        v = v.astype(BF)
        for i in range(2):
            for zz in range(4):
                plane[2 * n + i, zz, 0:192, :] = v[zz * 192 : (zz + 1) * 192, i * FB : (i + 1) * FB]
    for cp in copies[4:8]:
        cp.wait()
    for k in range(4):
        cols = pl.ds(pl.multiple_of((z ^ k) * FB, 128), FB)
        v = mm_tn(units[:, cols], shared[:, 2 * D : 3 * D]) + mm_tn(units2[:, cols], shared2[:, 2 * D : 3 * D])
        for q in range(4):
            if k == 0:
                mine[q] = v[q * 96 : (q + 1) * 96]
            else:
                outs[(q // 2) * 3 + k - 1][q % 2] = v[q * 96 : (q + 1) * 96].astype(BF)
    for cp in copies[8:]:
        cp.wait()
    v = mm_tn(shared[:, 0:D], units[:, 2 * wide : 2 * wide + FB]) + mm_tn(shared2[:, 0:D], units2[:, 2 * wide : 2 * wide + FB])
    v = v.astype(BF)
    for zz in range(4):
        for q in range(4):
            plane[q, zz, 192:240, :] = v[zz * 192 + q * 48 : zz * 192 + (q + 1) * 48]


def products_kernel(s, idx, *refs):
    products(s, idx, *(refs if s == 1 else refs[:-1]))


def chunkq_kernel(own, got, *outs):
    for k, ref in enumerate(outs):
        ref[...] = (own[k].astype(F32) + got[k].astype(F32)).astype(ref.dtype)


def chunk_kernel(idx, terms, *outs):
    z = idx[1]
    for k, ref in enumerate(outs):
        ref[...] = sum(terms[q, z ^ k].astype(F32) for q in range(4)).astype(ref.dtype)


def sum2_kernel(mine, *refs):
    parts, out = refs[:-1], refs[-1]
    for q in range(4):
        v = mine[q]
        for k in range(3):
            v = v + parts[(q // 2) * 3 + k][q % 2].astype(F32)
        out[q] = v.astype(out.dtype)


def sum_kernel(a0, a1, a2, a3, b, q0, q1, q2, q3, out):
    A, B = a0.shape
    C, E = b.shape[1], q0.shape[0]
    out[0:A, :] = (a0[...] + sum(a[...].astype(F32) for a in (a1, a2, a3))).astype(BF)
    v = sum(b[k].astype(F32) for k in range(4)).astype(BF)
    out[A : A + C, :] = v[:, :B]
    out[A + C : A + 2 * C, :] = v[:, B:]
    v = (q0[...] + sum(q[...].astype(F32) for q in (q1, q2, q3))).astype(BF)
    at = A + 2 * C
    out[at : at + E, :] = v[:, :B]
    out[at + E : at + 2 * E, :] = jnp.zeros((E, B), BF)
    out[at + E : at + 2 * E, 0 : 576 - B] = v[:, B:]


def out_kernel(idx, s1, r2, c1, c2, g_wq, g_wk, g_wv, g_wi, g_wa, g_wo, g_bq, g_bv, g_bi, *six):
    FB = s1.shape[2]
    c, z = idx[0], idx[1]
    refs = (s1, r2, c1, c2)
    for n, ref in enumerate(refs):
        for k in range(2):
            p = idx[6 + 2 * n + k]
            g_wi[:, pl.ds(pl.multiple_of(p * FB, 128), FB)] = ref[k, 0:192, :].astype(F32)
            rows = pl.ds(pl.multiple_of((p // 2) * 48, 16), 48)
            g_wa[rows, pl.ds(pl.multiple_of((p % 2) * FB, 128), FB)] = ref[k, 192:240, :].astype(F32)
            rows = pl.ds(pl.multiple_of((p % 2) * FB + (p // 2) * 96, 16), 96)
            g_wo[rows, 0:FB] = ref[k, 240:336, :].astype(F32)
            g_wo[rows, FB : 2 * FB] = ref[k, 336:432, :].astype(F32)
    lower = lax.broadcasted_iota(jnp.int32, (96, 128), 1) < 64
    left, right = jnp.zeros((8, FB), F32), jnp.zeros((8, FB), F32)
    top = lax.broadcasted_iota(jnp.int32, (8, FB), 0) == 0
    for (n, k), (m, j) in (((0, 0), (2, 0)), ((0, 1), (3, 0)), ((1, 0), (2, 1)), ((1, 1), (3, 1))):
        p = idx[6 + 2 * n + k]
        yy, xx = p // 4, (p // 2) % 2
        own, other = refs[n].at[k], refs[m].at[j]

        def tile(i, swap):
            at = slice(432, 528) if i < 3 else slice(536, 632)
            cols = slice((i % 3) * 128, (i % 3 + 1) * 128)
            u, v = own[at, cols].astype(F32), other[at, cols].astype(F32)
            return jnp.where((c == 0) != swap, u, v)

        rows = pl.ds(pl.multiple_of(yy * 96, 8), 96)
        for ref, i, third, low in ((g_wq, 0, 3, True), (g_wk, 1, 4, True), (g_wv, 2, 3, False)):
            ta, tb = tile(third, False), tile(third, True)
            turned = pltpu.roll(tile(i, True), 64, 1)
            if not low:
                ta = pltpu.roll(ta, 64, 1)
            else:
                tb = pltpu.roll(tb, 64, 1)
            base = xx * 384
            ref[rows, pl.ds(pl.multiple_of(base, 128), 128)] = tile(i, False)
            ref[rows, pl.ds(pl.multiple_of(base + 128, 128), 128)] = jnp.where(lower, ta, turned)
            ref[rows, pl.ds(pl.multiple_of(base + 256, 128), 128)] = jnp.where(lower, turned, tb)
        for ref, cc in ((own, c), (other, 1 - c)):
            here = (yy == 0) & (~top | (xx * 2 + cc == z))
            left = left + jnp.where(here, ref[528:536, :].astype(F32), 0.0)
            right = right + jnp.where(here, ref[632:640, :].astype(F32), 0.0)
    g_bq[...] = jnp.concatenate([left[0:1, 0:128], right[0:1, 0:64]], axis=1).reshape(192)
    g_bv[...] = jnp.concatenate([left[0:1, 256:384], right[0:1, 64:128]], axis=1).reshape(192)
    for i, ref in enumerate(six):
        row = 1 + i // 3
        ref[...] = (left[row : row + 1, 0:192], left[row : row + 1, 192:384], right[row : row + 1, 0:192])[i % 3].reshape(192)
    g_bi[...] = jnp.concatenate([left[3:4, :], right[3:4, 0:192], left[4:5, 0:192]], axis=1).reshape(768)


def tie(*values):
    return lax.optimization_barrier(values)


def block(shape, *at):
    return pl.BlockSpec(shape, lambda i: at)


def call(kernel, outs, in_specs, out_specs, scratch=(), name=None, grid=()):
    return pl.pallas_call(
        kernel,
        out_shape=outs,
        grid=grid,
        in_specs=in_specs,
        out_specs=out_specs,
        scratch_shapes=list(scratch),
        compiler_params=pltpu.CompilerParams(vmem_limit_bytes=VMEM_LIMIT),
        cost_estimate=pl.CostEstimate(flops=1, bytes_accessed=1, transcendentals=0),
        name=name,
    )


def make_body(sizes):
    pg = sizes["pg"]
    order = [sizes[a] for a in AX]

    def send(fn, a):
        pairs = []
        for flat in range(math.prod(order)):
            at, rest = [], flat
            for n in reversed(order):
                at.append(rest % n)
                rest //= n
            dest = 0
            for n, v in zip(order, fn(*reversed(at))):
                dest = dest * n + v
            pairs.append((flat, dest))
        return lax.ppermute(a, AX, pairs)

    to_x = functools.partial(send, lambda s, g, x, c, z: (s, g, 1 - x, c, z))
    to_y = functools.partial(send, lambda s, g, x, c, z: (1 - s, g, x, c, z))
    to_core = functools.partial(send, lambda s, g, x, c, z: (s, g, x, 1 - c, z))
    to_z = [functools.partial(send, lambda s, g, x, c, z, k=k: (s, g, x, c, z ^ k)) for k in (1, 2, 3)]
    mix_a = functools.partial(send, lambda s, g, x, c, z: (s, g, 1 - x, c, z) if c == 0 else (1 - s, g, x, c, z))
    mix_b = functools.partial(send, lambda s, g, x, c, z: (1 - s, g, x, c, z) if c == 0 else (s, g, 1 - x, c, z))

    to_d = functools.partial(send, lambda s, g, x, c, z: (1 - s, g, 1 - x, c, z))

    def over_plane(sent):
        return [f(v) for f, v in zip((to_x, to_y, to_d), sent)]

    def over_z(sent):
        return [f(v) for f, v in zip(to_z, sent if isinstance(sent, list) else [sent] * 3)]

    def body(
        tokens, cotangent, segment_ids, lengths, w_query, b_query, w_key, w_value, b_value, w_attn, b_attn,
        ln1_gain, ln1_shift, w_inner, b_inner, w_outer, b_outer, ln2_gain, ln2_shift,
    ):
        S, T, D = tokens.shape
        R = S * T
        y, x, c = (lax.axis_index(a) for a in ("seq", "x", "core"))
        mine, z = lax.axis_index("pg"), lax.axis_index("wt")
        h = x * 2 + c
        p = y * 4 + h
        L = 4 * pg * T
        FB = w_inner.shape[1] // 8

        a_of = jnp.where(c == 0, 2, 4)
        other = p ^ 1
        mates = [p, p ^ a_of, p ^ (6 - a_of), p ^ 6, other, other ^ (6 - a_of), other ^ a_of, other ^ 6]
        idx = jnp.stack([c, z, h, y, x, mine] + mates).astype(jnp.int32)

        vecs = (b_query, b_value, b_attn, ln1_gain, ln1_shift, b_outer, ln2_gain, ln2_shift, b_inner)
        w_own, pack, piece1, piece2 = call(
            prep_kernel,
            (
                jax.ShapeDtypeStruct((200, 576), BF), jax.ShapeDtypeStruct((104, 576), BF),
                jax.ShapeDtypeStruct((256, FB), BF), jax.ShapeDtypeStruct((96, D), BF),
            ),
            [SM] + [VM] * 15, (VM,) * 4, name="prep",
        )(idx, w_query, w_key, w_value, w_attn, w_inner, w_outer, *vecs)
        w_z = over_z(pack)
        tok_x, tok_c = to_x(tokens), to_core(tokens)
        w_z, tok_x, tok_c, piece1 = tie(w_z, tok_x, tok_c, piece1)
        w_y, tok_xc = to_y(jnp.stack(w_z)), to_core(tok_x)
        z1 = over_z(piece1)
        w_y, tok_xc, z1, piece2 = tie(w_y, tok_xc, z1, piece2)
        z2 = over_z(piece2)
        one = jnp.stack(z1)
        tok_xc, one = tie(tok_xc, one)
        one_a = mix_a(one)

        toks = [t[None] for t in (tokens, tok_x, tok_c, tok_xc)]
        if pg > 1:
            toks = [lax.all_gather(t, "pg", axis=0, tiled=True) for t in toks]
        head = jax.ShapeDtypeStruct((S, 3, L, 128), BF)
        own_head = jax.ShapeDtypeStruct((S, 3, 4 * T, 128), BF)
        q_aug, k_aug, v_aug, w_qkv = call(
            functools.partial(qkv_kernel, pg),
            (own_head, head, head, jax.ShapeDtypeStruct((4, 192, 576), BF)),
            [SM, SM] + [VM] * 4 + [ANY] * 5,
            (VM,) * 4,
            [pltpu.VMEM((4, 8, 576), BF), pltpu.SemaphoreType.DMA((11,))],
            name="qkv",
        )(lengths, idx, *toks, w_own, *w_z, w_y)
        w_qkv = w_qkv.reshape(D, 576)
        q_aug, one_a, z2 = tie(q_aug, one_a, z2)
        one, two = jnp.stack([one, one_a]), jnp.stack(z2)
        q_aug, one, two = tie(q_aug, one, two)
        one_b, two_a = mix_b(one), mix_a(two)
        o, q_aug = call(
            functools.partial(attn_fwd_kernel, 1024),
            (jax.ShapeDtypeStruct((4, T, 384), BF), own_head),
            [SM, SM] + [VM] * 3,
            (VM,) * 2,
            [pltpu.VMEM((3, T, 128), F32), pltpu.VMEM((3, T, 128), F32)],
            name="attn_fwd",
        )(lengths, idx, q_aug, k_aug, v_aug)
        o, one_b, two_a = tie(o, one_b, two_a)
        attn = lax.all_to_all(o, ("x", "core"), 0, 0, tiled=True)
        two = jnp.stack([two, two_a])
        two_b = mix_b(two)
        one = (one, one_b, to_core(one), to_core(one_b))
        attn, two_b = tie(attn, two_b)
        two = (two, two_b, to_core(two), to_core(two_b))

        layer_out, d_first, d_attn, sent, kept, extra = call(
            ffn_kernel,
            (
                jax.ShapeDtypeStruct((R, D), BF), jax.ShapeDtypeStruct((R, D), F32), jax.ShapeDtypeStruct((4, T, 384), BF),
                jax.ShapeDtypeStruct((R, 15 * FB), BF), jax.ShapeDtypeStruct((R, 9 * FB), BF), jax.ShapeDtypeStruct((4, 8, 576), F32),
            ),
            [SM, SM] + [VM] * 3 + [ANY] * 12,
            (VM, VM, VM, ANY, ANY, VM),
            [
                pltpu.VMEM((4, 192, 8 * FB), BF),
                pltpu.VMEM((4, 2 * FB, D), BF),
                pltpu.VMEM((4, 192, D), BF),
                pltpu.VMEM((4, 16, FB), BF),
                pltpu.VMEM((8, 8, FB), F32),
                pltpu.VMEM((R, D), BF),
                pltpu.VMEM((R, D), BF),
                pltpu.VMEM((R, D), F32),
                pltpu.VMEM((R, 128), F32),
                pltpu.VMEM((R, D), F32),
                pltpu.VMEM((R, 8 * FB), BF),
                pltpu.VMEM((R, 8 * FB), BF),
                pltpu.VMEM((R, D), BF),
                pltpu.VMEM((8, 8, D), F32),
                pltpu.SemaphoreType.DMA((79,)),
                pltpu.SemaphoreType.DMA((21,)),
            ],
            name="ffn",
        )(
            idx, lengths, attn, tokens.reshape(R, D), cotangent.reshape(R, D), piece1, w_inner, w_attn, w_outer, *one, *two
        )

        d_o = lax.all_to_all(d_attn, ("x", "core"), 0, 0, tiled=True)

        def add(*parts):
            return sum(v.astype(F32) for v in parts)

        def shares(n, m):
            return jax.ShapeDtypeStruct((*n, m), F32), *(jax.ShapeDtypeStruct((*n, m), BF),) * 3

        mat = jax.ShapeDtypeStruct((T, D), F32)
        toks = (tokens, tok_x, tok_c, tok_xc)

        def products_specs(s):
            first = (jax.ShapeDtypeStruct((D + 8, 576), F32),) if s == 0 else (jax.ShapeDtypeStruct((4, 104, 576), BF),) * 2
            return (
                (*first, mat, mat, jax.ShapeDtypeStruct((2, T, D), BF)),
                [VM, block((T, D), s, 0)] + [block((1, T, D), s, 0, 0)] * 4 + [VM] * (2 * s),
                (VM,) * (4 + s),
            )

        def attn_bwd(s, d_o, prev):
            args = (lengths, idx, q_aug, k_aug, v_aug, o, d_o)
            outs, ins, out_specs = products_specs(s)
            d_shape = jax.ShapeDtypeStruct((pg, 4, T, 576), BF)
            more = (w_qkv, d_first, *toks, *prev)
            if pg > 1:
                outs, ins, out_specs, more = d_shape, [], VM, ()
            res = call(
                functools.partial(attn_bwd_kernel, pg, 512, s), outs,
                [SM, SM, block((1, 3, 4 * T, 128), s, 0, 0, 0)] + [block((1, 3, L, 128), s, 0, 0, 0)] * 2 + [VM] * 2 + ins,
                out_specs,
                [
                    pltpu.VMEM((3, 4 * T, 128), F32), pltpu.VMEM((3, L, 128), F32), pltpu.VMEM((3, L, 128), F32),
                    pltpu.VMEM((3, T, 128), BF), pltpu.VMEM((1, 4, T, 576), BF), pltpu.VMEM((D + 8, 576), F32),
                ],
                name="attn_bwd", grid=(1,),
            )(*args, *more)
            if pg > 1:
                d = lax.psum_scatter(res, "pg", scatter_dimension=0, tiled=True)
                outs, ins, out_specs = products_specs(s)
                res = call(
                    functools.partial(products_kernel, s), outs, [SM, VM] + ins, out_specs, [pltpu.VMEM((D + 8, 576), F32)],
                    name="products", grid=(1,),
                )(idx, d, w_qkv, d_first, *toks, *prev)
            return res

        half = jax.ShapeDtypeStruct((2, 96, D), BF)
        q1, c2, *sent2 = call(
            weight_kernel,
            (jax.ShapeDtypeStruct((4, 4, 240, FB), BF), jax.ShapeDtypeStruct((4, 96, D), F32)) + (half,) * 6,
            [SM] + [ANY] * 3, (VM,) * 8,
            [
                pltpu.VMEM((R, 9 * FB), BF), pltpu.VMEM((R, 3 * D), BF), pltpu.VMEM((R, 9 * FB), BF), pltpu.VMEM((R, 3 * D), BF),
                pltpu.SemaphoreType.DMA((12,)),
            ],
            name="weights",
        )(idx, kept, to_core(sent), sent)
        n, m = q1.shape[2:]
        d_o, sent2, q1 = tie(d_o, sent2, q1)
        got_a, q1 = over_z(sent2[:3]), lax.all_to_all(q1, ("seq", "x"), 0, 0, tiled=True)
        gq, own0, x0, core0 = attn_bwd(0, d_o, ())
        gq, d_o, core0, got_a, sent2 = tie(gq, d_o, core0, got_a, sent2[3:])
        got_b, core0 = over_z(sent2), to_core(core0)
        gq_own, gq_other, own1, x1, core1 = attn_bwd(1, d_o, (gq, extra))
        gq_own, core0, core1, got_b = tie(gq_own, core0, core1, got_b)
        gq_y, core1 = to_y(gq_other), to_core(core1)
        x0 = add(x0, core0[1]).astype(BF)
        c1, *sent1 = call(chunk_kernel, shares((n,), m), [SM, VM], (VM,) * 4, name="chunks1")(idx, q1)
        sent1, x0 = tie(sent1, x0)
        got_z1 = over_z(sent1)
        q2 = call(sum2_kernel, jax.ShapeDtypeStruct((4, 96, D), BF), [VM] * 7, VM, name="sums2")(c2, *got_a, *got_b)
        q2 = lax.all_to_all(q2, ("seq", "x"), 0, 0, tiled=True)
        x0 = to_x(x0)
        cq, *sentq = call(chunkq_kernel, shares((104,), 576), [VM] * 2, (VM,) * 4, name="chunksq")(gq_own, gq_y)
        x1 = add(x1, core1[1]).astype(BF)
        sentq, got_z1, x0, x1 = tie(sentq, got_z1, x0, x1)
        got_zq, x1 = over_z(sentq), to_x(x1)
        q2, got_z1, got_zq, x1 = tie(q2, got_z1, got_zq, x1)
        total = call(sum_kernel, jax.ShapeDtypeStruct((640, FB), BF), [VM] * 9, VM, name="sums")(
            c1, *got_z1, q2, cq, *got_zq
        )
        if pg > 1:
            total = lax.psum(total.astype(F32), "pg").astype(BF)
        s1 = mix_a(total)
        total, s1, x0, x1 = tie(total, s1, x0, x1)
        s1 = jnp.stack([total, s1])
        r2, s1_core = mix_b(s1), to_core(s1)
        grad_input = jnp.stack([add(own0, core0[0], x0), add(own1, core1[0], x1)]).astype(BF)
        r2, s1_core, grad_input = tie(r2, s1_core, grad_input)
        mat, wide = jax.ShapeDtypeStruct((192, D), F32), jax.ShapeDtypeStruct((192, 8 * FB), F32)
        vec, long_vec = jax.ShapeDtypeStruct((192,), F32), jax.ShapeDtypeStruct((2 * FB,), F32)
        g_wq, g_wk, g_wv, g_wi, g_wa, g_wo, g_bq, g_bv, g_bi, *six = call(
            out_kernel, (mat, mat, mat, wide, mat, jax.ShapeDtypeStruct((D, D), F32), vec, vec, long_vec) + (vec,) * 6,
            [SM] + [VM] * 4, (VM,) * 15, name="outputs",
        )(idx, s1, r2, s1_core, to_core(r2))
        return (
            layer_out.reshape(tokens.shape), grad_input,
            g_wq, g_bq, g_wk, g_wv, g_bv, g_wa, six[0], six[1], six[2], g_wi, g_bi, g_wo, six[3], six[4], six[5],
        )

    return body


def solution(mesh):
    sizes = dict(mesh.shape)
    pg = sizes["ctx"] // 4
    fine = dict(zip(AX, (sizes["seq"], pg, 2, 2, sizes["wt"])))
    split = Mesh(mesh.devices.reshape(tuple(fine.values())), AX)
    rows = P(("seq", "wt"), ("pg", "x", "core"), None)
    mat, vec = P("wt", None), P("wt")
    in_specs = (
        rows, rows, P(("seq", "wt"), ("pg", "x", "core")), P(("seq", "wt"), None),
        mat, vec, mat, mat, vec, mat, vec, vec, vec, mat, vec, mat, vec, vec, vec,
    )
    out_specs = (rows, rows, mat, vec, mat, mat, vec, mat, vec, vec, vec, mat, vec, mat, vec, vec, vec)
    return jax.shard_map(make_body(fine), mesh=split, in_specs=in_specs, out_specs=out_specs, check_vma=False)
```

time: 349 us -> 311 us (0.89)
  local copies, waits for them, and re-layouts: 36.1 us -> 7.36 us
  other arithmetic: 27 us -> 8.51 us
  starting transfers between devices: 62.5 us -> 74.8 us
  waiting for transfers between devices: 107 us -> 96.7 us
  Pallas kernels: 112 us -> 122 us
    pallas_call x6 -> x11, Pallas kernels: 70.8 us -> 92.8 us  [the longest x2 35.3 us: attn_bwd(): call(functools.partial(attn_bwd_kernel, pg, 512, s), outs, [SM, SM, block...]
    convert_element_type x11 -> x2, other arithmetic: 21.7 us -> 3.11 us  [the longest x1 2.05 us: body(): x0 = add(x0, core0[1]).astype(BF)]
    slice x22 -> x0, local copies, waits for them, and re-layouts: 14.6 us -> none  [the longest x2 3.11 us: chunk(): got[0, 0]]
    ppermute x43, starting transfers between devices: 47.6 us -> 59.9 us  [send(): return lax.ppermute(a, AX, pairs)]
    pallas_call x1, Pallas kernels: 41 us -> 29.1 us  [body(): call(ffn_kernel, (jax.ShapeDtypeStruct((R, D), BF), jax.ShapeDtypeStruct(...]
    all_to_all x1, waiting for transfers between devices: 10.5 us -> 0.01 us  [body(): d_o = lax.all_to_all(d_attn, ('x', 'core'), 0, 0, tiled=True)]
    concatenate x6 -> x0, local copies, waits for them, and re-layouts: 8.15 us -> none  [the longest x1 6.12 us: body(): jnp.concatenate([b_query[:128], none, b_value[:128], b_query[128:], b_val...]
  transfers between devices with their start and end apart: 47 -> 47, of which waited for: 16 -> 17; matrix products, arithmetic and copies ran while one was open for 16% -> 2% of each run, Pallas kernels for 19% -> 27%
where the time goes in v3:
time: 311 us
  Pallas kernels  122 us (39%)
  waiting for transfers between devices  96.7 us (31%)
  starting transfers between devices  74.8 us (24%)
  other arithmetic  8.51 us (3%)
  local copies, waits for them, and re-layouts  7.36 us (2%)
    ppermute x43, waiting for transfers between devices, send(): return lax.ppermute(a, AX, pairs)  84.4 us
    ppermute x43, starting transfers between devices, send(): return lax.ppermute(a, AX, pairs)  59.9 us
    pallas_call x2, Pallas kernels, attn_bwd(): call(functools.partial(attn_bwd_kernel, pg, 512, s), outs, [SM, SM, block...  35.3 us
    pallas_call x1, Pallas kernels, body(): call(ffn_kernel, (jax.ShapeDtypeStruct((R, D), BF), jax.ShapeDtypeStruct(...  29.1 us
    pallas_call x1, Pallas kernels, body(): call(functools.partial(attn_fwd_kernel, 1024), (jax.ShapeDtypeStruct((4,...  19.1 us
    all_to_all x1, waiting for transfers between devices, body(): attn = lax.all_to_all(o, ('x', 'core'), 0, 0, tiled=True)  12.3 us
    pallas_call x1, Pallas kernels, body(): call(weight_kernel, (jax.ShapeDtypeStruct((4, 4, 240, FB), BF), jax.Shape...  11 us
    pallas_call x1, Pallas kernels, body(): call(functools.partial(qkv_kernel, pg), (own_head, head, head, jax.ShapeD...  8.4 us
  transfers between devices with their start and end apart: 47, of which 17 were waited for; matrix products, arithmetic and copies ran while one was open for 2% of the time, Pallas kernels for 27%

profile of v3, /device:TPU:0, one launch (start us, length us, event | category | flops | bytes accessed | tf_op | source)
XLA Modules:
  0.0 310.5 jit_solution(5099628869229524083)
XLA Ops:
  1.2 2.6 collective-permute-start.3
  4.4 3.0 prep.1
  7.5 3.6 %collective-permute-start.2 = (bf16[104,576]{1,0:T(8,128)(2,1)}, bf16[104,576]{1,0:T(8,128)(2,1)S(1)}, u32[]{:S(2)}, u32[]{:S(2)}) collective-permute-start(bf16[104,576]{1,0:T(8,128)(2,1)} %get-tuple-element.150), channel_id=1, source_target_pairs={{0,3},{1,2},{2,1},{3,0},{4,7},{5,6},{6,5},{7,4},{8,11},{9,10},{10,... | collective-permute-start | bytes 359432 | tf_op jit(solution)/shard_map/ppermute | solution.py:701
  11.9 4.1 %collective-permute-done.2.refs_7_ = bf16[104,576]{1,0:T(8,128)(2,1)S(1)} collective-permute-done((bf16[104,576]{1,0:T(8,128)(2,1)}, bf16[104,576]{1,0:T(8,128)(2,1)S(1)}, u32[]{:S(2)}, u32[]{:S(2)}) %collective-permute-start.2) | collective-permute-done | bytes 119840 | tf_op jit(solution)/shard_map/ppermute | solution.py:701
  15.9 7.0 %collective-permute-done.1.refs_6_ = bf16[104,576]{1,0:T(8,128)(2,1)S(1)} collective-permute-done((bf16[104,576]{1,0:T(8,128)(2,1)}, bf16[104,576]{1,0:T(8,128)(2,1)S(1)}, u32[]{:S(2)}, u32[]{:S(2)}) %collective-permute-start.1) | collective-permute-done | bytes 119840 | tf_op jit(solution)/shard_map/ppermute | solution.py:701
  23.2 1.6 collective-permute-start.5
  24.7 2.9 collective-permute-start.9
  27.6 1.5 collective-permute-start.7
  29.1 5.5 %collective-permute-done.9 = bf16[256,384]{1,0:T(8,128)(2,1)S(1)} collective-permute-done((bf16[256,384]{1,0:T(8,128)(2,1)}, bf16[256,384]{1,0:T(8,128)(2,1)S(1)}, u32[]{:S(2)}, u32[]{:S(2)}) %collective-permute-start.9) | collective-permute-done | bytes 196640 | tf_op jit(solution)/shard_map/ppermute | solution.py:701
  34.6 10.3 %collective-permute-done.8 = bf16[256,384]{1,0:T(8,128)(2,1)S(1)} collective-permute-done((bf16[256,384]{1,0:T(8,128)(2,1)}, bf16[256,384]{1,0:T(8,128)(2,1)S(1)}, u32[]{:S(2)}, u32[]{:S(2)}) %collective-permute-start.8) | collective-permute-done | bytes 196640 | tf_op jit(solution)/shard_map/ppermute | solution.py:701
  45.7 1.6 collective-permute-start.10
  47.3 2.5 collective-permute-start.13
  49.8 1.9 collective-permute-start.11
  51.7 8.4 %qkv.1 = (bf16[2,3,1024,128]{3,2,1,0:T(8,128)(2,1)}, bf16[2,3,1024,128]{3,2,1,0:T(8,128)(2,1)}, bf16[2,3,1024,128]{3,2,1,0:T(8,128)(2,1)}, bf16[4,192,576]{2,1,0:T(8,128)(2,1)}) custom-call(s32[2,4]{1,0:T(2,128)} %lengths.9, s32[14]{0:T(128)} %stack.131.idx, bf16[1,2,256,768]{3,2,1,0:T(8,128)(2,1)} %bitcast.56, bf16[1,2,256,768]{3,2,1,0:T(8,128)(2,1)} %bitcast.59, ...), custom_call_target="tpu_custom_call" | custom-call | flops 1 | bytes 1 | tf_op jit(solution)/shard_map/qkv/pallas_call | solution.py:761
  60.2 1.1 collective-permute-done.12
  61.4 1.5 pad_maximum_fusion.5
  63.7 1.3 collective-permute-start.15
  65.0 19.1 %attn_fwd.1 = (bf16[4,256,384]{2,1,0:T(8,128)(2,1)}, bf16[2,3,1024,128]{3,2,1,0:T(8,128)(2,1)}) custom-call(s32[2,4]{1,0:T(2,128)} %lengths.9, s32[14]{0:T(128)} %stack.131.idx, bf16[2,3,1024,128]{3,2,1,0:T(8,128)(2,1)} %get-tuple-element.174.q_ref, bf16[2,3,1024,128]{3,2,1,0:T(8,128)(2,1)} %get-tuple-element.175.k_ref, ...), custom_call_target="tpu_custom_call" | custom-call | flops 1 | bytes 1 | tf_op jit(solution)/shard_map/attn_fwd/pallas_call | solution.py:774
  84.1 1.0 copy-done.10
  86.1 3.7 %all-to-all-start = ((bf16[4,256,384]{2,1,0:T(8,128)(2,1)}), bf16[4,256,384]{2,1,0:T(8,128)(2,1)S(1)}, u32[]{:S(2)}, u32[]{:S(2)}) async-start(bf16[4,256,384]{2,1,0:T(8,128)(2,1)} %get-tuple-element.180.o_ref), calls=%async_computation | async-start | bytes 1572864 | tf_op jit(solution)/shard_map/all_to_all | solution.py:783
  90.6 12.3 %all-to-all-done.attn = bf16[4,256,384]{2,1,0:T(8,128)(2,1)S(1)} async-done(((bf16[4,256,384]{2,1,0:T(8,128)(2,1)}), bf16[4,256,384]{2,1,0:T(8,128)(2,1)S(1)}, u32[]{:S(2)}, u32[]{:S(2)}) %all-to-all-start) | async-done | bytes 786464 | tf_op jit(solution)/shard_map/all_to_all | solution.py:783
  102.8 1.9 collective-permute-start.20
  104.8 2.4 collective-permute-done.20.c2b
  107.2 29.1 %ffn.1 = (bf16[512,768]{1,0:T(8,128)(2,1)}, f32[512,768]{1,0:T(8,128)}, bf16[4,256,384]{2,1,0:T(8,128)(2,1)}, bf16[512,5760]{1,0:T(8,128)(2,1)}, bf16[512,3456]{1,0:T(8,128)(2,1)}, /*index=5*/f32[4,8,576]{2,1,0:T(8,128)}) custom-call(s32[14]{0:T(128)} %stack.131.idx, s32[2,4]{1,0:T(2,128)} %lengths.9, bf16[4,256,384]{2,1,0:T(8,128)(2,1)} %copy-done.8, ...), custom_call_target="tpu_custom_call" | custom-call | flops 1 | bytes 1 | tf_op jit(solution)/shard_map/ffn/pallas_call | solution.py:790
  136.7 3.5 %all-to-all-start.1 = ((bf16[4,256,384]{2,1,0:T(8,128)(2,1)}), bf16[4,256,384]{2,1,0:T(8,128)(2,1)S(1)}, u32[]{:S(2)}, u32[]{:S(2)}) async-start(bf16[4,256,384]{2,1,0:T(8,128)(2,1)} %get-tuple-element.186), calls=%async_computation.1 | async-start | bytes 1572864 | tf_op jit(solution)/shard_map/all_to_all | solution.py:821
  140.2 6.1 %collective-permute-done.21.mate = bf16[512,5760]{1,0:T(8,128)(2,1)} collective-permute-done((bf16[512,5760]{1,0:T(8,128)(2,1)}, bf16[512,5760]{1,0:T(8,128)(2,1)}, u32[]{:S(2)}, u32[]{:S(2)}) %collective-permute-start.21) | collective-permute-done | bytes 5898272 | tf_op jit(solution)/shard_map/ppermute | solution.py:701
  146.3 11.0 %weights.1 = (bf16[4,4,240,384]{3,2,1,0:T(8,128)(2,1)}, f32[4,96,768]{2,1,0:T(8,128)}, bf16[2,96,768]{2,1,0:T(8,128)(2,1)}, bf16[2,96,768]{2,1,0:T(8,128)(2,1)},...) custom-call(s32[14]{0:T(128)} %stack.131.idx, ...), custom_call_target="tpu_custom_call" | custom-call | flops 1 | bytes 1 | tf_op jit(solution)/shard_map/weights/pallas_call | solution.py:867
  158.2 3.9 %all-to-all-start.2 = ((bf16[4,4,240,384]{3,2,1,0:T(8,128)(2,1)}), bf16[4,4,240,384]{3,2,1,0:T(8,128)(2,1)S(1)}, u32[]{:S(2)}, u32[]{:S(2)}) async-start(bf16[4,4,240,384]{3,2,1,0:T(8,128)(2,1)} %get-tuple-element.196), calls=%async_computation.2 | async-start | bytes 5898240 | tf_op jit(solution)/shard_map/all_to_all | solution.py:879
  162.2 2.8 collective-permute-start.23
  165.0 1.6 collective-permute-start.24
  166.6 18.6 %attn_bwd.2 = (f32[776,576]{1,0:T(8,128)}, f32[256,768]{1,0:T(8,128)}, f32[256,768]{1,0:T(8,128)}, bf16[2,256,768]{2,1,0:T(8,128)(2,1)}) custom-call(s32[2,4]{1,0:T(2,128)} %lengths.9, s32[14]{0:T(128)} %stack.131.idx, bf16[2,3,1024,128]{3,2,1,0:T(8,128)(2,1)} %get-tuple-element.199.q_ref, bf16[2,3,1024,128]{3,2,1,0:T(8,128)(2,1)} %get-tuple-element.175.k_ref, ...), custom_call_target="tpu_custom_call" | custom-call | flops 1 | bytes 1 | tf_op jit(solution)/shard_map/attn_bwd/pallas_call | solution.py:847
  186.0 6.2 %collective-permute-start.26 = (bf16[2,96,768]{2,1,0:T(8,128)(2,1)}, bf16[2,96,768]{2,1,0:T(8,128)(2,1)}, u32[]{:S(2)}, u32[]{:S(2)}) collective-permute-start(bf16[2,96,768]{2,1,0:T(8,128)(2,1)} %get-tuple-element.220), channel_id=1, source_target_pairs={{0,1},{1,0},{2,3},{3,2},{4,5},{5,4},{6,7},{7,6},{8,9},{9,8},{10,11... | collective-permute-start | bytes 884744 | tf_op jit(solution)/shard_map/ppermute | solution.py:701
  193.1 1.6 collective-permute-start.28
  194.7 16.7 %attn_bwd.3 = (bf16[4,104,576]{2,1,0:T(8,128)(2,1)}, bf16[4,104,576]{2,1,0:T(8,128)(2,1)}, f32[256,768]{1,0:T(8,128)}, f32[256,768]{1,0:T(8,128)}, bf16[2,256,768]{2,1,0:T(8,128)(2,1)}) custom-call(s32[2,4]{1,0:T(2,128)} %lengths.9, s32[14]{0:T(128)} %stack.131.idx, bf16[2,3,1024,128]{3,2,1,0:T(8,128)(2,1)} %get-tuple-element.199.q_ref, ...), custom_call_target="tpu_custom_call" | custom-call | flops 1 | bytes 1 | tf_op jit(solution)/shard_map/attn_bwd/pallas_call | solution.py:847
  211.4 4.6 %collective-permute-done.27.refs_4_ = bf16[2,96,768]{2,1,0:T(8,128)(2,1)} collective-permute-done((bf16[2,96,768]{2,1,0:T(8,128)(2,1)}, bf16[2,96,768]{2,1,0:T(8,128)(2,1)}, u32[]{:S(2)}, u32[]{:S(2)}) %collective-permute-start.27) | collective-permute-done | bytes 294944 | tf_op jit(solution)/shard_map/ppermute | solution.py:701
  216.0 1.4 collective-permute-start.29
  217.4 2.0 fusion.5
  219.5 1.6 copy-done
  221.0 2.9 chunks1.1
  223.9 1.5 collective-permute-start.33
  225.4 2.8 sums2.1
  228.2 3.9 %all-to-all-start.3 = ((bf16[4,96,768]{2,1,0:T(8,128)(2,1)}), bf16[4,96,768]{2,1,0:T(8,128)(2,1)S(1)}, u32[]{:S(2)}, u32[]{:S(2)}) async-start(bf16[4,96,768]{2,1,0:T(8,128)(2,1)} %sums2.1), calls=%async_computation.3 | async-start | bytes 1179648 | tf_op jit(solution)/shard_map/all_to_all | solution.py:891
  232.9 2.1 chunksq.1
  235.0 6.2 %collective-permute-start.30 = (bf16[240,384]{1,0:T(8,128)(2,1)}, bf16[240,384]{1,0:T(8,128)(2,1)S(1)}, u32[]{:S(2)}, u32[]{:S(2)}) collective-permute-start(bf16[240,384]{1,0:T(8,128)(2,1)} %get-tuple-element.236), channel_id=1, source_target_pairs={{0,1},{1,0},{2,3},{3,2},{4,5},{5,4},{6,7},{7,6},{8,9},{9,8},{10,11... | collective-permute-start | bytes 552968 | tf_op jit(solution)/shard_map/ppermute | solution.py:701
  242.1 1.6 collective-permute-start.32
  243.6 1.1 fusion.4
  244.7 4.7 %collective-permute-done.30.a1 = bf16[240,384]{1,0:T(8,128)(2,1)S(1)} collective-permute-done((bf16[240,384]{1,0:T(8,128)(2,1)}, bf16[240,384]{1,0:T(8,128)(2,1)S(1)}, u32[]{:S(2)}, u32[]{:S(2)}) %collective-permute-start.30) | collective-permute-done | bytes 184352 | tf_op jit(solution)/shard_map/ppermute | solution.py:701
  249.4 8.1 %collective-permute-done.31.a2 = bf16[240,384]{1,0:T(8,128)(2,1)S(1)} collective-permute-done((bf16[240,384]{1,0:T(8,128)(2,1)S(1)}, bf16[240,384]{1,0:T(8,128)(2,1)S(1)}, u32[]{:S(2)}, u32[]{:S(2)}) %collective-permute-start.31) | collective-permute-done | bytes 184352 | tf_op jit(solution)/shard_map/ppermute | solution.py:701
  257.5 1.8 collective-permute-start.38
  259.4 2.8 collective-permute-start.35
  263.1 1.6 collective-permute-start.37
  264.6 1.6 collective-permute-done.35.q1
  266.2 7.4 %collective-permute-done.36.q2 = bf16[104,576]{1,0:T(8,128)(2,1)S(1)} collective-permute-done((bf16[104,576]{1,0:T(8,128)(2,1)S(1)}, bf16[104,576]{1,0:T(8,128)(2,1)S(1)}, u32[]{:S(2)}, u32[]{:S(2)}) %collective-permute-start.36) | collective-permute-done | bytes 119840 | tf_op jit(solution)/shard_map/ppermute | solution.py:701
  274.3 2.6 sums.1
  276.9 0.9 collective-permute-start.39
  277.8 8.1 %collective-permute-done.39 = bf16[640,384]{1,0:T(8,128)(2,1)S(1)} collective-permute-done((bf16[640,384]{1,0:T(8,128)(2,1)}, bf16[640,384]{1,0:T(8,128)(2,1)S(1)}, u32[]{:S(2)}, u32[]{:S(2)}) %collective-permute-start.39) | collective-permute-done | bytes 491552 | tf_op jit(solution)/shard_map/ppermute | solution.py:701
  286.0 1.1 pad_maximum_fusion.1.s1
  287.2 1.5 collective-permute-start.40
  288.7 1.4 fusion.6
  290.2 0.9 pad_maximum_fusion.3
  291.1 10.2 %collective-permute-done.40.r2 = bf16[2,640,384]{2,1,0:T(8,128)(2,1)S(1)} collective-permute-done((bf16[2,640,384]{2,1,0:T(8,128)(2,1)S(1)}, bf16[2,640,384]{2,1,0:T(8,128)(2,1)S(1)}, u32[]{:S(2)}, u32[]{:S(2)}) %collective-permute-start.40) | collective-permute-done | bytes 983072 | tf_op jit(solution)/shard_map/ppermute | solution.py:701
  301.4 2.6 collective-permute-done.42.c2
  303.9 1.0 copy-done.13
  304.9 5.4 %outputs.1 = (f32[192,768]{1,0:T(8,128)}, f32[192,768]{1,0:T(8,128)}, f32[192,768]{1,0:T(8,128)}, f32[192,3072]{1,0:T(8,128)}, f32[192,768]{1,0:T(8,128)}, /*ind...) custom-call(s32[14]{0:T(128)} %stack.131.idx, ...), custom_call_target="tpu_custom_call" | custom-call | flops 1 | bytes 1 | tf_op jit(solution)/shard_map/outputs/pallas_call | solution.py:911
  (127 shorter events, 12.1 us)
Async XLA Ops:
  0.7 22.3 %collective-permute-start.4 = (bf16[2,256,768]{2,1,0:T(8,128)(2,1)}, bf16[2,256,768]{2,1,0:T(8,128)(2,1)S(1)}, u32[]{:S(2)}, u32[]{:S(2)}) collective-permute-start(bf16[2,256,768]{2,1,0:T(8,128)(2,1)} %rest_2_.5), channel_id=1, source_target_pairs={{0,4},{1,5},{2,6},{3,7},{4,0},{5,1},{6,2},{7,3},{8,12},{9,13},{10,... | collective-permute-start | bytes 2359304 | tf_op jit(solution)/shard_map/ppermute | solution.py:701
  1.2 21.8 %collective-permute-start.3 = (bf16[2,256,768]{2,1,0:T(8,128)(2,1)}, bf16[2,256,768]{2,1,0:T(8,128)(2,1)S(1)}, u32[]{:S(2)}, u32[]{:S(2)}) collective-permute-start(bf16[2,256,768]{2,1,0:T(8,128)(2,1)} %rest_2_.5), channel_id=1, source_target_pairs={{0,8},{1,9},{2,10},{3,11},{4,12},{5,13},{6,14},{7,15},{8,0},{9,1},... | collective-permute-start | bytes 2359304 | tf_op jit(solution)/shard_map/ppermute | solution.py:701
  7.5 8.5 %collective-permute-start.2 = (bf16[104,576]{1,0:T(8,128)(2,1)}, bf16[104,576]{1,0:T(8,128)(2,1)S(1)}, u32[]{:S(2)}, u32[]{:S(2)}) collective-permute-start(bf16[104,576]{1,0:T(8,128)(2,1)} %get-tuple-element.150), channel_id=1, source_target_pairs={{0,3},{1,2},{2,1},{3,0},{4,7},{5,6},{6,5},{7,4},{8,11},{9,10},{10,... | collective-permute-start | bytes 359432 | tf_op jit(solution)/shard_map/ppermute | solution.py:701
  11.1 11.9 %collective-permute-start.1 = (bf16[104,576]{1,0:T(8,128)(2,1)}, bf16[104,576]{1,0:T(8,128)(2,1)S(1)}, u32[]{:S(2)}, u32[]{:S(2)}) collective-permute-start(bf16[104,576]{1,0:T(8,128)(2,1)} %get-tuple-element.150), channel_id=1, source_target_pairs={{0,2},{1,3},{2,0},{3,1},{4,6},{5,7},{6,4},{7,5},{8,10},{9,11},{10,... | collective-permute-start | bytes 359432 | tf_op jit(solution)/shard_map/ppermute | solution.py:701
  11.1 11.9 %collective-permute-start = (bf16[104,576]{1,0:T(8,128)(2,1)}, bf16[104,576]{1,0:T(8,128)(2,1)S(1)}, u32[]{:S(2)}, u32[]{:S(2)}) collective-permute-start(bf16[104,576]{1,0:T(8,128)(2,1)} %get-tuple-element.150), channel_id=1, source_target_pairs={{0,1},{1,0},{2,3},{3,2},{4,5},{5,4},{6,7},{7,6},{8,9},{9,8},{10,11... | collective-permute-start | bytes 359432 | tf_op jit(solution)/shard_map/ppermute | solution.py:701
  15.9 35.7 %copy-start.17 = (bf16[104,576]{1,0:T(8,128)(2,1)}, bf16[104,576]{1,0:T(8,128)(2,1)S(1)}, u32[]{:S(2)}) copy-start(bf16[104,576]{1,0:T(8,128)(2,1)S(1)} %collective-permute-done.2.refs_7_) | copy-start | bytes 359428
  23.0 28.7 %copy-start.18 = (bf16[104,576]{1,0:T(8,128)(2,1)}, bf16[104,576]{1,0:T(8,128)(2,1)S(1)}, u32[]{:S(2)}) copy-start(bf16[104,576]{1,0:T(8,128)(2,1)S(1)} %collective-permute-done.1.refs_6_) | copy-start | bytes 359428
  23.0 28.7 %copy-start.19 = (bf16[104,576]{1,0:T(8,128)(2,1)}, bf16[104,576]{1,0:T(8,128)(2,1)S(1)}, u32[]{:S(2)}) copy-start(bf16[104,576]{1,0:T(8,128)(2,1)S(1)} %collective-permute-done.refs_5_) | copy-start | bytes 359428
  23.0 28.7 %copy-start.2 = (bf16[2,256,768]{2,1,0:T(8,128)(2,1)}, bf16[2,256,768]{2,1,0:T(8,128)(2,1)S(1)}, u32[]{:S(2)}) copy-start(bf16[2,256,768]{2,1,0:T(8,128)(2,1)S(1)} %collective-permute-done.4.rest_4_) | copy-start | bytes 2359300
  23.0 28.7 %copy-start.3 = (bf16[2,256,768]{2,1,0:T(8,128)(2,1)}, bf16[2,256,768]{2,1,0:T(8,128)(2,1)S(1)}, u32[]{:S(2)}) copy-start(bf16[2,256,768]{2,1,0:T(8,128)(2,1)S(1)} %collective-permute-done.3.rest_3_) | copy-start | bytes 2359300
  23.0 21.9 %collective-permute-start.6 = (bf16[2,256,768]{2,1,0:T(8,128)(2,1)S(1)}, bf16[2,256,768]{2,1,0:T(8,128)(2,1)S(1)}, u32[]{:S(2)}, u32[]{:S(2)}) collective-permute-start(bf16[2,256,768]{2,1,0:T(8,128)(2,1)S(1)} %collective-permute-done.3.rest_3_), channel_id=1, source_target_pairs={{0,4},{1,5},{2,6},{3,7},{4,0},{5,1},{6,2},{7,3},{8,12},{9,13},{10,... | collective-permute-start | bytes 2359304 | tf_op jit(solution)/shard_map/ppermute | solution.py:701
  23.2 21.8 %collective-permute-start.5 = (bf16[3,104,576]{2,1,0:T(8,128)(2,1)S(1)}, bf16[3,104,576]{2,1,0:T(8,128)(2,1)S(1)}, u32[]{:S(2)}, u32[]{:S(2)}) collective-permute-start(bf16[3,104,576]{2,1,0:T(8,128)(2,1)S(1)} %pad_maximum_fusion.6), channel_id=1, source_target_pairs={{0,16},{1,17},{2,18},{3,19},{4,20},{5,21},{6,22},{7,23},{8,24},{9,... | collective-permute-start | bytes 1078280 | tf_op jit(solution)/shard_map/ppermute | solution.py:701
  24.7 9.9 %collective-permute-start.9 = (bf16[256,384]{1,0:T(8,128)(2,1)}, bf16[256,384]{1,0:T(8,128)(2,1)S(1)}, u32[]{:S(2)}, u32[]{:S(2)}) collective-permute-start(bf16[256,384]{1,0:T(8,128)(2,1)} %get-tuple-element.157.sm_own), channel_id=1, source_target_pairs={{0,3},{1,2},{2,1},{3,0},{4,7},{5,6},{6,5},{7,4},{8,11},{9,10},{10,... | collective-permute-start | bytes 589832 | tf_op jit(solution)/shard_map/ppermute | solution.py:701
  27.6 17.3 %collective-permute-start.8 = (bf16[256,384]{1,0:T(8,128)(2,1)}, bf16[256,384]{1,0:T(8,128)(2,1)S(1)}, u32[]{:S(2)}, u32[]{:S(2)}) collective-permute-start(bf16[256,384]{1,0:T(8,128)(2,1)} %get-tuple-element.157.sm_own), channel_id=1, source_target_pairs={{0,2},{1,3},{2,0},{3,1},{4,6},{5,7},{6,4},{7,5},{8,10},{9,11},{10,... | collective-permute-start | bytes 589832 | tf_op jit(solution)/shard_map/ppermute | solution.py:701
  27.6 17.3 %collective-permute-start.7 = (bf16[256,384]{1,0:T(8,128)(2,1)}, bf16[256,384]{1,0:T(8,128)(2,1)S(1)}, u32[]{:S(2)}, u32[]{:S(2)}) collective-permute-start(bf16[256,384]{1,0:T(8,128)(2,1)} %get-tuple-element.157.sm_own), channel_id=1, source_target_pairs={{0,1},{1,0},{2,3},{3,2},{4,5},{5,4},{6,7},{7,6},{8,9},{9,8},{10,11... | collective-permute-start | bytes 589832 | tf_op jit(solution)/shard_map/ppermute | solution.py:701
  45.7 15.5 %collective-permute-start.10 = (bf16[3,256,384]{2,1,0:T(8,128)(2,1)S(1)}, bf16[3,256,384]{2,1,0:T(8,128)(2,1)S(1)}, u32[]{:S(2)}, u32[]{:S(2)}) collective-permute-start(bf16[3,256,384]{2,1,0:T(8,128)(2,1)S(1)} %pad_maximum_fusion.4), channel_id=1, source_target_pairs={{0,8},{1,9},{2,10},{3,11},{4,20},{5,21},{6,22},{7,23},{8,0},{9,1},... | collective-permute-start | bytes 1769480 | tf_op jit(solution)/shard_map/ppermute | solution.py:701
  47.3 12.8 %collective-permute-start.13 = (bf16[96,768]{1,0:T(8,128)(2,1)}, bf16[96,768]{1,0:T(8,128)(2,1)S(1)}, u32[]{:S(2)}, u32[]{:S(2)}) collective-permute-start(bf16[96,768]{1,0:T(8,128)(2,1)} %get-tuple-element.168), channel_id=1, source_target_pairs={{0,3},{1,2},{2,1},{3,0},{4,7},{5,6},{6,5},{7,4},{8,11},{9,10},{10,... | collective-permute-start | bytes 442376 | tf_op jit(solution)/shard_map/ppermute | solution.py:701
  49.8 11.4 %collective-permute-start.12 = (bf16[96,768]{1,0:T(8,128)(2,1)}, bf16[96,768]{1,0:T(8,128)(2,1)}, u32[]{:S(2)}, u32[]{:S(2)}) collective-permute-start(bf16[96,768]{1,0:T(8,128)(2,1)} %get-tuple-element.168), channel_id=1, source_target_pairs={{0,2},{1,3},{2,0},{3,1},{4,6},{5,7},{6,4},{7,5},{8,10},{9,11},{10,... | collective-permute-start | bytes 442376 | tf_op jit(solution)/shard_map/ppermute | solution.py:701
  49.8 11.4 %collective-permute-start.11 = (bf16[96,768]{1,0:T(8,128)(2,1)}, bf16[96,768]{1,0:T(8,128)(2,1)}, u32[]{:S(2)}, u32[]{:S(2)}) collective-permute-start(bf16[96,768]{1,0:T(8,128)(2,1)} %get-tuple-element.168), channel_id=1, source_target_pairs={{0,1},{1,0},{2,3},{3,2},{4,5},{5,4},{6,7},{7,6},{8,9},{9,8},{10,11... | collective-permute-start | bytes 442376 | tf_op jit(solution)/shard_map/ppermute | solution.py:701
  61.4 28.4 %copy-start.5 = (bf16[2,3,256,384]{3,2,1,0:T(8,128)(2,1)}, bf16[2,3,256,384]{3,2,1,0:T(8,128)(2,1)S(1)}, u32[]{:S(2)}) copy-start(bf16[2,3,256,384]{3,2,1,0:T(8,128)(2,1)S(1)} %pad_maximum_fusion.s1a) | copy-start | bytes 3538948
  62.9 21.2 %collective-permute-start.14 = (bf16[2,3,256,384]{3,2,1,0:T(8,128)(2,1)S(1)}, bf16[2,3,256,384]{3,2,1,0:T(8,128)(2,1)S(1)}, u32[]{:S(2)}, u32[]{:S(2)}) collective-permute-start(bf16[2,3,256,384]{3,2,1,0:T(8,128)(2,1)S(1)} %pad_maximum_fusion.s1a), channel_id=1, source_target_pairs={{0,16},{1,17},{2,18},{3,19},{4,12},{5,13},{6,14},{7,15},{8,24},{9,... | collective-permute-start | bytes 3538952 | tf_op jit(solution)/shard_map/ppermute | solution.py:701
  63.7 20.4 %collective-permute-start.15 = (bf16[3,96,768]{2,1,0:T(8,128)(2,1)S(1)}, bf16[3,96,768]{2,1,0:T(8,128)(2,1)S(1)}, u32[]{:S(2)}, u32[]{:S(2)}) collective-permute-start(bf16[3,96,768]{2,1,0:T(8,128)(2,1)S(1)} %pad_maximum_fusion.5), channel_id=1, source_target_pairs={{0,8},{1,9},{2,10},{3,11},{4,20},{5,21},{6,22},{7,23},{8,0},{9,1},... | collective-permute-start | bytes 1327112 | tf_op jit(solution)/shard_map/ppermute | solution.py:701
  85.2 22.0 %copy-start.7 = (bf16[2,3,96,768]{3,2,1,0:T(8,128)(2,1)}, bf16[2,3,96,768]{3,2,1,0:T(8,128)(2,1)S(1)}, u32[]{:S(2)}) copy-start(bf16[2,3,96,768]{3,2,1,0:T(8,128)(2,1)S(1)} %pad_maximum_fusion.2.s1b) | copy-start | bytes 2654212
  85.2 17.6 %collective-permute-start.16 = (bf16[2,3,96,768]{3,2,1,0:T(8,128)(2,1)S(1)}, bf16[2,3,96,768]{3,2,1,0:T(8,128)(2,1)}, u32[]{:S(2)}, u32[]{:S(2)}) collective-permute-start(bf16[2,3,96,768]{3,2,1,0:T(8,128)(2,1)S(1)} %pad_maximum_fusion.2.s1b), channel_id=1, source_target_pairs={{0,16},{1,17},{2,18},{3,19},{4,12},{5,13},{6,14},{7,15},{8,24},{9,... | collective-permute-start | bytes 2654216 | tf_op jit(solution)/shard_map/ppermute | solution.py:701
  86.1 16.7 %all-to-all-start = ((bf16[4,256,384]{2,1,0:T(8,128)(2,1)}), bf16[4,256,384]{2,1,0:T(8,128)(2,1)S(1)}, u32[]{:S(2)}, u32[]{:S(2)}) async-start(bf16[4,256,384]{2,1,0:T(8,128)(2,1)} %get-tuple-element.180.o_ref), calls=%async_computation | async-start | bytes 1572864 | tf_op jit(solution)/shard_map/all_to_all | solution.py:783
  89.8 15.0 %collective-permute-start.17 = (bf16[2,3,256,384]{3,2,1,0:T(8,128)(2,1)S(1)}, bf16[2,3,256,384]{3,2,1,0:T(8,128)(2,1)}, u32[]{:S(2)}, u32[]{:S(2)}) collective-permute-start(bf16[2,3,256,384]{3,2,1,0:T(8,128)(2,1)S(1)} %pad_maximum_fusion.s1a), channel_id=1, source_target_pairs={{0,4},{1,5},{2,6},{3,7},{4,0},{5,1},{6,2},{7,3},{8,12},{9,13},{10,... | collective-permute-start | bytes 3538952 | tf_op jit(solution)/shard_map/ppermute | solution.py:701
  90.1 14.7 %collective-permute-start.18 = (bf16[2,3,256,384]{3,2,1,0:T(8,128)(2,1)}, bf16[2,3,256,384]{3,2,1,0:T(8,128)(2,1)}, u32[]{:S(2)}, u32[]{:S(2)}) collective-permute-start(bf16[2,3,256,384]{3,2,1,0:T(8,128)(2,1)} %copy-done.10), channel_id=1, source_target_pairs={{0,4},{1,5},{2,6},{3,7},{4,0},{5,1},{6,2},{7,3},{8,12},{9,13},{10,... | collective-permute-start | bytes 3538952 | tf_op jit(solution)/shard_map/ppermute | solution.py:701
  90.3 14.4 %collective-permute-start.19 = (bf16[2,3,96,768]{3,2,1,0:T(8,128)(2,1)S(1)}, bf16[2,3,96,768]{3,2,1,0:T(8,128)(2,1)}, u32[]{:S(2)}, u32[]{:S(2)}) collective-permute-start(bf16[2,3,96,768]{3,2,1,0:T(8,128)(2,1)S(1)} %pad_maximum_fusion.2.s1b), channel_id=1, source_target_pairs={{0,4},{1,5},{2,6},{3,7},{4,0},{5,1},{6,2},{7,3},{8,12},{9,13},{10,... | collective-permute-start | bytes 2654216 | tf_op jit(solution)/shard_map/ppermute | solution.py:701
  102.8 4.3 %collective-permute-start.20 = (bf16[2,3,96,768]{3,2,1,0:T(8,128)(2,1)}, bf16[2,3,96,768]{3,2,1,0:T(8,128)(2,1)}, u32[]{:S(2)}, u32[]{:S(2)}) collective-permute-start(bf16[2,3,96,768]{3,2,1,0:T(8,128)(2,1)} %collective-permute-done.16.r2b), channel_id=1, source_target_pairs={{0,4},{1,5},{2,6},{3,7},{4,0},{5,1},{6,2},{7,3},{8,12},{9,13},{10,... | collective-permute-start | bytes 2654216 | tf_op jit(solution)/shard_map/ppermute | solution.py:701
  136.3 10.0 %collective-permute-start.21 = (bf16[512,5760]{1,0:T(8,128)(2,1)}, bf16[512,5760]{1,0:T(8,128)(2,1)}, u32[]{:S(2)}, u32[]{:S(2)}) collective-permute-start(bf16[512,5760]{1,0:T(8,128)(2,1)} %get-tuple-element.188.sent), channel_id=1, source_target_pairs={{0,4},{1,5},{2,6},{3,7},{4,0},{5,1},{6,2},{7,3},{8,12},{9,13},{10,... | collective-permute-start | bytes 17694728 | tf_op jit(solution)/shard_map/ppermute | solution.py:701
  136.7 20.6 %all-to-all-start.1 = ((bf16[4,256,384]{2,1,0:T(8,128)(2,1)}), bf16[4,256,384]{2,1,0:T(8,128)(2,1)S(1)}, u32[]{:S(2)}, u32[]{:S(2)}) async-start(bf16[4,256,384]{2,1,0:T(8,128)(2,1)} %get-tuple-element.186), calls=%async_computation.1 | async-start | bytes 1572864 | tf_op jit(solution)/shard_map/all_to_all | solution.py:821
  158.2 61.2 %all-to-all-start.2 = ((bf16[4,4,240,384]{3,2,1,0:T(8,128)(2,1)}), bf16[4,4,240,384]{3,2,1,0:T(8,128)(2,1)S(1)}, u32[]{:S(2)}, u32[]{:S(2)}) async-start(bf16[4,4,240,384]{3,2,1,0:T(8,128)(2,1)} %get-tuple-element.196), calls=%async_computation.2 | async-start | bytes 5898240 | tf_op jit(solution)/shard_map/all_to_all | solution.py:879
  162.1 23.1 %collective-permute-start.22 = (bf16[2,96,768]{2,1,0:T(8,128)(2,1)}, bf16[2,96,768]{2,1,0:T(8,128)(2,1)S(1)}, u32[]{:S(2)}, u32[]{:S(2)}) collective-permute-start(bf16[2,96,768]{2,1,0:T(8,128)(2,1)} %get-tuple-element.205), channel_id=1, source_target_pairs={{0,1},{1,0},{2,3},{3,2},{4,5},{5,4},{6,7},{7,6},{8,9},{9,8},{10,11... | collective-permute-start | bytes 884744 | tf_op jit(solution)/shard_map/ppermute | solution.py:701
  162.2 23.7 %collective-permute-start.23 = (bf16[2,96,768]{2,1,0:T(8,128)(2,1)}, bf16[2,96,768]{2,1,0:T(8,128)(2,1)S(1)}, u32[]{:S(2)}, u32[]{:S(2)}) collective-permute-start(bf16[2,96,768]{2,1,0:T(8,128)(2,1)} %get-tuple-element.206), channel_id=1, source_target_pairs={{0,2},{1,3},{2,0},{3,1},{4,6},{5,7},{6,4},{7,5},{8,10},{9,11},{10,... | collective-permute-start | bytes 884744 | tf_op jit(solution)/shard_map/ppermute | solution.py:701
  165.0 20.9 %collective-permute-start.24 = (bf16[2,96,768]{2,1,0:T(8,128)(2,1)}, bf16[2,96,768]{2,1,0:T(8,128)(2,1)S(1)}, u32[]{:S(2)}, u32[]{:S(2)}) collective-permute-start(bf16[2,96,768]{2,1,0:T(8,128)(2,1)} %get-tuple-element.207), channel_id=1, source_target_pairs={{0,3},{1,2},{2,1},{3,0},{4,7},{5,6},{6,5},{7,4},{8,11},{9,10},{10,... | collective-permute-start | bytes 884744 | tf_op jit(solution)/shard_map/ppermute | solution.py:701
  185.2 26.1 %copy-start.22 = (bf16[2,96,768]{2,1,0:T(8,128)(2,1)}, bf16[2,96,768]{2,1,0:T(8,128)(2,1)S(1)}, u32[]{:S(2)}) copy-start(bf16[2,96,768]{2,1,0:T(8,128)(2,1)S(1)} %collective-permute-done.22.refs_0_) | copy-start | bytes 884740
  185.9 25.5 %copy-start.23 = (bf16[2,96,768]{2,1,0:T(8,128)(2,1)}, bf16[2,96,768]{2,1,0:T(8,128)(2,1)S(1)}, u32[]{:S(2)}) copy-start(bf16[2,96,768]{2,1,0:T(8,128)(2,1)S(1)} %collective-permute-done.23.refs_1_) | copy-start | bytes 884740
  185.9 25.5 %copy-start.24 = (bf16[2,96,768]{2,1,0:T(8,128)(2,1)}, bf16[2,96,768]{2,1,0:T(8,128)(2,1)S(1)}, u32[]{:S(2)}) copy-start(bf16[2,96,768]{2,1,0:T(8,128)(2,1)S(1)} %collective-permute-done.24.refs_2_) | copy-start | bytes 884740
  185.9 30.1 %collective-permute-start.25 = (bf16[2,256,768]{2,1,0:T(8,128)(2,1)}, bf16[2,256,768]{2,1,0:T(8,128)(2,1)}, u32[]{:S(2)}, u32[]{:S(2)}) collective-permute-start(bf16[2,256,768]{2,1,0:T(8,128)(2,1)} %get-tuple-element.218), channel_id=1, source_target_pairs={{0,4},{1,5},{2,6},{3,7},{4,0},{5,1},{6,2},{7,3},{8,12},{9,13},{10,... | collective-permute-start | bytes 2359304 | tf_op jit(solution)/shard_map/ppermute | solution.py:701
  186.0 25.4 %collective-permute-start.26 = (bf16[2,96,768]{2,1,0:T(8,128)(2,1)}, bf16[2,96,768]{2,1,0:T(8,128)(2,1)}, u32[]{:S(2)}, u32[]{:S(2)}) collective-permute-start(bf16[2,96,768]{2,1,0:T(8,128)(2,1)} %get-tuple-element.220), channel_id=1, source_target_pairs={{0,1},{1,0},{2,3},{3,2},{4,5},{5,4},{6,7},{7,6},{8,9},{9,8},{10,11... | collective-permute-start | bytes 884744 | tf_op jit(solution)/shard_map/ppermute | solution.py:701
  192.2 23.7 %collective-permute-start.27 = (bf16[2,96,768]{2,1,0:T(8,128)(2,1)}, bf16[2,96,768]{2,1,0:T(8,128)(2,1)}, u32[]{:S(2)}, u32[]{:S(2)}) collective-permute-start(bf16[2,96,768]{2,1,0:T(8,128)(2,1)} %get-tuple-element.221), channel_id=1, source_target_pairs={{0,2},{1,3},{2,0},{3,1},{4,6},{5,7},{6,4},{7,5},{8,10},{9,11},{10,... | collective-permute-start | bytes 884744 | tf_op jit(solution)/shard_map/ppermute | solution.py:701
  193.1 22.9 %collective-permute-start.28 = (bf16[2,96,768]{2,1,0:T(8,128)(2,1)}, bf16[2,96,768]{2,1,0:T(8,128)(2,1)}, u32[]{:S(2)}, u32[]{:S(2)}) collective-permute-start(bf16[2,96,768]{2,1,0:T(8,128)(2,1)} %get-tuple-element.222), channel_id=1, source_target_pairs={{0,3},{1,2},{2,1},{3,0},{4,7},{5,6},{6,5},{7,4},{8,11},{9,10},{10,... | collective-permute-start | bytes 884744 | tf_op jit(solution)/shard_map/ppermute | solution.py:701
  216.0 27.7 %collective-permute-start.34 = (bf16[2,256,768]{2,1,0:T(8,128)(2,1)}, bf16[2,256,768]{2,1,0:T(8,128)(2,1)}, u32[]{:S(2)}, u32[]{:S(2)}) collective-permute-start(bf16[2,256,768]{2,1,0:T(8,128)(2,1)} %get-tuple-element.241), channel_id=1, source_target_pairs={{0,4},{1,5},{2,6},{3,7},{4,0},{5,1},{6,2},{7,3},{8,12},{9,13},{10,... | collective-permute-start | bytes 2359304 | tf_op jit(solution)/shard_map/ppermute | solution.py:701
  216.0 16.1 %collective-permute-start.29 = (bf16[4,104,576]{2,1,0:T(8,128)(2,1)}, bf16[4,104,576]{2,1,0:T(8,128)(2,1)S(1)}, u32[]{:S(2)}, u32[]{:S(2)}) collective-permute-start(bf16[4,104,576]{2,1,0:T(8,128)(2,1)} %get-tuple-element.227), channel_id=1, source_target_pairs={{0,16},{1,17},{2,18},{3,19},{4,20},{5,21},{6,22},{7,23},{8,24},{9,... | collective-permute-start | bytes 1437704 | tf_op jit(solution)/shard_map/ppermute | solution.py:701
  223.9 33.6 %collective-permute-start.33 = (bf16[256,768]{1,0:T(8,128)(2,1)}, bf16[256,768]{1,0:T(8,128)(2,1)S(1)}, u32[]{:S(2)}, u32[]{:S(2)}) collective-permute-start(bf16[256,768]{1,0:T(8,128)(2,1)} %fusion.5), channel_id=1, source_target_pairs={{0,8},{1,9},{2,10},{3,11},{4,12},{5,13},{6,14},{7,15},{8,0},{9,1},... | collective-permute-start | bytes 1179656 | tf_op jit(solution)/shard_map/ppermute | solution.py:701
  228.2 15.4 %copy-start.14 = (f32[256,768]{1,0:T(8,128)S(1)}, f32[256,768]{1,0:T(8,128)}, u32[]{:S(2)}) copy-start(f32[256,768]{1,0:T(8,128)} %get-tuple-element.240) | copy-start | bytes 2359300
  228.2 36.4 %all-to-all-start.3 = ((bf16[4,96,768]{2,1,0:T(8,128)(2,1)}), bf16[4,96,768]{2,1,0:T(8,128)(2,1)S(1)}, u32[]{:S(2)}, u32[]{:S(2)}) async-start(bf16[4,96,768]{2,1,0:T(8,128)(2,1)} %sums2.1), calls=%async_computation.3 | async-start | bytes 1179648 | tf_op jit(solution)/shard_map/all_to_all | solution.py:891
  235.0 24.4 %copy-start.36 = (bf16[104,576]{1,0:T(8,128)(2,1)S(1)}, bf16[104,576]{1,0:T(8,128)(2,1)}, u32[]{:S(2)}) copy-start(bf16[104,576]{1,0:T(8,128)(2,1)} %get-tuple-element.245) | copy-start | bytes 359428
  235.0 27.2 %copy-start.35 = (bf16[104,576]{1,0:T(8,128)(2,1)S(1)}, bf16[104,576]{1,0:T(8,128)(2,1)}, u32[]{:S(2)}) copy-start(bf16[104,576]{1,0:T(8,128)(2,1)} %get-tuple-element.246) | copy-start | bytes 359428
  235.0 28.1 %copy-start.34 = (bf16[104,576]{1,0:T(8,128)(2,1)S(1)}, bf16[104,576]{1,0:T(8,128)(2,1)}, u32[]{:S(2)}) copy-start(bf16[104,576]{1,0:T(8,128)(2,1)} %get-tuple-element.247) | copy-start | bytes 359428
  235.0 14.4 %collective-permute-start.30 = (bf16[240,384]{1,0:T(8,128)(2,1)}, bf16[240,384]{1,0:T(8,128)(2,1)S(1)}, u32[]{:S(2)}, u32[]{:S(2)}) collective-permute-start(bf16[240,384]{1,0:T(8,128)(2,1)} %get-tuple-element.236), channel_id=1, source_target_pairs={{0,1},{1,0},{2,3},{3,2},{4,5},{5,4},{6,7},{7,6},{8,9},{9,8},{10,11... | collective-permute-start | bytes 552968 | tf_op jit(solution)/shard_map/ppermute | solution.py:701
  241.2 16.3 %collective-permute-start.31 = (bf16[240,384]{1,0:T(8,128)(2,1)S(1)}, bf16[240,384]{1,0:T(8,128)(2,1)S(1)}, u32[]{:S(2)}, u32[]{:S(2)}) collective-permute-start(bf16[240,384]{1,0:T(8,128)(2,1)S(1)} %copy-done.33), channel_id=1, source_target_pairs={{0,2},{1,3},{2,0},{3,1},{4,6},{5,7},{6,4},{7,5},{8,10},{9,11},{10,... | collective-permute-start | bytes 552968 | tf_op jit(solution)/shard_map/ppermute | solution.py:701
  242.1 15.5 %collective-permute-start.32 = (bf16[240,384]{1,0:T(8,128)(2,1)S(1)}, bf16[240,384]{1,0:T(8,128)(2,1)S(1)}, u32[]{:S(2)}, u32[]{:S(2)}) collective-permute-start(bf16[240,384]{1,0:T(8,128)(2,1)S(1)} %copy-done.32), channel_id=1, source_target_pairs={{0,3},{1,2},{2,1},{3,0},{4,7},{5,6},{6,5},{7,4},{8,11},{9,10},{10,... | collective-permute-start | bytes 552968 | tf_op jit(solution)/shard_map/ppermute | solution.py:701
  249.4 24.3 %copy-start.25 = (bf16[240,384]{1,0:T(8,128)(2,1)}, bf16[240,384]{1,0:T(8,128)(2,1)S(1)}, u32[]{:S(2)}) copy-start(bf16[240,384]{1,0:T(8,128)(2,1)S(1)} %collective-permute-done.30.a1) | copy-start | bytes 552964
  257.5 16.1 %copy-start.26 = (bf16[240,384]{1,0:T(8,128)(2,1)}, bf16[240,384]{1,0:T(8,128)(2,1)S(1)}, u32[]{:S(2)}) copy-start(bf16[240,384]{1,0:T(8,128)(2,1)S(1)} %collective-permute-done.31.a2) | copy-start | bytes 552964
  257.5 16.1 %copy-start.27 = (bf16[240,384]{1,0:T(8,128)(2,1)}, bf16[240,384]{1,0:T(8,128)(2,1)S(1)}, u32[]{:S(2)}) copy-start(bf16[240,384]{1,0:T(8,128)(2,1)S(1)} %collective-permute-done.32.a3) | copy-start | bytes 552964
  257.5 16.1 %collective-permute-start.38 = (bf16[256,768]{1,0:T(8,128)(2,1)S(1)}, bf16[256,768]{1,0:T(8,128)(2,1)S(1)}, u32[]{:S(2)}, u32[]{:S(2)}) collective-permute-start(bf16[256,768]{1,0:T(8,128)(2,1)S(1)} %fusion.4), channel_id=1, source_target_pairs={{0,8},{1,9},{2,10},{3,11},{4,12},{5,13},{6,14},{7,15},{8,0},{9,1},... | collective-permute-start | bytes 1179656 | tf_op jit(solution)/shard_map/ppermute | solution.py:701
  259.4 6.9 %collective-permute-start.35 = (bf16[104,576]{1,0:T(8,128)(2,1)S(1)}, bf16[104,576]{1,0:T(8,128)(2,1)S(1)}, u32[]{:S(2)}, u32[]{:S(2)}) collective-permute-start(bf16[104,576]{1,0:T(8,128)(2,1)S(1)} %copy-done.36), channel_id=1, source_target_pairs={{0,1},{1,0},{2,3},{3,2},{4,5},{5,4},{6,7},{7,6},{8,9},{9,8},{10,11... | collective-permute-start | bytes 359432 | tf_op jit(solution)/shard_map/ppermute | solution.py:701
  262.2 11.4 %collective-permute-start.36 = (bf16[104,576]{1,0:T(8,128)(2,1)S(1)}, bf16[104,576]{1,0:T(8,128)(2,1)S(1)}, u32[]{:S(2)}, u32[]{:S(2)}) collective-permute-start(bf16[104,576]{1,0:T(8,128)(2,1)S(1)} %copy-done.35), channel_id=1, source_target_pairs={{0,2},{1,3},{2,0},{3,1},{4,6},{5,7},{6,4},{7,5},{8,10},{9,11},{10,... | collective-permute-start | bytes 359432 | tf_op jit(solution)/shard_map/ppermute | solution.py:701
  263.1 10.6 %collective-permute-start.37 = (bf16[104,576]{1,0:T(8,128)(2,1)S(1)}, bf16[104,576]{1,0:T(8,128)(2,1)S(1)}, u32[]{:S(2)}, u32[]{:S(2)}) collective-permute-start(bf16[104,576]{1,0:T(8,128)(2,1)S(1)} %copy-done.34), channel_id=1, source_target_pairs={{0,3},{1,2},{2,1},{3,0},{4,7},{5,6},{6,5},{7,4},{8,11},{9,10},{10,... | collective-permute-start | bytes 359432 | tf_op jit(solution)/shard_map/ppermute | solution.py:701
  276.9 9.0 %collective-permute-start.39 = (bf16[640,384]{1,0:T(8,128)(2,1)}, bf16[640,384]{1,0:T(8,128)(2,1)S(1)}, u32[]{:S(2)}, u32[]{:S(2)}) collective-permute-start(bf16[640,384]{1,0:T(8,128)(2,1)} %sums.1), channel_id=1, source_target_pairs={{0,8},{1,9},{2,10},{3,11},{4,20},{5,21},{6,22},{7,23},{8,0},{9,1},... | collective-permute-start | bytes 1474568 | tf_op jit(solution)/shard_map/ppermute | solution.py:701
  287.1 4.0 %collective-permute-start.41 = (bf16[2,640,384]{2,1,0:T(8,128)(2,1)S(1)}, bf16[2,640,384]{2,1,0:T(8,128)(2,1)S(1)}, u32[]{:S(2)}, u32[]{:S(2)}) collective-permute-start(bf16[2,640,384]{2,1,0:T(8,128)(2,1)S(1)} %pad_maximum_fusion.1.s1), channel_id=1, source_target_pairs={{0,4},{1,5},{2,6},{3,7},{4,0},{5,1},{6,2},{7,3},{8,12},{9,13},{10,... | collective-permute-start | bytes 2949128 | tf_op jit(solution)/shard_map/ppermute | solution.py:701
  287.2 14.2 %collective-permute-start.40 = (bf16[2,640,384]{2,1,0:T(8,128)(2,1)S(1)}, bf16[2,640,384]{2,1,0:T(8,128)(2,1)S(1)}, u32[]{:S(2)}, u32[]{:S(2)}) collective-permute-start(bf16[2,640,384]{2,1,0:T(8,128)(2,1)S(1)} %pad_maximum_fusion.1.s1), channel_id=1, source_target_pairs={{0,16},{1,17},{2,18},{3,19},{4,12},{5,13},{6,14},{7,15},{8,24},{9,... | collective-permute-start | bytes 2949128 | tf_op jit(solution)/shard_map/ppermute | solution.py:701
  301.4 2.6 collective-permute-start.42
  (20 other events, 105.0 us)

commit v4 on v3

--- a/solution.py
+++ b/solution.py
@@ -199,12 +199,16 @@
     lax.fori_loop(0, 8, per_tile, 0)
 
 
-def attn_bwd_kernel(pg, KC, s, lengths, idx, q_ref, k_ref, v_ref, o_ref, do_ref, *rest):
-    *rest, dq_s, dk_s, dv_s, do_s, d_ref, gq_s = rest
-    if s == 1:
-        rest = (*rest, gq_s)
-    if pg > 1:
-        d_ref = rest[0]
+def attn_bwd_kernel(pg, KC, lengths, idx, *refs):
+    ins, (w, t0, t1, t2, t3, extra), outs, scratch = refs[:5], refs[5:11], refs[11:-6], refs[-6:]
+    gq_s = scratch[-1]
+    for s in range(2):
+        attn_bwd(pg, KC, s, lengths, idx, *ins, *scratch[:4], outs[0].at[s] if pg > 1 else scratch[4])
+        if pg == 1:
+            products(s, idx, scratch[4], w, (t0, t1, t2, t3), extra, gq_s, *outs)
+
+
+def attn_bwd(pg, KC, s, lengths, idx, q_ref, k_ref, v_ref, o_ref, do_ref, dq_s, dk_s, dv_s, do_s, d_ref):
     c, mine = idx[2], idx[5]
     T, L = o_ref.shape[1], k_ref.shape[2]
     bounds = limits(lengths, s, L)
@@ -245,11 +249,11 @@
         def step(kt, _):
             at = pl.multiple_of(kt * KC, KC)
             for h in range(3):
-                q = q_ref[0, h, pl.ds(here, T)]
-                k = k_ref[0, h, pl.ds(at, KC)]
+                q = q_ref[s, h, pl.ds(here, T)]
+                k = k_ref[s, h, pl.ds(at, KC)]
                 d = do_s[h]
                 pt = jnp.exp(mm_nt(k, q))
-                ds = (pt * mm_nt(v_ref[0, h, pl.ds(at, KC)], d)).astype(BF)
+                ds = (pt * mm_nt(v_ref[s, h, pl.ds(at, KC)], d)).astype(BF)
                 dv_s[h, pl.ds(at, KC)] += mm(pt.astype(BF), d)
                 dk_s[h, pl.ds(at, KC)] += mm(ds, q)
                 dq_s[h, pl.ds(here, T)] += mm_tn(ds, k)
@@ -272,36 +276,29 @@
             d_ref[g, n, :, 256:384] = jnp.where(lower, dv[0], dv[1]).astype(BF)
             d_ref[g, n, :, 384:512] = jnp.where(lower, dq[2], dv[2]).astype(BF)
             d_ref[g, n, :, 512:576] = dk[2][:, 0:64].astype(BF)
-    if pg == 1:
-        products(s, idx, d_ref, *rest)
-
-
-def products(s, idx, d, w, dfirst, t0, t1, t2, t3, *rest):
-    if s == 0:
-        gq, gi_own, gi_x, gi_b = rest
-    else:
-        prev, extra, gq_own, gq_other, gi_own, gi_x, gi_b, gq = rest
+
+
+def products(s, idx, d, w, toks, extra, acc, gq_own, gq_other, gi):
     zw, h, y = idx[1], idx[2], idx[3]
     D = w.shape[0]
-    for n in range(2):
-        gi_b[n] = mm_nt(d[0, n + 2], w[...]).astype(BF)
-    gi_x[...] = mm_nt(d[0, 1], w[...])
-    gi_own[...] = mm_nt(d[0, 0], w[...]) + dfirst[...]
-    toks = (t0, t1, t2, t3)
-    acc = sum(mm_tn(t[0], d[0, n]) for n, t in enumerate(toks))
+    T = d.shape[2]
+    rows = slice(s * T, (s + 1) * T)
+    for n, off in enumerate(OFFS):
+        gi[h ^ off, rows, :] = mm_nt(d[0, n], w[...]).astype(BF)
+    v = sum(mm_tn(t[s], d[0, n]) for n, t in enumerate(toks))
     col = sum(fold8(d[0, n].astype(F32)) for n in range(4))
     if s == 0:
-        gq[0:D, :] = acc
-        gq[D : D + 8, :] = col
+        acc[0:D, :] = v
+        acc[D : D + 8, :] = col
         return
-    gq[0:D, :] = acc + prev[0:D, :]
-    col = jnp.sum(col + prev[D : D + 8, :], axis=0, keepdims=True)
+    acc[0:D, :] += v
+    col = jnp.sum(col + acc[D : D + 8, :], axis=0, keepdims=True)
     top = lax.broadcasted_iota(jnp.int32, (8, 576), 0) == 0
     for k in range(4):
         z = zw ^ k
         tail = jnp.where(top & (h == z), col, extra[z]).astype(BF)
         for ref, yy in ((gq_own, y), (gq_other, 1 - y)):
-            ref[k, 0:96, :] = gq[pl.ds(pl.multiple_of(z * 192 + yy * 96, 8), 96), :].astype(BF)
+            ref[k, 0:96, :] = acc[pl.ds(pl.multiple_of(z * 192 + yy * 96, 8), 96), :].astype(BF)
             ref[k, 96:104, :] = tail
 
 
@@ -529,7 +526,7 @@
 
 
 def weight_kernel(idx, kept, mate, sent, plane, mine, *rest):
-    outs, (units, shared, units2, shared2, sem) = rest[:6], rest[6:]
+    outs, (units, shared, units2, shared2, sem) = rest[:3], rest[3:]
     z = idx[1]
     D = shared.shape[1] // 3
     FB = D // 2
@@ -562,7 +559,7 @@
             if k == 0:
                 mine[q] = v[q * 96 : (q + 1) * 96]
             else:
-                outs[(q // 2) * 3 + k - 1][q % 2] = v[q * 96 : (q + 1) * 96].astype(BF)
+                outs[k - 1][q] = v[q * 96 : (q + 1) * 96].astype(BF)
     for cp in copies[8:]:
         cp.wait()
     v = mm_tn(shared[:, 0:D], units[:, 2 * wide : 2 * wide + FB]) + mm_tn(shared2[:, 0:D], units2[:, 2 * wide : 2 * wide + FB])
@@ -572,8 +569,9 @@
             plane[q, zz, 192:240, :] = v[zz * 192 + q * 48 : zz * 192 + (q + 1) * 48]
 
 
-def products_kernel(s, idx, *refs):
-    products(s, idx, *(refs if s == 1 else refs[:-1]))
+def products_kernel(idx, d, w, t0, t1, t2, t3, extra, *outs):
+    for s in range(2):
+        products(s, idx, d.at[s], w, (t0, t1, t2, t3), extra, outs[-1], *outs[:-1])
 
 
 def chunkq_kernel(own, got, *outs):
@@ -587,32 +585,33 @@
         ref[...] = sum(terms[q, z ^ k].astype(F32) for q in range(4)).astype(ref.dtype)
 
 
-def sum2_kernel(mine, *refs):
-    parts, out = refs[:-1], refs[-1]
-    for q in range(4):
-        v = mine[q]
-        for k in range(3):
-            v = v + parts[(q // 2) * 3 + k][q % 2].astype(F32)
-        out[q] = v.astype(out.dtype)
-
-
-def sum_kernel(a0, a1, a2, a3, b, q0, q1, q2, q3, out):
+def sum2_kernel(idx, a0, a1, a2, a3, *outs):
+    here = idx[3] * 2 + idx[4]
+    for k, ref in enumerate(outs):
+        q = here ^ k
+        ref[...] = (a0[q] + sum(a[q].astype(F32) for a in (a1, a2, a3))).astype(ref.dtype)
+
+
+def sum_kernel(a0, a1, a2, a3, b0, b1, b2, b3, out):
     A, B = a0.shape
-    C, E = b.shape[1], q0.shape[0]
+    C = b0.shape[0]
     out[0:A, :] = (a0[...] + sum(a[...].astype(F32) for a in (a1, a2, a3))).astype(BF)
-    v = sum(b[k].astype(F32) for k in range(4)).astype(BF)
+    v = (b0[...] + sum(b[...].astype(F32) for b in (b1, b2, b3))).astype(BF)
     out[A : A + C, :] = v[:, :B]
     out[A + C : A + 2 * C, :] = v[:, B:]
+
+
+def sumq_kernel(q0, q1, q2, q3, out):
+    E, W = q0.shape
+    B = out.shape[1]
     v = (q0[...] + sum(q[...].astype(F32) for q in (q1, q2, q3))).astype(BF)
-    at = A + 2 * C
-    out[at : at + E, :] = v[:, :B]
-    out[at + E : at + 2 * E, :] = jnp.zeros((E, B), BF)
-    out[at + E : at + 2 * E, 0 : 576 - B] = v[:, B:]
-
-
-def out_kernel(idx, s1, r2, c1, c2, g_wq, g_wk, g_wv, g_wi, g_wa, g_wo, g_bq, g_bv, g_bi, *six):
+    out[0:E, :] = v[:, :B]
+    out[E : 2 * E, :] = jnp.zeros((E, B), BF)
+    out[E : 2 * E, 0 : W - B] = v[:, B:]
+
+
+def out_ffn_kernel(idx, s1, r2, c1, c2, g_wi, g_wa, g_wo):
     FB = s1.shape[2]
-    c, z = idx[0], idx[1]
     refs = (s1, r2, c1, c2)
     for n, ref in enumerate(refs):
         for k in range(2):
@@ -623,6 +622,12 @@
             rows = pl.ds(pl.multiple_of((p % 2) * FB + (p // 2) * 96, 16), 96)
             g_wo[rows, 0:FB] = ref[k, 240:336, :].astype(F32)
             g_wo[rows, FB : 2 * FB] = ref[k, 336:432, :].astype(F32)
+
+
+def out_qkv_kernel(idx, s1, r2, c1, c2, g_wq, g_wk, g_wv, g_bq, g_bv, g_bi, *six):
+    FB = s1.shape[2]
+    c, z = idx[0], idx[1]
+    refs = (s1, r2, c1, c2)
     lower = lax.broadcasted_iota(jnp.int32, (96, 128), 1) < 64
     left, right = jnp.zeros((8, FB), F32), jnp.zeros((8, FB), F32)
     top = lax.broadcasted_iota(jnp.int32, (8, FB), 0) == 0
@@ -632,7 +637,7 @@
         own, other = refs[n].at[k], refs[m].at[j]
 
         def tile(i, swap):
-            at = slice(432, 528) if i < 3 else slice(536, 632)
+            at = slice(0, 96) if i < 3 else slice(104, 200)
             cols = slice((i % 3) * 128, (i % 3 + 1) * 128)
             u, v = own[at, cols].astype(F32), other[at, cols].astype(F32)
             return jnp.where((c == 0) != swap, u, v)
@@ -651,8 +656,8 @@
             ref[rows, pl.ds(pl.multiple_of(base + 256, 128), 128)] = jnp.where(lower, turned, tb)
         for ref, cc in ((own, c), (other, 1 - c)):
             here = (yy == 0) & (~top | (xx * 2 + cc == z))
-            left = left + jnp.where(here, ref[528:536, :].astype(F32), 0.0)
-            right = right + jnp.where(here, ref[632:640, :].astype(F32), 0.0)
+            left = left + jnp.where(here, ref[96:104, :].astype(F32), 0.0)
+            right = right + jnp.where(here, ref[200:208, :].astype(F32), 0.0)
     g_bq[...] = jnp.concatenate([left[0:1, 0:128], right[0:1, 0:64]], axis=1).reshape(192)
     g_bv[...] = jnp.concatenate([left[0:1, 256:384], right[0:1, 64:128]], axis=1).reshape(192)
     for i, ref in enumerate(six):
@@ -708,9 +713,6 @@
     mix_b = functools.partial(send, lambda s, g, x, c, z: (1 - s, g, x, c, z) if c == 0 else (s, g, 1 - x, c, z))
 
     to_d = functools.partial(send, lambda s, g, x, c, z: (1 - s, g, 1 - x, c, z))
-
-    def over_plane(sent):
-        return [f(v) for f, v in zip((to_x, to_y, to_d), sent)]
 
     def over_z(sent):
         return [f(v) for f, v in zip(to_z, sent if isinstance(sent, list) else [sent] * 3)]
@@ -826,48 +828,32 @@
         def shares(n, m):
             return jax.ShapeDtypeStruct((*n, m), F32), *(jax.ShapeDtypeStruct((*n, m), BF),) * 3
 
-        mat = jax.ShapeDtypeStruct((T, D), F32)
-        toks = (tokens, tok_x, tok_c, tok_xc)
-
-        def products_specs(s):
-            first = (jax.ShapeDtypeStruct((D + 8, 576), F32),) if s == 0 else (jax.ShapeDtypeStruct((4, 104, 576), BF),) * 2
-            return (
-                (*first, mat, mat, jax.ShapeDtypeStruct((2, T, D), BF)),
-                [VM, block((T, D), s, 0)] + [block((1, T, D), s, 0, 0)] * 4 + [VM] * (2 * s),
-                (VM,) * (4 + s),
-            )
-
-        def attn_bwd(s, d_o, prev):
-            args = (lengths, idx, q_aug, k_aug, v_aug, o, d_o)
-            outs, ins, out_specs = products_specs(s)
-            d_shape = jax.ShapeDtypeStruct((pg, 4, T, 576), BF)
-            more = (w_qkv, d_first, *toks, *prev)
-            if pg > 1:
-                outs, ins, out_specs, more = d_shape, [], VM, ()
+        def attn_back(d_o):
+            part = jax.ShapeDtypeStruct((4, 104, 576), BF)
+            outs = (part, part, jax.ShapeDtypeStruct((4, R, D), BF))
+            more = (w_qkv, tokens, tok_x, tok_c, tok_xc, extra)
+            total = pltpu.VMEM((D + 8, 576), F32)
             res = call(
-                functools.partial(attn_bwd_kernel, pg, 512, s), outs,
-                [SM, SM, block((1, 3, 4 * T, 128), s, 0, 0, 0)] + [block((1, 3, L, 128), s, 0, 0, 0)] * 2 + [VM] * 2 + ins,
-                out_specs,
+                functools.partial(attn_bwd_kernel, pg, 512),
+                outs if pg == 1 else (jax.ShapeDtypeStruct((S, pg, 4, T, 576), BF),),
+                [SM, SM] + [VM] * 5 + [VM if pg == 1 else ANY] * 6,
+                (VM,) * (3 if pg == 1 else 1),
                 [
                     pltpu.VMEM((3, 4 * T, 128), F32), pltpu.VMEM((3, L, 128), F32), pltpu.VMEM((3, L, 128), F32),
-                    pltpu.VMEM((3, T, 128), BF), pltpu.VMEM((1, 4, T, 576), BF), pltpu.VMEM((D + 8, 576), F32),
+                    pltpu.VMEM((3, T, 128), BF), pltpu.VMEM((1, 4, T, 576), BF), total,
                 ],
-                name="attn_bwd", grid=(1,),
-            )(*args, *more)
+                name="attn_bwd",
+            )(lengths, idx, q_aug, k_aug, v_aug, o, d_o, *more)
             if pg > 1:
-                d = lax.psum_scatter(res, "pg", scatter_dimension=0, tiled=True)
-                outs, ins, out_specs = products_specs(s)
-                res = call(
-                    functools.partial(products_kernel, s), outs, [SM, VM] + ins, out_specs, [pltpu.VMEM((D + 8, 576), F32)],
-                    name="products", grid=(1,),
-                )(idx, d, w_qkv, d_first, *toks, *prev)
+                d = lax.psum_scatter(res[0], "pg", scatter_dimension=1, tiled=True)
+                res = call(products_kernel, outs, [SM] + [VM] * 7, (VM,) * 3, [total], name="products")(idx, d, *more)
             return res
 
-        half = jax.ShapeDtypeStruct((2, 96, D), BF)
+        part = jax.ShapeDtypeStruct((4, 96, D), BF)
         q1, c2, *sent2 = call(
             weight_kernel,
-            (jax.ShapeDtypeStruct((4, 4, 240, FB), BF), jax.ShapeDtypeStruct((4, 96, D), F32)) + (half,) * 6,
-            [SM] + [ANY] * 3, (VM,) * 8,
+            (jax.ShapeDtypeStruct((4, 4, 240, FB), BF), jax.ShapeDtypeStruct((4, 96, D), F32)) + (part,) * 3,
+            [SM] + [ANY] * 3, (VM,) * 5,
             [
                 pltpu.VMEM((R, 9 * FB), BF), pltpu.VMEM((R, 3 * D), BF), pltpu.VMEM((R, 9 * FB), BF), pltpu.VMEM((R, 3 * D), BF),
                 pltpu.SemaphoreType.DMA((12,)),
@@ -876,42 +862,41 @@
         )(idx, kept, to_core(sent), sent)
         n, m = q1.shape[2:]
         d_o, sent2, q1 = tie(d_o, sent2, q1)
-        got_a, q1 = over_z(sent2[:3]), lax.all_to_all(q1, ("seq", "x"), 0, 0, tiled=True)
-        gq, own0, x0, core0 = attn_bwd(0, d_o, ())
-        gq, d_o, core0, got_a, sent2 = tie(gq, d_o, core0, got_a, sent2[3:])
-        got_b, core0 = over_z(sent2), to_core(core0)
-        gq_own, gq_other, own1, x1, core1 = attn_bwd(1, d_o, (gq, extra))
-        gq_own, core0, core1, got_b = tie(gq_own, core0, core1, got_b)
-        gq_y, core1 = to_y(gq_other), to_core(core1)
-        x0 = add(x0, core0[1]).astype(BF)
+        got_z2, q1 = over_z(sent2), lax.all_to_all(q1, ("seq", "x"), 0, 0, tiled=True)
+        gq_own, gq_other, gi = attn_back(d_o)
+        gq_y = to_y(gq_other)
         c1, *sent1 = call(chunk_kernel, shares((n,), m), [SM, VM], (VM,) * 4, name="chunks1")(idx, q1)
-        sent1, x0 = tie(sent1, x0)
+        sent1, got_z2 = tie(sent1, got_z2)
         got_z1 = over_z(sent1)
-        q2 = call(sum2_kernel, jax.ShapeDtypeStruct((4, 96, D), BF), [VM] * 7, VM, name="sums2")(c2, *got_a, *got_b)
-        q2 = lax.all_to_all(q2, ("seq", "x"), 0, 0, tiled=True)
-        x0 = to_x(x0)
+        gi = lax.all_to_all(gi, ("x", "core"), 0, 0, tiled=True)
         cq, *sentq = call(chunkq_kernel, shares((104,), 576), [VM] * 2, (VM,) * 4, name="chunksq")(gq_own, gq_y)
-        x1 = add(x1, core1[1]).astype(BF)
-        sentq, got_z1, x0, x1 = tie(sentq, got_z1, x0, x1)
-        got_zq, x1 = over_z(sentq), to_x(x1)
-        q2, got_z1, got_zq, x1 = tie(q2, got_z1, got_zq, x1)
-        total = call(sum_kernel, jax.ShapeDtypeStruct((640, FB), BF), [VM] * 9, VM, name="sums")(
-            c1, *got_z1, q2, cq, *got_zq
-        )
+        p2, *sent2 = call(sum2_kernel, shares((96,), D), [SM] + [VM] * 4, (VM,) * 4, name="sums2")(idx, c2, *got_z2)
+        sent2, got_z1, sentq = tie(sent2, got_z1, sentq)
+        got_zq = over_z(sentq)
+        got_p2 = [f(v) for f, v in zip((to_x, to_y, to_d), sent2)]
+
+        total = call(sum_kernel, jax.ShapeDtypeStruct((432, FB), BF), [VM] * 8, VM, name="sums")(c1, *got_z1, p2, *got_p2)
+        total, got_zq = tie(total, got_zq)
+        total_q = call(sumq_kernel, jax.ShapeDtypeStruct((208, FB), BF), [VM] * 4, VM, name="sumsq")(cq, *got_zq)
         if pg > 1:
-            total = lax.psum(total.astype(F32), "pg").astype(BF)
-        s1 = mix_a(total)
-        total, s1, x0, x1 = tie(total, s1, x0, x1)
-        s1 = jnp.stack([total, s1])
+            total, total_q = (lax.psum(v.astype(F32), "pg").astype(BF) for v in (total, total_q))
+
+        mate, mate_q = mix_a(total), mix_a(total_q)
+        s1 = jnp.stack([total, mate])
         r2, s1_core = mix_b(s1), to_core(s1)
-        grad_input = jnp.stack([add(own0, core0[0], x0), add(own1, core1[0], x1)]).astype(BF)
-        r2, s1_core, grad_input = tie(r2, s1_core, grad_input)
+        r2, s1_core, mate_q = tie(r2, s1_core, mate_q)
+        s1_q = jnp.stack([total_q, mate_q])
+        r2_q = mix_b(s1_q)
+        grad_input = add(d_first, *(gi[k] for k in range(4))).astype(BF).reshape(tokens.shape)
         mat, wide = jax.ShapeDtypeStruct((192, D), F32), jax.ShapeDtypeStruct((192, 8 * FB), F32)
         vec, long_vec = jax.ShapeDtypeStruct((192,), F32), jax.ShapeDtypeStruct((2 * FB,), F32)
-        g_wq, g_wk, g_wv, g_wi, g_wa, g_wo, g_bq, g_bv, g_bi, *six = call(
-            out_kernel, (mat, mat, mat, wide, mat, jax.ShapeDtypeStruct((D, D), F32), vec, vec, long_vec) + (vec,) * 6,
-            [SM] + [VM] * 4, (VM,) * 15, name="outputs",
+        g_wi, g_wa, g_wo = call(
+            out_ffn_kernel, (wide, mat, jax.ShapeDtypeStruct((D, D), F32)), [SM] + [VM] * 4, (VM,) * 3, name="out_ffn"
         )(idx, s1, r2, s1_core, to_core(r2))
+        g_wi, g_wa, g_wo, r2_q, grad_input = tie(g_wi, g_wa, g_wo, r2_q, grad_input)
+        g_wq, g_wk, g_wv, g_bq, g_bv, g_bi, *six = call(
+            out_qkv_kernel, (mat, mat, mat, vec, vec, long_vec) + (vec,) * 6, [SM] + [VM] * 4, (VM,) * 12, name="out_qkv"
+        )(idx, s1_q, r2_q, to_core(s1_q), to_core(r2_q))
         return (
             layer_out.reshape(tokens.shape), grad_input,
             g_wq, g_bq, g_wk, g_wv, g_bv, g_wa, six[0], six[1], six[2], g_wi, g_bi, g_wo, six[3], six[4], six[5],

time: 311 us -> 290 us (0.932)
  waiting for transfers between devices: 96.7 us -> 79 us
    ppermute x43, waiting for transfers between devices: 84.4 us -> 66.7 us  [send(): return lax.ppermute(a, AX, pairs)]
    unnamed x74 -> x46, local copies, waits for them, and re-layouts: 6.67 us -> 6.53 us
    pallas_call x5 -> x6, Pallas kernels: 46.2 us -> 46.2 us  [the longest x1 32 us: attn_back(): call(functools.partial(attn_bwd_kernel, pg, 512), outs if pg == 1 else (j...]
  transfers between devices with their start and end apart: 47 -> 47, of which waited for: 17 -> 15; matrix products, arithmetic and copies ran while one was open for 2% -> 2% of each run, Pallas kernels for 27% -> 31%
where the time goes in v4:
time: 290 us; the launch traced here: 289 us
  Pallas kernels  122 us (42%)
  waiting for transfers between devices  79 us (27%)
  starting transfers between devices  72.4 us (25%)
  other arithmetic  7.47 us (3%)
  local copies, waits for them, and re-layouts  7.19 us (2%)
    ppermute x43, waiting for transfers between devices, send(): return lax.ppermute(a, AX, pairs)  66.7 us
    ppermute x43, starting transfers between devices, send(): return lax.ppermute(a, AX, pairs)  57.3 us
    pallas_call x1, Pallas kernels, attn_back(): call(functools.partial(attn_bwd_kernel, pg, 512), outs if pg == 1 else (j...  32 us
    pallas_call x1, Pallas kernels, body(): call(ffn_kernel, (jax.ShapeDtypeStruct((R, D), BF), jax.ShapeDtypeStruct(...  29.1 us
    pallas_call x1, Pallas kernels, body(): call(functools.partial(attn_fwd_kernel, 1024), (jax.ShapeDtypeStruct((4,...  19.1 us
    all_to_all x1, waiting for transfers between devices, body(): attn = lax.all_to_all(o, ('x', 'core'), 0, 0, tiled=True)  12.3 us
    pallas_call x1, Pallas kernels, body(): call(weight_kernel, (jax.ShapeDtypeStruct((4, 4, 240, FB), BF), jax.Shape...  11 us
    pallas_call x1, Pallas kernels, body(): call(functools.partial(qkv_kernel, pg), (own_head, head, head, jax.ShapeD...  8.44 us
  transfers between devices with their start and end apart: 47, of which 15 were waited for; matrix products, arithmetic and copies ran while one was open for 2% of the time, Pallas kernels for 31%

profile of v4, /device:TPU:0, one launch (start us, length us, event | category | flops | bytes accessed | tf_op | source)
XLA Modules:
  0.0 289.1 jit_solution(8287244412502781276)
XLA Ops:
  1.2 2.6 collective-permute-start.3
  4.4 3.0 %prep.1 = (bf16[200,576]{1,0:T(8,128)(2,1)}, bf16[104,576]{1,0:T(8,128)(2,1)}, bf16[256,384]{1,0:T(8,128)(2,1)}, bf16[96,768]{1,0:T(8,128)(2,1)}) custom-call(s32[14]{0:T(128)} %stack.128.idx, bf16[192,768]{1,0:T(8,128)(2,1)} %wq.1, bf16[192,768]{1,0:T(8,128)(2,1)} %wk.1, bf16[192,768]{1,0:T(8,128)(2,1)} %wv.1, bf16[192,768]{1,0:T(8,128)(2,1)} %w_at.3, ...), custom_call_target="tpu_custom_call" | custom-call | flops 1 | bytes 1 | tf_op jit(solution)/shard_map/prep/pallas_call | solution.py:739
  7.4 3.6 %collective-permute-start.2 = (bf16[104,576]{1,0:T(8,128)(2,1)}, bf16[104,576]{1,0:T(8,128)(2,1)S(1)}, u32[]{:S(2)}, u32[]{:S(2)}) collective-permute-start(bf16[104,576]{1,0:T(8,128)(2,1)} %get-tuple-element.127), channel_id=1, source_target_pairs={{0,3},{1,2},{2,1},{3,0},{4,7},{5,6},{6,5},{7,4},{8,11},{9,10},{10,... | collective-permute-start | bytes 359432 | tf_op jit(solution)/shard_map/ppermute | solution.py:706
  11.8 4.1 %collective-permute-done.2.refs_7_ = bf16[104,576]{1,0:T(8,128)(2,1)S(1)} collective-permute-done((bf16[104,576]{1,0:T(8,128)(2,1)}, bf16[104,576]{1,0:T(8,128)(2,1)S(1)}, u32[]{:S(2)}, u32[]{:S(2)}) %collective-permute-start.2) | collective-permute-done | bytes 119840 | tf_op jit(solution)/shard_map/ppermute | solution.py:706
  15.9 7.0 %collective-permute-done.1.refs_6_ = bf16[104,576]{1,0:T(8,128)(2,1)S(1)} collective-permute-done((bf16[104,576]{1,0:T(8,128)(2,1)}, bf16[104,576]{1,0:T(8,128)(2,1)S(1)}, u32[]{:S(2)}, u32[]{:S(2)}) %collective-permute-start.1) | collective-permute-done | bytes 119840 | tf_op jit(solution)/shard_map/ppermute | solution.py:706
  23.1 1.6 collective-permute-start.5
  24.7 2.9 %collective-permute-start.9 = (bf16[256,384]{1,0:T(8,128)(2,1)}, bf16[256,384]{1,0:T(8,128)(2,1)S(1)}, u32[]{:S(2)}, u32[]{:S(2)}) collective-permute-start(bf16[256,384]{1,0:T(8,128)(2,1)} %get-tuple-element.134.sm_own), channel_id=1, source_target_pairs={{0,3},{1,2},{2,1},{3,0},{4,7},{5,6},{6,5},{7,4},{8,11},{9,10},{10,... | collective-permute-start | bytes 589832 | tf_op jit(solution)/shard_map/ppermute | solution.py:706
  27.6 1.5 collective-permute-start.7
  29.1 5.5 %collective-permute-done.9 = bf16[256,384]{1,0:T(8,128)(2,1)S(1)} collective-permute-done((bf16[256,384]{1,0:T(8,128)(2,1)}, bf16[256,384]{1,0:T(8,128)(2,1)S(1)}, u32[]{:S(2)}, u32[]{:S(2)}) %collective-permute-start.9) | collective-permute-done | bytes 196640 | tf_op jit(solution)/shard_map/ppermute | solution.py:706
  34.6 10.3 %collective-permute-done.8 = bf16[256,384]{1,0:T(8,128)(2,1)S(1)} collective-permute-done((bf16[256,384]{1,0:T(8,128)(2,1)}, bf16[256,384]{1,0:T(8,128)(2,1)S(1)}, u32[]{:S(2)}, u32[]{:S(2)}) %collective-permute-start.8) | collective-permute-done | bytes 196640 | tf_op jit(solution)/shard_map/ppermute | solution.py:706
  45.7 1.6 collective-permute-start.10
  47.3 2.5 collective-permute-start.13
  49.8 1.9 collective-permute-start.11
  51.7 8.4 %qkv.1 = (bf16[2,3,1024,128]{3,2,1,0:T(8,128)(2,1)}, bf16[2,3,1024,128]{3,2,1,0:T(8,128)(2,1)}, bf16[2,3,1024,128]{3,2,1,0:T(8,128)(2,1)}, bf16[4,192,576]{2,1,0:T(8,128)(2,1)}) custom-call(s32[2,4]{1,0:T(2,128)} %lengths.7, s32[14]{0:T(128)} %stack.128.idx, bf16[1,2,256,768]{3,2,1,0:T(8,128)(2,1)} %bitcast.59, bf16[1,2,256,768]{3,2,1,0:T(8,128)(2,1)} %bitcast.62, ...), custom_call_target="tpu_custom_call" | custom-call | flops 1 | bytes 1 | tf_op jit(solution)/shard_map/qkv/pallas_call | solution.py:763
  60.2 1.0 collective-permute-done.12
  61.4 1.5 pad_maximum_fusion.4
  62.9 0.8 collective-permute-start.14
  63.7 1.3 collective-permute-start.15
  65.0 19.1 %attn_fwd.1 = (bf16[4,256,384]{2,1,0:T(8,128)(2,1)}, bf16[2,3,1024,128]{3,2,1,0:T(8,128)(2,1)}) custom-call(s32[2,4]{1,0:T(2,128)} %lengths.7, s32[14]{0:T(128)} %stack.128.idx, bf16[2,3,1024,128]{3,2,1,0:T(8,128)(2,1)} %get-tuple-element.151.q_ref, bf16[2,3,1024,128]{3,2,1,0:T(8,128)(2,1)} %get-tuple-element.152.k_ref.refs_1_, ...), custom_call_target="tpu_custom_call" | custom-call | flops 1 | bytes 1 | tf_op jit(solution)/shard_map/attn_fwd/pallas_call | solution.py:776
  84.1 1.0 copy-done.9
  85.3 0.9 collective-permute-start.16
  86.1 3.7 %all-to-all-start = ((bf16[4,256,384]{2,1,0:T(8,128)(2,1)}), bf16[4,256,384]{2,1,0:T(8,128)(2,1)S(1)}, u32[]{:S(2)}, u32[]{:S(2)}) async-start(bf16[4,256,384]{2,1,0:T(8,128)(2,1)} %get-tuple-element.157.refs_3_), calls=%async_computation | async-start | bytes 1572864 | tf_op jit(solution)/shard_map/all_to_all | solution.py:785
  90.6 12.3 %all-to-all-done.attn = bf16[4,256,384]{2,1,0:T(8,128)(2,1)S(1)} async-done(((bf16[4,256,384]{2,1,0:T(8,128)(2,1)}), bf16[4,256,384]{2,1,0:T(8,128)(2,1)S(1)}, u32[]{:S(2)}, u32[]{:S(2)}) %all-to-all-start) | async-done | bytes 786464 | tf_op jit(solution)/shard_map/all_to_all | solution.py:785
  102.9 1.9 collective-permute-start.20
  104.8 2.4 collective-permute-done.20.c2b
  107.2 29.1 %ffn.1 = (bf16[512,768]{1,0:T(8,128)(2,1)}, f32[512,768]{1,0:T(8,128)}, bf16[4,256,384]{2,1,0:T(8,128)(2,1)}, bf16[512,5760]{1,0:T(8,128)(2,1)}, bf16[512,3456]{1,0:T(8,128)(2,1)}, /*index=5*/f32[4,8,576]{2,1,0:T(8,128)}) custom-call(s32[14]{0:T(128)} %stack.128.idx, s32[2,4]{1,0:T(2,128)} %lengths.7, bf16[4,256,384]{2,1,0:T(8,128)(2,1)} %copy-done.4, ...), custom_call_target="tpu_custom_call" | custom-call | flops 1 | bytes 1 | tf_op jit(solution)/shard_map/ffn/pallas_call | solution.py:792
  136.8 3.5 %all-to-all-start.1 = ((bf16[4,256,384]{2,1,0:T(8,128)(2,1)}), bf16[4,256,384]{2,1,0:T(8,128)(2,1)S(1)}, u32[]{:S(2)}, u32[]{:S(2)}) async-start(bf16[4,256,384]{2,1,0:T(8,128)(2,1)} %get-tuple-element.163), calls=%async_computation.1 | async-start | bytes 1572864 | tf_op jit(solution)/shard_map/all_to_all | solution.py:823
  140.3 6.1 %collective-permute-done.21.mate = bf16[512,5760]{1,0:T(8,128)(2,1)} collective-permute-done((bf16[512,5760]{1,0:T(8,128)(2,1)}, bf16[512,5760]{1,0:T(8,128)(2,1)}, u32[]{:S(2)}, u32[]{:S(2)}) %collective-permute-start.21) | collective-permute-done | bytes 5898272 | tf_op jit(solution)/shard_map/ppermute | solution.py:706
  146.3 11.0 %weights.1 = (bf16[4,4,240,384]{3,2,1,0:T(8,128)(2,1)}, f32[4,96,768]{2,1,0:T(8,128)}, bf16[4,96,768]{2,1,0:T(8,128)(2,1)}, bf16[4,96,768]{2,1,0:T(8,128)(2,1)}, bf16[4,96,768]{2,1,0:T(8,128)(2,1)}) custom-call(s32[14]{0:T(128)} %stack.128.idx, bf16[512,3456]{1,0:T(8,128)(2,1)} %get-tuple-element.164.kept, bf16[512,5760]{1,0:T(8,128)(2,1)} %collective-permute-done.21.mate, ...), custom_call_target="tpu_custom_call" | custom-call | flops 1 | bytes 1 | tf_op jit(solution)/shard_map/weights/pallas_call | solution.py:853
  157.4 0.9 copy-done.3
  158.2 3.9 %all-to-all-start.2 = ((bf16[4,4,240,384]{3,2,1,0:T(8,128)(2,1)}), bf16[4,4,240,384]{3,2,1,0:T(8,128)(2,1)S(1)}, u32[]{:S(2)}, u32[]{:S(2)}) async-start(bf16[4,4,240,384]{3,2,1,0:T(8,128)(2,1)} %get-tuple-element.170), calls=%async_computation.2 | async-start | bytes 5898240 | tf_op jit(solution)/shard_map/all_to_all | solution.py:865
  162.2 2.8 collective-permute-start.23
  165.1 1.6 collective-permute-start.24
  166.6 32.0 %attn_bwd.1 = (bf16[4,104,576]{2,1,0:T(8,128)(2,1)}, bf16[4,104,576]{2,1,0:T(8,128)(2,1)}, bf16[4,512,768]{2,1,0:T(8,128)(2,1)}) custom-call(s32[2,4]{1,0:T(2,128)} %lengths.7, s32[14]{0:T(128)} %stack.128.idx, bf16[2,3,1024,128]{3,2,1,0:T(8,128)(2,1)} %get-tuple-element.188.refs_0_, bf16[2,3,1024,128]{3,2,1,0:T(8,128)(2,1)} %get-tuple-element.152.k_ref.refs_1_, ...), custom_call_target="tpu_custom_call" | custom-call | flops 1 | bytes 1 | tf_op jit(solution)/shard_map/attn_bwd/pallas_call | solution.py:836
  198.6 1.6 copy-done
  200.2 4.0 %all-to-all-start.3 = ((bf16[4,512,768]{2,1,0:T(8,128)(2,1)}), bf16[4,512,768]{2,1,0:T(8,128)(2,1)S(1)}, u32[]{:S(2)}, u32[]{:S(2)}) async-start(bf16[4,512,768]{2,1,0:T(8,128)(2,1)} %get-tuple-element.219), calls=%async_computation.3 | async-start | bytes 6291456 | tf_op jit(solution)/shard_map/all_to_all | solution.py:871
  204.3 2.9 %chunks1.1 = (f32[240,384]{1,0:T(8,128)}, bf16[240,384]{1,0:T(8,128)(2,1)}, bf16[240,384]{1,0:T(8,128)(2,1)}, bf16[240,384]{1,0:T(8,128)(2,1)}) custom-call(s32[14]{0:T(128)} %stack.128.idx, bf16[4,4,240,384]{3,2,1,0:T(8,128)(2,1)} %copy-done), custom_call_target="tpu_custom_call" | custom-call | flops 1 | bytes 1 | tf_op jit(solution)/shard_map/chunks1/pallas_call | solution.py:868
  207.2 10.5 %collective-permute-start.25 = (bf16[240,384]{1,0:T(8,128)(2,1)}, bf16[240,384]{1,0:T(8,128)(2,1)S(1)}, u32[]{:S(2)}, u32[]{:S(2)}) collective-permute-start(bf16[240,384]{1,0:T(8,128)(2,1)} %get-tuple-element.185), channel_id=1, source_target_pairs={{0,1},{1,0},{2,3},{3,2},{4,5},{5,4},{6,7},{7,6},{8,9},{9,8},{10,11... | collective-permute-start | bytes 552968 | tf_op jit(solution)/shard_map/ppermute | solution.py:706
  217.6 0.8 collective-permute-start.26
  218.4 1.6 collective-permute-start.27
  220.0 0.8 copy-done.13
  220.8 2.1 chunksq.1
  222.9 2.8 sums2.1
  225.7 8.6 %collective-permute-done.26.a2 = bf16[240,384]{1,0:T(8,128)(2,1)S(1)} collective-permute-done((bf16[240,384]{1,0:T(8,128)(2,1)}, bf16[240,384]{1,0:T(8,128)(2,1)S(1)}, u32[]{:S(2)}, u32[]{:S(2)}) %collective-permute-start.26) | collective-permute-done | bytes 184352 | tf_op jit(solution)/shard_map/ppermute | solution.py:706
  234.2 1.2 collective-permute-start.29
  235.5 1.5 collective-permute-start.30
  236.9 0.8 collective-permute-start.31
  237.7 2.9 %collective-permute-start.32 = (bf16[104,576]{1,0:T(8,128)(2,1)}, bf16[104,576]{1,0:T(8,128)(2,1)}, u32[]{:S(2)}, u32[]{:S(2)}) collective-permute-start(bf16[104,576]{1,0:T(8,128)(2,1)} %get-tuple-element.204), channel_id=1, source_target_pairs={{0,1},{1,0},{2,3},{3,2},{4,5},{5,4},{6,7},{7,6},{8,9},{9,8},{10,11... | collective-permute-start | bytes 359432 | tf_op jit(solution)/shard_map/ppermute | solution.py:706
  241.4 3.0 %collective-permute-done.29.b1 = bf16[96,768]{1,0:T(8,128)(2,1)S(1)} collective-permute-done((bf16[96,768]{1,0:T(8,128)(2,1)}, bf16[96,768]{1,0:T(8,128)(2,1)S(1)}, u32[]{:S(2)}, u32[]{:S(2)}) %collective-permute-start.29) | collective-permute-done | bytes 147488 | tf_op jit(solution)/shard_map/ppermute | solution.py:706
  244.5 2.3 collective-permute-start.34
  247.5 2.3 sums.1
  249.8 2.0 collective-permute-done.33.q2
  252.6 6.6 %collective-permute-done.35 = bf16[432,384]{1,0:T(8,128)(2,1)S(1)} collective-permute-done((bf16[432,384]{1,0:T(8,128)(2,1)}, bf16[432,384]{1,0:T(8,128)(2,1)S(1)}, u32[]{:S(2)}, u32[]{:S(2)}) %collective-permute-start.35) | collective-permute-done | bytes 331808 | tf_op jit(solution)/shard_map/ppermute | solution.py:706
  259.1 1.9 pad_maximum_fusion.2.s1
  261.0 1.4 collective-permute-start.36
  262.5 1.8 sumsq.1
  265.1 6.5 %collective-permute-done.38 = bf16[208,384]{1,0:T(8,128)(2,1)S(1)} collective-permute-done((bf16[208,384]{1,0:T(8,128)(2,1)}, bf16[208,384]{1,0:T(8,128)(2,1)S(1)}, u32[]{:S(2)}, u32[]{:S(2)}) %collective-permute-start.38) | collective-permute-done | bytes 159776 | tf_op jit(solution)/shard_map/ppermute | solution.py:706
  271.6 2.2 collective-permute-done.36.r2
  273.7 1.0 pad_maximum_fusion.6.s1
  274.7 1.5 collective-permute-start.40
  276.2 2.7 fusion
  278.9 4.4 %out_ffn.1 = (f32[192,3072]{1,0:T(8,128)}, f32[192,768]{1,0:T(8,128)}, f32[768,768]{1,0:T(8,128)}) custom-call(s32[14]{0:T(128)} %stack.128.idx, bf16[2,432,384]{2,1,0:T(8,128)(2,1)} %pad_maximum_fusion.2.s1, bf16[2,432,384]{2,1,0:T(8,128)(2,1)} %collective-permute-done.36.r2, bf16[2,432,384]{2,1,0:T(8,128)(2,1)} %collective-permute-done.37.c1, ...), custom_call_target="tpu_custom_call" | custom-call | flops 1 | bytes 1 | tf_op jit(solution)/shard_map/out_ffn/pallas_call | solution.py:893
  283.8 1.4 collective-permute-done.42.c2
  286.0 2.8 out_qkv.1
  (98 shorter events, 8.9 us)
Async XLA Ops:
  0.7 22.3 %collective-permute-start.4 = (bf16[2,256,768]{2,1,0:T(8,128)(2,1)}, bf16[2,256,768]{2,1,0:T(8,128)(2,1)S(1)}, u32[]{:S(2)}, u32[]{:S(2)}) collective-permute-start(bf16[2,256,768]{2,1,0:T(8,128)(2,1)} %refs_6_.1), channel_id=1, source_target_pairs={{0,4},{1,5},{2,6},{3,7},{4,0},{5,1},{6,2},{7,3},{8,12},{9,13},{10,... | collective-permute-start | bytes 2359304 | tf_op jit(solution)/shard_map/ppermute | solution.py:706
  1.2 21.8 %collective-permute-start.3 = (bf16[2,256,768]{2,1,0:T(8,128)(2,1)}, bf16[2,256,768]{2,1,0:T(8,128)(2,1)S(1)}, u32[]{:S(2)}, u32[]{:S(2)}) collective-permute-start(bf16[2,256,768]{2,1,0:T(8,128)(2,1)} %refs_6_.1), channel_id=1, source_target_pairs={{0,8},{1,9},{2,10},{3,11},{4,12},{5,13},{6,14},{7,15},{8,0},{9,1},... | collective-permute-start | bytes 2359304 | tf_op jit(solution)/shard_map/ppermute | solution.py:706
  7.4 8.5 %collective-permute-start.2 = (bf16[104,576]{1,0:T(8,128)(2,1)}, bf16[104,576]{1,0:T(8,128)(2,1)S(1)}, u32[]{:S(2)}, u32[]{:S(2)}) collective-permute-start(bf16[104,576]{1,0:T(8,128)(2,1)} %get-tuple-element.127), channel_id=1, source_target_pairs={{0,3},{1,2},{2,1},{3,0},{4,7},{5,6},{6,5},{7,4},{8,11},{9,10},{10,... | collective-permute-start | bytes 359432 | tf_op jit(solution)/shard_map/ppermute | solution.py:706
  11.0 11.9 %collective-permute-start.1 = (bf16[104,576]{1,0:T(8,128)(2,1)}, bf16[104,576]{1,0:T(8,128)(2,1)S(1)}, u32[]{:S(2)}, u32[]{:S(2)}) collective-permute-start(bf16[104,576]{1,0:T(8,128)(2,1)} %get-tuple-element.127), channel_id=1, source_target_pairs={{0,2},{1,3},{2,0},{3,1},{4,6},{5,7},{6,4},{7,5},{8,10},{9,11},{10,... | collective-permute-start | bytes 359432 | tf_op jit(solution)/shard_map/ppermute | solution.py:706
  11.0 11.9 %collective-permute-start = (bf16[104,576]{1,0:T(8,128)(2,1)}, bf16[104,576]{1,0:T(8,128)(2,1)S(1)}, u32[]{:S(2)}, u32[]{:S(2)}) collective-permute-start(bf16[104,576]{1,0:T(8,128)(2,1)} %get-tuple-element.127), channel_id=1, source_target_pairs={{0,1},{1,0},{2,3},{3,2},{4,5},{5,4},{6,7},{7,6},{8,9},{9,8},{10,11... | collective-permute-start | bytes 359432 | tf_op jit(solution)/shard_map/ppermute | solution.py:706
  15.9 35.8 %copy-start.10 = (bf16[104,576]{1,0:T(8,128)(2,1)}, bf16[104,576]{1,0:T(8,128)(2,1)S(1)}, u32[]{:S(2)}) copy-start(bf16[104,576]{1,0:T(8,128)(2,1)S(1)} %collective-permute-done.2.refs_7_) | copy-start | bytes 359428
  22.9 28.8 %copy-start.11 = (bf16[104,576]{1,0:T(8,128)(2,1)}, bf16[104,576]{1,0:T(8,128)(2,1)S(1)}, u32[]{:S(2)}) copy-start(bf16[104,576]{1,0:T(8,128)(2,1)S(1)} %collective-permute-done.1.refs_6_) | copy-start | bytes 359428
  22.9 28.8 %copy-start.12 = (bf16[104,576]{1,0:T(8,128)(2,1)}, bf16[104,576]{1,0:T(8,128)(2,1)S(1)}, u32[]{:S(2)}) copy-start(bf16[104,576]{1,0:T(8,128)(2,1)S(1)} %collective-permute-done.refs_5_) | copy-start | bytes 359428
  22.9 28.8 %copy-start.5 = (bf16[2,256,768]{2,1,0:T(8,128)(2,1)}, bf16[2,256,768]{2,1,0:T(8,128)(2,1)S(1)}, u32[]{:S(2)}) copy-start(bf16[2,256,768]{2,1,0:T(8,128)(2,1)S(1)} %collective-permute-done.4.refs_8_) | copy-start | bytes 2359300
  23.0 28.7 %copy-start.6 = (bf16[2,256,768]{2,1,0:T(8,128)(2,1)}, bf16[2,256,768]{2,1,0:T(8,128)(2,1)S(1)}, u32[]{:S(2)}) copy-start(bf16[2,256,768]{2,1,0:T(8,128)(2,1)S(1)} %collective-permute-done.3.refs_7_) | copy-start | bytes 2359300
  23.0 21.9 %collective-permute-start.6 = (bf16[2,256,768]{2,1,0:T(8,128)(2,1)S(1)}, bf16[2,256,768]{2,1,0:T(8,128)(2,1)S(1)}, u32[]{:S(2)}, u32[]{:S(2)}) collective-permute-start(bf16[2,256,768]{2,1,0:T(8,128)(2,1)S(1)} %collective-permute-done.3.refs_7_), channel_id=1, source_target_pairs={{0,4},{1,5},{2,6},{3,7},{4,0},{5,1},{6,2},{7,3},{8,12},{9,13},{10,... | collective-permute-start | bytes 2359304 | tf_op jit(solution)/shard_map/ppermute | solution.py:706
  23.1 21.8 %collective-permute-start.5 = (bf16[3,104,576]{2,1,0:T(8,128)(2,1)S(1)}, bf16[3,104,576]{2,1,0:T(8,128)(2,1)S(1)}, u32[]{:S(2)}, u32[]{:S(2)}) collective-permute-start(bf16[3,104,576]{2,1,0:T(8,128)(2,1)S(1)} %pad_maximum_fusion.5), channel_id=1, source_target_pairs={{0,16},{1,17},{2,18},{3,19},{4,20},{5,21},{6,22},{7,23},{8,24},{9,... | collective-permute-start | bytes 1078280 | tf_op jit(solution)/shard_map/ppermute | solution.py:706
  24.7 9.9 %collective-permute-start.9 = (bf16[256,384]{1,0:T(8,128)(2,1)}, bf16[256,384]{1,0:T(8,128)(2,1)S(1)}, u32[]{:S(2)}, u32[]{:S(2)}) collective-permute-start(bf16[256,384]{1,0:T(8,128)(2,1)} %get-tuple-element.134.sm_own), channel_id=1, source_target_pairs={{0,3},{1,2},{2,1},{3,0},{4,7},{5,6},{6,5},{7,4},{8,11},{9,10},{10,... | collective-permute-start | bytes 589832 | tf_op jit(solution)/shard_map/ppermute | solution.py:706
  27.6 17.3 %collective-permute-start.8 = (bf16[256,384]{1,0:T(8,128)(2,1)}, bf16[256,384]{1,0:T(8,128)(2,1)S(1)}, u32[]{:S(2)}, u32[]{:S(2)}) collective-permute-start(bf16[256,384]{1,0:T(8,128)(2,1)} %get-tuple-element.134.sm_own), channel_id=1, source_target_pairs={{0,2},{1,3},{2,0},{3,1},{4,6},{5,7},{6,4},{7,5},{8,10},{9,11},{10,... | collective-permute-start | bytes 589832 | tf_op jit(solution)/shard_map/ppermute | solution.py:706
  27.6 17.3 %collective-permute-start.7 = (bf16[256,384]{1,0:T(8,128)(2,1)}, bf16[256,384]{1,0:T(8,128)(2,1)S(1)}, u32[]{:S(2)}, u32[]{:S(2)}) collective-permute-start(bf16[256,384]{1,0:T(8,128)(2,1)} %get-tuple-element.134.sm_own), channel_id=1, source_target_pairs={{0,1},{1,0},{2,3},{3,2},{4,5},{5,4},{6,7},{7,6},{8,9},{9,8},{10,11... | collective-permute-start | bytes 589832 | tf_op jit(solution)/shard_map/ppermute | solution.py:706
  44.9 6.8 %copy-start.7 = (bf16[2,256,768]{2,1,0:T(8,128)(2,1)}, bf16[2,256,768]{2,1,0:T(8,128)(2,1)S(1)}, u32[]{:S(2)}) copy-start(bf16[2,256,768]{2,1,0:T(8,128)(2,1)S(1)} %collective-permute-done.6.refs_9_) | copy-start | bytes 2359300
  45.7 15.5 %collective-permute-start.10 = (bf16[3,256,384]{2,1,0:T(8,128)(2,1)S(1)}, bf16[3,256,384]{2,1,0:T(8,128)(2,1)S(1)}, u32[]{:S(2)}, u32[]{:S(2)}) collective-permute-start(bf16[3,256,384]{2,1,0:T(8,128)(2,1)S(1)} %pad_maximum_fusion.3), channel_id=1, source_target_pairs={{0,8},{1,9},{2,10},{3,11},{4,20},{5,21},{6,22},{7,23},{8,0},{9,1},... | collective-permute-start | bytes 1769480 | tf_op jit(solution)/shard_map/ppermute | solution.py:706
  47.3 12.9 %collective-permute-start.13 = (bf16[96,768]{1,0:T(8,128)(2,1)}, bf16[96,768]{1,0:T(8,128)(2,1)S(1)}, u32[]{:S(2)}, u32[]{:S(2)}) collective-permute-start(bf16[96,768]{1,0:T(8,128)(2,1)} %get-tuple-element.145), channel_id=1, source_target_pairs={{0,3},{1,2},{2,1},{3,0},{4,7},{5,6},{6,5},{7,4},{8,11},{9,10},{10,... | collective-permute-start | bytes 442376 | tf_op jit(solution)/shard_map/ppermute | solution.py:706
  49.8 11.4 %collective-permute-start.12 = (bf16[96,768]{1,0:T(8,128)(2,1)}, bf16[96,768]{1,0:T(8,128)(2,1)}, u32[]{:S(2)}, u32[]{:S(2)}) collective-permute-start(bf16[96,768]{1,0:T(8,128)(2,1)} %get-tuple-element.145), channel_id=1, source_target_pairs={{0,2},{1,3},{2,0},{3,1},{4,6},{5,7},{6,4},{7,5},{8,10},{9,11},{10,... | collective-permute-start | bytes 442376 | tf_op jit(solution)/shard_map/ppermute | solution.py:706
  49.8 11.4 %collective-permute-start.11 = (bf16[96,768]{1,0:T(8,128)(2,1)}, bf16[96,768]{1,0:T(8,128)(2,1)}, u32[]{:S(2)}, u32[]{:S(2)}) collective-permute-start(bf16[96,768]{1,0:T(8,128)(2,1)} %get-tuple-element.145), channel_id=1, source_target_pairs={{0,1},{1,0},{2,3},{3,2},{4,5},{5,4},{6,7},{7,6},{8,9},{9,8},{10,11... | collective-permute-start | bytes 442376 | tf_op jit(solution)/shard_map/ppermute | solution.py:706
  60.2 1.2 copy-start.19
  61.4 28.5 %copy-start.1 = (bf16[2,3,256,384]{3,2,1,0:T(8,128)(2,1)}, bf16[2,3,256,384]{3,2,1,0:T(8,128)(2,1)S(1)}, u32[]{:S(2)}) copy-start(bf16[2,3,256,384]{3,2,1,0:T(8,128)(2,1)S(1)} %pad_maximum_fusion.s1a) | copy-start | bytes 3538948
  62.9 21.2 %collective-permute-start.14 = (bf16[2,3,256,384]{3,2,1,0:T(8,128)(2,1)S(1)}, bf16[2,3,256,384]{3,2,1,0:T(8,128)(2,1)S(1)}, u32[]{:S(2)}, u32[]{:S(2)}) collective-permute-start(bf16[2,3,256,384]{3,2,1,0:T(8,128)(2,1)S(1)} %pad_maximum_fusion.s1a), channel_id=1, source_target_pairs={{0,16},{1,17},{2,18},{3,19},{4,12},{5,13},{6,14},{7,15},{8,24},{9,... | collective-permute-start | bytes 3538952 | tf_op jit(solution)/shard_map/ppermute | solution.py:706
  63.7 20.4 %collective-permute-start.15 = (bf16[3,96,768]{2,1,0:T(8,128)(2,1)S(1)}, bf16[3,96,768]{2,1,0:T(8,128)(2,1)S(1)}, u32[]{:S(2)}, u32[]{:S(2)}) collective-permute-start(bf16[3,96,768]{2,1,0:T(8,128)(2,1)S(1)} %pad_maximum_fusion.4), channel_id=1, source_target_pairs={{0,8},{1,9},{2,10},{3,11},{4,20},{5,21},{6,22},{7,23},{8,0},{9,1},... | collective-permute-start | bytes 1327112 | tf_op jit(solution)/shard_map/ppermute | solution.py:706
  84.1 1.1 copy-start.9
  85.2 22.0 %copy-start.2 = (bf16[2,3,96,768]{3,2,1,0:T(8,128)(2,1)}, bf16[2,3,96,768]{3,2,1,0:T(8,128)(2,1)S(1)}, u32[]{:S(2)}) copy-start(bf16[2,3,96,768]{3,2,1,0:T(8,128)(2,1)S(1)} %pad_maximum_fusion.1.s1b) | copy-start | bytes 2654212
  85.3 17.6 %collective-permute-start.16 = (bf16[2,3,96,768]{3,2,1,0:T(8,128)(2,1)S(1)}, bf16[2,3,96,768]{3,2,1,0:T(8,128)(2,1)}, u32[]{:S(2)}, u32[]{:S(2)}) collective-permute-start(bf16[2,3,96,768]{3,2,1,0:T(8,128)(2,1)S(1)} %pad_maximum_fusion.1.s1b), channel_id=1, source_target_pairs={{0,16},{1,17},{2,18},{3,19},{4,12},{5,13},{6,14},{7,15},{8,24},{9,... | collective-permute-start | bytes 2654216 | tf_op jit(solution)/shard_map/ppermute | solution.py:706
  86.1 16.7 %all-to-all-start = ((bf16[4,256,384]{2,1,0:T(8,128)(2,1)}), bf16[4,256,384]{2,1,0:T(8,128)(2,1)S(1)}, u32[]{:S(2)}, u32[]{:S(2)}) async-start(bf16[4,256,384]{2,1,0:T(8,128)(2,1)} %get-tuple-element.157.refs_3_), calls=%async_computation | async-start | bytes 1572864 | tf_op jit(solution)/shard_map/all_to_all | solution.py:785
  89.8 15.0 %collective-permute-start.17 = (bf16[2,3,256,384]{3,2,1,0:T(8,128)(2,1)S(1)}, bf16[2,3,256,384]{3,2,1,0:T(8,128)(2,1)}, u32[]{:S(2)}, u32[]{:S(2)}) collective-permute-start(bf16[2,3,256,384]{3,2,1,0:T(8,128)(2,1)S(1)} %pad_maximum_fusion.s1a), channel_id=1, source_target_pairs={{0,4},{1,5},{2,6},{3,7},{4,0},{5,1},{6,2},{7,3},{8,12},{9,13},{10,... | collective-permute-start | bytes 3538952 | tf_op jit(solution)/shard_map/ppermute | solution.py:706
  90.1 14.7 %collective-permute-start.18 = (bf16[2,3,256,384]{3,2,1,0:T(8,128)(2,1)}, bf16[2,3,256,384]{3,2,1,0:T(8,128)(2,1)}, u32[]{:S(2)}, u32[]{:S(2)}) collective-permute-start(bf16[2,3,256,384]{3,2,1,0:T(8,128)(2,1)} %copy-done.9), channel_id=1, source_target_pairs={{0,4},{1,5},{2,6},{3,7},{4,0},{5,1},{6,2},{7,3},{8,12},{9,13},{10,... | collective-permute-start | bytes 3538952 | tf_op jit(solution)/shard_map/ppermute | solution.py:706
  90.4 14.4 %collective-permute-start.19 = (bf16[2,3,96,768]{3,2,1,0:T(8,128)(2,1)S(1)}, bf16[2,3,96,768]{3,2,1,0:T(8,128)(2,1)}, u32[]{:S(2)}, u32[]{:S(2)}) collective-permute-start(bf16[2,3,96,768]{3,2,1,0:T(8,128)(2,1)S(1)} %pad_maximum_fusion.1.s1b), channel_id=1, source_target_pairs={{0,4},{1,5},{2,6},{3,7},{4,0},{5,1},{6,2},{7,3},{8,12},{9,13},{10,... | collective-permute-start | bytes 2654216 | tf_op jit(solution)/shard_map/ppermute | solution.py:706
  102.9 4.3 %copy-start.4 = (bf16[4,256,384]{2,1,0:T(8,128)(2,1)}, bf16[4,256,384]{2,1,0:T(8,128)(2,1)S(1)}, u32[]{:S(2)}) copy-start(bf16[4,256,384]{2,1,0:T(8,128)(2,1)S(1)} %all-to-all-done.attn) | copy-start | bytes 2359300
  102.9 4.3 %collective-permute-start.20 = (bf16[2,3,96,768]{3,2,1,0:T(8,128)(2,1)}, bf16[2,3,96,768]{3,2,1,0:T(8,128)(2,1)}, u32[]{:S(2)}, u32[]{:S(2)}) collective-permute-start(bf16[2,3,96,768]{3,2,1,0:T(8,128)(2,1)} %collective-permute-done.16.r2b), channel_id=1, source_target_pairs={{0,4},{1,5},{2,6},{3,7},{4,0},{5,1},{6,2},{7,3},{8,12},{9,13},{10,... | collective-permute-start | bytes 2654216 | tf_op jit(solution)/shard_map/ppermute | solution.py:706
  136.3 10.0 %collective-permute-start.21 = (bf16[512,5760]{1,0:T(8,128)(2,1)}, bf16[512,5760]{1,0:T(8,128)(2,1)}, u32[]{:S(2)}, u32[]{:S(2)}) collective-permute-start(bf16[512,5760]{1,0:T(8,128)(2,1)} %get-tuple-element.165.sent), channel_id=1, source_target_pairs={{0,4},{1,5},{2,6},{3,7},{4,0},{5,1},{6,2},{7,3},{8,12},{9,13},{10,... | collective-permute-start | bytes 17694728 | tf_op jit(solution)/shard_map/ppermute | solution.py:706
  136.8 20.6 %all-to-all-start.1 = ((bf16[4,256,384]{2,1,0:T(8,128)(2,1)}), bf16[4,256,384]{2,1,0:T(8,128)(2,1)S(1)}, u32[]{:S(2)}, u32[]{:S(2)}) async-start(bf16[4,256,384]{2,1,0:T(8,128)(2,1)} %get-tuple-element.163), calls=%async_computation.1 | async-start | bytes 1572864 | tf_op jit(solution)/shard_map/all_to_all | solution.py:823
  158.2 40.4 %all-to-all-start.2 = ((bf16[4,4,240,384]{3,2,1,0:T(8,128)(2,1)}), bf16[4,4,240,384]{3,2,1,0:T(8,128)(2,1)S(1)}, u32[]{:S(2)}, u32[]{:S(2)}) async-start(bf16[4,4,240,384]{3,2,1,0:T(8,128)(2,1)} %get-tuple-element.170), calls=%async_computation.2 | async-start | bytes 5898240 | tf_op jit(solution)/shard_map/all_to_all | solution.py:865
  162.1 45.0 %collective-permute-start.22 = (bf16[4,96,768]{2,1,0:T(8,128)(2,1)}, bf16[4,96,768]{2,1,0:T(8,128)(2,1)}, u32[]{:S(2)}, u32[]{:S(2)}) collective-permute-start(bf16[4,96,768]{2,1,0:T(8,128)(2,1)} %get-tuple-element.176), channel_id=1, source_target_pairs={{0,1},{1,0},{2,3},{3,2},{4,5},{5,4},{6,7},{7,6},{8,9},{9,8},{10,11... | collective-permute-start | bytes 1769480 | tf_op jit(solution)/shard_map/ppermute | solution.py:706
  162.2 44.9 %collective-permute-start.23 = (bf16[4,96,768]{2,1,0:T(8,128)(2,1)}, bf16[4,96,768]{2,1,0:T(8,128)(2,1)}, u32[]{:S(2)}, u32[]{:S(2)}) collective-permute-start(bf16[4,96,768]{2,1,0:T(8,128)(2,1)} %get-tuple-element.177), channel_id=1, source_target_pairs={{0,2},{1,3},{2,0},{3,1},{4,6},{5,7},{6,4},{7,5},{8,10},{9,11},{10,... | collective-permute-start | bytes 1769480 | tf_op jit(solution)/shard_map/ppermute | solution.py:706
  165.1 42.1 %collective-permute-start.24 = (bf16[4,96,768]{2,1,0:T(8,128)(2,1)}, bf16[4,96,768]{2,1,0:T(8,128)(2,1)}, u32[]{:S(2)}, u32[]{:S(2)}) collective-permute-start(bf16[4,96,768]{2,1,0:T(8,128)(2,1)} %get-tuple-element.178), channel_id=1, source_target_pairs={{0,3},{1,2},{2,1},{3,0},{4,7},{5,6},{6,5},{7,4},{8,11},{9,10},{10,... | collective-permute-start | bytes 1769480 | tf_op jit(solution)/shard_map/ppermute | solution.py:706
  198.6 1.6 copy-start
  200.2 76.0 %all-to-all-start.3 = ((bf16[4,512,768]{2,1,0:T(8,128)(2,1)}), bf16[4,512,768]{2,1,0:T(8,128)(2,1)S(1)}, u32[]{:S(2)}, u32[]{:S(2)}) async-start(bf16[4,512,768]{2,1,0:T(8,128)(2,1)} %get-tuple-element.219), calls=%async_computation.3 | async-start | bytes 6291456 | tf_op jit(solution)/shard_map/all_to_all | solution.py:871
  204.2 15.8 %collective-permute-start.28 = (bf16[4,104,576]{2,1,0:T(8,128)(2,1)}, bf16[4,104,576]{2,1,0:T(8,128)(2,1)S(1)}, u32[]{:S(2)}, u32[]{:S(2)}) collective-permute-start(bf16[4,104,576]{2,1,0:T(8,128)(2,1)} %get-tuple-element.193), channel_id=1, source_target_pairs={{0,16},{1,17},{2,18},{3,19},{4,20},{5,21},{6,22},{7,23},{8,24},{9,... | collective-permute-start | bytes 1437704 | tf_op jit(solution)/shard_map/ppermute | solution.py:706
  207.2 18.5 %collective-permute-start.25 = (bf16[240,384]{1,0:T(8,128)(2,1)}, bf16[240,384]{1,0:T(8,128)(2,1)S(1)}, u32[]{:S(2)}, u32[]{:S(2)}) collective-permute-start(bf16[240,384]{1,0:T(8,128)(2,1)} %get-tuple-element.185), channel_id=1, source_target_pairs={{0,1},{1,0},{2,3},{3,2},{4,5},{5,4},{6,7},{7,6},{8,9},{9,8},{10,11... | collective-permute-start | bytes 552968 | tf_op jit(solution)/shard_map/ppermute | solution.py:706
  217.6 16.6 %collective-permute-start.26 = (bf16[240,384]{1,0:T(8,128)(2,1)}, bf16[240,384]{1,0:T(8,128)(2,1)S(1)}, u32[]{:S(2)}, u32[]{:S(2)}) collective-permute-start(bf16[240,384]{1,0:T(8,128)(2,1)} %get-tuple-element.186), channel_id=1, source_target_pairs={{0,2},{1,3},{2,0},{3,1},{4,6},{5,7},{6,4},{7,5},{8,10},{9,11},{10,... | collective-permute-start | bytes 552968 | tf_op jit(solution)/shard_map/ppermute | solution.py:706
  218.4 15.8 %collective-permute-start.27 = (bf16[240,384]{1,0:T(8,128)(2,1)}, bf16[240,384]{1,0:T(8,128)(2,1)}, u32[]{:S(2)}, u32[]{:S(2)}) collective-permute-start(bf16[240,384]{1,0:T(8,128)(2,1)} %get-tuple-element.187), channel_id=1, source_target_pairs={{0,3},{1,2},{2,1},{3,0},{4,7},{5,6},{6,5},{7,4},{8,11},{9,10},{10,... | collective-permute-start | bytes 552968 | tf_op jit(solution)/shard_map/ppermute | solution.py:706
  225.7 21.1 %copy-start.17 = (bf16[240,384]{1,0:T(8,128)(2,1)}, bf16[240,384]{1,0:T(8,128)(2,1)S(1)}, u32[]{:S(2)}) copy-start(bf16[240,384]{1,0:T(8,128)(2,1)S(1)} %collective-permute-done.25.a1) | copy-start | bytes 552964
  234.2 12.5 %copy-start.18 = (bf16[240,384]{1,0:T(8,128)(2,1)}, bf16[240,384]{1,0:T(8,128)(2,1)S(1)}, u32[]{:S(2)}) copy-start(bf16[240,384]{1,0:T(8,128)(2,1)S(1)} %collective-permute-done.26.a2) | copy-start | bytes 552964
  234.2 10.2 %collective-permute-start.29 = (bf16[96,768]{1,0:T(8,128)(2,1)}, bf16[96,768]{1,0:T(8,128)(2,1)S(1)}, u32[]{:S(2)}, u32[]{:S(2)}) collective-permute-start(bf16[96,768]{1,0:T(8,128)(2,1)} %get-tuple-element.201), channel_id=1, source_target_pairs={{0,8},{1,9},{2,10},{3,11},{4,12},{5,13},{6,14},{7,15},{8,0},{9,1},... | collective-permute-start | bytes 442376 | tf_op jit(solution)/shard_map/ppermute | solution.py:706
  235.5 11.3 %collective-permute-start.30 = (bf16[96,768]{1,0:T(8,128)(2,1)}, bf16[96,768]{1,0:T(8,128)(2,1)S(1)}, u32[]{:S(2)}, u32[]{:S(2)}) collective-permute-start(bf16[96,768]{1,0:T(8,128)(2,1)} %get-tuple-element.202), channel_id=1, source_target_pairs={{0,16},{1,17},{2,18},{3,19},{4,20},{5,21},{6,22},{7,23},{8,24},{9,... | collective-permute-start | bytes 442376 | tf_op jit(solution)/shard_map/ppermute | solution.py:706
  236.9 9.8 %collective-permute-start.31 = (bf16[96,768]{1,0:T(8,128)(2,1)}, bf16[96,768]{1,0:T(8,128)(2,1)S(1)}, u32[]{:S(2)}, u32[]{:S(2)}) collective-permute-start(bf16[96,768]{1,0:T(8,128)(2,1)} %get-tuple-element.203), channel_id=1, source_target_pairs={{0,24},{1,25},{2,26},{3,27},{4,28},{5,29},{6,30},{7,31},{8,16},{9,... | collective-permute-start | bytes 442376 | tf_op jit(solution)/shard_map/ppermute | solution.py:706
  237.7 12.1 %collective-permute-start.32 = (bf16[104,576]{1,0:T(8,128)(2,1)}, bf16[104,576]{1,0:T(8,128)(2,1)}, u32[]{:S(2)}, u32[]{:S(2)}) collective-permute-start(bf16[104,576]{1,0:T(8,128)(2,1)} %get-tuple-element.204), channel_id=1, source_target_pairs={{0,1},{1,0},{2,3},{3,2},{4,5},{5,4},{6,7},{7,6},{8,9},{9,8},{10,11... | collective-permute-start | bytes 359432 | tf_op jit(solution)/shard_map/ppermute | solution.py:706
  240.6 11.2 %collective-permute-start.33 = (bf16[104,576]{1,0:T(8,128)(2,1)}, bf16[104,576]{1,0:T(8,128)(2,1)}, u32[]{:S(2)}, u32[]{:S(2)}) collective-permute-start(bf16[104,576]{1,0:T(8,128)(2,1)} %get-tuple-element.205), channel_id=1, source_target_pairs={{0,2},{1,3},{2,0},{3,1},{4,6},{5,7},{6,4},{7,5},{8,10},{9,11},{10,... | collective-permute-start | bytes 359432 | tf_op jit(solution)/shard_map/ppermute | solution.py:706
  244.5 2.3 copy-start.20
  244.5 7.3 %collective-permute-start.34 = (bf16[104,576]{1,0:T(8,128)(2,1)}, bf16[104,576]{1,0:T(8,128)(2,1)}, u32[]{:S(2)}, u32[]{:S(2)}) collective-permute-start(bf16[104,576]{1,0:T(8,128)(2,1)} %get-tuple-element.206), channel_id=1, source_target_pairs={{0,3},{1,2},{2,1},{3,0},{4,7},{5,6},{6,5},{7,4},{8,11},{9,10},{10,... | collective-permute-start | bytes 359432 | tf_op jit(solution)/shard_map/ppermute | solution.py:706
  251.8 7.3 %collective-permute-start.35 = (bf16[432,384]{1,0:T(8,128)(2,1)}, bf16[432,384]{1,0:T(8,128)(2,1)S(1)}, u32[]{:S(2)}, u32[]{:S(2)}) collective-permute-start(bf16[432,384]{1,0:T(8,128)(2,1)} %sums.1), channel_id=1, source_target_pairs={{0,8},{1,9},{2,10},{3,11},{4,20},{5,21},{6,22},{7,23},{8,0},{9,1},... | collective-permute-start | bytes 995336 | tf_op jit(solution)/shard_map/ppermute | solution.py:706
  261.0 10.5 %collective-permute-start.37 = (bf16[2,432,384]{2,1,0:T(8,128)(2,1)}, bf16[2,432,384]{2,1,0:T(8,128)(2,1)}, u32[]{:S(2)}, u32[]{:S(2)}) collective-permute-start(bf16[2,432,384]{2,1,0:T(8,128)(2,1)} %pad_maximum_fusion.2.s1), channel_id=1, source_target_pairs={{0,4},{1,5},{2,6},{3,7},{4,0},{5,1},{6,2},{7,3},{8,12},{9,13},{10,... | collective-permute-start | bytes 1990664 | tf_op jit(solution)/shard_map/ppermute | solution.py:706
  261.0 12.7 %collective-permute-start.36 = (bf16[2,432,384]{2,1,0:T(8,128)(2,1)}, bf16[2,432,384]{2,1,0:T(8,128)(2,1)}, u32[]{:S(2)}, u32[]{:S(2)}) collective-permute-start(bf16[2,432,384]{2,1,0:T(8,128)(2,1)} %pad_maximum_fusion.2.s1), channel_id=1, source_target_pairs={{0,16},{1,17},{2,18},{3,19},{4,12},{5,13},{6,14},{7,15},{8,24},{9,... | collective-permute-start | bytes 1990664 | tf_op jit(solution)/shard_map/ppermute | solution.py:706
  264.3 7.3 %collective-permute-start.38 = (bf16[208,384]{1,0:T(8,128)(2,1)}, bf16[208,384]{1,0:T(8,128)(2,1)S(1)}, u32[]{:S(2)}, u32[]{:S(2)}) collective-permute-start(bf16[208,384]{1,0:T(8,128)(2,1)} %sumsq.1), channel_id=1, source_target_pairs={{0,8},{1,9},{2,10},{3,11},{4,20},{5,21},{6,22},{7,23},{8,0},{9,1},... | collective-permute-start | bytes 479240 | tf_op jit(solution)/shard_map/ppermute | solution.py:706
  273.7 5.2 %collective-permute-start.39 = (bf16[2,432,384]{2,1,0:T(8,128)(2,1)}, bf16[2,432,384]{2,1,0:T(8,128)(2,1)}, u32[]{:S(2)}, u32[]{:S(2)}) collective-permute-start(bf16[2,432,384]{2,1,0:T(8,128)(2,1)} %collective-permute-done.36.r2), channel_id=1, source_target_pairs={{0,4},{1,5},{2,6},{3,7},{4,0},{5,1},{6,2},{7,3},{8,12},{9,13},{10,... | collective-permute-start | bytes 1990664 | tf_op jit(solution)/shard_map/ppermute | solution.py:706
  274.7 4.2 %copy-start.8 = (bf16[2,208,384]{2,1,0:T(8,128)(2,1)}, bf16[2,208,384]{2,1,0:T(8,128)(2,1)S(1)}, u32[]{:S(2)}) copy-start(bf16[2,208,384]{2,1,0:T(8,128)(2,1)S(1)} %pad_maximum_fusion.6.s1) | copy-start | bytes 958468
  274.7 8.6 %collective-permute-start.40 = (bf16[2,208,384]{2,1,0:T(8,128)(2,1)S(1)}, bf16[2,208,384]{2,1,0:T(8,128)(2,1)}, u32[]{:S(2)}, u32[]{:S(2)}) collective-permute-start(bf16[2,208,384]{2,1,0:T(8,128)(2,1)S(1)} %pad_maximum_fusion.6.s1), channel_id=1, source_target_pairs={{0,16},{1,17},{2,18},{3,19},{4,12},{5,13},{6,14},{7,15},{8,24},{9,... | collective-permute-start | bytes 958472 | tf_op jit(solution)/shard_map/ppermute | solution.py:706
  278.9 4.9 %collective-permute-start.41 = (bf16[2,208,384]{2,1,0:T(8,128)(2,1)S(1)}, bf16[2,208,384]{2,1,0:T(8,128)(2,1)S(1)}, u32[]{:S(2)}, u32[]{:S(2)}) collective-permute-start(bf16[2,208,384]{2,1,0:T(8,128)(2,1)S(1)} %pad_maximum_fusion.6.s1), channel_id=1, source_target_pairs={{0,4},{1,5},{2,6},{3,7},{4,0},{5,1},{6,2},{7,3},{8,12},{9,13},{10,... | collective-permute-start | bytes 958472 | tf_op jit(solution)/shard_map/ppermute | solution.py:706
  283.3 2.0 collective-permute-start.42
  283.8 1.5 copy-start.15
  (6 other events, 4.5 us)

commit v5 on v4

--- a/solution.py
+++ b/solution.py
@@ -151,24 +151,44 @@
         here = pl.multiple_of(i * T, T)
         first = (mine * 4 + i) * T
         low, high = span(limits(lengths, s, L), first, first + T - 1)
-        for h in range(3):
-            m_s[h] = jnp.full((T, 128), -jnp.inf, F32)
-            acc_s[h] = jnp.zeros((T, 128), F32)
-
-        def step(kt, _):
-            at = pl.multiple_of(kt * KC, KC)
+        def whole(width):
+            at = pl.multiple_of(jnp.minimum(low // T * T, L - width), T)
             for h in range(3):
-                sc = mm_nt(q_ref[s, h, pl.ds(here, T)], k_ref[s, h, pl.ds(at, KC)])
-                old = m_s[h]
-                parts = [sc[:, j * 128 : (j + 1) * 128] for j in range(KC // 128)]
-                top = functools.reduce(jnp.maximum, parts)
-                new = jnp.maximum(old, jnp.broadcast_to(jnp.max(top, axis=1, keepdims=True), (T, 128)))
-                p = jnp.concatenate([jnp.exp(v - new).astype(BF) for v in parts], axis=1)
-                acc_s[h] = acc_s[h] * jnp.exp(old - new) + mm(p, v_ref[s, h, pl.ds(at, KC)])
-                m_s[h] = new
-            return 0
-
-        lax.fori_loop(low // KC, (high + KC - 1) // KC, step, 0)
+                sc = mm_nt(q_ref[s, h, pl.ds(here, T)], k_ref[s, h, pl.ds(at, width)])
+                parts = [sc[:, j * 128 : (j + 1) * 128] for j in range(width // 128)]
+                top = jnp.max(functools.reduce(jnp.maximum, parts), axis=1, keepdims=True)
+                top = jnp.broadcast_to(top, (T, 128))
+                p = jnp.concatenate([jnp.exp(v - top).astype(BF) for v in parts], axis=1)
+                acc_s[h] = mm(p, v_ref[s, h, pl.ds(at, width)])
+                m_s[h] = top
+
+        def running():
+            for h in range(3):
+                m_s[h] = jnp.full((T, 128), -jnp.inf, F32)
+                acc_s[h] = jnp.zeros((T, 128), F32)
+
+            def step(kt, _):
+                at = pl.multiple_of(kt * KC, KC)
+                for h in range(3):
+                    sc = mm_nt(q_ref[s, h, pl.ds(here, T)], k_ref[s, h, pl.ds(at, KC)])
+                    old = m_s[h]
+                    parts = [sc[:, j * 128 : (j + 1) * 128] for j in range(KC // 128)]
+                    top = functools.reduce(jnp.maximum, parts)
+                    new = jnp.maximum(old, jnp.broadcast_to(jnp.max(top, axis=1, keepdims=True), (T, 128)))
+                    p = jnp.concatenate([jnp.exp(v - new).astype(BF) for v in parts], axis=1)
+                    acc_s[h] = acc_s[h] * jnp.exp(old - new) + mm(p, v_ref[s, h, pl.ds(at, KC)])
+                    m_s[h] = new
+                return 0
+
+            lax.fori_loop(low // KC, (high + KC - 1) // KC, step, 0)
+
+        tiles = (high + T - 1) // T - low // T
+        pl.when(tiles <= 2)(functools.partial(whole, 2 * T))
+        pl.when(tiles == 3)(functools.partial(whole, 3 * T))
+        if L == 4 * T:
+            pl.when(tiles == 4)(functools.partial(whole, 4 * T))
+        else:
+            pl.when(tiles > 3)(running)
         outs = []
         for h in range(3):
             acc = acc_s[h]
@@ -331,7 +351,7 @@
     R, D = tok.shape
     T = attn.shape[1]
     FB = w_in.shape[1] // 8
-    TR = 128
+    TR, GR = 256, 128
     first_copies = [(w_at, wa.at[z]), (sm_own.at[240:256], sm.at[0])]
     first_copies += [(s1a.at[0, k, 240:256], sm.at[k + 1]) for k in range(3)]
     copies = [(w_in, w1.at[z]), (w_out, w2.at[z])]
@@ -418,8 +438,8 @@
     def forward(zz, _):
         cols = pl.ds(pl.multiple_of(zz * D, 128), D)
         u = mm(hlow[...], w1[:, :, cols].reshape(D, D)) + jnp.concatenate([b1[2 * zz, 0:1, :], b1[2 * zz + 1, 0:1, :]], axis=1)
-        for r in range(R // TR):
-            rows = slice(r * TR, (r + 1) * TR)
+        for r in range(R // GR):
+            rows = slice(r * GR, (r + 1) * GR)
             a, d = gelu_parts(u[rows])
             act[rows, cols] = a.astype(BF)
             gp[rows, cols] = d.astype(BF)
@@ -467,8 +487,8 @@
         cols = pl.ds(pl.multiple_of(zz * D, 128), D)
         da = mm_nt(dlow[...], w2[zz])
         gsum = jnp.zeros((8, D), F32)
-        for r in range(R // TR):
-            rows = slice(r * TR, (r + 1) * TR)
+        for r in range(R // GR):
+            rows = slice(r * GR, (r + 1) * GR)
             di = (da[rows] * gp[rows, cols].astype(F32)).astype(BF)
             act[rows, cols] = di
             gsum = gsum + fold8(di.astype(F32))
@@ -525,8 +545,7 @@
     kept_all(19, 2)
 
 
-def weight_kernel(idx, kept, mate, sent, plane, mine, *rest):
-    outs, (units, shared, units2, shared2, sem) = rest[:3], rest[3:]
+def weight_kernel(idx, kept, mate, sent, plane, mine, s1, s2, s3, units, shared, units2, shared2, plane_s, mine_s, sent_s, sem, osem):
     z = idx[1]
     D = shared.shape[1] // 3
     FB = D // 2
@@ -537,36 +556,48 @@
             copies.append((refs[0].at[:, at : at + size], us.at[:, at : at + size]))
         for at in (D, 2 * D, 0):
             copies.append((refs[1].at[:, 9 * FB + at : 9 * FB + at + D], sh.at[:, at : at + D]))
-    order = (0, 3, 6, 9, 1, 4, 7, 10, 2, 5, 8, 11)
+    order = (1, 4, 7, 10, 0, 3, 6, 9, 2, 5, 8, 11)
     copies = [pltpu.make_async_copy(*copies[n], sem.at[n]) for n in order]
     for cp in copies:
         cp.start()
     for cp in copies[:4]:
         cp.wait()
+    outs = []
+
+    def emit(src, to):
+        cp = pltpu.make_async_copy(src, to, osem.at[len(outs)])
+        cp.start()
+        outs.append(cp)
+
+    for k in (1, 2, 3, 0):
+        cols = pl.ds(pl.multiple_of((z ^ k) * FB, 128), FB)
+        v = mm_tn(units[:, cols], shared[:, 2 * D : 3 * D]) + mm_tn(units2[:, cols], shared2[:, 2 * D : 3 * D])
+        for q in range(4):
+            if k == 0:
+                mine_s[q] = v[q * 96 : (q + 1) * 96]
+            else:
+                sent_s[k - 1, q] = v[q * 96 : (q + 1) * 96].astype(BF)
+        if k == 0:
+            emit(mine_s, mine)
+        else:
+            emit(sent_s.at[k - 1], (s1, s2, s3)[k - 1])
+    for cp in copies[4:]:
+        cp.wait()
+    v = mm_tn(shared[:, 0:D], units[:, 2 * wide : 2 * wide + FB]) + mm_tn(shared2[:, 0:D], units2[:, 2 * wide : 2 * wide + FB])
+    v = v.astype(BF)
+    for zz in range(4):
+        for q in range(4):
+            plane_s[q, zz, 192:240, :] = v[zz * 192 + q * 48 : zz * 192 + (q + 1) * 48]
     for n in range(2):
         cols = slice(wide + n * D, wide + (n + 1) * D)
         v = mm_tn(shared[:, D : 2 * D], units[:, cols]) + mm_tn(shared2[:, D : 2 * D], units2[:, cols])
         v = v.astype(BF)
         for i in range(2):
             for zz in range(4):
-                plane[2 * n + i, zz, 0:192, :] = v[zz * 192 : (zz + 1) * 192, i * FB : (i + 1) * FB]
-    for cp in copies[4:8]:
+                plane_s[2 * n + i, zz, 0:192, :] = v[zz * 192 : (zz + 1) * 192, i * FB : (i + 1) * FB]
+        emit(plane_s.at[2 * n : 2 * n + 2], plane.at[2 * n : 2 * n + 2])
+    for cp in outs:
         cp.wait()
-    for k in range(4):
-        cols = pl.ds(pl.multiple_of((z ^ k) * FB, 128), FB)
-        v = mm_tn(units[:, cols], shared[:, 2 * D : 3 * D]) + mm_tn(units2[:, cols], shared2[:, 2 * D : 3 * D])
-        for q in range(4):
-            if k == 0:
-                mine[q] = v[q * 96 : (q + 1) * 96]
-            else:
-                outs[k - 1][q] = v[q * 96 : (q + 1) * 96].astype(BF)
-    for cp in copies[8:]:
-        cp.wait()
-    v = mm_tn(shared[:, 0:D], units[:, 2 * wide : 2 * wide + FB]) + mm_tn(shared2[:, 0:D], units2[:, 2 * wide : 2 * wide + FB])
-    v = v.astype(BF)
-    for zz in range(4):
-        for q in range(4):
-            plane[q, zz, 192:240, :] = v[zz * 192 + q * 48 : zz * 192 + (q + 1) * 48]
 
 
 def products_kernel(idx, d, w, t0, t1, t2, t3, extra, *outs):
@@ -853,10 +884,11 @@
         q1, c2, *sent2 = call(
             weight_kernel,
             (jax.ShapeDtypeStruct((4, 4, 240, FB), BF), jax.ShapeDtypeStruct((4, 96, D), F32)) + (part,) * 3,
-            [SM] + [ANY] * 3, (VM,) * 5,
+            [SM] + [ANY] * 3, (ANY,) * 5,
             [
                 pltpu.VMEM((R, 9 * FB), BF), pltpu.VMEM((R, 3 * D), BF), pltpu.VMEM((R, 9 * FB), BF), pltpu.VMEM((R, 3 * D), BF),
-                pltpu.SemaphoreType.DMA((12,)),
+                pltpu.VMEM((4, 4, 240, FB), BF), pltpu.VMEM((4, 96, D), F32),
+                pltpu.VMEM((3, 4, 96, D), BF), pltpu.SemaphoreType.DMA((12,)), pltpu.SemaphoreType.DMA((6,)),
             ],
             name="weights",
         )(idx, kept, to_core(sent), sent)

time: 290 us -> 288 us (level)
  no operation moved by 1% of the time
where the time goes in v5:
time: 288 us; the launch traced here: 287 us
  Pallas kernels  120 us (42%)
  waiting for transfers between devices  78.5 us (27%)
  starting transfers between devices  72.9 us (25%)
  other arithmetic  7.47 us (3%)
  local copies, waits for them, and re-layouts  7.19 us (2%)
    ppermute x43, waiting for transfers between devices, send(): return lax.ppermute(a, AX, pairs)  66.7 us
    ppermute x43, starting transfers between devices, send(): return lax.ppermute(a, AX, pairs)  57.9 us
    pallas_call x1, Pallas kernels, attn_back(): call(functools.partial(attn_bwd_kernel, pg, 512), outs if pg == 1 else (j...  32 us
    pallas_call x1, Pallas kernels, body(): call(ffn_kernel, (jax.ShapeDtypeStruct((R, D), BF), jax.ShapeDtypeStruct(...  28.7 us
    pallas_call x1, Pallas kernels, body(): call(functools.partial(attn_fwd_kernel, 1024), (jax.ShapeDtypeStruct((4,...  18.1 us
    all_to_all x1, waiting for transfers between devices, body(): attn = lax.all_to_all(o, ('x', 'core'), 0, 0, tiled=True)  11.8 us
    pallas_call x1, Pallas kernels, body(): call(weight_kernel, (jax.ShapeDtypeStruct((4, 4, 240, FB), BF), jax.Shape...  10.4 us
    pallas_call x1, Pallas kernels, body(): call(functools.partial(qkv_kernel, pg), (own_head, head, head, jax.ShapeD...  8.44 us
  transfers between devices with their start and end apart: 47, of which 15 were waited for; matrix products, arithmetic and copies ran while one was open for 2% of the time, Pallas kernels for 31%

profile of v5, /device:TPU:0, one launch (start us, length us, event | category | flops | bytes accessed | tf_op | source)
XLA Modules:
  0.0 287.2 jit_solution(17791337755028559063)
XLA Ops:
  1.2 2.6 collective-permute-start.3
  4.4 3.0 %prep.1 = (bf16[200,576]{1,0:T(8,128)(2,1)}, bf16[104,576]{1,0:T(8,128)(2,1)}, bf16[256,384]{1,0:T(8,128)(2,1)}, bf16[96,768]{1,0:T(8,128)(2,1)}) custom-call(s32[14]{0:T(128)} %stack.128.idx, bf16[192,768]{1,0:T(8,128)(2,1)} %wq.1, bf16[192,768]{1,0:T(8,128)(2,1)} %wk.1, bf16[192,768]{1,0:T(8,128)(2,1)} %wv.1, bf16[192,768]{1,0:T(8,128)(2,1)} %w_at.3, ...), custom_call_target="tpu_custom_call" | custom-call | flops 1 | bytes 1 | tf_op jit(solution)/shard_map/prep/pallas_call | solution.py:770
  7.4 3.6 %collective-permute-start.2 = (bf16[104,576]{1,0:T(8,128)(2,1)}, bf16[104,576]{1,0:T(8,128)(2,1)S(1)}, u32[]{:S(2)}, u32[]{:S(2)}) collective-permute-start(bf16[104,576]{1,0:T(8,128)(2,1)} %get-tuple-element.127), channel_id=1, source_target_pairs={{0,3},{1,2},{2,1},{3,0},{4,7},{5,6},{6,5},{7,4},{8,11},{9,10},{10,... | collective-permute-start | bytes 359432 | tf_op jit(solution)/shard_map/ppermute | solution.py:737
  11.8 4.1 %collective-permute-done.2.refs_7_ = bf16[104,576]{1,0:T(8,128)(2,1)S(1)} collective-permute-done((bf16[104,576]{1,0:T(8,128)(2,1)}, bf16[104,576]{1,0:T(8,128)(2,1)S(1)}, u32[]{:S(2)}, u32[]{:S(2)}) %collective-permute-start.2) | collective-permute-done | bytes 119840 | tf_op jit(solution)/shard_map/ppermute | solution.py:737
  15.9 7.0 %collective-permute-done.1.refs_6_ = bf16[104,576]{1,0:T(8,128)(2,1)S(1)} collective-permute-done((bf16[104,576]{1,0:T(8,128)(2,1)}, bf16[104,576]{1,0:T(8,128)(2,1)S(1)}, u32[]{:S(2)}, u32[]{:S(2)}) %collective-permute-start.1) | collective-permute-done | bytes 119840 | tf_op jit(solution)/shard_map/ppermute | solution.py:737
  23.1 1.6 collective-permute-start.5
  24.7 2.9 %collective-permute-start.9 = (bf16[256,384]{1,0:T(8,128)(2,1)}, bf16[256,384]{1,0:T(8,128)(2,1)S(1)}, u32[]{:S(2)}, u32[]{:S(2)}) collective-permute-start(bf16[256,384]{1,0:T(8,128)(2,1)} %get-tuple-element.134.sm_own), channel_id=1, source_target_pairs={{0,3},{1,2},{2,1},{3,0},{4,7},{5,6},{6,5},{7,4},{8,11},{9,10},{10,... | collective-permute-start | bytes 589832 | tf_op jit(solution)/shard_map/ppermute | solution.py:737
  27.6 1.5 collective-permute-start.7
  29.1 5.5 %collective-permute-done.9 = bf16[256,384]{1,0:T(8,128)(2,1)S(1)} collective-permute-done((bf16[256,384]{1,0:T(8,128)(2,1)}, bf16[256,384]{1,0:T(8,128)(2,1)S(1)}, u32[]{:S(2)}, u32[]{:S(2)}) %collective-permute-start.9) | collective-permute-done | bytes 196640 | tf_op jit(solution)/shard_map/ppermute | solution.py:737
  34.6 10.3 %collective-permute-done.8 = bf16[256,384]{1,0:T(8,128)(2,1)S(1)} collective-permute-done((bf16[256,384]{1,0:T(8,128)(2,1)}, bf16[256,384]{1,0:T(8,128)(2,1)S(1)}, u32[]{:S(2)}, u32[]{:S(2)}) %collective-permute-start.8) | collective-permute-done | bytes 196640 | tf_op jit(solution)/shard_map/ppermute | solution.py:737
  45.7 1.6 collective-permute-start.10
  47.3 2.5 collective-permute-start.13
  49.8 1.9 collective-permute-start.11
  51.7 8.4 %qkv.1 = (bf16[2,3,1024,128]{3,2,1,0:T(8,128)(2,1)}, bf16[2,3,1024,128]{3,2,1,0:T(8,128)(2,1)}, bf16[2,3,1024,128]{3,2,1,0:T(8,128)(2,1)}, bf16[4,192,576]{2,1,0:T(8,128)(2,1)}) custom-call(s32[2,4]{1,0:T(2,128)} %lengths.7, s32[14]{0:T(128)} %stack.128.idx, bf16[1,2,256,768]{3,2,1,0:T(8,128)(2,1)} %bitcast.59, bf16[1,2,256,768]{3,2,1,0:T(8,128)(2,1)} %bitcast.62, ...), custom_call_target="tpu_custom_call" | custom-call | flops 1 | bytes 1 | tf_op jit(solution)/shard_map/qkv/pallas_call | solution.py:794
  60.2 1.0 collective-permute-done.12
  61.4 1.5 pad_maximum_fusion.4
  62.9 0.8 collective-permute-start.14
  63.7 1.3 collective-permute-start.15
  65.0 18.1 %attn_fwd.1 = (bf16[4,256,384]{2,1,0:T(8,128)(2,1)}, bf16[2,3,1024,128]{3,2,1,0:T(8,128)(2,1)}) custom-call(s32[2,4]{1,0:T(2,128)} %lengths.7, s32[14]{0:T(128)} %stack.128.idx, bf16[2,3,1024,128]{3,2,1,0:T(8,128)(2,1)} %get-tuple-element.151.q_ref, bf16[2,3,1024,128]{3,2,1,0:T(8,128)(2,1)} %get-tuple-element.152.k_ref.refs_1_, ...), custom_call_target="tpu_custom_call" | custom-call | flops 1 | bytes 1 | tf_op jit(solution)/shard_map/attn_fwd/pallas_call | solution.py:807
  83.1 1.0 copy-done.9
  84.2 1.4 collective-permute-start.16
  85.6 3.7 %all-to-all-start = ((bf16[4,256,384]{2,1,0:T(8,128)(2,1)}), bf16[4,256,384]{2,1,0:T(8,128)(2,1)S(1)}, u32[]{:S(2)}, u32[]{:S(2)}) async-start(bf16[4,256,384]{2,1,0:T(8,128)(2,1)} %get-tuple-element.157.refs_3_), calls=%async_computation | async-start | bytes 1572864 | tf_op jit(solution)/shard_map/all_to_all | solution.py:816
  90.1 11.8 %all-to-all-done.attn = bf16[4,256,384]{2,1,0:T(8,128)(2,1)S(1)} async-done(((bf16[4,256,384]{2,1,0:T(8,128)(2,1)}), bf16[4,256,384]{2,1,0:T(8,128)(2,1)S(1)}, u32[]{:S(2)}, u32[]{:S(2)}) %all-to-all-start) | async-done | bytes 786464 | tf_op jit(solution)/shard_map/all_to_all | solution.py:816
  101.8 1.9 collective-permute-start.20
  103.8 2.4 collective-permute-done.20.c2b
  106.2 28.7 %ffn.1 = (bf16[512,768]{1,0:T(8,128)(2,1)}, f32[512,768]{1,0:T(8,128)}, bf16[4,256,384]{2,1,0:T(8,128)(2,1)}, bf16[512,5760]{1,0:T(8,128)(2,1)}, bf16[512,3456]{1,0:T(8,128)(2,1)}, /*index=5*/f32[4,8,576]{2,1,0:T(8,128)}) custom-call(s32[14]{0:T(128)} %stack.128.idx, s32[2,4]{1,0:T(2,128)} %lengths.7, bf16[4,256,384]{2,1,0:T(8,128)(2,1)} %copy-done.4, ...), custom_call_target="tpu_custom_call" | custom-call | flops 1 | bytes 1 | tf_op jit(solution)/shard_map/ffn/pallas_call | solution.py:823
  135.4 3.5 %all-to-all-start.1 = ((bf16[4,256,384]{2,1,0:T(8,128)(2,1)}), bf16[4,256,384]{2,1,0:T(8,128)(2,1)S(1)}, u32[]{:S(2)}, u32[]{:S(2)}) async-start(bf16[4,256,384]{2,1,0:T(8,128)(2,1)} %get-tuple-element.163), calls=%async_computation.1 | async-start | bytes 1572864 | tf_op jit(solution)/shard_map/all_to_all | solution.py:854
  138.9 6.1 %collective-permute-done.21.mate = bf16[512,5760]{1,0:T(8,128)(2,1)} collective-permute-done((bf16[512,5760]{1,0:T(8,128)(2,1)}, bf16[512,5760]{1,0:T(8,128)(2,1)}, u32[]{:S(2)}, u32[]{:S(2)}) %collective-permute-start.21) | collective-permute-done | bytes 5898272 | tf_op jit(solution)/shard_map/ppermute | solution.py:737
  145.0 10.4 %weights.1 = (bf16[4,4,240,384]{3,2,1,0:T(8,128)(2,1)}, f32[4,96,768]{2,1,0:T(8,128)}, bf16[4,96,768]{2,1,0:T(8,128)(2,1)}, bf16[4,96,768]{2,1,0:T(8,128)(2,1)}, bf16[4,96,768]{2,1,0:T(8,128)(2,1)}) custom-call(s32[14]{0:T(128)} %stack.128.idx, bf16[512,3456]{1,0:T(8,128)(2,1)} %get-tuple-element.164.kept, bf16[512,5760]{1,0:T(8,128)(2,1)} %collective-permute-done.21.mate, ...), custom_call_target="tpu_custom_call" | custom-call | flops 1 | bytes 1 | tf_op jit(solution)/shard_map/weights/pallas_call | solution.py:884
  155.4 0.9 copy-done.3
  156.3 3.9 %all-to-all-start.2 = ((bf16[4,4,240,384]{3,2,1,0:T(8,128)(2,1)}), bf16[4,4,240,384]{3,2,1,0:T(8,128)(2,1)S(1)}, u32[]{:S(2)}, u32[]{:S(2)}) async-start(bf16[4,4,240,384]{3,2,1,0:T(8,128)(2,1)} %get-tuple-element.170), calls=%async_computation.2 | async-start | bytes 5898240 | tf_op jit(solution)/shard_map/all_to_all | solution.py:897
  160.3 2.8 collective-permute-start.23
  163.1 1.6 collective-permute-start.24
  164.6 32.0 %attn_bwd.1 = (bf16[4,104,576]{2,1,0:T(8,128)(2,1)}, bf16[4,104,576]{2,1,0:T(8,128)(2,1)}, bf16[4,512,768]{2,1,0:T(8,128)(2,1)}) custom-call(s32[2,4]{1,0:T(2,128)} %lengths.7, s32[14]{0:T(128)} %stack.128.idx, bf16[2,3,1024,128]{3,2,1,0:T(8,128)(2,1)} %get-tuple-element.188.refs_0_, bf16[2,3,1024,128]{3,2,1,0:T(8,128)(2,1)} %get-tuple-element.152.k_ref.refs_1_, ...), custom_call_target="tpu_custom_call" | custom-call | flops 1 | bytes 1 | tf_op jit(solution)/shard_map/attn_bwd/pallas_call | solution.py:867
  196.7 1.6 copy-done
  198.3 4.0 %all-to-all-start.3 = ((bf16[4,512,768]{2,1,0:T(8,128)(2,1)}), bf16[4,512,768]{2,1,0:T(8,128)(2,1)S(1)}, u32[]{:S(2)}, u32[]{:S(2)}) async-start(bf16[4,512,768]{2,1,0:T(8,128)(2,1)} %get-tuple-element.219), calls=%async_computation.3 | async-start | bytes 6291456 | tf_op jit(solution)/shard_map/all_to_all | solution.py:903
  202.3 2.9 %chunks1.1 = (f32[240,384]{1,0:T(8,128)}, bf16[240,384]{1,0:T(8,128)(2,1)}, bf16[240,384]{1,0:T(8,128)(2,1)}, bf16[240,384]{1,0:T(8,128)(2,1)}) custom-call(s32[14]{0:T(128)} %stack.128.idx, bf16[4,4,240,384]{3,2,1,0:T(8,128)(2,1)} %copy-done), custom_call_target="tpu_custom_call" | custom-call | flops 1 | bytes 1 | tf_op jit(solution)/shard_map/chunks1/pallas_call | solution.py:900
  205.2 10.5 %collective-permute-start.25 = (bf16[240,384]{1,0:T(8,128)(2,1)}, bf16[240,384]{1,0:T(8,128)(2,1)S(1)}, u32[]{:S(2)}, u32[]{:S(2)}) collective-permute-start(bf16[240,384]{1,0:T(8,128)(2,1)} %get-tuple-element.185), channel_id=1, source_target_pairs={{0,1},{1,0},{2,3},{3,2},{4,5},{5,4},{6,7},{7,6},{8,9},{9,8},{10,11... | collective-permute-start | bytes 552968 | tf_op jit(solution)/shard_map/ppermute | solution.py:737
  215.7 0.8 collective-permute-start.26
  216.5 1.6 collective-permute-start.27
  218.0 0.8 copy-done.13
  218.8 2.1 chunksq.1
  220.9 2.8 sums2.1
  223.7 8.6 %collective-permute-done.26.a2 = bf16[240,384]{1,0:T(8,128)(2,1)S(1)} collective-permute-done((bf16[240,384]{1,0:T(8,128)(2,1)}, bf16[240,384]{1,0:T(8,128)(2,1)S(1)}, u32[]{:S(2)}, u32[]{:S(2)}) %collective-permute-start.26) | collective-permute-done | bytes 184352 | tf_op jit(solution)/shard_map/ppermute | solution.py:737
  232.3 1.2 collective-permute-start.29
  233.5 1.5 collective-permute-start.30
  235.0 0.8 collective-permute-start.31
  235.8 2.9 %collective-permute-start.32 = (bf16[104,576]{1,0:T(8,128)(2,1)}, bf16[104,576]{1,0:T(8,128)(2,1)}, u32[]{:S(2)}, u32[]{:S(2)}) collective-permute-start(bf16[104,576]{1,0:T(8,128)(2,1)} %get-tuple-element.204), channel_id=1, source_target_pairs={{0,1},{1,0},{2,3},{3,2},{4,5},{5,4},{6,7},{7,6},{8,9},{9,8},{10,11... | collective-permute-start | bytes 359432 | tf_op jit(solution)/shard_map/ppermute | solution.py:737
  239.5 3.0 %collective-permute-done.29.b1 = bf16[96,768]{1,0:T(8,128)(2,1)S(1)} collective-permute-done((bf16[96,768]{1,0:T(8,128)(2,1)}, bf16[96,768]{1,0:T(8,128)(2,1)S(1)}, u32[]{:S(2)}, u32[]{:S(2)}) %collective-permute-start.29) | collective-permute-done | bytes 147488 | tf_op jit(solution)/shard_map/ppermute | solution.py:737
  242.5 2.3 collective-permute-start.34
  245.5 2.3 sums.1
  247.8 2.0 collective-permute-done.33.q2
  250.6 6.6 %collective-permute-done.35 = bf16[432,384]{1,0:T(8,128)(2,1)S(1)} collective-permute-done((bf16[432,384]{1,0:T(8,128)(2,1)}, bf16[432,384]{1,0:T(8,128)(2,1)S(1)}, u32[]{:S(2)}, u32[]{:S(2)}) %collective-permute-start.35) | collective-permute-done | bytes 331808 | tf_op jit(solution)/shard_map/ppermute | solution.py:737
  257.2 1.9 pad_maximum_fusion.2.s1
  259.1 1.5 collective-permute-start.36
  260.6 1.8 sumsq.1
  263.1 6.6 %collective-permute-done.38 = bf16[208,384]{1,0:T(8,128)(2,1)S(1)} collective-permute-done((bf16[208,384]{1,0:T(8,128)(2,1)}, bf16[208,384]{1,0:T(8,128)(2,1)S(1)}, u32[]{:S(2)}, u32[]{:S(2)}) %collective-permute-start.38) | collective-permute-done | bytes 159776 | tf_op jit(solution)/shard_map/ppermute | solution.py:737
  269.7 2.1 collective-permute-done.36.r2
  271.8 1.0 pad_maximum_fusion.6.s1
  272.7 1.6 collective-permute-start.40
  274.3 2.7 fusion
  277.1 4.4 %out_ffn.1 = (f32[192,3072]{1,0:T(8,128)}, f32[192,768]{1,0:T(8,128)}, f32[768,768]{1,0:T(8,128)}) custom-call(s32[14]{0:T(128)} %stack.128.idx, bf16[2,432,384]{2,1,0:T(8,128)(2,1)} %pad_maximum_fusion.2.s1, bf16[2,432,384]{2,1,0:T(8,128)(2,1)} %collective-permute-done.36.r2, bf16[2,432,384]{2,1,0:T(8,128)(2,1)} %collective-permute-done.37.c1, ...), custom_call_target="tpu_custom_call" | custom-call | flops 1 | bytes 1 | tf_op jit(solution)/shard_map/out_ffn/pallas_call | solution.py:925
  282.0 1.4 collective-permute-done.42.c2
  284.1 2.8 out_qkv.1
  (98 shorter events, 8.8 us)
Async XLA Ops:
  0.7 22.3 %collective-permute-start.4 = (bf16[2,256,768]{2,1,0:T(8,128)(2,1)}, bf16[2,256,768]{2,1,0:T(8,128)(2,1)S(1)}, u32[]{:S(2)}, u32[]{:S(2)}) collective-permute-start(bf16[2,256,768]{2,1,0:T(8,128)(2,1)} %refs_6_.1), channel_id=1, source_target_pairs={{0,4},{1,5},{2,6},{3,7},{4,0},{5,1},{6,2},{7,3},{8,12},{9,13},{10,... | collective-permute-start | bytes 2359304 | tf_op jit(solution)/shard_map/ppermute | solution.py:737
  1.2 21.8 %collective-permute-start.3 = (bf16[2,256,768]{2,1,0:T(8,128)(2,1)}, bf16[2,256,768]{2,1,0:T(8,128)(2,1)S(1)}, u32[]{:S(2)}, u32[]{:S(2)}) collective-permute-start(bf16[2,256,768]{2,1,0:T(8,128)(2,1)} %refs_6_.1), channel_id=1, source_target_pairs={{0,8},{1,9},{2,10},{3,11},{4,12},{5,13},{6,14},{7,15},{8,0},{9,1},... | collective-permute-start | bytes 2359304 | tf_op jit(solution)/shard_map/ppermute | solution.py:737
  7.4 8.5 %collective-permute-start.2 = (bf16[104,576]{1,0:T(8,128)(2,1)}, bf16[104,576]{1,0:T(8,128)(2,1)S(1)}, u32[]{:S(2)}, u32[]{:S(2)}) collective-permute-start(bf16[104,576]{1,0:T(8,128)(2,1)} %get-tuple-element.127), channel_id=1, source_target_pairs={{0,3},{1,2},{2,1},{3,0},{4,7},{5,6},{6,5},{7,4},{8,11},{9,10},{10,... | collective-permute-start | bytes 359432 | tf_op jit(solution)/shard_map/ppermute | solution.py:737
  11.0 11.9 %collective-permute-start.1 = (bf16[104,576]{1,0:T(8,128)(2,1)}, bf16[104,576]{1,0:T(8,128)(2,1)S(1)}, u32[]{:S(2)}, u32[]{:S(2)}) collective-permute-start(bf16[104,576]{1,0:T(8,128)(2,1)} %get-tuple-element.127), channel_id=1, source_target_pairs={{0,2},{1,3},{2,0},{3,1},{4,6},{5,7},{6,4},{7,5},{8,10},{9,11},{10,... | collective-permute-start | bytes 359432 | tf_op jit(solution)/shard_map/ppermute | solution.py:737
  11.0 11.9 %collective-permute-start = (bf16[104,576]{1,0:T(8,128)(2,1)}, bf16[104,576]{1,0:T(8,128)(2,1)S(1)}, u32[]{:S(2)}, u32[]{:S(2)}) collective-permute-start(bf16[104,576]{1,0:T(8,128)(2,1)} %get-tuple-element.127), channel_id=1, source_target_pairs={{0,1},{1,0},{2,3},{3,2},{4,5},{5,4},{6,7},{7,6},{8,9},{9,8},{10,11... | collective-permute-start | bytes 359432 | tf_op jit(solution)/shard_map/ppermute | solution.py:737
  15.9 35.8 %copy-start.10 = (bf16[104,576]{1,0:T(8,128)(2,1)}, bf16[104,576]{1,0:T(8,128)(2,1)S(1)}, u32[]{:S(2)}) copy-start(bf16[104,576]{1,0:T(8,128)(2,1)S(1)} %collective-permute-done.2.refs_7_) | copy-start | bytes 359428
  22.9 28.8 %copy-start.11 = (bf16[104,576]{1,0:T(8,128)(2,1)}, bf16[104,576]{1,0:T(8,128)(2,1)S(1)}, u32[]{:S(2)}) copy-start(bf16[104,576]{1,0:T(8,128)(2,1)S(1)} %collective-permute-done.1.refs_6_) | copy-start | bytes 359428
  22.9 28.8 %copy-start.12 = (bf16[104,576]{1,0:T(8,128)(2,1)}, bf16[104,576]{1,0:T(8,128)(2,1)S(1)}, u32[]{:S(2)}) copy-start(bf16[104,576]{1,0:T(8,128)(2,1)S(1)} %collective-permute-done.refs_5_) | copy-start | bytes 359428
  22.9 28.8 %copy-start.5 = (bf16[2,256,768]{2,1,0:T(8,128)(2,1)}, bf16[2,256,768]{2,1,0:T(8,128)(2,1)S(1)}, u32[]{:S(2)}) copy-start(bf16[2,256,768]{2,1,0:T(8,128)(2,1)S(1)} %collective-permute-done.4.refs_8_) | copy-start | bytes 2359300
  23.0 28.7 %copy-start.6 = (bf16[2,256,768]{2,1,0:T(8,128)(2,1)}, bf16[2,256,768]{2,1,0:T(8,128)(2,1)S(1)}, u32[]{:S(2)}) copy-start(bf16[2,256,768]{2,1,0:T(8,128)(2,1)S(1)} %collective-permute-done.3.refs_7_) | copy-start | bytes 2359300
  23.0 21.9 %collective-permute-start.6 = (bf16[2,256,768]{2,1,0:T(8,128)(2,1)S(1)}, bf16[2,256,768]{2,1,0:T(8,128)(2,1)S(1)}, u32[]{:S(2)}, u32[]{:S(2)}) collective-permute-start(bf16[2,256,768]{2,1,0:T(8,128)(2,1)S(1)} %collective-permute-done.3.refs_7_), channel_id=1, source_target_pairs={{0,4},{1,5},{2,6},{3,7},{4,0},{5,1},{6,2},{7,3},{8,12},{9,13},{10,... | collective-permute-start | bytes 2359304 | tf_op jit(solution)/shard_map/ppermute | solution.py:737
  23.1 21.8 %collective-permute-start.5 = (bf16[3,104,576]{2,1,0:T(8,128)(2,1)S(1)}, bf16[3,104,576]{2,1,0:T(8,128)(2,1)S(1)}, u32[]{:S(2)}, u32[]{:S(2)}) collective-permute-start(bf16[3,104,576]{2,1,0:T(8,128)(2,1)S(1)} %pad_maximum_fusion.5), channel_id=1, source_target_pairs={{0,16},{1,17},{2,18},{3,19},{4,20},{5,21},{6,22},{7,23},{8,24},{9,... | collective-permute-start | bytes 1078280 | tf_op jit(solution)/shard_map/ppermute | solution.py:737
  24.7 9.9 %collective-permute-start.9 = (bf16[256,384]{1,0:T(8,128)(2,1)}, bf16[256,384]{1,0:T(8,128)(2,1)S(1)}, u32[]{:S(2)}, u32[]{:S(2)}) collective-permute-start(bf16[256,384]{1,0:T(8,128)(2,1)} %get-tuple-element.134.sm_own), channel_id=1, source_target_pairs={{0,3},{1,2},{2,1},{3,0},{4,7},{5,6},{6,5},{7,4},{8,11},{9,10},{10,... | collective-permute-start | bytes 589832 | tf_op jit(solution)/shard_map/ppermute | solution.py:737
  27.6 17.3 %collective-permute-start.8 = (bf16[256,384]{1,0:T(8,128)(2,1)}, bf16[256,384]{1,0:T(8,128)(2,1)S(1)}, u32[]{:S(2)}, u32[]{:S(2)}) collective-permute-start(bf16[256,384]{1,0:T(8,128)(2,1)} %get-tuple-element.134.sm_own), channel_id=1, source_target_pairs={{0,2},{1,3},{2,0},{3,1},{4,6},{5,7},{6,4},{7,5},{8,10},{9,11},{10,... | collective-permute-start | bytes 589832 | tf_op jit(solution)/shard_map/ppermute | solution.py:737
  27.6 17.3 %collective-permute-start.7 = (bf16[256,384]{1,0:T(8,128)(2,1)}, bf16[256,384]{1,0:T(8,128)(2,1)S(1)}, u32[]{:S(2)}, u32[]{:S(2)}) collective-permute-start(bf16[256,384]{1,0:T(8,128)(2,1)} %get-tuple-element.134.sm_own), channel_id=1, source_target_pairs={{0,1},{1,0},{2,3},{3,2},{4,5},{5,4},{6,7},{7,6},{8,9},{9,8},{10,11... | collective-permute-start | bytes 589832 | tf_op jit(solution)/shard_map/ppermute | solution.py:737
  44.9 6.8 %copy-start.7 = (bf16[2,256,768]{2,1,0:T(8,128)(2,1)}, bf16[2,256,768]{2,1,0:T(8,128)(2,1)S(1)}, u32[]{:S(2)}) copy-start(bf16[2,256,768]{2,1,0:T(8,128)(2,1)S(1)} %collective-permute-done.6.refs_9_) | copy-start | bytes 2359300
  45.7 15.5 %collective-permute-start.10 = (bf16[3,256,384]{2,1,0:T(8,128)(2,1)S(1)}, bf16[3,256,384]{2,1,0:T(8,128)(2,1)S(1)}, u32[]{:S(2)}, u32[]{:S(2)}) collective-permute-start(bf16[3,256,384]{2,1,0:T(8,128)(2,1)S(1)} %pad_maximum_fusion.3), channel_id=1, source_target_pairs={{0,8},{1,9},{2,10},{3,11},{4,20},{5,21},{6,22},{7,23},{8,0},{9,1},... | collective-permute-start | bytes 1769480 | tf_op jit(solution)/shard_map/ppermute | solution.py:737
  47.3 12.9 %collective-permute-start.13 = (bf16[96,768]{1,0:T(8,128)(2,1)}, bf16[96,768]{1,0:T(8,128)(2,1)S(1)}, u32[]{:S(2)}, u32[]{:S(2)}) collective-permute-start(bf16[96,768]{1,0:T(8,128)(2,1)} %get-tuple-element.145), channel_id=1, source_target_pairs={{0,3},{1,2},{2,1},{3,0},{4,7},{5,6},{6,5},{7,4},{8,11},{9,10},{10,... | collective-permute-start | bytes 442376 | tf_op jit(solution)/shard_map/ppermute | solution.py:737
  49.8 11.4 %collective-permute-start.12 = (bf16[96,768]{1,0:T(8,128)(2,1)}, bf16[96,768]{1,0:T(8,128)(2,1)}, u32[]{:S(2)}, u32[]{:S(2)}) collective-permute-start(bf16[96,768]{1,0:T(8,128)(2,1)} %get-tuple-element.145), channel_id=1, source_target_pairs={{0,2},{1,3},{2,0},{3,1},{4,6},{5,7},{6,4},{7,5},{8,10},{9,11},{10,... | collective-permute-start | bytes 442376 | tf_op jit(solution)/shard_map/ppermute | solution.py:737
  49.8 11.4 %collective-permute-start.11 = (bf16[96,768]{1,0:T(8,128)(2,1)}, bf16[96,768]{1,0:T(8,128)(2,1)}, u32[]{:S(2)}, u32[]{:S(2)}) collective-permute-start(bf16[96,768]{1,0:T(8,128)(2,1)} %get-tuple-element.145), channel_id=1, source_target_pairs={{0,1},{1,0},{2,3},{3,2},{4,5},{5,4},{6,7},{7,6},{8,9},{9,8},{10,11... | collective-permute-start | bytes 442376 | tf_op jit(solution)/shard_map/ppermute | solution.py:737
  60.2 1.2 copy-start.19
  61.4 27.9 %copy-start.1 = (bf16[2,3,256,384]{3,2,1,0:T(8,128)(2,1)}, bf16[2,3,256,384]{3,2,1,0:T(8,128)(2,1)S(1)}, u32[]{:S(2)}) copy-start(bf16[2,3,256,384]{3,2,1,0:T(8,128)(2,1)S(1)} %pad_maximum_fusion.s1a) | copy-start | bytes 3538948
  62.9 20.2 %collective-permute-start.14 = (bf16[2,3,256,384]{3,2,1,0:T(8,128)(2,1)S(1)}, bf16[2,3,256,384]{3,2,1,0:T(8,128)(2,1)S(1)}, u32[]{:S(2)}, u32[]{:S(2)}) collective-permute-start(bf16[2,3,256,384]{3,2,1,0:T(8,128)(2,1)S(1)} %pad_maximum_fusion.s1a), channel_id=1, source_target_pairs={{0,16},{1,17},{2,18},{3,19},{4,12},{5,13},{6,14},{7,15},{8,24},{9,... | collective-permute-start | bytes 3538952 | tf_op jit(solution)/shard_map/ppermute | solution.py:737
  63.7 19.4 %collective-permute-start.15 = (bf16[3,96,768]{2,1,0:T(8,128)(2,1)S(1)}, bf16[3,96,768]{2,1,0:T(8,128)(2,1)S(1)}, u32[]{:S(2)}, u32[]{:S(2)}) collective-permute-start(bf16[3,96,768]{2,1,0:T(8,128)(2,1)S(1)} %pad_maximum_fusion.4), channel_id=1, source_target_pairs={{0,8},{1,9},{2,10},{3,11},{4,20},{5,21},{6,22},{7,23},{8,0},{9,1},... | collective-permute-start | bytes 1327112 | tf_op jit(solution)/shard_map/ppermute | solution.py:737
  83.1 1.1 copy-start.9
  84.2 22.0 %copy-start.2 = (bf16[2,3,96,768]{3,2,1,0:T(8,128)(2,1)}, bf16[2,3,96,768]{3,2,1,0:T(8,128)(2,1)S(1)}, u32[]{:S(2)}) copy-start(bf16[2,3,96,768]{3,2,1,0:T(8,128)(2,1)S(1)} %pad_maximum_fusion.1.s1b) | copy-start | bytes 2654212
  84.2 17.6 %collective-permute-start.16 = (bf16[2,3,96,768]{3,2,1,0:T(8,128)(2,1)S(1)}, bf16[2,3,96,768]{3,2,1,0:T(8,128)(2,1)}, u32[]{:S(2)}, u32[]{:S(2)}) collective-permute-start(bf16[2,3,96,768]{3,2,1,0:T(8,128)(2,1)S(1)} %pad_maximum_fusion.1.s1b), channel_id=1, source_target_pairs={{0,16},{1,17},{2,18},{3,19},{4,12},{5,13},{6,14},{7,15},{8,24},{9,... | collective-permute-start | bytes 2654216 | tf_op jit(solution)/shard_map/ppermute | solution.py:737
  85.6 16.2 %all-to-all-start = ((bf16[4,256,384]{2,1,0:T(8,128)(2,1)}), bf16[4,256,384]{2,1,0:T(8,128)(2,1)S(1)}, u32[]{:S(2)}, u32[]{:S(2)}) async-start(bf16[4,256,384]{2,1,0:T(8,128)(2,1)} %get-tuple-element.157.refs_3_), calls=%async_computation | async-start | bytes 1572864 | tf_op jit(solution)/shard_map/all_to_all | solution.py:816
  89.3 14.5 %collective-permute-start.17 = (bf16[2,3,256,384]{3,2,1,0:T(8,128)(2,1)S(1)}, bf16[2,3,256,384]{3,2,1,0:T(8,128)(2,1)}, u32[]{:S(2)}, u32[]{:S(2)}) collective-permute-start(bf16[2,3,256,384]{3,2,1,0:T(8,128)(2,1)S(1)} %pad_maximum_fusion.s1a), channel_id=1, source_target_pairs={{0,4},{1,5},{2,6},{3,7},{4,0},{5,1},{6,2},{7,3},{8,12},{9,13},{10,... | collective-permute-start | bytes 3538952 | tf_op jit(solution)/shard_map/ppermute | solution.py:737
  89.6 14.2 %collective-permute-start.18 = (bf16[2,3,256,384]{3,2,1,0:T(8,128)(2,1)}, bf16[2,3,256,384]{3,2,1,0:T(8,128)(2,1)}, u32[]{:S(2)}, u32[]{:S(2)}) collective-permute-start(bf16[2,3,256,384]{3,2,1,0:T(8,128)(2,1)} %copy-done.9), channel_id=1, source_target_pairs={{0,4},{1,5},{2,6},{3,7},{4,0},{5,1},{6,2},{7,3},{8,12},{9,13},{10,... | collective-permute-start | bytes 3538952 | tf_op jit(solution)/shard_map/ppermute | solution.py:737
  89.9 13.9 %collective-permute-start.19 = (bf16[2,3,96,768]{3,2,1,0:T(8,128)(2,1)S(1)}, bf16[2,3,96,768]{3,2,1,0:T(8,128)(2,1)}, u32[]{:S(2)}, u32[]{:S(2)}) collective-permute-start(bf16[2,3,96,768]{3,2,1,0:T(8,128)(2,1)S(1)} %pad_maximum_fusion.1.s1b), channel_id=1, source_target_pairs={{0,4},{1,5},{2,6},{3,7},{4,0},{5,1},{6,2},{7,3},{8,12},{9,13},{10,... | collective-permute-start | bytes 2654216 | tf_op jit(solution)/shard_map/ppermute | solution.py:737
  101.8 4.3 %copy-start.4 = (bf16[4,256,384]{2,1,0:T(8,128)(2,1)}, bf16[4,256,384]{2,1,0:T(8,128)(2,1)S(1)}, u32[]{:S(2)}) copy-start(bf16[4,256,384]{2,1,0:T(8,128)(2,1)S(1)} %all-to-all-done.attn) | copy-start | bytes 2359300
  101.8 4.3 %collective-permute-start.20 = (bf16[2,3,96,768]{3,2,1,0:T(8,128)(2,1)}, bf16[2,3,96,768]{3,2,1,0:T(8,128)(2,1)}, u32[]{:S(2)}, u32[]{:S(2)}) collective-permute-start(bf16[2,3,96,768]{3,2,1,0:T(8,128)(2,1)} %collective-permute-done.16.r2b), channel_id=1, source_target_pairs={{0,4},{1,5},{2,6},{3,7},{4,0},{5,1},{6,2},{7,3},{8,12},{9,13},{10,... | collective-permute-start | bytes 2654216 | tf_op jit(solution)/shard_map/ppermute | solution.py:737
  134.9 10.0 %collective-permute-start.21 = (bf16[512,5760]{1,0:T(8,128)(2,1)}, bf16[512,5760]{1,0:T(8,128)(2,1)}, u32[]{:S(2)}, u32[]{:S(2)}) collective-permute-start(bf16[512,5760]{1,0:T(8,128)(2,1)} %get-tuple-element.165.sent), channel_id=1, source_target_pairs={{0,4},{1,5},{2,6},{3,7},{4,0},{5,1},{6,2},{7,3},{8,12},{9,13},{10,... | collective-permute-start | bytes 17694728 | tf_op jit(solution)/shard_map/ppermute | solution.py:737
  135.4 20.0 %all-to-all-start.1 = ((bf16[4,256,384]{2,1,0:T(8,128)(2,1)}), bf16[4,256,384]{2,1,0:T(8,128)(2,1)S(1)}, u32[]{:S(2)}, u32[]{:S(2)}) async-start(bf16[4,256,384]{2,1,0:T(8,128)(2,1)} %get-tuple-element.163), calls=%async_computation.1 | async-start | bytes 1572864 | tf_op jit(solution)/shard_map/all_to_all | solution.py:854
  156.3 40.4 %all-to-all-start.2 = ((bf16[4,4,240,384]{3,2,1,0:T(8,128)(2,1)}), bf16[4,4,240,384]{3,2,1,0:T(8,128)(2,1)S(1)}, u32[]{:S(2)}, u32[]{:S(2)}) async-start(bf16[4,4,240,384]{3,2,1,0:T(8,128)(2,1)} %get-tuple-element.170), calls=%async_computation.2 | async-start | bytes 5898240 | tf_op jit(solution)/shard_map/all_to_all | solution.py:897
  160.2 45.0 %collective-permute-start.22 = (bf16[4,96,768]{2,1,0:T(8,128)(2,1)}, bf16[4,96,768]{2,1,0:T(8,128)(2,1)}, u32[]{:S(2)}, u32[]{:S(2)}) collective-permute-start(bf16[4,96,768]{2,1,0:T(8,128)(2,1)} %get-tuple-element.176), channel_id=1, source_target_pairs={{0,1},{1,0},{2,3},{3,2},{4,5},{5,4},{6,7},{7,6},{8,9},{9,8},{10,11... | collective-permute-start | bytes 1769480 | tf_op jit(solution)/shard_map/ppermute | solution.py:737
  160.3 44.9 %collective-permute-start.23 = (bf16[4,96,768]{2,1,0:T(8,128)(2,1)}, bf16[4,96,768]{2,1,0:T(8,128)(2,1)}, u32[]{:S(2)}, u32[]{:S(2)}) collective-permute-start(bf16[4,96,768]{2,1,0:T(8,128)(2,1)} %get-tuple-element.177), channel_id=1, source_target_pairs={{0,2},{1,3},{2,0},{3,1},{4,6},{5,7},{6,4},{7,5},{8,10},{9,11},{10,... | collective-permute-start | bytes 1769480 | tf_op jit(solution)/shard_map/ppermute | solution.py:737
  163.1 42.1 %collective-permute-start.24 = (bf16[4,96,768]{2,1,0:T(8,128)(2,1)}, bf16[4,96,768]{2,1,0:T(8,128)(2,1)}, u32[]{:S(2)}, u32[]{:S(2)}) collective-permute-start(bf16[4,96,768]{2,1,0:T(8,128)(2,1)} %get-tuple-element.178), channel_id=1, source_target_pairs={{0,3},{1,2},{2,1},{3,0},{4,7},{5,6},{6,5},{7,4},{8,11},{9,10},{10,... | collective-permute-start | bytes 1769480 | tf_op jit(solution)/shard_map/ppermute | solution.py:737
  196.6 1.6 copy-start
  198.3 76.1 %all-to-all-start.3 = ((bf16[4,512,768]{2,1,0:T(8,128)(2,1)}), bf16[4,512,768]{2,1,0:T(8,128)(2,1)S(1)}, u32[]{:S(2)}, u32[]{:S(2)}) async-start(bf16[4,512,768]{2,1,0:T(8,128)(2,1)} %get-tuple-element.219), calls=%async_computation.3 | async-start | bytes 6291456 | tf_op jit(solution)/shard_map/all_to_all | solution.py:903
  202.2 15.8 %collective-permute-start.28 = (bf16[4,104,576]{2,1,0:T(8,128)(2,1)}, bf16[4,104,576]{2,1,0:T(8,128)(2,1)S(1)}, u32[]{:S(2)}, u32[]{:S(2)}) collective-permute-start(bf16[4,104,576]{2,1,0:T(8,128)(2,1)} %get-tuple-element.193), channel_id=1, source_target_pairs={{0,16},{1,17},{2,18},{3,19},{4,20},{5,21},{6,22},{7,23},{8,24},{9,... | collective-permute-start | bytes 1437704 | tf_op jit(solution)/shard_map/ppermute | solution.py:737
  205.2 18.5 %collective-permute-start.25 = (bf16[240,384]{1,0:T(8,128)(2,1)}, bf16[240,384]{1,0:T(8,128)(2,1)S(1)}, u32[]{:S(2)}, u32[]{:S(2)}) collective-permute-start(bf16[240,384]{1,0:T(8,128)(2,1)} %get-tuple-element.185), channel_id=1, source_target_pairs={{0,1},{1,0},{2,3},{3,2},{4,5},{5,4},{6,7},{7,6},{8,9},{9,8},{10,11... | collective-permute-start | bytes 552968 | tf_op jit(solution)/shard_map/ppermute | solution.py:737
  215.7 16.6 %collective-permute-start.26 = (bf16[240,384]{1,0:T(8,128)(2,1)}, bf16[240,384]{1,0:T(8,128)(2,1)S(1)}, u32[]{:S(2)}, u32[]{:S(2)}) collective-permute-start(bf16[240,384]{1,0:T(8,128)(2,1)} %get-tuple-element.186), channel_id=1, source_target_pairs={{0,2},{1,3},{2,0},{3,1},{4,6},{5,7},{6,4},{7,5},{8,10},{9,11},{10,... | collective-permute-start | bytes 552968 | tf_op jit(solution)/shard_map/ppermute | solution.py:737
  216.5 15.8 %collective-permute-start.27 = (bf16[240,384]{1,0:T(8,128)(2,1)}, bf16[240,384]{1,0:T(8,128)(2,1)}, u32[]{:S(2)}, u32[]{:S(2)}) collective-permute-start(bf16[240,384]{1,0:T(8,128)(2,1)} %get-tuple-element.187), channel_id=1, source_target_pairs={{0,3},{1,2},{2,1},{3,0},{4,7},{5,6},{6,5},{7,4},{8,11},{9,10},{10,... | collective-permute-start | bytes 552968 | tf_op jit(solution)/shard_map/ppermute | solution.py:737
  223.7 21.1 %copy-start.17 = (bf16[240,384]{1,0:T(8,128)(2,1)}, bf16[240,384]{1,0:T(8,128)(2,1)S(1)}, u32[]{:S(2)}) copy-start(bf16[240,384]{1,0:T(8,128)(2,1)S(1)} %collective-permute-done.25.a1) | copy-start | bytes 552964
  232.3 12.5 %copy-start.18 = (bf16[240,384]{1,0:T(8,128)(2,1)}, bf16[240,384]{1,0:T(8,128)(2,1)S(1)}, u32[]{:S(2)}) copy-start(bf16[240,384]{1,0:T(8,128)(2,1)S(1)} %collective-permute-done.26.a2) | copy-start | bytes 552964
  232.3 10.2 %collective-permute-start.29 = (bf16[96,768]{1,0:T(8,128)(2,1)}, bf16[96,768]{1,0:T(8,128)(2,1)S(1)}, u32[]{:S(2)}, u32[]{:S(2)}) collective-permute-start(bf16[96,768]{1,0:T(8,128)(2,1)} %get-tuple-element.201), channel_id=1, source_target_pairs={{0,8},{1,9},{2,10},{3,11},{4,12},{5,13},{6,14},{7,15},{8,0},{9,1},... | collective-permute-start | bytes 442376 | tf_op jit(solution)/shard_map/ppermute | solution.py:737
  233.5 11.3 %collective-permute-start.30 = (bf16[96,768]{1,0:T(8,128)(2,1)}, bf16[96,768]{1,0:T(8,128)(2,1)S(1)}, u32[]{:S(2)}, u32[]{:S(2)}) collective-permute-start(bf16[96,768]{1,0:T(8,128)(2,1)} %get-tuple-element.202), channel_id=1, source_target_pairs={{0,16},{1,17},{2,18},{3,19},{4,20},{5,21},{6,22},{7,23},{8,24},{9,... | collective-permute-start | bytes 442376 | tf_op jit(solution)/shard_map/ppermute | solution.py:737
  235.0 9.8 %collective-permute-start.31 = (bf16[96,768]{1,0:T(8,128)(2,1)}, bf16[96,768]{1,0:T(8,128)(2,1)S(1)}, u32[]{:S(2)}, u32[]{:S(2)}) collective-permute-start(bf16[96,768]{1,0:T(8,128)(2,1)} %get-tuple-element.203), channel_id=1, source_target_pairs={{0,24},{1,25},{2,26},{3,27},{4,28},{5,29},{6,30},{7,31},{8,16},{9,... | collective-permute-start | bytes 442376 | tf_op jit(solution)/shard_map/ppermute | solution.py:737
  235.8 12.1 %collective-permute-start.32 = (bf16[104,576]{1,0:T(8,128)(2,1)}, bf16[104,576]{1,0:T(8,128)(2,1)}, u32[]{:S(2)}, u32[]{:S(2)}) collective-permute-start(bf16[104,576]{1,0:T(8,128)(2,1)} %get-tuple-element.204), channel_id=1, source_target_pairs={{0,1},{1,0},{2,3},{3,2},{4,5},{5,4},{6,7},{7,6},{8,9},{9,8},{10,11... | collective-permute-start | bytes 359432 | tf_op jit(solution)/shard_map/ppermute | solution.py:737
  238.7 11.2 %collective-permute-start.33 = (bf16[104,576]{1,0:T(8,128)(2,1)}, bf16[104,576]{1,0:T(8,128)(2,1)}, u32[]{:S(2)}, u32[]{:S(2)}) collective-permute-start(bf16[104,576]{1,0:T(8,128)(2,1)} %get-tuple-element.205), channel_id=1, source_target_pairs={{0,2},{1,3},{2,0},{3,1},{4,6},{5,7},{6,4},{7,5},{8,10},{9,11},{10,... | collective-permute-start | bytes 359432 | tf_op jit(solution)/shard_map/ppermute | solution.py:737
  242.5 2.3 copy-start.20
  242.5 7.3 %collective-permute-start.34 = (bf16[104,576]{1,0:T(8,128)(2,1)}, bf16[104,576]{1,0:T(8,128)(2,1)}, u32[]{:S(2)}, u32[]{:S(2)}) collective-permute-start(bf16[104,576]{1,0:T(8,128)(2,1)} %get-tuple-element.206), channel_id=1, source_target_pairs={{0,3},{1,2},{2,1},{3,0},{4,7},{5,6},{6,5},{7,4},{8,11},{9,10},{10,... | collective-permute-start | bytes 359432 | tf_op jit(solution)/shard_map/ppermute | solution.py:737
  249.8 7.3 %collective-permute-start.35 = (bf16[432,384]{1,0:T(8,128)(2,1)}, bf16[432,384]{1,0:T(8,128)(2,1)S(1)}, u32[]{:S(2)}, u32[]{:S(2)}) collective-permute-start(bf16[432,384]{1,0:T(8,128)(2,1)} %sums.1), channel_id=1, source_target_pairs={{0,8},{1,9},{2,10},{3,11},{4,20},{5,21},{6,22},{7,23},{8,0},{9,1},... | collective-permute-start | bytes 995336 | tf_op jit(solution)/shard_map/ppermute | solution.py:737
  259.1 10.6 %collective-permute-start.37 = (bf16[2,432,384]{2,1,0:T(8,128)(2,1)}, bf16[2,432,384]{2,1,0:T(8,128)(2,1)}, u32[]{:S(2)}, u32[]{:S(2)}) collective-permute-start(bf16[2,432,384]{2,1,0:T(8,128)(2,1)} %pad_maximum_fusion.2.s1), channel_id=1, source_target_pairs={{0,4},{1,5},{2,6},{3,7},{4,0},{5,1},{6,2},{7,3},{8,12},{9,13},{10,... | collective-permute-start | bytes 1990664 | tf_op jit(solution)/shard_map/ppermute | solution.py:737
  259.1 12.7 %collective-permute-start.36 = (bf16[2,432,384]{2,1,0:T(8,128)(2,1)}, bf16[2,432,384]{2,1,0:T(8,128)(2,1)}, u32[]{:S(2)}, u32[]{:S(2)}) collective-permute-start(bf16[2,432,384]{2,1,0:T(8,128)(2,1)} %pad_maximum_fusion.2.s1), channel_id=1, source_target_pairs={{0,16},{1,17},{2,18},{3,19},{4,12},{5,13},{6,14},{7,15},{8,24},{9,... | collective-permute-start | bytes 1990664 | tf_op jit(solution)/shard_map/ppermute | solution.py:737
  262.4 7.3 %collective-permute-start.38 = (bf16[208,384]{1,0:T(8,128)(2,1)}, bf16[208,384]{1,0:T(8,128)(2,1)S(1)}, u32[]{:S(2)}, u32[]{:S(2)}) collective-permute-start(bf16[208,384]{1,0:T(8,128)(2,1)} %sumsq.1), channel_id=1, source_target_pairs={{0,8},{1,9},{2,10},{3,11},{4,20},{5,21},{6,22},{7,23},{8,0},{9,1},... | collective-permute-start | bytes 479240 | tf_op jit(solution)/shard_map/ppermute | solution.py:737
  271.8 5.3 %collective-permute-start.39 = (bf16[2,432,384]{2,1,0:T(8,128)(2,1)}, bf16[2,432,384]{2,1,0:T(8,128)(2,1)}, u32[]{:S(2)}, u32[]{:S(2)}) collective-permute-start(bf16[2,432,384]{2,1,0:T(8,128)(2,1)} %collective-permute-done.36.r2), channel_id=1, source_target_pairs={{0,4},{1,5},{2,6},{3,7},{4,0},{5,1},{6,2},{7,3},{8,12},{9,13},{10,... | collective-permute-start | bytes 1990664 | tf_op jit(solution)/shard_map/ppermute | solution.py:737
  272.7 4.3 %copy-start.8 = (bf16[2,208,384]{2,1,0:T(8,128)(2,1)}, bf16[2,208,384]{2,1,0:T(8,128)(2,1)S(1)}, u32[]{:S(2)}) copy-start(bf16[2,208,384]{2,1,0:T(8,128)(2,1)S(1)} %pad_maximum_fusion.6.s1) | copy-start | bytes 958468
  272.7 8.7 %collective-permute-start.40 = (bf16[2,208,384]{2,1,0:T(8,128)(2,1)S(1)}, bf16[2,208,384]{2,1,0:T(8,128)(2,1)}, u32[]{:S(2)}, u32[]{:S(2)}) collective-permute-start(bf16[2,208,384]{2,1,0:T(8,128)(2,1)S(1)} %pad_maximum_fusion.6.s1), channel_id=1, source_target_pairs={{0,16},{1,17},{2,18},{3,19},{4,12},{5,13},{6,14},{7,15},{8,24},{9,... | collective-permute-start | bytes 958472 | tf_op jit(solution)/shard_map/ppermute | solution.py:737
  277.1 4.9 %collective-permute-start.41 = (bf16[2,208,384]{2,1,0:T(8,128)(2,1)S(1)}, bf16[2,208,384]{2,1,0:T(8,128)(2,1)S(1)}, u32[]{:S(2)}, u32[]{:S(2)}) collective-permute-start(bf16[2,208,384]{2,1,0:T(8,128)(2,1)S(1)} %pad_maximum_fusion.6.s1), channel_id=1, source_target_pairs={{0,4},{1,5},{2,6},{3,7},{4,0},{5,1},{6,2},{7,3},{8,12},{9,13},{10,... | collective-permute-start | bytes 958472 | tf_op jit(solution)/shard_map/ppermute | solution.py:737
  281.5 2.0 collective-permute-start.42
  282.0 1.5 copy-start.15
  (6 other events, 4.5 us)

commit v6 on v5

--- a/solution.py
+++ b/solution.py
@@ -19,6 +19,7 @@
 ANY = pl.BlockSpec(memory_space=pl.ANY)
 OFFS = (0, 2, 1, 3)
 VMEM_LIMIT = 60 * 2**20
+GQ = 112
 
 
 def mm(a, b):
@@ -68,21 +69,23 @@
             w_own[0:192, 448:512] = wv[:, a + 128 : a + 192]
             w_own[0:192, 512:576] = wk[:, a + 128 : a + 192]
 
-    bq, bv = (v[...].reshape(1, 192) for v in vecs[:2])
-    w_own[192:200, :] = jnp.zeros((8, 576), BF)
-    w_own[192:193, 0:128] = bq[:, 0:128]
-    w_own[192:193, 256:384] = bv[:, 0:128]
-    w_own[192:193, 384:448] = bq[:, 128:192]
-    w_own[192:193, 448:512] = bv[:, 128:192]
+    row = lax.broadcasted_iota(jnp.int32, (16, 576), 0)
+    bq, bv = (v[...].astype(F32).reshape(1, 192) for v in vecs[:2])
+    none = jnp.zeros((1, 128), F32)
+    bias = jnp.concatenate([bq[:, :128], none, bv[:, :128], bq[:, 128:], bv[:, 128:], none[:, :64]], axis=1)
+    w_own[192:208, :] = jnp.where(row == 0, jnp.broadcast_to(bias, (16, 576)), 0.0).astype(BF)
     pack[0:96, :] = w_own[pl.ds(pl.multiple_of(y * 96, 16), 96), :]
-    pack[96:104, :] = w_own[192:200, :]
+    pack[96:112, :] = w_own[192:208, :]
     piece1[0:192, :] = w_in[:, pl.ds(pl.multiple_of(p * FB, 128), FB)]
     piece1[192:240, :] = w_at[pl.ds(pl.multiple_of((p // 2) * 48, 16), 48), pl.ds(pl.multiple_of(c * FB, 128), FB)]
-    piece1[240:256, :] = jnp.zeros((16, FB), BF)
-    for i, v in enumerate(vecs[:8]):
-        piece1[240 + i : 241 + i, 0:192] = v[...].reshape(1, 192)
-    for i in range(4):
-        piece1[248 + i : 249 + i, 0:192] = vecs[8][i * 192 : (i + 1) * 192].reshape(1, 192)
+    row = lax.broadcasted_iota(jnp.int32, (16, FB), 0)
+    long = vecs[8][...].astype(F32).reshape(1, 768)
+    small = [v[...].astype(F32).reshape(1, 192) for v in vecs[:8]] + [long[:, i * 192 : (i + 1) * 192] for i in range(4)]
+    tall = jnp.zeros((16, FB), F32)
+    for i, v in enumerate(small):
+        v = jnp.concatenate([v, jnp.zeros((1, FB - 192), F32)], axis=1)
+        tall = jnp.where(row == i, jnp.broadcast_to(v, (16, FB)), tall)
+    piece1[240:256, :] = tall.astype(BF)
     piece2[...] = w_out[pl.ds(pl.multiple_of(c * FB + (p // 2) * 96, 16), 96), :]
 
 
@@ -90,10 +93,10 @@
     toks, (w_own, w_z1, w_z2, w_z3, w_y, q_out, k_out, v_out, w, bs, sem) = refs[:4], refs[4:]
     z, c, y, mine = idx[1], idx[2], idx[3], idx[5]
     T, D = toks[0].shape[2:]
-    copies = [(w_own.at[0:192], w.at[z]), (w_own.at[192:200], bs.at[0])]
+    copies = [(w_own.at[0:192], w.at[z]), (w_own.at[192:208], bs.at[0])]
     for k, ref in enumerate((w_z1, w_z2, w_z3)):
         copies.append((ref.at[0:96], w.at[z ^ (k + 1), pl.ds(pl.multiple_of(y * 96, 16), 96)]))
-        copies.append((ref.at[96:104], bs.at[k + 1]))
+        copies.append((ref.at[96:112], bs.at[k + 1]))
         copies.append((w_y.at[k, 0:96], w.at[z ^ (k + 1), pl.ds(pl.multiple_of((1 - y) * 96, 16), 96)]))
     copies = [pltpu.make_async_copy(a, b, sem.at[i]) for i, (a, b) in enumerate(copies)]
     for cp in copies:
@@ -106,7 +109,7 @@
     rel = lane & 63
     zero64 = jnp.zeros((T, 64), F32)
 
-    bias = bs[c ^ z, 0:1, :].astype(F32)
+    bias = bs[c ^ z].astype(F32)[0:1]
     for g in range(pg):
         for n, off in enumerate(OFFS):
             place = pl.multiple_of((g * 4 + (c ^ off)) * T, T)
@@ -316,10 +319,11 @@
     top = lax.broadcasted_iota(jnp.int32, (8, 576), 0) == 0
     for k in range(4):
         z = zw ^ k
-        tail = jnp.where(top & (h == z), col, extra[z]).astype(BF)
+        tail = jnp.where(top & (h == z), col, extra[z])
+        tail = jnp.concatenate([tail, jnp.zeros_like(tail)], axis=0).astype(BF)
         for ref, yy in ((gq_own, y), (gq_other, 1 - y)):
             ref[k, 0:96, :] = acc[pl.ds(pl.multiple_of(z * 192 + yy * 96, 8), 96), :].astype(BF)
-            ref[k, 96:104, :] = tail
+            ref[k, 96:GQ, :] = tail
 
 
 def gelu_parts(u):
@@ -391,12 +395,14 @@
     for cp in first_copies:
         cp.wait()
 
+    small = [sm[k ^ z].astype(F32) for k in range(4)]
+
     def whole(i):
-        return jnp.concatenate([sm[k ^ z, i : i + 1, 0:192].astype(F32) for k in range(4)], axis=1)
+        return jnp.concatenate([v[i : i + 1, 0:192] for v in small], axis=1)
 
     b_attn, g1v, s1v, b_out, g2v, s2v = (whole(i) for i in range(2, 8))
     for k in range(4):
-        row = jnp.concatenate([sm[k ^ z, i : i + 1, 0:192].astype(F32) for i in range(8, 12)], axis=1)
+        row = jnp.concatenate([small[k][i : i + 1, 0:192] for i in range(8, 12)], axis=1)
         for half in range(2):
             b1[2 * k + half, 0:1, :] = row[:, half * FB : (half + 1) * FB]
 
@@ -660,15 +666,15 @@
     c, z = idx[0], idx[1]
     refs = (s1, r2, c1, c2)
     lower = lax.broadcasted_iota(jnp.int32, (96, 128), 1) < 64
-    left, right = jnp.zeros((8, FB), F32), jnp.zeros((8, FB), F32)
-    top = lax.broadcasted_iota(jnp.int32, (8, FB), 0) == 0
+    left, right = jnp.zeros((16, FB), F32), jnp.zeros((16, FB), F32)
+    top = lax.broadcasted_iota(jnp.int32, (16, FB), 0) == 0
     for (n, k), (m, j) in (((0, 0), (2, 0)), ((0, 1), (3, 0)), ((1, 0), (2, 1)), ((1, 1), (3, 1))):
         p = idx[6 + 2 * n + k]
         yy, xx = p // 4, (p // 2) % 2
         own, other = refs[n].at[k], refs[m].at[j]
 
         def tile(i, swap):
-            at = slice(0, 96) if i < 3 else slice(104, 200)
+            at = slice(0, 96) if i < 3 else slice(GQ, GQ + 96)
             cols = slice((i % 3) * 128, (i % 3 + 1) * 128)
             u, v = own[at, cols].astype(F32), other[at, cols].astype(F32)
             return jnp.where((c == 0) != swap, u, v)
@@ -687,8 +693,8 @@
             ref[rows, pl.ds(pl.multiple_of(base + 256, 128), 128)] = jnp.where(lower, turned, tb)
         for ref, cc in ((own, c), (other, 1 - c)):
             here = (yy == 0) & (~top | (xx * 2 + cc == z))
-            left = left + jnp.where(here, ref[96:104, :].astype(F32), 0.0)
-            right = right + jnp.where(here, ref[200:208, :].astype(F32), 0.0)
+            left = left + jnp.where(here, ref[96:GQ, :].astype(F32), 0.0)
+            right = right + jnp.where(here, ref[GQ + 96 : 2 * GQ, :].astype(F32), 0.0)
     g_bq[...] = jnp.concatenate([left[0:1, 0:128], right[0:1, 0:64]], axis=1).reshape(192)
     g_bv[...] = jnp.concatenate([left[0:1, 256:384], right[0:1, 64:128]], axis=1).reshape(192)
     for i, ref in enumerate(six):
@@ -770,7 +776,7 @@
         w_own, pack, piece1, piece2 = call(
             prep_kernel,
             (
-                jax.ShapeDtypeStruct((200, 576), BF), jax.ShapeDtypeStruct((104, 576), BF),
+                jax.ShapeDtypeStruct((208, 576), BF), jax.ShapeDtypeStruct((GQ, 576), BF),
                 jax.ShapeDtypeStruct((256, FB), BF), jax.ShapeDtypeStruct((96, D), BF),
             ),
             [SM] + [VM] * 15, (VM,) * 4, name="prep",
@@ -796,7 +802,7 @@
             (own_head, head, head, jax.ShapeDtypeStruct((4, 192, 576), BF)),
             [SM, SM] + [VM] * 4 + [ANY] * 5,
             (VM,) * 4,
-            [pltpu.VMEM((4, 8, 576), BF), pltpu.SemaphoreType.DMA((11,))],
+            [pltpu.VMEM((4, 16, 576), BF), pltpu.SemaphoreType.DMA((11,))],
             name="qkv",
         )(lengths, idx, *toks, w_own, *w_z, w_y)
         w_qkv = w_qkv.reshape(D, 576)
@@ -860,7 +866,7 @@
             return jax.ShapeDtypeStruct((*n, m), F32), *(jax.ShapeDtypeStruct((*n, m), BF),) * 3
 
         def attn_back(d_o):
-            part = jax.ShapeDtypeStruct((4, 104, 576), BF)
+            part = jax.ShapeDtypeStruct((4, GQ, 576), BF)
             outs = (part, part, jax.ShapeDtypeStruct((4, R, D), BF))
             more = (w_qkv, tokens, tok_x, tok_c, tok_xc, extra)
             total = pltpu.VMEM((D + 8, 576), F32)
@@ -901,7 +907,7 @@
         sent1, got_z2 = tie(sent1, got_z2)
         got_z1 = over_z(sent1)
         gi = lax.all_to_all(gi, ("x", "core"), 0, 0, tiled=True)
-        cq, *sentq = call(chunkq_kernel, shares((104,), 576), [VM] * 2, (VM,) * 4, name="chunksq")(gq_own, gq_y)
+        cq, *sentq = call(chunkq_kernel, shares((GQ,), 576), [VM] * 2, (VM,) * 4, name="chunksq")(gq_own, gq_y)
         p2, *sent2 = call(sum2_kernel, shares((96,), D), [SM] + [VM] * 4, (VM,) * 4, name="sums2")(idx, c2, *got_z2)
         sent2, got_z1, sentq = tie(sent2, got_z1, sentq)
         got_zq = over_z(sentq)
@@ -909,7 +915,7 @@
 
         total = call(sum_kernel, jax.ShapeDtypeStruct((432, FB), BF), [VM] * 8, VM, name="sums")(c1, *got_z1, p2, *got_p2)
         total, got_zq = tie(total, got_zq)
-        total_q = call(sumq_kernel, jax.ShapeDtypeStruct((208, FB), BF), [VM] * 4, VM, name="sumsq")(cq, *got_zq)
+        total_q = call(sumq_kernel, jax.ShapeDtypeStruct((2 * GQ, FB), BF), [VM] * 4, VM, name="sumsq")(cq, *got_zq)
         if pg > 1:
             total, total_q = (lax.psum(v.astype(F32), "pg").astype(BF) for v in (total, total_q))
 

time: 288 us -> 289 us (level)
    unnamed x46 -> x44, local copies, waits for them, and re-layouts: 6.53 us -> 6.52 us
  transfers between devices with their start and end apart: 47 -> 47, of which waited for: 15 -> 16; matrix products, arithmetic and copies ran while one was open for 2% -> 2% of each run, Pallas kernels for 31% -> 31%
where the time goes in v6:
time: 289 us; the launch traced here: 288 us
  Pallas kernels  120 us (42%)
  waiting for transfers between devices  79.1 us (27%)
  starting transfers between devices  72.9 us (25%)
  other arithmetic  7.5 us (3%)
  local copies, waits for them, and re-layouts  7.2 us (2%)
    ppermute x43, waiting for transfers between devices, send(): return lax.ppermute(a, AX, pairs)  67.4 us
    ppermute x43, starting transfers between devices, send(): return lax.ppermute(a, AX, pairs)  57.9 us
    pallas_call x1, Pallas kernels, attn_back(): call(functools.partial(attn_bwd_kernel, pg, 512), outs if pg == 1 else (j...  32 us
    pallas_call x1, Pallas kernels, body(): call(ffn_kernel, (jax.ShapeDtypeStruct((R, D), BF), jax.ShapeDtypeStruct(...  28.7 us
    pallas_call x1, Pallas kernels, body(): call(functools.partial(attn_fwd_kernel, 1024), (jax.ShapeDtypeStruct((4,...  18.1 us
    all_to_all x1, waiting for transfers between devices, body(): attn = lax.all_to_all(o, ('x', 'core'), 0, 0, tiled=True)  11.8 us
    pallas_call x1, Pallas kernels, body(): call(weight_kernel, (jax.ShapeDtypeStruct((4, 4, 240, FB), BF), jax.Shape...  10.4 us
    pallas_call x1, Pallas kernels, body(): call(functools.partial(qkv_kernel, pg), (own_head, head, head, jax.ShapeD...  8.41 us
  transfers between devices with their start and end apart: 47, of which 16 were waited for; matrix products, arithmetic and copies ran while one was open for 2% of the time, Pallas kernels for 31%

profile of v6, /device:TPU:0, one launch (start us, length us, event | category | flops | bytes accessed | tf_op | source)
XLA Modules:
  0.0 287.9 jit_solution(13825681803157372224)
XLA Ops:
  1.2 2.6 collective-permute-start.3
  4.4 3.0 %prep.1 = (bf16[208,576]{1,0:T(8,128)(2,1)}, bf16[112,576]{1,0:T(8,128)(2,1)}, bf16[256,384]{1,0:T(8,128)(2,1)}, bf16[96,768]{1,0:T(8,128)(2,1)}) custom-call(s32[14]{0:T(128)} %stack.128.idx, bf16[192,768]{1,0:T(8,128)(2,1)} %wq.1, bf16[192,768]{1,0:T(8,128)(2,1)} %wk.1, bf16[192,768]{1,0:T(8,128)(2,1)} %wv.1, bf16[192,768]{1,0:T(8,128)(2,1)} %w_at.3, ...), custom_call_target="tpu_custom_call" | custom-call | flops 1 | bytes 1 | tf_op jit(solution)/shard_map/prep/pallas_call | solution.py:776
  7.5 3.6 %collective-permute-start.2 = (bf16[112,576]{1,0:T(8,128)(2,1)}, bf16[112,576]{1,0:T(8,128)(2,1)S(1)}, u32[]{:S(2)}, u32[]{:S(2)}) collective-permute-start(bf16[112,576]{1,0:T(8,128)(2,1)} %get-tuple-element.127), channel_id=1, source_target_pairs={{0,3},{1,2},{2,1},{3,0},{4,7},{5,6},{6,5},{7,4},{8,11},{9,10},{10,... | collective-permute-start | bytes 387080 | tf_op jit(solution)/shard_map/ppermute | solution.py:743
  11.8 4.3 %collective-permute-done.2.refs_7_ = bf16[112,576]{1,0:T(8,128)(2,1)S(1)} collective-permute-done((bf16[112,576]{1,0:T(8,128)(2,1)}, bf16[112,576]{1,0:T(8,128)(2,1)S(1)}, u32[]{:S(2)}, u32[]{:S(2)}) %collective-permute-start.2) | collective-permute-done | bytes 129056 | tf_op jit(solution)/shard_map/ppermute | solution.py:743
  16.2 7.7 %collective-permute-done.1.refs_6_ = bf16[112,576]{1,0:T(8,128)(2,1)S(1)} collective-permute-done((bf16[112,576]{1,0:T(8,128)(2,1)}, bf16[112,576]{1,0:T(8,128)(2,1)S(1)}, u32[]{:S(2)}, u32[]{:S(2)}) %collective-permute-start.1) | collective-permute-done | bytes 129056 | tf_op jit(solution)/shard_map/ppermute | solution.py:743
  24.0 1.6 collective-permute-start.5
  25.6 2.5 collective-permute-start.9
  28.1 1.9 collective-permute-start.7
  30.0 5.5 %collective-permute-done.9 = bf16[256,384]{1,0:T(8,128)(2,1)S(1)} collective-permute-done((bf16[256,384]{1,0:T(8,128)(2,1)}, bf16[256,384]{1,0:T(8,128)(2,1)S(1)}, u32[]{:S(2)}, u32[]{:S(2)}) %collective-permute-start.9) | collective-permute-done | bytes 196640 | tf_op jit(solution)/shard_map/ppermute | solution.py:743
  35.5 9.4 %collective-permute-done.8 = bf16[256,384]{1,0:T(8,128)(2,1)S(1)} collective-permute-done((bf16[256,384]{1,0:T(8,128)(2,1)}, bf16[256,384]{1,0:T(8,128)(2,1)S(1)}, u32[]{:S(2)}, u32[]{:S(2)}) %collective-permute-start.8) | collective-permute-done | bytes 196640 | tf_op jit(solution)/shard_map/ppermute | solution.py:743
  45.8 1.6 collective-permute-start.10
  47.3 2.5 collective-permute-start.13
  49.8 1.9 collective-permute-start.11
  51.7 8.4 %qkv.1 = (bf16[2,3,1024,128]{3,2,1,0:T(8,128)(2,1)}, bf16[2,3,1024,128]{3,2,1,0:T(8,128)(2,1)}, bf16[2,3,1024,128]{3,2,1,0:T(8,128)(2,1)}, bf16[4,192,576]{2,1,0:T(8,128)(2,1)}) custom-call(s32[2,4]{1,0:T(2,128)} %lengths.7, s32[14]{0:T(128)} %stack.128.idx, bf16[1,2,256,768]{3,2,1,0:T(8,128)(2,1)} %bitcast.59, bf16[1,2,256,768]{3,2,1,0:T(8,128)(2,1)} %bitcast.62, ...), custom_call_target="tpu_custom_call" | custom-call | flops 1 | bytes 1 | tf_op jit(solution)/shard_map/qkv/pallas_call | solution.py:800
  60.2 1.1 collective-permute-done.12
  61.4 1.5 pad_maximum_fusion.4
  63.7 1.3 collective-permute-start.15
  65.0 18.1 %attn_fwd.1 = (bf16[4,256,384]{2,1,0:T(8,128)(2,1)}, bf16[2,3,1024,128]{3,2,1,0:T(8,128)(2,1)}) custom-call(s32[2,4]{1,0:T(2,128)} %lengths.7, s32[14]{0:T(128)} %stack.128.idx, bf16[2,3,1024,128]{3,2,1,0:T(8,128)(2,1)} %get-tuple-element.151.q_ref, bf16[2,3,1024,128]{3,2,1,0:T(8,128)(2,1)} %get-tuple-element.152.k_ref.refs_1_, ...), custom_call_target="tpu_custom_call" | custom-call | flops 1 | bytes 1 | tf_op jit(solution)/shard_map/attn_fwd/pallas_call | solution.py:813
  83.1 1.0 copy-done.9
  84.2 1.4 collective-permute-start.16
  85.6 3.7 %all-to-all-start = ((bf16[4,256,384]{2,1,0:T(8,128)(2,1)}), bf16[4,256,384]{2,1,0:T(8,128)(2,1)S(1)}, u32[]{:S(2)}, u32[]{:S(2)}) async-start(bf16[4,256,384]{2,1,0:T(8,128)(2,1)} %get-tuple-element.157.refs_3_), calls=%async_computation | async-start | bytes 1572864 | tf_op jit(solution)/shard_map/all_to_all | solution.py:822
  90.1 11.8 %all-to-all-done.attn = bf16[4,256,384]{2,1,0:T(8,128)(2,1)S(1)} async-done(((bf16[4,256,384]{2,1,0:T(8,128)(2,1)}), bf16[4,256,384]{2,1,0:T(8,128)(2,1)S(1)}, u32[]{:S(2)}, u32[]{:S(2)}) %all-to-all-start) | async-done | bytes 786464 | tf_op jit(solution)/shard_map/all_to_all | solution.py:822
  101.9 1.9 collective-permute-start.20
  103.8 2.4 collective-permute-done.20.c2b
  106.2 28.7 %ffn.1 = (bf16[512,768]{1,0:T(8,128)(2,1)}, f32[512,768]{1,0:T(8,128)}, bf16[4,256,384]{2,1,0:T(8,128)(2,1)}, bf16[512,5760]{1,0:T(8,128)(2,1)}, bf16[512,3456]{1,0:T(8,128)(2,1)}, /*index=5*/f32[4,8,576]{2,1,0:T(8,128)}) custom-call(s32[14]{0:T(128)} %stack.128.idx, s32[2,4]{1,0:T(2,128)} %lengths.7, bf16[4,256,384]{2,1,0:T(8,128)(2,1)} %copy-done.7, ...), custom_call_target="tpu_custom_call" | custom-call | flops 1 | bytes 1 | tf_op jit(solution)/shard_map/ffn/pallas_call | solution.py:829
  135.4 3.5 %all-to-all-start.1 = ((bf16[4,256,384]{2,1,0:T(8,128)(2,1)}), bf16[4,256,384]{2,1,0:T(8,128)(2,1)S(1)}, u32[]{:S(2)}, u32[]{:S(2)}) async-start(bf16[4,256,384]{2,1,0:T(8,128)(2,1)} %get-tuple-element.163), calls=%async_computation.1 | async-start | bytes 1572864 | tf_op jit(solution)/shard_map/all_to_all | solution.py:860
  138.9 6.1 %collective-permute-done.21.mate = bf16[512,5760]{1,0:T(8,128)(2,1)} collective-permute-done((bf16[512,5760]{1,0:T(8,128)(2,1)}, bf16[512,5760]{1,0:T(8,128)(2,1)}, u32[]{:S(2)}, u32[]{:S(2)}) %collective-permute-start.21) | collective-permute-done | bytes 5898272 | tf_op jit(solution)/shard_map/ppermute | solution.py:743
  144.9 10.4 %weights.1 = (bf16[4,4,240,384]{3,2,1,0:T(8,128)(2,1)}, f32[4,96,768]{2,1,0:T(8,128)}, bf16[4,96,768]{2,1,0:T(8,128)(2,1)}, bf16[4,96,768]{2,1,0:T(8,128)(2,1)}, bf16[4,96,768]{2,1,0:T(8,128)(2,1)}) custom-call(s32[14]{0:T(128)} %stack.128.idx, bf16[512,3456]{1,0:T(8,128)(2,1)} %get-tuple-element.164.kept, bf16[512,5760]{1,0:T(8,128)(2,1)} %collective-permute-done.21.mate, ...), custom_call_target="tpu_custom_call" | custom-call | flops 1 | bytes 1 | tf_op jit(solution)/shard_map/weights/pallas_call | solution.py:890
  155.4 0.9 copy-done.6
  156.3 3.9 %all-to-all-start.2 = ((bf16[4,4,240,384]{3,2,1,0:T(8,128)(2,1)}), bf16[4,4,240,384]{3,2,1,0:T(8,128)(2,1)S(1)}, u32[]{:S(2)}, u32[]{:S(2)}) async-start(bf16[4,4,240,384]{3,2,1,0:T(8,128)(2,1)} %get-tuple-element.170), calls=%async_computation.2 | async-start | bytes 5898240 | tf_op jit(solution)/shard_map/all_to_all | solution.py:903
  160.2 2.8 collective-permute-start.23
  163.1 1.6 collective-permute-start.24
  164.6 32.0 %attn_bwd.1 = (bf16[4,112,576]{2,1,0:T(8,128)(2,1)}, bf16[4,112,576]{2,1,0:T(8,128)(2,1)}, bf16[4,512,768]{2,1,0:T(8,128)(2,1)}) custom-call(s32[2,4]{1,0:T(2,128)} %lengths.7, s32[14]{0:T(128)} %stack.128.idx, bf16[2,3,1024,128]{3,2,1,0:T(8,128)(2,1)} %get-tuple-element.188.refs_0_, bf16[2,3,1024,128]{3,2,1,0:T(8,128)(2,1)} %get-tuple-element.152.k_ref.refs_1_, ...), custom_call_target="tpu_custom_call" | custom-call | flops 1 | bytes 1 | tf_op jit(solution)/shard_map/attn_bwd/pallas_call | solution.py:873
  196.6 1.6 copy-done
  198.3 4.0 %all-to-all-start.3 = ((bf16[4,512,768]{2,1,0:T(8,128)(2,1)}), bf16[4,512,768]{2,1,0:T(8,128)(2,1)S(1)}, u32[]{:S(2)}, u32[]{:S(2)}) async-start(bf16[4,512,768]{2,1,0:T(8,128)(2,1)} %get-tuple-element.219), calls=%async_computation.3 | async-start | bytes 6291456 | tf_op jit(solution)/shard_map/all_to_all | solution.py:909
  202.2 1.8 collective-permute-start.28
  204.0 2.9 %chunks1.1 = (f32[240,384]{1,0:T(8,128)}, bf16[240,384]{1,0:T(8,128)(2,1)}, bf16[240,384]{1,0:T(8,128)(2,1)}, bf16[240,384]{1,0:T(8,128)(2,1)}) custom-call(s32[14]{0:T(128)} %stack.128.idx, bf16[4,4,240,384]{3,2,1,0:T(8,128)(2,1)} %copy-done), custom_call_target="tpu_custom_call" | custom-call | flops 1 | bytes 1 | tf_op jit(solution)/shard_map/chunks1/pallas_call | solution.py:906
  206.9 8.8 %collective-permute-start.25 = (bf16[240,384]{1,0:T(8,128)(2,1)}, bf16[240,384]{1,0:T(8,128)(2,1)S(1)}, u32[]{:S(2)}, u32[]{:S(2)}) collective-permute-start(bf16[240,384]{1,0:T(8,128)(2,1)} %get-tuple-element.185), channel_id=1, source_target_pairs={{0,1},{1,0},{2,3},{3,2},{4,5},{5,4},{6,7},{7,6},{8,9},{9,8},{10,11... | collective-permute-start | bytes 552968 | tf_op jit(solution)/shard_map/ppermute | solution.py:743
  216.5 1.6 collective-permute-start.27
  218.8 2.1 chunksq.1
  220.9 2.8 sums2.1
  223.7 8.5 %collective-permute-done.26.a2 = bf16[240,384]{1,0:T(8,128)(2,1)S(1)} collective-permute-done((bf16[240,384]{1,0:T(8,128)(2,1)}, bf16[240,384]{1,0:T(8,128)(2,1)S(1)}, u32[]{:S(2)}, u32[]{:S(2)}) %collective-permute-start.26) | collective-permute-done | bytes 184352 | tf_op jit(solution)/shard_map/ppermute | solution.py:743
  232.2 1.2 collective-permute-start.29
  233.5 1.5 collective-permute-start.30
  235.7 2.9 %collective-permute-start.32 = (bf16[112,576]{1,0:T(8,128)(2,1)}, bf16[112,576]{1,0:T(8,128)(2,1)}, u32[]{:S(2)}, u32[]{:S(2)}) collective-permute-start(bf16[112,576]{1,0:T(8,128)(2,1)} %get-tuple-element.204), channel_id=1, source_target_pairs={{0,1},{1,0},{2,3},{3,2},{4,5},{5,4},{6,7},{7,6},{8,9},{9,8},{10,11... | collective-permute-start | bytes 387080 | tf_op jit(solution)/shard_map/ppermute | solution.py:743
  239.4 3.0 %collective-permute-done.29.b1 = bf16[96,768]{1,0:T(8,128)(2,1)S(1)} collective-permute-done((bf16[96,768]{1,0:T(8,128)(2,1)}, bf16[96,768]{1,0:T(8,128)(2,1)S(1)}, u32[]{:S(2)}, u32[]{:S(2)}) %collective-permute-start.29) | collective-permute-done | bytes 147488 | tf_op jit(solution)/shard_map/ppermute | solution.py:743
  242.5 2.3 collective-permute-start.34
  244.8 1.6 collective-permute-done.31.b3
  247.0 2.3 sums.1
  249.3 1.1 collective-permute-done.33.q2
  250.5 0.8 collective-permute-start.35
  251.3 6.5 %collective-permute-done.35 = bf16[432,384]{1,0:T(8,128)(2,1)S(1)} collective-permute-done((bf16[432,384]{1,0:T(8,128)(2,1)}, bf16[432,384]{1,0:T(8,128)(2,1)S(1)}, u32[]{:S(2)}, u32[]{:S(2)}) %collective-permute-start.35) | collective-permute-done | bytes 331808 | tf_op jit(solution)/shard_map/ppermute | solution.py:743
  257.8 1.9 pad_maximum_fusion.2.s1
  259.7 1.4 collective-permute-start.36
  261.1 1.9 sumsq.1
  262.9 0.9 collective-permute-start.38
  263.9 6.6 %collective-permute-done.38 = bf16[224,384]{1,0:T(8,128)(2,1)S(1)} collective-permute-done((bf16[224,384]{1,0:T(8,128)(2,1)}, bf16[224,384]{1,0:T(8,128)(2,1)S(1)}, u32[]{:S(2)}, u32[]{:S(2)}) %collective-permute-start.38) | collective-permute-done | bytes 172064 | tf_op jit(solution)/shard_map/ppermute | solution.py:743
  270.5 2.1 collective-permute-done.36.r2
  272.5 1.0 pad_maximum_fusion.6.s1
  273.5 1.4 collective-permute-start.40
  274.9 2.7 fusion
  277.7 4.4 %out_ffn.1 = (f32[192,3072]{1,0:T(8,128)}, f32[192,768]{1,0:T(8,128)}, f32[768,768]{1,0:T(8,128)}) custom-call(s32[14]{0:T(128)} %stack.128.idx, bf16[2,432,384]{2,1,0:T(8,128)(2,1)} %pad_maximum_fusion.2.s1, bf16[2,432,384]{2,1,0:T(8,128)(2,1)} %collective-permute-done.36.r2, bf16[2,432,384]{2,1,0:T(8,128)(2,1)} %collective-permute-done.37.c1, ...), custom_call_target="tpu_custom_call" | custom-call | flops 1 | bytes 1 | tf_op jit(solution)/shard_map/out_ffn/pallas_call | solution.py:931
  282.6 1.5 collective-permute-done.42.c2
  284.8 2.9 out_qkv.1
  (96 shorter events, 10.5 us)
Async XLA Ops:
  0.7 23.2 %collective-permute-start.4 = (bf16[2,256,768]{2,1,0:T(8,128)(2,1)}, bf16[2,256,768]{2,1,0:T(8,128)(2,1)S(1)}, u32[]{:S(2)}, u32[]{:S(2)}) collective-permute-start(bf16[2,256,768]{2,1,0:T(8,128)(2,1)} %refs_6_.1), channel_id=1, source_target_pairs={{0,4},{1,5},{2,6},{3,7},{4,0},{5,1},{6,2},{7,3},{8,12},{9,13},{10,... | collective-permute-start | bytes 2359304 | tf_op jit(solution)/shard_map/ppermute | solution.py:743
  1.2 22.7 %collective-permute-start.3 = (bf16[2,256,768]{2,1,0:T(8,128)(2,1)}, bf16[2,256,768]{2,1,0:T(8,128)(2,1)S(1)}, u32[]{:S(2)}, u32[]{:S(2)}) collective-permute-start(bf16[2,256,768]{2,1,0:T(8,128)(2,1)} %refs_6_.1), channel_id=1, source_target_pairs={{0,8},{1,9},{2,10},{3,11},{4,12},{5,13},{6,14},{7,15},{8,0},{9,1},... | collective-permute-start | bytes 2359304 | tf_op jit(solution)/shard_map/ppermute | solution.py:743
  7.5 8.7 %collective-permute-start.2 = (bf16[112,576]{1,0:T(8,128)(2,1)}, bf16[112,576]{1,0:T(8,128)(2,1)S(1)}, u32[]{:S(2)}, u32[]{:S(2)}) collective-permute-start(bf16[112,576]{1,0:T(8,128)(2,1)} %get-tuple-element.127), channel_id=1, source_target_pairs={{0,3},{1,2},{2,1},{3,0},{4,7},{5,6},{6,5},{7,4},{8,11},{9,10},{10,... | collective-permute-start | bytes 387080 | tf_op jit(solution)/shard_map/ppermute | solution.py:743
  11.1 12.8 %collective-permute-start.1 = (bf16[112,576]{1,0:T(8,128)(2,1)}, bf16[112,576]{1,0:T(8,128)(2,1)S(1)}, u32[]{:S(2)}, u32[]{:S(2)}) collective-permute-start(bf16[112,576]{1,0:T(8,128)(2,1)} %get-tuple-element.127), channel_id=1, source_target_pairs={{0,2},{1,3},{2,0},{3,1},{4,6},{5,7},{6,4},{7,5},{8,10},{9,11},{10,... | collective-permute-start | bytes 387080 | tf_op jit(solution)/shard_map/ppermute | solution.py:743
  11.1 12.8 %collective-permute-start = (bf16[112,576]{1,0:T(8,128)(2,1)}, bf16[112,576]{1,0:T(8,128)(2,1)S(1)}, u32[]{:S(2)}, u32[]{:S(2)}) collective-permute-start(bf16[112,576]{1,0:T(8,128)(2,1)} %get-tuple-element.127), channel_id=1, source_target_pairs={{0,1},{1,0},{2,3},{3,2},{4,5},{5,4},{6,7},{7,6},{8,9},{9,8},{10,11... | collective-permute-start | bytes 387080 | tf_op jit(solution)/shard_map/ppermute | solution.py:743
  16.2 35.6 %copy-start.11 = (bf16[112,576]{1,0:T(8,128)(2,1)}, bf16[112,576]{1,0:T(8,128)(2,1)S(1)}, u32[]{:S(2)}) copy-start(bf16[112,576]{1,0:T(8,128)(2,1)S(1)} %collective-permute-done.2.refs_7_) | copy-start | bytes 387076
  23.8 27.9 %copy-start.12 = (bf16[112,576]{1,0:T(8,128)(2,1)}, bf16[112,576]{1,0:T(8,128)(2,1)S(1)}, u32[]{:S(2)}) copy-start(bf16[112,576]{1,0:T(8,128)(2,1)S(1)} %collective-permute-done.1.refs_6_) | copy-start | bytes 387076
  23.8 27.9 %copy-start.13 = (bf16[112,576]{1,0:T(8,128)(2,1)}, bf16[112,576]{1,0:T(8,128)(2,1)S(1)}, u32[]{:S(2)}) copy-start(bf16[112,576]{1,0:T(8,128)(2,1)S(1)} %collective-permute-done.refs_5_) | copy-start | bytes 387076
  23.8 27.9 %copy-start.3 = (bf16[2,256,768]{2,1,0:T(8,128)(2,1)}, bf16[2,256,768]{2,1,0:T(8,128)(2,1)S(1)}, u32[]{:S(2)}) copy-start(bf16[2,256,768]{2,1,0:T(8,128)(2,1)S(1)} %collective-permute-done.4.refs_8_) | copy-start | bytes 2359300
  23.9 27.9 %copy-start.4 = (bf16[2,256,768]{2,1,0:T(8,128)(2,1)}, bf16[2,256,768]{2,1,0:T(8,128)(2,1)S(1)}, u32[]{:S(2)}) copy-start(bf16[2,256,768]{2,1,0:T(8,128)(2,1)S(1)} %collective-permute-done.3.refs_7_) | copy-start | bytes 2359300
  23.9 21.1 %collective-permute-start.6 = (bf16[2,256,768]{2,1,0:T(8,128)(2,1)S(1)}, bf16[2,256,768]{2,1,0:T(8,128)(2,1)S(1)}, u32[]{:S(2)}, u32[]{:S(2)}) collective-permute-start(bf16[2,256,768]{2,1,0:T(8,128)(2,1)S(1)} %collective-permute-done.3.refs_7_), channel_id=1, source_target_pairs={{0,4},{1,5},{2,6},{3,7},{4,0},{5,1},{6,2},{7,3},{8,12},{9,13},{10,... | collective-permute-start | bytes 2359304 | tf_op jit(solution)/shard_map/ppermute | solution.py:743
  24.0 20.9 %collective-permute-start.5 = (bf16[3,112,576]{2,1,0:T(8,128)(2,1)S(1)}, bf16[3,112,576]{2,1,0:T(8,128)(2,1)S(1)}, u32[]{:S(2)}, u32[]{:S(2)}) collective-permute-start(bf16[3,112,576]{2,1,0:T(8,128)(2,1)S(1)} %pad_maximum_fusion.5), channel_id=1, source_target_pairs={{0,16},{1,17},{2,18},{3,19},{4,20},{5,21},{6,22},{7,23},{8,24},{9,... | collective-permute-start | bytes 1161224 | tf_op jit(solution)/shard_map/ppermute | solution.py:743
  25.6 9.9 %collective-permute-start.9 = (bf16[256,384]{1,0:T(8,128)(2,1)}, bf16[256,384]{1,0:T(8,128)(2,1)S(1)}, u32[]{:S(2)}, u32[]{:S(2)}) collective-permute-start(bf16[256,384]{1,0:T(8,128)(2,1)} %get-tuple-element.134.sm_own), channel_id=1, source_target_pairs={{0,3},{1,2},{2,1},{3,0},{4,7},{5,6},{6,5},{7,4},{8,11},{9,10},{10,... | collective-permute-start | bytes 589832 | tf_op jit(solution)/shard_map/ppermute | solution.py:743
  28.1 16.8 %collective-permute-start.8 = (bf16[256,384]{1,0:T(8,128)(2,1)}, bf16[256,384]{1,0:T(8,128)(2,1)S(1)}, u32[]{:S(2)}, u32[]{:S(2)}) collective-permute-start(bf16[256,384]{1,0:T(8,128)(2,1)} %get-tuple-element.134.sm_own), channel_id=1, source_target_pairs={{0,2},{1,3},{2,0},{3,1},{4,6},{5,7},{6,4},{7,5},{8,10},{9,11},{10,... | collective-permute-start | bytes 589832 | tf_op jit(solution)/shard_map/ppermute | solution.py:743
  28.1 16.8 %collective-permute-start.7 = (bf16[256,384]{1,0:T(8,128)(2,1)}, bf16[256,384]{1,0:T(8,128)(2,1)S(1)}, u32[]{:S(2)}, u32[]{:S(2)}) collective-permute-start(bf16[256,384]{1,0:T(8,128)(2,1)} %get-tuple-element.134.sm_own), channel_id=1, source_target_pairs={{0,1},{1,0},{2,3},{3,2},{4,5},{5,4},{6,7},{7,6},{8,9},{9,8},{10,11... | collective-permute-start | bytes 589832 | tf_op jit(solution)/shard_map/ppermute | solution.py:743
  44.9 6.8 %copy-start.5 = (bf16[2,256,768]{2,1,0:T(8,128)(2,1)}, bf16[2,256,768]{2,1,0:T(8,128)(2,1)S(1)}, u32[]{:S(2)}) copy-start(bf16[2,256,768]{2,1,0:T(8,128)(2,1)S(1)} %collective-permute-done.6.refs_9_) | copy-start | bytes 2359300
  45.8 15.5 %collective-permute-start.10 = (bf16[3,256,384]{2,1,0:T(8,128)(2,1)S(1)}, bf16[3,256,384]{2,1,0:T(8,128)(2,1)S(1)}, u32[]{:S(2)}, u32[]{:S(2)}) collective-permute-start(bf16[3,256,384]{2,1,0:T(8,128)(2,1)S(1)} %pad_maximum_fusion.3), channel_id=1, source_target_pairs={{0,8},{1,9},{2,10},{3,11},{4,20},{5,21},{6,22},{7,23},{8,0},{9,1},... | collective-permute-start | bytes 1769480 | tf_op jit(solution)/shard_map/ppermute | solution.py:743
  47.3 12.8 %collective-permute-start.13 = (bf16[96,768]{1,0:T(8,128)(2,1)}, bf16[96,768]{1,0:T(8,128)(2,1)}, u32[]{:S(2)}, u32[]{:S(2)}) collective-permute-start(bf16[96,768]{1,0:T(8,128)(2,1)} %get-tuple-element.145), channel_id=1, source_target_pairs={{0,3},{1,2},{2,1},{3,0},{4,7},{5,6},{6,5},{7,4},{8,11},{9,10},{10,... | collective-permute-start | bytes 442376 | tf_op jit(solution)/shard_map/ppermute | solution.py:743
  49.8 11.4 %collective-permute-start.12 = (bf16[96,768]{1,0:T(8,128)(2,1)}, bf16[96,768]{1,0:T(8,128)(2,1)}, u32[]{:S(2)}, u32[]{:S(2)}) collective-permute-start(bf16[96,768]{1,0:T(8,128)(2,1)} %get-tuple-element.145), channel_id=1, source_target_pairs={{0,2},{1,3},{2,0},{3,1},{4,6},{5,7},{6,4},{7,5},{8,10},{9,11},{10,... | collective-permute-start | bytes 442376 | tf_op jit(solution)/shard_map/ppermute | solution.py:743
  49.8 11.4 %collective-permute-start.11 = (bf16[96,768]{1,0:T(8,128)(2,1)}, bf16[96,768]{1,0:T(8,128)(2,1)}, u32[]{:S(2)}, u32[]{:S(2)}) collective-permute-start(bf16[96,768]{1,0:T(8,128)(2,1)} %get-tuple-element.145), channel_id=1, source_target_pairs={{0,1},{1,0},{2,3},{3,2},{4,5},{5,4},{6,7},{7,6},{8,9},{9,8},{10,11... | collective-permute-start | bytes 442376 | tf_op jit(solution)/shard_map/ppermute | solution.py:743
  61.4 27.9 %copy-start.1 = (bf16[2,3,256,384]{3,2,1,0:T(8,128)(2,1)}, bf16[2,3,256,384]{3,2,1,0:T(8,128)(2,1)S(1)}, u32[]{:S(2)}) copy-start(bf16[2,3,256,384]{3,2,1,0:T(8,128)(2,1)S(1)} %pad_maximum_fusion.s1a) | copy-start | bytes 3538948
  62.9 20.2 %collective-permute-start.14 = (bf16[2,3,256,384]{3,2,1,0:T(8,128)(2,1)S(1)}, bf16[2,3,256,384]{3,2,1,0:T(8,128)(2,1)S(1)}, u32[]{:S(2)}, u32[]{:S(2)}) collective-permute-start(bf16[2,3,256,384]{3,2,1,0:T(8,128)(2,1)S(1)} %pad_maximum_fusion.s1a), channel_id=1, source_target_pairs={{0,16},{1,17},{2,18},{3,19},{4,12},{5,13},{6,14},{7,15},{8,24},{9,... | collective-permute-start | bytes 3538952 | tf_op jit(solution)/shard_map/ppermute | solution.py:743
  63.7 19.4 %collective-permute-start.15 = (bf16[3,96,768]{2,1,0:T(8,128)(2,1)S(1)}, bf16[3,96,768]{2,1,0:T(8,128)(2,1)S(1)}, u32[]{:S(2)}, u32[]{:S(2)}) collective-permute-start(bf16[3,96,768]{2,1,0:T(8,128)(2,1)S(1)} %pad_maximum_fusion.4), channel_id=1, source_target_pairs={{0,8},{1,9},{2,10},{3,11},{4,20},{5,21},{6,22},{7,23},{8,0},{9,1},... | collective-permute-start | bytes 1327112 | tf_op jit(solution)/shard_map/ppermute | solution.py:743
  83.1 1.1 copy-start.9
  84.2 22.0 %copy-start.2 = (bf16[2,3,96,768]{3,2,1,0:T(8,128)(2,1)}, bf16[2,3,96,768]{3,2,1,0:T(8,128)(2,1)S(1)}, u32[]{:S(2)}) copy-start(bf16[2,3,96,768]{3,2,1,0:T(8,128)(2,1)S(1)} %pad_maximum_fusion.1.s1b) | copy-start | bytes 2654212
  84.2 17.6 %collective-permute-start.16 = (bf16[2,3,96,768]{3,2,1,0:T(8,128)(2,1)S(1)}, bf16[2,3,96,768]{3,2,1,0:T(8,128)(2,1)}, u32[]{:S(2)}, u32[]{:S(2)}) collective-permute-start(bf16[2,3,96,768]{3,2,1,0:T(8,128)(2,1)S(1)} %pad_maximum_fusion.1.s1b), channel_id=1, source_target_pairs={{0,16},{1,17},{2,18},{3,19},{4,12},{5,13},{6,14},{7,15},{8,24},{9,... | collective-permute-start | bytes 2654216 | tf_op jit(solution)/shard_map/ppermute | solution.py:743
  85.6 16.3 %all-to-all-start = ((bf16[4,256,384]{2,1,0:T(8,128)(2,1)}), bf16[4,256,384]{2,1,0:T(8,128)(2,1)S(1)}, u32[]{:S(2)}, u32[]{:S(2)}) async-start(bf16[4,256,384]{2,1,0:T(8,128)(2,1)} %get-tuple-element.157.refs_3_), calls=%async_computation | async-start | bytes 1572864 | tf_op jit(solution)/shard_map/all_to_all | solution.py:822
  89.3 14.5 %collective-permute-start.17 = (bf16[2,3,256,384]{3,2,1,0:T(8,128)(2,1)S(1)}, bf16[2,3,256,384]{3,2,1,0:T(8,128)(2,1)}, u32[]{:S(2)}, u32[]{:S(2)}) collective-permute-start(bf16[2,3,256,384]{3,2,1,0:T(8,128)(2,1)S(1)} %pad_maximum_fusion.s1a), channel_id=1, source_target_pairs={{0,4},{1,5},{2,6},{3,7},{4,0},{5,1},{6,2},{7,3},{8,12},{9,13},{10,... | collective-permute-start | bytes 3538952 | tf_op jit(solution)/shard_map/ppermute | solution.py:743
  89.6 14.2 %collective-permute-start.18 = (bf16[2,3,256,384]{3,2,1,0:T(8,128)(2,1)}, bf16[2,3,256,384]{3,2,1,0:T(8,128)(2,1)}, u32[]{:S(2)}, u32[]{:S(2)}) collective-permute-start(bf16[2,3,256,384]{3,2,1,0:T(8,128)(2,1)} %copy-done.9), channel_id=1, source_target_pairs={{0,4},{1,5},{2,6},{3,7},{4,0},{5,1},{6,2},{7,3},{8,12},{9,13},{10,... | collective-permute-start | bytes 3538952 | tf_op jit(solution)/shard_map/ppermute | solution.py:743
  89.9 13.9 %collective-permute-start.19 = (bf16[2,3,96,768]{3,2,1,0:T(8,128)(2,1)S(1)}, bf16[2,3,96,768]{3,2,1,0:T(8,128)(2,1)}, u32[]{:S(2)}, u32[]{:S(2)}) collective-permute-start(bf16[2,3,96,768]{3,2,1,0:T(8,128)(2,1)S(1)} %pad_maximum_fusion.1.s1b), channel_id=1, source_target_pairs={{0,4},{1,5},{2,6},{3,7},{4,0},{5,1},{6,2},{7,3},{8,12},{9,13},{10,... | collective-permute-start | bytes 2654216 | tf_op jit(solution)/shard_map/ppermute | solution.py:743
  101.9 4.3 %copy-start.7 = (bf16[4,256,384]{2,1,0:T(8,128)(2,1)}, bf16[4,256,384]{2,1,0:T(8,128)(2,1)S(1)}, u32[]{:S(2)}) copy-start(bf16[4,256,384]{2,1,0:T(8,128)(2,1)S(1)} %all-to-all-done.attn) | copy-start | bytes 2359300
  101.9 4.3 %collective-permute-start.20 = (bf16[2,3,96,768]{3,2,1,0:T(8,128)(2,1)}, bf16[2,3,96,768]{3,2,1,0:T(8,128)(2,1)}, u32[]{:S(2)}, u32[]{:S(2)}) collective-permute-start(bf16[2,3,96,768]{3,2,1,0:T(8,128)(2,1)} %collective-permute-done.16.r2b), channel_id=1, source_target_pairs={{0,4},{1,5},{2,6},{3,7},{4,0},{5,1},{6,2},{7,3},{8,12},{9,13},{10,... | collective-permute-start | bytes 2654216 | tf_op jit(solution)/shard_map/ppermute | solution.py:743
  134.9 10.0 %collective-permute-start.21 = (bf16[512,5760]{1,0:T(8,128)(2,1)}, bf16[512,5760]{1,0:T(8,128)(2,1)}, u32[]{:S(2)}, u32[]{:S(2)}) collective-permute-start(bf16[512,5760]{1,0:T(8,128)(2,1)} %get-tuple-element.165.sent), channel_id=1, source_target_pairs={{0,4},{1,5},{2,6},{3,7},{4,0},{5,1},{6,2},{7,3},{8,12},{9,13},{10,... | collective-permute-start | bytes 17694728 | tf_op jit(solution)/shard_map/ppermute | solution.py:743
  135.4 20.0 %all-to-all-start.1 = ((bf16[4,256,384]{2,1,0:T(8,128)(2,1)}), bf16[4,256,384]{2,1,0:T(8,128)(2,1)S(1)}, u32[]{:S(2)}, u32[]{:S(2)}) async-start(bf16[4,256,384]{2,1,0:T(8,128)(2,1)} %get-tuple-element.163), calls=%async_computation.1 | async-start | bytes 1572864 | tf_op jit(solution)/shard_map/all_to_all | solution.py:860
  156.3 40.4 %all-to-all-start.2 = ((bf16[4,4,240,384]{3,2,1,0:T(8,128)(2,1)}), bf16[4,4,240,384]{3,2,1,0:T(8,128)(2,1)S(1)}, u32[]{:S(2)}, u32[]{:S(2)}) async-start(bf16[4,4,240,384]{3,2,1,0:T(8,128)(2,1)} %get-tuple-element.170), calls=%async_computation.2 | async-start | bytes 5898240 | tf_op jit(solution)/shard_map/all_to_all | solution.py:903
  160.2 46.7 %collective-permute-start.22 = (bf16[4,96,768]{2,1,0:T(8,128)(2,1)}, bf16[4,96,768]{2,1,0:T(8,128)(2,1)}, u32[]{:S(2)}, u32[]{:S(2)}) collective-permute-start(bf16[4,96,768]{2,1,0:T(8,128)(2,1)} %get-tuple-element.176), channel_id=1, source_target_pairs={{0,1},{1,0},{2,3},{3,2},{4,5},{5,4},{6,7},{7,6},{8,9},{9,8},{10,11... | collective-permute-start | bytes 1769480 | tf_op jit(solution)/shard_map/ppermute | solution.py:743
  160.2 46.6 %collective-permute-start.23 = (bf16[4,96,768]{2,1,0:T(8,128)(2,1)}, bf16[4,96,768]{2,1,0:T(8,128)(2,1)}, u32[]{:S(2)}, u32[]{:S(2)}) collective-permute-start(bf16[4,96,768]{2,1,0:T(8,128)(2,1)} %get-tuple-element.177), channel_id=1, source_target_pairs={{0,2},{1,3},{2,0},{3,1},{4,6},{5,7},{6,4},{7,5},{8,10},{9,11},{10,... | collective-permute-start | bytes 1769480 | tf_op jit(solution)/shard_map/ppermute | solution.py:743
  163.1 43.8 %collective-permute-start.24 = (bf16[4,96,768]{2,1,0:T(8,128)(2,1)}, bf16[4,96,768]{2,1,0:T(8,128)(2,1)}, u32[]{:S(2)}, u32[]{:S(2)}) collective-permute-start(bf16[4,96,768]{2,1,0:T(8,128)(2,1)} %get-tuple-element.178), channel_id=1, source_target_pairs={{0,3},{1,2},{2,1},{3,0},{4,7},{5,6},{6,5},{7,4},{8,11},{9,10},{10,... | collective-permute-start | bytes 1769480 | tf_op jit(solution)/shard_map/ppermute | solution.py:743
  196.6 1.6 copy-start
  198.3 76.7 %all-to-all-start.3 = ((bf16[4,512,768]{2,1,0:T(8,128)(2,1)}), bf16[4,512,768]{2,1,0:T(8,128)(2,1)S(1)}, u32[]{:S(2)}, u32[]{:S(2)}) async-start(bf16[4,512,768]{2,1,0:T(8,128)(2,1)} %get-tuple-element.219), calls=%async_computation.3 | async-start | bytes 6291456 | tf_op jit(solution)/shard_map/all_to_all | solution.py:909
  202.2 15.8 %collective-permute-start.28 = (bf16[4,112,576]{2,1,0:T(8,128)(2,1)}, bf16[4,112,576]{2,1,0:T(8,128)(2,1)S(1)}, u32[]{:S(2)}, u32[]{:S(2)}) collective-permute-start(bf16[4,112,576]{2,1,0:T(8,128)(2,1)} %get-tuple-element.193), channel_id=1, source_target_pairs={{0,16},{1,17},{2,18},{3,19},{4,20},{5,21},{6,22},{7,23},{8,24},{9,... | collective-permute-start | bytes 1548296 | tf_op jit(solution)/shard_map/ppermute | solution.py:743
  206.9 16.8 %collective-permute-start.25 = (bf16[240,384]{1,0:T(8,128)(2,1)}, bf16[240,384]{1,0:T(8,128)(2,1)S(1)}, u32[]{:S(2)}, u32[]{:S(2)}) collective-permute-start(bf16[240,384]{1,0:T(8,128)(2,1)} %get-tuple-element.185), channel_id=1, source_target_pairs={{0,1},{1,0},{2,3},{3,2},{4,5},{5,4},{6,7},{7,6},{8,9},{9,8},{10,11... | collective-permute-start | bytes 552968 | tf_op jit(solution)/shard_map/ppermute | solution.py:743
  215.7 16.6 %collective-permute-start.26 = (bf16[240,384]{1,0:T(8,128)(2,1)}, bf16[240,384]{1,0:T(8,128)(2,1)S(1)}, u32[]{:S(2)}, u32[]{:S(2)}) collective-permute-start(bf16[240,384]{1,0:T(8,128)(2,1)} %get-tuple-element.186), channel_id=1, source_target_pairs={{0,2},{1,3},{2,0},{3,1},{4,6},{5,7},{6,4},{7,5},{8,10},{9,11},{10,... | collective-permute-start | bytes 552968 | tf_op jit(solution)/shard_map/ppermute | solution.py:743
  216.5 15.8 %collective-permute-start.27 = (bf16[240,384]{1,0:T(8,128)(2,1)}, bf16[240,384]{1,0:T(8,128)(2,1)}, u32[]{:S(2)}, u32[]{:S(2)}) collective-permute-start(bf16[240,384]{1,0:T(8,128)(2,1)} %get-tuple-element.187), channel_id=1, source_target_pairs={{0,3},{1,2},{2,1},{3,0},{4,7},{5,6},{6,5},{7,4},{8,11},{9,10},{10,... | collective-permute-start | bytes 552968 | tf_op jit(solution)/shard_map/ppermute | solution.py:743
  223.7 22.6 %copy-start.17 = (bf16[240,384]{1,0:T(8,128)(2,1)}, bf16[240,384]{1,0:T(8,128)(2,1)S(1)}, u32[]{:S(2)}) copy-start(bf16[240,384]{1,0:T(8,128)(2,1)S(1)} %collective-permute-done.25.a1) | copy-start | bytes 552964
  232.2 14.1 %copy-start.18 = (bf16[240,384]{1,0:T(8,128)(2,1)}, bf16[240,384]{1,0:T(8,128)(2,1)S(1)}, u32[]{:S(2)}) copy-start(bf16[240,384]{1,0:T(8,128)(2,1)S(1)} %collective-permute-done.26.a2) | copy-start | bytes 552964
  232.2 10.2 %collective-permute-start.29 = (bf16[96,768]{1,0:T(8,128)(2,1)}, bf16[96,768]{1,0:T(8,128)(2,1)S(1)}, u32[]{:S(2)}, u32[]{:S(2)}) collective-permute-start(bf16[96,768]{1,0:T(8,128)(2,1)} %get-tuple-element.201), channel_id=1, source_target_pairs={{0,8},{1,9},{2,10},{3,11},{4,12},{5,13},{6,14},{7,15},{8,0},{9,1},... | collective-permute-start | bytes 442376 | tf_op jit(solution)/shard_map/ppermute | solution.py:743
  233.5 11.3 %collective-permute-start.30 = (bf16[96,768]{1,0:T(8,128)(2,1)}, bf16[96,768]{1,0:T(8,128)(2,1)S(1)}, u32[]{:S(2)}, u32[]{:S(2)}) collective-permute-start(bf16[96,768]{1,0:T(8,128)(2,1)} %get-tuple-element.202), channel_id=1, source_target_pairs={{0,16},{1,17},{2,18},{3,19},{4,20},{5,21},{6,22},{7,23},{8,24},{9,... | collective-permute-start | bytes 442376 | tf_op jit(solution)/shard_map/ppermute | solution.py:743
  234.9 11.4 %collective-permute-start.31 = (bf16[96,768]{1,0:T(8,128)(2,1)}, bf16[96,768]{1,0:T(8,128)(2,1)S(1)}, u32[]{:S(2)}, u32[]{:S(2)}) collective-permute-start(bf16[96,768]{1,0:T(8,128)(2,1)} %get-tuple-element.203), channel_id=1, source_target_pairs={{0,24},{1,25},{2,26},{3,27},{4,28},{5,29},{6,30},{7,31},{8,16},{9,... | collective-permute-start | bytes 442376 | tf_op jit(solution)/shard_map/ppermute | solution.py:743
  235.7 13.6 %collective-permute-start.32 = (bf16[112,576]{1,0:T(8,128)(2,1)}, bf16[112,576]{1,0:T(8,128)(2,1)}, u32[]{:S(2)}, u32[]{:S(2)}) collective-permute-start(bf16[112,576]{1,0:T(8,128)(2,1)} %get-tuple-element.204), channel_id=1, source_target_pairs={{0,1},{1,0},{2,3},{3,2},{4,5},{5,4},{6,7},{7,6},{8,9},{9,8},{10,11... | collective-permute-start | bytes 387080 | tf_op jit(solution)/shard_map/ppermute | solution.py:743
  238.6 11.8 %collective-permute-start.33 = (bf16[112,576]{1,0:T(8,128)(2,1)}, bf16[112,576]{1,0:T(8,128)(2,1)}, u32[]{:S(2)}, u32[]{:S(2)}) collective-permute-start(bf16[112,576]{1,0:T(8,128)(2,1)} %get-tuple-element.205), channel_id=1, source_target_pairs={{0,2},{1,3},{2,0},{3,1},{4,6},{5,7},{6,4},{7,5},{8,10},{9,11},{10,... | collective-permute-start | bytes 387080 | tf_op jit(solution)/shard_map/ppermute | solution.py:743
  242.5 3.8 %copy-start.19 = (bf16[96,768]{1,0:T(8,128)(2,1)}, bf16[96,768]{1,0:T(8,128)(2,1)S(1)}, u32[]{:S(2)}) copy-start(bf16[96,768]{1,0:T(8,128)(2,1)S(1)} %collective-permute-done.29.b1) | copy-start | bytes 442372
  242.5 8.0 %collective-permute-start.34 = (bf16[112,576]{1,0:T(8,128)(2,1)}, bf16[112,576]{1,0:T(8,128)(2,1)}, u32[]{:S(2)}, u32[]{:S(2)}) collective-permute-start(bf16[112,576]{1,0:T(8,128)(2,1)} %get-tuple-element.206), channel_id=1, source_target_pairs={{0,3},{1,2},{2,1},{3,0},{4,7},{5,6},{6,5},{7,4},{8,11},{9,10},{10,... | collective-permute-start | bytes 387080 | tf_op jit(solution)/shard_map/ppermute | solution.py:743
  244.8 1.6 copy-start.20
  250.5 7.3 %collective-permute-start.35 = (bf16[432,384]{1,0:T(8,128)(2,1)}, bf16[432,384]{1,0:T(8,128)(2,1)S(1)}, u32[]{:S(2)}, u32[]{:S(2)}) collective-permute-start(bf16[432,384]{1,0:T(8,128)(2,1)} %sums.1), channel_id=1, source_target_pairs={{0,8},{1,9},{2,10},{3,11},{4,20},{5,21},{6,22},{7,23},{8,0},{9,1},... | collective-permute-start | bytes 995336 | tf_op jit(solution)/shard_map/ppermute | solution.py:743
  259.7 10.8 %collective-permute-start.37 = (bf16[2,432,384]{2,1,0:T(8,128)(2,1)}, bf16[2,432,384]{2,1,0:T(8,128)(2,1)}, u32[]{:S(2)}, u32[]{:S(2)}) collective-permute-start(bf16[2,432,384]{2,1,0:T(8,128)(2,1)} %pad_maximum_fusion.2.s1), channel_id=1, source_target_pairs={{0,4},{1,5},{2,6},{3,7},{4,0},{5,1},{6,2},{7,3},{8,12},{9,13},{10,... | collective-permute-start | bytes 1990664 | tf_op jit(solution)/shard_map/ppermute | solution.py:743
  259.7 12.8 %collective-permute-start.36 = (bf16[2,432,384]{2,1,0:T(8,128)(2,1)}, bf16[2,432,384]{2,1,0:T(8,128)(2,1)}, u32[]{:S(2)}, u32[]{:S(2)}) collective-permute-start(bf16[2,432,384]{2,1,0:T(8,128)(2,1)} %pad_maximum_fusion.2.s1), channel_id=1, source_target_pairs={{0,16},{1,17},{2,18},{3,19},{4,12},{5,13},{6,14},{7,15},{8,24},{9,... | collective-permute-start | bytes 1990664 | tf_op jit(solution)/shard_map/ppermute | solution.py:743
  262.9 7.5 %collective-permute-start.38 = (bf16[224,384]{1,0:T(8,128)(2,1)}, bf16[224,384]{1,0:T(8,128)(2,1)S(1)}, u32[]{:S(2)}, u32[]{:S(2)}) collective-permute-start(bf16[224,384]{1,0:T(8,128)(2,1)} %sumsq.1), channel_id=1, source_target_pairs={{0,8},{1,9},{2,10},{3,11},{4,20},{5,21},{6,22},{7,23},{8,0},{9,1},... | collective-permute-start | bytes 516104 | tf_op jit(solution)/shard_map/ppermute | solution.py:743
  272.5 5.1 %collective-permute-start.39 = (bf16[2,432,384]{2,1,0:T(8,128)(2,1)}, bf16[2,432,384]{2,1,0:T(8,128)(2,1)}, u32[]{:S(2)}, u32[]{:S(2)}) collective-permute-start(bf16[2,432,384]{2,1,0:T(8,128)(2,1)} %collective-permute-done.36.r2), channel_id=1, source_target_pairs={{0,4},{1,5},{2,6},{3,7},{4,0},{5,1},{6,2},{7,3},{8,12},{9,13},{10,... | collective-permute-start | bytes 1990664 | tf_op jit(solution)/shard_map/ppermute | solution.py:743
  273.5 4.2 %copy-start.8 = (bf16[2,224,384]{2,1,0:T(8,128)(2,1)}, bf16[2,224,384]{2,1,0:T(8,128)(2,1)S(1)}, u32[]{:S(2)}) copy-start(bf16[2,224,384]{2,1,0:T(8,128)(2,1)S(1)} %pad_maximum_fusion.6.s1) | copy-start | bytes 1032196
  273.5 8.6 %collective-permute-start.40 = (bf16[2,224,384]{2,1,0:T(8,128)(2,1)S(1)}, bf16[2,224,384]{2,1,0:T(8,128)(2,1)}, u32[]{:S(2)}, u32[]{:S(2)}) collective-permute-start(bf16[2,224,384]{2,1,0:T(8,128)(2,1)S(1)} %pad_maximum_fusion.6.s1), channel_id=1, source_target_pairs={{0,16},{1,17},{2,18},{3,19},{4,12},{5,13},{6,14},{7,15},{8,24},{9,... | collective-permute-start | bytes 1032200 | tf_op jit(solution)/shard_map/ppermute | solution.py:743
  277.7 4.9 %collective-permute-start.41 = (bf16[2,224,384]{2,1,0:T(8,128)(2,1)S(1)}, bf16[2,224,384]{2,1,0:T(8,128)(2,1)S(1)}, u32[]{:S(2)}, u32[]{:S(2)}) collective-permute-start(bf16[2,224,384]{2,1,0:T(8,128)(2,1)S(1)} %pad_maximum_fusion.6.s1), channel_id=1, source_target_pairs={{0,4},{1,5},{2,6},{3,7},{4,0},{5,1},{6,2},{7,3},{8,12},{9,13},{10,... | collective-permute-start | bytes 1032200 | tf_op jit(solution)/shard_map/ppermute | solution.py:743
  282.1 2.0 collective-permute-start.42
  282.6 1.5 copy-start.15
  (5 other events, 3.9 us)

commit v7 on v6

--- a/solution.py
+++ b/solution.py
@@ -919,12 +919,14 @@
         if pg > 1:
             total, total_q = (lax.psum(v.astype(F32), "pg").astype(BF) for v in (total, total_q))
 
-        mate, mate_q = mix_a(total), mix_a(total_q)
+        mate = mix_a(total)
+        mate, total_q = tie(mate, total_q)
+        mate_q = mix_a(total_q)
         s1 = jnp.stack([total, mate])
         r2, s1_core = mix_b(s1), to_core(s1)
-        r2, s1_core, mate_q = tie(r2, s1_core, mate_q)
         s1_q = jnp.stack([total_q, mate_q])
         r2_q = mix_b(s1_q)
+        r2, s1_core, s1_q = tie(r2, s1_core, s1_q)
         grad_input = add(d_first, *(gi[k] for k in range(4))).astype(BF).reshape(tokens.shape)
         mat, wide = jax.ShapeDtypeStruct((192, D), F32), jax.ShapeDtypeStruct((192, 8 * FB), F32)
         vec, long_vec = jax.ShapeDtypeStruct((192,), F32), jax.ShapeDtypeStruct((2 * FB,), F32)

time: 289 us -> 287 us (level)
    unnamed x44 -> x48, local copies, waits for them, and re-layouts: 6.52 us -> 6.52 us
where the time goes in v7:
time: 287 us; the launch traced here: 286 us
  Pallas kernels  120 us (42%)
  waiting for transfers between devices  77.7 us (27%)
  starting transfers between devices  73 us (25%)
  local copies, waits for them, and re-layouts  7.2 us (3%)
  other arithmetic  6.64 us (2%)
    ppermute x43, waiting for transfers between devices, send(): return lax.ppermute(a, AX, pairs)  65.9 us
    ppermute x43, starting transfers between devices, send(): return lax.ppermute(a, AX, pairs)  57.9 us
    pallas_call x1, Pallas kernels, attn_back(): call(functools.partial(attn_bwd_kernel, pg, 512), outs if pg == 1 else (j...  32 us
    pallas_call x1, Pallas kernels, body(): call(ffn_kernel, (jax.ShapeDtypeStruct((R, D), BF), jax.ShapeDtypeStruct(...  28.7 us
    pallas_call x1, Pallas kernels, body(): call(functools.partial(attn_fwd_kernel, 1024), (jax.ShapeDtypeStruct((4,...  18.1 us
    all_to_all x1, waiting for transfers between devices, body(): attn = lax.all_to_all(o, ('x', 'core'), 0, 0, tiled=True)  11.8 us
    pallas_call x1, Pallas kernels, body(): call(weight_kernel, (jax.ShapeDtypeStruct((4, 4, 240, FB), BF), jax.Shape...  10.4 us
    pallas_call x1, Pallas kernels, body(): call(functools.partial(qkv_kernel, pg), (own_head, head, head, jax.ShapeD...  8.41 us
  transfers between devices with their start and end apart: 47, of which 16 were waited for; matrix products, arithmetic and copies ran while one was open for 2% of the time, Pallas kernels for 31%

profile of v7, /device:TPU:0, one launch (start us, length us, event | category | flops | bytes accessed | tf_op | source)
XLA Modules:
  0.0 285.6 jit_solution(527215039532941603)
XLA Ops:
  1.2 2.6 collective-permute-start.3
  4.4 3.0 %prep.1 = (bf16[208,576]{1,0:T(8,128)(2,1)}, bf16[112,576]{1,0:T(8,128)(2,1)}, bf16[256,384]{1,0:T(8,128)(2,1)}, bf16[96,768]{1,0:T(8,128)(2,1)}) custom-call(s32[14]{0:T(128)} %stack.128.idx, bf16[192,768]{1,0:T(8,128)(2,1)} %wq.1, bf16[192,768]{1,0:T(8,128)(2,1)} %wk.1, bf16[192,768]{1,0:T(8,128)(2,1)} %wv.1, bf16[192,768]{1,0:T(8,128)(2,1)} %w_at.3, ...), custom_call_target="tpu_custom_call" | custom-call | flops 1 | bytes 1 | tf_op jit(solution)/shard_map/prep/pallas_call | solution.py:776
  7.5 3.6 %collective-permute-start.2 = (bf16[112,576]{1,0:T(8,128)(2,1)}, bf16[112,576]{1,0:T(8,128)(2,1)S(1)}, u32[]{:S(2)}, u32[]{:S(2)}) collective-permute-start(bf16[112,576]{1,0:T(8,128)(2,1)} %get-tuple-element.129), channel_id=1, source_target_pairs={{0,3},{1,2},{2,1},{3,0},{4,7},{5,6},{6,5},{7,4},{8,11},{9,10},{10,... | collective-permute-start | bytes 387080 | tf_op jit(solution)/shard_map/ppermute | solution.py:743
  11.8 4.3 %collective-permute-done.2.refs_7_ = bf16[112,576]{1,0:T(8,128)(2,1)S(1)} collective-permute-done((bf16[112,576]{1,0:T(8,128)(2,1)}, bf16[112,576]{1,0:T(8,128)(2,1)S(1)}, u32[]{:S(2)}, u32[]{:S(2)}) %collective-permute-start.2) | collective-permute-done | bytes 129056 | tf_op jit(solution)/shard_map/ppermute | solution.py:743
  16.2 7.7 %collective-permute-done.1.refs_6_ = bf16[112,576]{1,0:T(8,128)(2,1)S(1)} collective-permute-done((bf16[112,576]{1,0:T(8,128)(2,1)}, bf16[112,576]{1,0:T(8,128)(2,1)S(1)}, u32[]{:S(2)}, u32[]{:S(2)}) %collective-permute-start.1) | collective-permute-done | bytes 129056 | tf_op jit(solution)/shard_map/ppermute | solution.py:743
  24.0 1.6 collective-permute-start.5
  25.6 2.5 collective-permute-start.9
  28.1 1.9 collective-permute-start.7
  30.0 5.5 %collective-permute-done.9 = bf16[256,384]{1,0:T(8,128)(2,1)S(1)} collective-permute-done((bf16[256,384]{1,0:T(8,128)(2,1)}, bf16[256,384]{1,0:T(8,128)(2,1)S(1)}, u32[]{:S(2)}, u32[]{:S(2)}) %collective-permute-start.9) | collective-permute-done | bytes 196640 | tf_op jit(solution)/shard_map/ppermute | solution.py:743
  35.5 9.4 %collective-permute-done.8 = bf16[256,384]{1,0:T(8,128)(2,1)S(1)} collective-permute-done((bf16[256,384]{1,0:T(8,128)(2,1)}, bf16[256,384]{1,0:T(8,128)(2,1)S(1)}, u32[]{:S(2)}, u32[]{:S(2)}) %collective-permute-start.8) | collective-permute-done | bytes 196640 | tf_op jit(solution)/shard_map/ppermute | solution.py:743
  45.8 1.6 collective-permute-start.10
  47.3 2.5 collective-permute-start.13
  49.8 1.9 collective-permute-start.11
  51.7 8.4 %qkv.1 = (bf16[2,3,1024,128]{3,2,1,0:T(8,128)(2,1)}, bf16[2,3,1024,128]{3,2,1,0:T(8,128)(2,1)}, bf16[2,3,1024,128]{3,2,1,0:T(8,128)(2,1)}, bf16[4,192,576]{2,1,0:T(8,128)(2,1)}) custom-call(s32[2,4]{1,0:T(2,128)} %lengths.7, s32[14]{0:T(128)} %stack.128.idx, bf16[1,2,256,768]{3,2,1,0:T(8,128)(2,1)} %bitcast.59, bf16[1,2,256,768]{3,2,1,0:T(8,128)(2,1)} %bitcast.62, ...), custom_call_target="tpu_custom_call" | custom-call | flops 1 | bytes 1 | tf_op jit(solution)/shard_map/qkv/pallas_call | solution.py:800
  60.2 1.1 collective-permute-done.12
  61.4 1.5 pad_maximum_fusion.4
  63.7 1.3 collective-permute-start.15
  65.0 18.1 %attn_fwd.1 = (bf16[4,256,384]{2,1,0:T(8,128)(2,1)}, bf16[2,3,1024,128]{3,2,1,0:T(8,128)(2,1)}) custom-call(s32[2,4]{1,0:T(2,128)} %lengths.7, s32[14]{0:T(128)} %stack.128.idx, bf16[2,3,1024,128]{3,2,1,0:T(8,128)(2,1)} %get-tuple-element.153.q_ref, bf16[2,3,1024,128]{3,2,1,0:T(8,128)(2,1)} %get-tuple-element.154.k_ref.refs_1_, ...), custom_call_target="tpu_custom_call" | custom-call | flops 1 | bytes 1 | tf_op jit(solution)/shard_map/attn_fwd/pallas_call | solution.py:813
  83.1 1.0 copy-done.10
  84.2 1.4 collective-permute-start.16
  85.6 3.7 %all-to-all-start = ((bf16[4,256,384]{2,1,0:T(8,128)(2,1)}), bf16[4,256,384]{2,1,0:T(8,128)(2,1)S(1)}, u32[]{:S(2)}, u32[]{:S(2)}) async-start(bf16[4,256,384]{2,1,0:T(8,128)(2,1)} %get-tuple-element.159.refs_3_), calls=%async_computation | async-start | bytes 1572864 | tf_op jit(solution)/shard_map/all_to_all | solution.py:822
  90.1 11.8 %all-to-all-done.attn = bf16[4,256,384]{2,1,0:T(8,128)(2,1)S(1)} async-done(((bf16[4,256,384]{2,1,0:T(8,128)(2,1)}), bf16[4,256,384]{2,1,0:T(8,128)(2,1)S(1)}, u32[]{:S(2)}, u32[]{:S(2)}) %all-to-all-start) | async-done | bytes 786464 | tf_op jit(solution)/shard_map/all_to_all | solution.py:822
  101.9 1.9 collective-permute-start.20
  103.8 2.4 collective-permute-done.20.c2b
  106.2 28.7 %ffn.1 = (bf16[512,768]{1,0:T(8,128)(2,1)}, f32[512,768]{1,0:T(8,128)}, bf16[4,256,384]{2,1,0:T(8,128)(2,1)}, bf16[512,5760]{1,0:T(8,128)(2,1)}, bf16[512,3456]{1,0:T(8,128)(2,1)}, /*index=5*/f32[4,8,576]{2,1,0:T(8,128)}) custom-call(s32[14]{0:T(128)} %stack.128.idx, s32[2,4]{1,0:T(2,128)} %lengths.7, bf16[4,256,384]{2,1,0:T(8,128)(2,1)} %copy-done.7, ...), custom_call_target="tpu_custom_call" | custom-call | flops 1 | bytes 1 | tf_op jit(solution)/shard_map/ffn/pallas_call | solution.py:829
  135.3 3.5 %all-to-all-start.1 = ((bf16[4,256,384]{2,1,0:T(8,128)(2,1)}), bf16[4,256,384]{2,1,0:T(8,128)(2,1)S(1)}, u32[]{:S(2)}, u32[]{:S(2)}) async-start(bf16[4,256,384]{2,1,0:T(8,128)(2,1)} %get-tuple-element.165), calls=%async_computation.1 | async-start | bytes 1572864 | tf_op jit(solution)/shard_map/all_to_all | solution.py:860
  138.8 6.1 %collective-permute-done.21.mate = bf16[512,5760]{1,0:T(8,128)(2,1)} collective-permute-done((bf16[512,5760]{1,0:T(8,128)(2,1)}, bf16[512,5760]{1,0:T(8,128)(2,1)}, u32[]{:S(2)}, u32[]{:S(2)}) %collective-permute-start.21) | collective-permute-done | bytes 5898272 | tf_op jit(solution)/shard_map/ppermute | solution.py:743
  144.9 10.4 %weights.1 = (bf16[4,4,240,384]{3,2,1,0:T(8,128)(2,1)}, f32[4,96,768]{2,1,0:T(8,128)}, bf16[4,96,768]{2,1,0:T(8,128)(2,1)}, bf16[4,96,768]{2,1,0:T(8,128)(2,1)}, bf16[4,96,768]{2,1,0:T(8,128)(2,1)}) custom-call(s32[14]{0:T(128)} %stack.128.idx, bf16[512,3456]{1,0:T(8,128)(2,1)} %get-tuple-element.166.kept, bf16[512,5760]{1,0:T(8,128)(2,1)} %collective-permute-done.21.mate, ...), custom_call_target="tpu_custom_call" | custom-call | flops 1 | bytes 1 | tf_op jit(solution)/shard_map/weights/pallas_call | solution.py:890
  156.2 3.9 %all-to-all-start.2 = ((bf16[4,4,240,384]{3,2,1,0:T(8,128)(2,1)}), bf16[4,4,240,384]{3,2,1,0:T(8,128)(2,1)S(1)}, u32[]{:S(2)}, u32[]{:S(2)}) async-start(bf16[4,4,240,384]{3,2,1,0:T(8,128)(2,1)} %get-tuple-element.172), calls=%async_computation.2 | async-start | bytes 5898240 | tf_op jit(solution)/shard_map/all_to_all | solution.py:903
  160.4 2.6 collective-permute-start.23
  163.0 1.6 collective-permute-start.24
  164.6 32.0 %attn_bwd.1 = (bf16[4,112,576]{2,1,0:T(8,128)(2,1)}, bf16[4,112,576]{2,1,0:T(8,128)(2,1)}, bf16[4,512,768]{2,1,0:T(8,128)(2,1)}) custom-call(s32[2,4]{1,0:T(2,128)} %lengths.7, s32[14]{0:T(128)} %stack.128.idx, bf16[2,3,1024,128]{3,2,1,0:T(8,128)(2,1)} %get-tuple-element.190.refs_0_, bf16[2,3,1024,128]{3,2,1,0:T(8,128)(2,1)} %get-tuple-element.154.k_ref.refs_1_, ...), custom_call_target="tpu_custom_call" | custom-call | flops 1 | bytes 1 | tf_op jit(solution)/shard_map/attn_bwd/pallas_call | solution.py:873
  196.6 1.6 copy-done
  198.2 4.0 %all-to-all-start.3 = ((bf16[4,512,768]{2,1,0:T(8,128)(2,1)}), bf16[4,512,768]{2,1,0:T(8,128)(2,1)S(1)}, u32[]{:S(2)}, u32[]{:S(2)}) async-start(bf16[4,512,768]{2,1,0:T(8,128)(2,1)} %get-tuple-element.222), calls=%async_computation.3 | async-start | bytes 6291456 | tf_op jit(solution)/shard_map/all_to_all | solution.py:909
  202.2 1.8 collective-permute-start.28
  204.0 2.9 %chunks1.1 = (f32[240,384]{1,0:T(8,128)}, bf16[240,384]{1,0:T(8,128)(2,1)}, bf16[240,384]{1,0:T(8,128)(2,1)}, bf16[240,384]{1,0:T(8,128)(2,1)}) custom-call(s32[14]{0:T(128)} %stack.128.idx, bf16[4,4,240,384]{3,2,1,0:T(8,128)(2,1)} %copy-done), custom_call_target="tpu_custom_call" | custom-call | flops 1 | bytes 1 | tf_op jit(solution)/shard_map/chunks1/pallas_call | solution.py:906
  206.9 8.7 %collective-permute-start.25 = (bf16[240,384]{1,0:T(8,128)(2,1)}, bf16[240,384]{1,0:T(8,128)(2,1)S(1)}, u32[]{:S(2)}, u32[]{:S(2)}) collective-permute-start(bf16[240,384]{1,0:T(8,128)(2,1)} %get-tuple-element.187), channel_id=1, source_target_pairs={{0,1},{1,0},{2,3},{3,2},{4,5},{5,4},{6,7},{7,6},{8,9},{9,8},{10,11... | collective-permute-start | bytes 552968 | tf_op jit(solution)/shard_map/ppermute | solution.py:743
  216.4 1.6 collective-permute-start.27
  218.8 2.1 chunksq.1
  220.9 2.8 sums2.1
  223.7 8.5 %collective-permute-done.26.a2 = bf16[240,384]{1,0:T(8,128)(2,1)S(1)} collective-permute-done((bf16[240,384]{1,0:T(8,128)(2,1)}, bf16[240,384]{1,0:T(8,128)(2,1)S(1)}, u32[]{:S(2)}, u32[]{:S(2)}) %collective-permute-start.26) | collective-permute-done | bytes 184352 | tf_op jit(solution)/shard_map/ppermute | solution.py:743
  232.2 1.1 collective-permute-start.29
  233.3 1.5 collective-permute-start.30
  234.7 1.0 collective-permute-start.31
  235.7 2.7 collective-permute-start.32
  238.4 1.0 collective-permute-start.33
  239.4 3.1 %collective-permute-done.29.b1 = bf16[96,768]{1,0:T(8,128)(2,1)S(1)} collective-permute-done((bf16[96,768]{1,0:T(8,128)(2,1)}, bf16[96,768]{1,0:T(8,128)(2,1)S(1)}, u32[]{:S(2)}, u32[]{:S(2)}) %collective-permute-start.29) | collective-permute-done | bytes 147488 | tf_op jit(solution)/shard_map/ppermute | solution.py:743
  242.5 2.3 collective-permute-start.34
  244.7 1.6 collective-permute-done.31.b3
  247.0 2.3 sums.1
  249.3 1.1 collective-permute-done.33.q2
  251.3 1.9 sumsq.1
  253.2 4.5 %collective-permute-done.35 = bf16[432,384]{1,0:T(8,128)(2,1)S(1)} collective-permute-done((bf16[432,384]{1,0:T(8,128)(2,1)}, bf16[432,384]{1,0:T(8,128)(2,1)S(1)}, u32[]{:S(2)}, u32[]{:S(2)}) %collective-permute-start.35) | collective-permute-done | bytes 331808 | tf_op jit(solution)/shard_map/ppermute | solution.py:743
  257.7 1.1 pad_maximum_fusion.2.s1
  258.8 1.1 collective-permute-start.36
  260.0 1.4 collective-permute-start.38
  261.4 6.2 %collective-permute-done.38 = bf16[224,384]{1,0:T(8,128)(2,1)S(1)} collective-permute-done((bf16[224,384]{1,0:T(8,128)(2,1)}, bf16[224,384]{1,0:T(8,128)(2,1)S(1)}, u32[]{:S(2)}, u32[]{:S(2)}) %collective-permute-start.38) | collective-permute-done | bytes 172064 | tf_op jit(solution)/shard_map/ppermute | solution.py:743
  267.5 1.0 pad_maximum_fusion.6.s1
  268.5 3.0 %collective-permute-done.36.r2 = bf16[2,432,384]{2,1,0:T(8,128)(2,1)} collective-permute-done((bf16[2,432,384]{2,1,0:T(8,128)(2,1)S(1)}, bf16[2,432,384]{2,1,0:T(8,128)(2,1)}, u32[]{:S(2)}, u32[]{:S(2)}) %collective-permute-start.36) | collective-permute-done | bytes 663584 | tf_op jit(solution)/shard_map/ppermute | solution.py:743
  271.5 1.1 collective-permute-start.40
  272.7 2.7 fusion
  275.4 4.4 %out_ffn.1 = (f32[192,3072]{1,0:T(8,128)}, f32[192,768]{1,0:T(8,128)}, f32[768,768]{1,0:T(8,128)}) custom-call(s32[14]{0:T(128)} %stack.128.idx, bf16[2,432,384]{2,1,0:T(8,128)(2,1)} %copy-done.8, bf16[2,432,384]{2,1,0:T(8,128)(2,1)} %collective-permute-done.36.r2, bf16[2,432,384]{2,1,0:T(8,128)(2,1)} %copy-done.11, ...), custom_call_target="tpu_custom_call" | custom-call | flops 1 | bytes 1 | tf_op jit(solution)/shard_map/out_ffn/pallas_call | solution.py:933
  280.3 1.5 collective-permute-done.42.c2
  282.6 2.9 %out_qkv.1 = (f32[192,768]{1,0:T(8,128)}, f32[192,768]{1,0:T(8,128)}, f32[192,768]{1,0:T(8,128)}, f32[192]{0:T(256)}, f32[192]{0:T(256)}, /*index=5*/f32[768]{0:...) custom-call(s32[14]{0:T(128)} %stack.128.idx, ...), custom_call_target="tpu_custom_call" | custom-call | flops 1 | bytes 1 | tf_op jit(solution)/shard_map/out_qkv/pallas_call | solution.py:937
  (100 shorter events, 11.0 us)
Async XLA Ops:
  0.7 23.2 %collective-permute-start.4 = (bf16[2,256,768]{2,1,0:T(8,128)(2,1)}, bf16[2,256,768]{2,1,0:T(8,128)(2,1)S(1)}, u32[]{:S(2)}, u32[]{:S(2)}) collective-permute-start(bf16[2,256,768]{2,1,0:T(8,128)(2,1)} %refs_6_.1), channel_id=1, source_target_pairs={{0,4},{1,5},{2,6},{3,7},{4,0},{5,1},{6,2},{7,3},{8,12},{9,13},{10,... | collective-permute-start | bytes 2359304 | tf_op jit(solution)/shard_map/ppermute | solution.py:743
  1.2 22.7 %collective-permute-start.3 = (bf16[2,256,768]{2,1,0:T(8,128)(2,1)}, bf16[2,256,768]{2,1,0:T(8,128)(2,1)S(1)}, u32[]{:S(2)}, u32[]{:S(2)}) collective-permute-start(bf16[2,256,768]{2,1,0:T(8,128)(2,1)} %refs_6_.1), channel_id=1, source_target_pairs={{0,8},{1,9},{2,10},{3,11},{4,12},{5,13},{6,14},{7,15},{8,0},{9,1},... | collective-permute-start | bytes 2359304 | tf_op jit(solution)/shard_map/ppermute | solution.py:743
  7.5 8.7 %collective-permute-start.2 = (bf16[112,576]{1,0:T(8,128)(2,1)}, bf16[112,576]{1,0:T(8,128)(2,1)S(1)}, u32[]{:S(2)}, u32[]{:S(2)}) collective-permute-start(bf16[112,576]{1,0:T(8,128)(2,1)} %get-tuple-element.129), channel_id=1, source_target_pairs={{0,3},{1,2},{2,1},{3,0},{4,7},{5,6},{6,5},{7,4},{8,11},{9,10},{10,... | collective-permute-start | bytes 387080 | tf_op jit(solution)/shard_map/ppermute | solution.py:743
  11.1 12.8 %collective-permute-start.1 = (bf16[112,576]{1,0:T(8,128)(2,1)}, bf16[112,576]{1,0:T(8,128)(2,1)S(1)}, u32[]{:S(2)}, u32[]{:S(2)}) collective-permute-start(bf16[112,576]{1,0:T(8,128)(2,1)} %get-tuple-element.129), channel_id=1, source_target_pairs={{0,2},{1,3},{2,0},{3,1},{4,6},{5,7},{6,4},{7,5},{8,10},{9,11},{10,... | collective-permute-start | bytes 387080 | tf_op jit(solution)/shard_map/ppermute | solution.py:743
  11.1 12.8 %collective-permute-start = (bf16[112,576]{1,0:T(8,128)(2,1)}, bf16[112,576]{1,0:T(8,128)(2,1)S(1)}, u32[]{:S(2)}, u32[]{:S(2)}) collective-permute-start(bf16[112,576]{1,0:T(8,128)(2,1)} %get-tuple-element.129), channel_id=1, source_target_pairs={{0,1},{1,0},{2,3},{3,2},{4,5},{5,4},{6,7},{7,6},{8,9},{9,8},{10,11... | collective-permute-start | bytes 387080 | tf_op jit(solution)/shard_map/ppermute | solution.py:743
  16.2 35.6 %copy-start.13 = (bf16[112,576]{1,0:T(8,128)(2,1)}, bf16[112,576]{1,0:T(8,128)(2,1)S(1)}, u32[]{:S(2)}) copy-start(bf16[112,576]{1,0:T(8,128)(2,1)S(1)} %collective-permute-done.2.refs_7_) | copy-start | bytes 387076
  23.8 27.9 %copy-start.14 = (bf16[112,576]{1,0:T(8,128)(2,1)}, bf16[112,576]{1,0:T(8,128)(2,1)S(1)}, u32[]{:S(2)}) copy-start(bf16[112,576]{1,0:T(8,128)(2,1)S(1)} %collective-permute-done.1.refs_6_) | copy-start | bytes 387076
  23.8 27.9 %copy-start.15 = (bf16[112,576]{1,0:T(8,128)(2,1)}, bf16[112,576]{1,0:T(8,128)(2,1)S(1)}, u32[]{:S(2)}) copy-start(bf16[112,576]{1,0:T(8,128)(2,1)S(1)} %collective-permute-done.refs_5_) | copy-start | bytes 387076
  23.8 27.9 %copy-start.3 = (bf16[2,256,768]{2,1,0:T(8,128)(2,1)}, bf16[2,256,768]{2,1,0:T(8,128)(2,1)S(1)}, u32[]{:S(2)}) copy-start(bf16[2,256,768]{2,1,0:T(8,128)(2,1)S(1)} %collective-permute-done.4.refs_8_) | copy-start | bytes 2359300
  23.9 27.9 %copy-start.4 = (bf16[2,256,768]{2,1,0:T(8,128)(2,1)}, bf16[2,256,768]{2,1,0:T(8,128)(2,1)S(1)}, u32[]{:S(2)}) copy-start(bf16[2,256,768]{2,1,0:T(8,128)(2,1)S(1)} %collective-permute-done.3.refs_7_) | copy-start | bytes 2359300
  23.9 21.1 %collective-permute-start.6 = (bf16[2,256,768]{2,1,0:T(8,128)(2,1)S(1)}, bf16[2,256,768]{2,1,0:T(8,128)(2,1)S(1)}, u32[]{:S(2)}, u32[]{:S(2)}) collective-permute-start(bf16[2,256,768]{2,1,0:T(8,128)(2,1)S(1)} %collective-permute-done.3.refs_7_), channel_id=1, source_target_pairs={{0,4},{1,5},{2,6},{3,7},{4,0},{5,1},{6,2},{7,3},{8,12},{9,13},{10,... | collective-permute-start | bytes 2359304 | tf_op jit(solution)/shard_map/ppermute | solution.py:743
  24.0 20.9 %collective-permute-start.5 = (bf16[3,112,576]{2,1,0:T(8,128)(2,1)S(1)}, bf16[3,112,576]{2,1,0:T(8,128)(2,1)S(1)}, u32[]{:S(2)}, u32[]{:S(2)}) collective-permute-start(bf16[3,112,576]{2,1,0:T(8,128)(2,1)S(1)} %pad_maximum_fusion.5), channel_id=1, source_target_pairs={{0,16},{1,17},{2,18},{3,19},{4,20},{5,21},{6,22},{7,23},{8,24},{9,... | collective-permute-start | bytes 1161224 | tf_op jit(solution)/shard_map/ppermute | solution.py:743
  25.6 9.9 %collective-permute-start.9 = (bf16[256,384]{1,0:T(8,128)(2,1)}, bf16[256,384]{1,0:T(8,128)(2,1)S(1)}, u32[]{:S(2)}, u32[]{:S(2)}) collective-permute-start(bf16[256,384]{1,0:T(8,128)(2,1)} %get-tuple-element.136.sm_own), channel_id=1, source_target_pairs={{0,3},{1,2},{2,1},{3,0},{4,7},{5,6},{6,5},{7,4},{8,11},{9,10},{10,... | collective-permute-start | bytes 589832 | tf_op jit(solution)/shard_map/ppermute | solution.py:743
  28.1 16.8 %collective-permute-start.8 = (bf16[256,384]{1,0:T(8,128)(2,1)}, bf16[256,384]{1,0:T(8,128)(2,1)S(1)}, u32[]{:S(2)}, u32[]{:S(2)}) collective-permute-start(bf16[256,384]{1,0:T(8,128)(2,1)} %get-tuple-element.136.sm_own), channel_id=1, source_target_pairs={{0,2},{1,3},{2,0},{3,1},{4,6},{5,7},{6,4},{7,5},{8,10},{9,11},{10,... | collective-permute-start | bytes 589832 | tf_op jit(solution)/shard_map/ppermute | solution.py:743
  28.1 16.8 %collective-permute-start.7 = (bf16[256,384]{1,0:T(8,128)(2,1)}, bf16[256,384]{1,0:T(8,128)(2,1)S(1)}, u32[]{:S(2)}, u32[]{:S(2)}) collective-permute-start(bf16[256,384]{1,0:T(8,128)(2,1)} %get-tuple-element.136.sm_own), channel_id=1, source_target_pairs={{0,1},{1,0},{2,3},{3,2},{4,5},{5,4},{6,7},{7,6},{8,9},{9,8},{10,11... | collective-permute-start | bytes 589832 | tf_op jit(solution)/shard_map/ppermute | solution.py:743
  44.9 6.8 %copy-start.5 = (bf16[2,256,768]{2,1,0:T(8,128)(2,1)}, bf16[2,256,768]{2,1,0:T(8,128)(2,1)S(1)}, u32[]{:S(2)}) copy-start(bf16[2,256,768]{2,1,0:T(8,128)(2,1)S(1)} %collective-permute-done.6.refs_9_) | copy-start | bytes 2359300
  45.8 15.5 %collective-permute-start.10 = (bf16[3,256,384]{2,1,0:T(8,128)(2,1)S(1)}, bf16[3,256,384]{2,1,0:T(8,128)(2,1)S(1)}, u32[]{:S(2)}, u32[]{:S(2)}) collective-permute-start(bf16[3,256,384]{2,1,0:T(8,128)(2,1)S(1)} %pad_maximum_fusion.3), channel_id=1, source_target_pairs={{0,8},{1,9},{2,10},{3,11},{4,20},{5,21},{6,22},{7,23},{8,0},{9,1},... | collective-permute-start | bytes 1769480 | tf_op jit(solution)/shard_map/ppermute | solution.py:743
  47.3 12.8 %collective-permute-start.13 = (bf16[96,768]{1,0:T(8,128)(2,1)}, bf16[96,768]{1,0:T(8,128)(2,1)}, u32[]{:S(2)}, u32[]{:S(2)}) collective-permute-start(bf16[96,768]{1,0:T(8,128)(2,1)} %get-tuple-element.147), channel_id=1, source_target_pairs={{0,3},{1,2},{2,1},{3,0},{4,7},{5,6},{6,5},{7,4},{8,11},{9,10},{10,... | collective-permute-start | bytes 442376 | tf_op jit(solution)/shard_map/ppermute | solution.py:743
  49.8 11.4 %collective-permute-start.12 = (bf16[96,768]{1,0:T(8,128)(2,1)}, bf16[96,768]{1,0:T(8,128)(2,1)}, u32[]{:S(2)}, u32[]{:S(2)}) collective-permute-start(bf16[96,768]{1,0:T(8,128)(2,1)} %get-tuple-element.147), channel_id=1, source_target_pairs={{0,2},{1,3},{2,0},{3,1},{4,6},{5,7},{6,4},{7,5},{8,10},{9,11},{10,... | collective-permute-start | bytes 442376 | tf_op jit(solution)/shard_map/ppermute | solution.py:743
  49.8 11.4 %collective-permute-start.11 = (bf16[96,768]{1,0:T(8,128)(2,1)}, bf16[96,768]{1,0:T(8,128)(2,1)}, u32[]{:S(2)}, u32[]{:S(2)}) collective-permute-start(bf16[96,768]{1,0:T(8,128)(2,1)} %get-tuple-element.147), channel_id=1, source_target_pairs={{0,1},{1,0},{2,3},{3,2},{4,5},{5,4},{6,7},{7,6},{8,9},{9,8},{10,11... | collective-permute-start | bytes 442376 | tf_op jit(solution)/shard_map/ppermute | solution.py:743
  61.4 27.9 %copy-start.1 = (bf16[2,3,256,384]{3,2,1,0:T(8,128)(2,1)}, bf16[2,3,256,384]{3,2,1,0:T(8,128)(2,1)S(1)}, u32[]{:S(2)}) copy-start(bf16[2,3,256,384]{3,2,1,0:T(8,128)(2,1)S(1)} %pad_maximum_fusion.s1a) | copy-start | bytes 3538948
  62.9 20.2 %collective-permute-start.14 = (bf16[2,3,256,384]{3,2,1,0:T(8,128)(2,1)S(1)}, bf16[2,3,256,384]{3,2,1,0:T(8,128)(2,1)S(1)}, u32[]{:S(2)}, u32[]{:S(2)}) collective-permute-start(bf16[2,3,256,384]{3,2,1,0:T(8,128)(2,1)S(1)} %pad_maximum_fusion.s1a), channel_id=1, source_target_pairs={{0,16},{1,17},{2,18},{3,19},{4,12},{5,13},{6,14},{7,15},{8,24},{9,... | collective-permute-start | bytes 3538952 | tf_op jit(solution)/shard_map/ppermute | solution.py:743
  63.7 19.4 %collective-permute-start.15 = (bf16[3,96,768]{2,1,0:T(8,128)(2,1)S(1)}, bf16[3,96,768]{2,1,0:T(8,128)(2,1)S(1)}, u32[]{:S(2)}, u32[]{:S(2)}) collective-permute-start(bf16[3,96,768]{2,1,0:T(8,128)(2,1)S(1)} %pad_maximum_fusion.4), channel_id=1, source_target_pairs={{0,8},{1,9},{2,10},{3,11},{4,20},{5,21},{6,22},{7,23},{8,0},{9,1},... | collective-permute-start | bytes 1327112 | tf_op jit(solution)/shard_map/ppermute | solution.py:743
  84.2 22.0 %copy-start.2 = (bf16[2,3,96,768]{3,2,1,0:T(8,128)(2,1)}, bf16[2,3,96,768]{3,2,1,0:T(8,128)(2,1)S(1)}, u32[]{:S(2)}) copy-start(bf16[2,3,96,768]{3,2,1,0:T(8,128)(2,1)S(1)} %pad_maximum_fusion.1.s1b) | copy-start | bytes 2654212
  84.2 17.6 %collective-permute-start.16 = (bf16[2,3,96,768]{3,2,1,0:T(8,128)(2,1)S(1)}, bf16[2,3,96,768]{3,2,1,0:T(8,128)(2,1)}, u32[]{:S(2)}, u32[]{:S(2)}) collective-permute-start(bf16[2,3,96,768]{3,2,1,0:T(8,128)(2,1)S(1)} %pad_maximum_fusion.1.s1b), channel_id=1, source_target_pairs={{0,16},{1,17},{2,18},{3,19},{4,12},{5,13},{6,14},{7,15},{8,24},{9,... | collective-permute-start | bytes 2654216 | tf_op jit(solution)/shard_map/ppermute | solution.py:743
  85.6 16.3 %all-to-all-start = ((bf16[4,256,384]{2,1,0:T(8,128)(2,1)}), bf16[4,256,384]{2,1,0:T(8,128)(2,1)S(1)}, u32[]{:S(2)}, u32[]{:S(2)}) async-start(bf16[4,256,384]{2,1,0:T(8,128)(2,1)} %get-tuple-element.159.refs_3_), calls=%async_computation | async-start | bytes 1572864 | tf_op jit(solution)/shard_map/all_to_all | solution.py:822
  89.3 14.5 %collective-permute-start.17 = (bf16[2,3,256,384]{3,2,1,0:T(8,128)(2,1)S(1)}, bf16[2,3,256,384]{3,2,1,0:T(8,128)(2,1)}, u32[]{:S(2)}, u32[]{:S(2)}) collective-permute-start(bf16[2,3,256,384]{3,2,1,0:T(8,128)(2,1)S(1)} %pad_maximum_fusion.s1a), channel_id=1, source_target_pairs={{0,4},{1,5},{2,6},{3,7},{4,0},{5,1},{6,2},{7,3},{8,12},{9,13},{10,... | collective-permute-start | bytes 3538952 | tf_op jit(solution)/shard_map/ppermute | solution.py:743
  89.6 14.2 %collective-permute-start.18 = (bf16[2,3,256,384]{3,2,1,0:T(8,128)(2,1)}, bf16[2,3,256,384]{3,2,1,0:T(8,128)(2,1)}, u32[]{:S(2)}, u32[]{:S(2)}) collective-permute-start(bf16[2,3,256,384]{3,2,1,0:T(8,128)(2,1)} %copy-done.10), channel_id=1, source_target_pairs={{0,4},{1,5},{2,6},{3,7},{4,0},{5,1},{6,2},{7,3},{8,12},{9,13},{10,... | collective-permute-start | bytes 3538952 | tf_op jit(solution)/shard_map/ppermute | solution.py:743
  89.9 13.9 %collective-permute-start.19 = (bf16[2,3,96,768]{3,2,1,0:T(8,128)(2,1)S(1)}, bf16[2,3,96,768]{3,2,1,0:T(8,128)(2,1)}, u32[]{:S(2)}, u32[]{:S(2)}) collective-permute-start(bf16[2,3,96,768]{3,2,1,0:T(8,128)(2,1)S(1)} %pad_maximum_fusion.1.s1b), channel_id=1, source_target_pairs={{0,4},{1,5},{2,6},{3,7},{4,0},{5,1},{6,2},{7,3},{8,12},{9,13},{10,... | collective-permute-start | bytes 2654216 | tf_op jit(solution)/shard_map/ppermute | solution.py:743
  101.9 4.3 %copy-start.7 = (bf16[4,256,384]{2,1,0:T(8,128)(2,1)}, bf16[4,256,384]{2,1,0:T(8,128)(2,1)S(1)}, u32[]{:S(2)}) copy-start(bf16[4,256,384]{2,1,0:T(8,128)(2,1)S(1)} %all-to-all-done.attn) | copy-start | bytes 2359300
  101.9 4.3 %collective-permute-start.20 = (bf16[2,3,96,768]{3,2,1,0:T(8,128)(2,1)}, bf16[2,3,96,768]{3,2,1,0:T(8,128)(2,1)}, u32[]{:S(2)}, u32[]{:S(2)}) collective-permute-start(bf16[2,3,96,768]{3,2,1,0:T(8,128)(2,1)} %collective-permute-done.16.r2b), channel_id=1, source_target_pairs={{0,4},{1,5},{2,6},{3,7},{4,0},{5,1},{6,2},{7,3},{8,12},{9,13},{10,... | collective-permute-start | bytes 2654216 | tf_op jit(solution)/shard_map/ppermute | solution.py:743
  134.9 10.0 %collective-permute-start.21 = (bf16[512,5760]{1,0:T(8,128)(2,1)}, bf16[512,5760]{1,0:T(8,128)(2,1)}, u32[]{:S(2)}, u32[]{:S(2)}) collective-permute-start(bf16[512,5760]{1,0:T(8,128)(2,1)} %get-tuple-element.167.sent), channel_id=1, source_target_pairs={{0,4},{1,5},{2,6},{3,7},{4,0},{5,1},{6,2},{7,3},{8,12},{9,13},{10,... | collective-permute-start | bytes 17694728 | tf_op jit(solution)/shard_map/ppermute | solution.py:743
  135.3 20.0 %all-to-all-start.1 = ((bf16[4,256,384]{2,1,0:T(8,128)(2,1)}), bf16[4,256,384]{2,1,0:T(8,128)(2,1)S(1)}, u32[]{:S(2)}, u32[]{:S(2)}) async-start(bf16[4,256,384]{2,1,0:T(8,128)(2,1)} %get-tuple-element.165), calls=%async_computation.1 | async-start | bytes 1572864 | tf_op jit(solution)/shard_map/all_to_all | solution.py:860
  156.2 40.4 %all-to-all-start.2 = ((bf16[4,4,240,384]{3,2,1,0:T(8,128)(2,1)}), bf16[4,4,240,384]{3,2,1,0:T(8,128)(2,1)S(1)}, u32[]{:S(2)}, u32[]{:S(2)}) async-start(bf16[4,4,240,384]{3,2,1,0:T(8,128)(2,1)} %get-tuple-element.172), calls=%async_computation.2 | async-start | bytes 5898240 | tf_op jit(solution)/shard_map/all_to_all | solution.py:903
  160.1 46.7 %collective-permute-start.22 = (bf16[4,96,768]{2,1,0:T(8,128)(2,1)}, bf16[4,96,768]{2,1,0:T(8,128)(2,1)}, u32[]{:S(2)}, u32[]{:S(2)}) collective-permute-start(bf16[4,96,768]{2,1,0:T(8,128)(2,1)} %get-tuple-element.178), channel_id=1, source_target_pairs={{0,1},{1,0},{2,3},{3,2},{4,5},{5,4},{6,7},{7,6},{8,9},{9,8},{10,11... | collective-permute-start | bytes 1769480 | tf_op jit(solution)/shard_map/ppermute | solution.py:743
  160.4 46.4 %collective-permute-start.23 = (bf16[4,96,768]{2,1,0:T(8,128)(2,1)}, bf16[4,96,768]{2,1,0:T(8,128)(2,1)}, u32[]{:S(2)}, u32[]{:S(2)}) collective-permute-start(bf16[4,96,768]{2,1,0:T(8,128)(2,1)} %get-tuple-element.179), channel_id=1, source_target_pairs={{0,2},{1,3},{2,0},{3,1},{4,6},{5,7},{6,4},{7,5},{8,10},{9,11},{10,... | collective-permute-start | bytes 1769480 | tf_op jit(solution)/shard_map/ppermute | solution.py:743
  163.0 43.8 %collective-permute-start.24 = (bf16[4,96,768]{2,1,0:T(8,128)(2,1)}, bf16[4,96,768]{2,1,0:T(8,128)(2,1)}, u32[]{:S(2)}, u32[]{:S(2)}) collective-permute-start(bf16[4,96,768]{2,1,0:T(8,128)(2,1)} %get-tuple-element.180), channel_id=1, source_target_pairs={{0,3},{1,2},{2,1},{3,0},{4,7},{5,6},{6,5},{7,4},{8,11},{9,10},{10,... | collective-permute-start | bytes 1769480 | tf_op jit(solution)/shard_map/ppermute | solution.py:743
  196.6 1.6 copy-start
  198.2 74.5 %all-to-all-start.3 = ((bf16[4,512,768]{2,1,0:T(8,128)(2,1)}), bf16[4,512,768]{2,1,0:T(8,128)(2,1)S(1)}, u32[]{:S(2)}, u32[]{:S(2)}) async-start(bf16[4,512,768]{2,1,0:T(8,128)(2,1)} %get-tuple-element.222), calls=%async_computation.3 | async-start | bytes 6291456 | tf_op jit(solution)/shard_map/all_to_all | solution.py:909
  202.2 15.8 %collective-permute-start.28 = (bf16[4,112,576]{2,1,0:T(8,128)(2,1)}, bf16[4,112,576]{2,1,0:T(8,128)(2,1)S(1)}, u32[]{:S(2)}, u32[]{:S(2)}) collective-permute-start(bf16[4,112,576]{2,1,0:T(8,128)(2,1)} %get-tuple-element.195), channel_id=1, source_target_pairs={{0,16},{1,17},{2,18},{3,19},{4,20},{5,21},{6,22},{7,23},{8,24},{9,... | collective-permute-start | bytes 1548296 | tf_op jit(solution)/shard_map/ppermute | solution.py:743
  206.9 16.8 %collective-permute-start.25 = (bf16[240,384]{1,0:T(8,128)(2,1)}, bf16[240,384]{1,0:T(8,128)(2,1)S(1)}, u32[]{:S(2)}, u32[]{:S(2)}) collective-permute-start(bf16[240,384]{1,0:T(8,128)(2,1)} %get-tuple-element.187), channel_id=1, source_target_pairs={{0,1},{1,0},{2,3},{3,2},{4,5},{5,4},{6,7},{7,6},{8,9},{9,8},{10,11... | collective-permute-start | bytes 552968 | tf_op jit(solution)/shard_map/ppermute | solution.py:743
  215.6 16.6 %collective-permute-start.26 = (bf16[240,384]{1,0:T(8,128)(2,1)}, bf16[240,384]{1,0:T(8,128)(2,1)S(1)}, u32[]{:S(2)}, u32[]{:S(2)}) collective-permute-start(bf16[240,384]{1,0:T(8,128)(2,1)} %get-tuple-element.188), channel_id=1, source_target_pairs={{0,2},{1,3},{2,0},{3,1},{4,6},{5,7},{6,4},{7,5},{8,10},{9,11},{10,... | collective-permute-start | bytes 552968 | tf_op jit(solution)/shard_map/ppermute | solution.py:743
  216.4 15.8 %collective-permute-start.27 = (bf16[240,384]{1,0:T(8,128)(2,1)}, bf16[240,384]{1,0:T(8,128)(2,1)}, u32[]{:S(2)}, u32[]{:S(2)}) collective-permute-start(bf16[240,384]{1,0:T(8,128)(2,1)} %get-tuple-element.189), channel_id=1, source_target_pairs={{0,3},{1,2},{2,1},{3,0},{4,7},{5,6},{6,5},{7,4},{8,11},{9,10},{10,... | collective-permute-start | bytes 552968 | tf_op jit(solution)/shard_map/ppermute | solution.py:743
  223.7 22.6 %copy-start.19 = (bf16[240,384]{1,0:T(8,128)(2,1)}, bf16[240,384]{1,0:T(8,128)(2,1)S(1)}, u32[]{:S(2)}) copy-start(bf16[240,384]{1,0:T(8,128)(2,1)S(1)} %collective-permute-done.25.a1) | copy-start | bytes 552964
  232.2 14.1 %copy-start.20 = (bf16[240,384]{1,0:T(8,128)(2,1)}, bf16[240,384]{1,0:T(8,128)(2,1)S(1)}, u32[]{:S(2)}) copy-start(bf16[240,384]{1,0:T(8,128)(2,1)S(1)} %collective-permute-done.26.a2) | copy-start | bytes 552964
  232.2 10.3 %collective-permute-start.29 = (bf16[96,768]{1,0:T(8,128)(2,1)}, bf16[96,768]{1,0:T(8,128)(2,1)S(1)}, u32[]{:S(2)}, u32[]{:S(2)}) collective-permute-start(bf16[96,768]{1,0:T(8,128)(2,1)} %get-tuple-element.203), channel_id=1, source_target_pairs={{0,8},{1,9},{2,10},{3,11},{4,12},{5,13},{6,14},{7,15},{8,0},{9,1},... | collective-permute-start | bytes 442376 | tf_op jit(solution)/shard_map/ppermute | solution.py:743
  233.3 11.5 %collective-permute-start.30 = (bf16[96,768]{1,0:T(8,128)(2,1)}, bf16[96,768]{1,0:T(8,128)(2,1)S(1)}, u32[]{:S(2)}, u32[]{:S(2)}) collective-permute-start(bf16[96,768]{1,0:T(8,128)(2,1)} %get-tuple-element.204), channel_id=1, source_target_pairs={{0,16},{1,17},{2,18},{3,19},{4,20},{5,21},{6,22},{7,23},{8,24},{9,... | collective-permute-start | bytes 442376 | tf_op jit(solution)/shard_map/ppermute | solution.py:743
  234.7 11.6 %collective-permute-start.31 = (bf16[96,768]{1,0:T(8,128)(2,1)}, bf16[96,768]{1,0:T(8,128)(2,1)S(1)}, u32[]{:S(2)}, u32[]{:S(2)}) collective-permute-start(bf16[96,768]{1,0:T(8,128)(2,1)} %get-tuple-element.205), channel_id=1, source_target_pairs={{0,24},{1,25},{2,26},{3,27},{4,28},{5,29},{6,30},{7,31},{8,16},{9,... | collective-permute-start | bytes 442376 | tf_op jit(solution)/shard_map/ppermute | solution.py:743
  235.7 13.6 %collective-permute-start.32 = (bf16[112,576]{1,0:T(8,128)(2,1)}, bf16[112,576]{1,0:T(8,128)(2,1)}, u32[]{:S(2)}, u32[]{:S(2)}) collective-permute-start(bf16[112,576]{1,0:T(8,128)(2,1)} %get-tuple-element.206), channel_id=1, source_target_pairs={{0,1},{1,0},{2,3},{3,2},{4,5},{5,4},{6,7},{7,6},{8,9},{9,8},{10,11... | collective-permute-start | bytes 387080 | tf_op jit(solution)/shard_map/ppermute | solution.py:743
  238.4 12.0 %collective-permute-start.33 = (bf16[112,576]{1,0:T(8,128)(2,1)}, bf16[112,576]{1,0:T(8,128)(2,1)}, u32[]{:S(2)}, u32[]{:S(2)}) collective-permute-start(bf16[112,576]{1,0:T(8,128)(2,1)} %get-tuple-element.207), channel_id=1, source_target_pairs={{0,2},{1,3},{2,0},{3,1},{4,6},{5,7},{6,4},{7,5},{8,10},{9,11},{10,... | collective-permute-start | bytes 387080 | tf_op jit(solution)/shard_map/ppermute | solution.py:743
  242.5 3.8 %copy-start.21 = (bf16[96,768]{1,0:T(8,128)(2,1)}, bf16[96,768]{1,0:T(8,128)(2,1)S(1)}, u32[]{:S(2)}) copy-start(bf16[96,768]{1,0:T(8,128)(2,1)S(1)} %collective-permute-done.29.b1) | copy-start | bytes 442372
  242.5 7.9 %collective-permute-start.34 = (bf16[112,576]{1,0:T(8,128)(2,1)}, bf16[112,576]{1,0:T(8,128)(2,1)}, u32[]{:S(2)}, u32[]{:S(2)}) collective-permute-start(bf16[112,576]{1,0:T(8,128)(2,1)} %get-tuple-element.208), channel_id=1, source_target_pairs={{0,3},{1,2},{2,1},{3,0},{4,7},{5,6},{6,5},{7,4},{8,11},{9,10},{10,... | collective-permute-start | bytes 387080 | tf_op jit(solution)/shard_map/ppermute | solution.py:743
  244.7 1.6 copy-start.22
  250.4 7.3 %collective-permute-start.35 = (bf16[432,384]{1,0:T(8,128)(2,1)}, bf16[432,384]{1,0:T(8,128)(2,1)S(1)}, u32[]{:S(2)}, u32[]{:S(2)}) collective-permute-start(bf16[432,384]{1,0:T(8,128)(2,1)} %sums.1), channel_id=1, source_target_pairs={{0,8},{1,9},{2,10},{3,11},{4,20},{5,21},{6,22},{7,23},{8,0},{9,1},... | collective-permute-start | bytes 995336 | tf_op jit(solution)/shard_map/ppermute | solution.py:743
  258.8 12.8 %copy-start.8 = (bf16[2,432,384]{2,1,0:T(8,128)(2,1)}, bf16[2,432,384]{2,1,0:T(8,128)(2,1)S(1)}, u32[]{:S(2)}) copy-start(bf16[2,432,384]{2,1,0:T(8,128)(2,1)S(1)} %pad_maximum_fusion.2.s1) | copy-start | bytes 1990660
  258.8 9.7 %collective-permute-start.37 = (bf16[2,432,384]{2,1,0:T(8,128)(2,1)S(1)}, bf16[2,432,384]{2,1,0:T(8,128)(2,1)S(1)}, u32[]{:S(2)}, u32[]{:S(2)}) collective-permute-start(bf16[2,432,384]{2,1,0:T(8,128)(2,1)S(1)} %pad_maximum_fusion.2.s1), channel_id=1, source_target_pairs={{0,4},{1,5},{2,6},{3,7},{4,0},{5,1},{6,2},{7,3},{8,12},{9,13},{10,... | collective-permute-start | bytes 1990664 | tf_op jit(solution)/shard_map/ppermute | solution.py:743
  258.8 12.7 %collective-permute-start.36 = (bf16[2,432,384]{2,1,0:T(8,128)(2,1)S(1)}, bf16[2,432,384]{2,1,0:T(8,128)(2,1)}, u32[]{:S(2)}, u32[]{:S(2)}) collective-permute-start(bf16[2,432,384]{2,1,0:T(8,128)(2,1)S(1)} %pad_maximum_fusion.2.s1), channel_id=1, source_target_pairs={{0,16},{1,17},{2,18},{3,19},{4,12},{5,13},{6,14},{7,15},{8,24},{9,... | collective-permute-start | bytes 1990664 | tf_op jit(solution)/shard_map/ppermute | solution.py:743
  260.0 7.5 %collective-permute-start.38 = (bf16[224,384]{1,0:T(8,128)(2,1)}, bf16[224,384]{1,0:T(8,128)(2,1)S(1)}, u32[]{:S(2)}, u32[]{:S(2)}) collective-permute-start(bf16[224,384]{1,0:T(8,128)(2,1)} %sumsq.1), channel_id=1, source_target_pairs={{0,8},{1,9},{2,10},{3,11},{4,20},{5,21},{6,22},{7,23},{8,0},{9,1},... | collective-permute-start | bytes 516104 | tf_op jit(solution)/shard_map/ppermute | solution.py:743
  268.5 6.9 %copy-start.9 = (bf16[2,224,384]{2,1,0:T(8,128)(2,1)}, bf16[2,224,384]{2,1,0:T(8,128)(2,1)S(1)}, u32[]{:S(2)}) copy-start(bf16[2,224,384]{2,1,0:T(8,128)(2,1)S(1)} %pad_maximum_fusion.6.s1) | copy-start | bytes 1032196
  268.5 3.0 %copy-start.11 = (bf16[2,432,384]{2,1,0:T(8,128)(2,1)}, bf16[2,432,384]{2,1,0:T(8,128)(2,1)S(1)}, u32[]{:S(2)}) copy-start(bf16[2,432,384]{2,1,0:T(8,128)(2,1)S(1)} %collective-permute-done.37.c1) | copy-start | bytes 1990660
  271.5 3.9 %collective-permute-start.39 = (bf16[2,432,384]{2,1,0:T(8,128)(2,1)}, bf16[2,432,384]{2,1,0:T(8,128)(2,1)}, u32[]{:S(2)}, u32[]{:S(2)}) collective-permute-start(bf16[2,432,384]{2,1,0:T(8,128)(2,1)} %collective-permute-done.36.r2), channel_id=1, source_target_pairs={{0,4},{1,5},{2,6},{3,7},{4,0},{5,1},{6,2},{7,3},{8,12},{9,13},{10,... | collective-permute-start | bytes 1990664 | tf_op jit(solution)/shard_map/ppermute | solution.py:743
  271.5 8.3 %collective-permute-start.40 = (bf16[2,224,384]{2,1,0:T(8,128)(2,1)S(1)}, bf16[2,224,384]{2,1,0:T(8,128)(2,1)}, u32[]{:S(2)}, u32[]{:S(2)}) collective-permute-start(bf16[2,224,384]{2,1,0:T(8,128)(2,1)S(1)} %pad_maximum_fusion.6.s1), channel_id=1, source_target_pairs={{0,16},{1,17},{2,18},{3,19},{4,12},{5,13},{6,14},{7,15},{8,24},{9,... | collective-permute-start | bytes 1032200 | tf_op jit(solution)/shard_map/ppermute | solution.py:743
  275.4 4.9 %collective-permute-start.41 = (bf16[2,224,384]{2,1,0:T(8,128)(2,1)S(1)}, bf16[2,224,384]{2,1,0:T(8,128)(2,1)S(1)}, u32[]{:S(2)}, u32[]{:S(2)}) collective-permute-start(bf16[2,224,384]{2,1,0:T(8,128)(2,1)S(1)} %pad_maximum_fusion.6.s1), channel_id=1, source_target_pairs={{0,4},{1,5},{2,6},{3,7},{4,0},{5,1},{6,2},{7,3},{8,12},{9,13},{10,... | collective-permute-start | bytes 1032200 | tf_op jit(solution)/shard_map/ppermute | solution.py:743
  279.8 2.0 collective-permute-start.42
  (7 other events, 6.4 us)
